TPU v7x, 256 devices: a whole 4x4x8 slice. The times are simulated.
256 devices in a mesh: row: 8 (over x, y_hi), col: 32 (over y_lo, z, core).
Axes of the slice: x: 4, y: 4 (y_hi: 2, y_lo: 2; y = y_hi * 2 + y_lo), z: 8, core: 2. Of those that a mesh axis runs over, the one named last changes fastest.
Arguments:
- jacobian: bfloat16 [1024, 131072], P('row', 'col'), may hold values from -6 to 6
- cov_rows: bfloat16 [512, 131072], P('row', 'col'), may hold values from -6 to 9, as said below
- sens_carry: bfloat16 [1024, 131072], P('row', 'col'), may hold values from -6 to 6
Outputs:
- sensitivity: bfloat16 [1024, 131072], P('row', 'col')
- innovation: float32 [1024, 1024], P('row', 'col')
Inputs may be any that keep to these rules, and one draw needn't show every extreme that they name: cov_rows row k holds parameter k's prior cross-terms with every parameter; no symmetry or definiteness of these rows is promised.
All inputs are finite; a program needn't handle non-finite values.
Results may differ from a plain program's by a relative error of at most 0.0031.
Values may be sent and summed in bfloat16 or wider, within the bound.
No kernel may reach another device: no remote copies, remote signals or barrier semaphores. Data moves between devices by JAX's collectives and lax.ppermute only.
A program may use at most 64 MiB of HBM per device.

v0:
```python
import math

import jax
import jax.numpy as jnp
from jax import lax
from jax.sharding import PartitionSpec as P

PARAMS = 131072
PANEL = 256
PANELS = 2


def spread(value, axis, root):
    mine = lax.axis_index(axis) == root
    return lax.psum(jnp.where(mine, value, jnp.zeros_like(value)), axis)


def body(jacobian, cov_rows, sens_carry):
    tgt_dev = jacobian.shape[0]
    width = PANELS * PANEL
    own_panel = jacobian[:, :width]
    jac_panel = spread(own_panel, "col", 0)
    summed = jnp.dot(
        jac_panel,
        lax.all_gather(cov_rows, "row", axis=0, tiled=True),
        preferred_element_type=jnp.float32,
    )
    sensitivity = (sens_carry.astype(jnp.float32) + summed * (1.0 / math.sqrt(width))).astype(
        jnp.bfloat16
    )
    row_count = lax.axis_size("row")
    col_count = lax.axis_size("col")
    targets = tgt_dev * row_count
    sens_all, jac_all = (
        lax.all_to_all(sensitivity, "row", split_axis=1, concat_axis=0, tiled=True),
        lax.all_to_all(jacobian, "row", split_axis=1, concat_axis=0, tiled=True),
    )
    sens_blocks = sens_all.reshape(row_count, tgt_dev, sens_all.shape[1])
    jac_blocks = jac_all.reshape(col_count, targets // col_count, jac_all.shape[1])
    partial_value = jnp.einsum(
        "rik,cjk->rcij", sens_blocks, jac_blocks, preferred_element_type=jnp.float32
    )
    partial_value = partial_value.reshape(row_count * col_count, tgt_dev * (targets // col_count))
    reduced = lax.psum_scatter(partial_value, ("row", "col"), scatter_dimension=0, tiled=True)
    reduced = reduced.reshape(tgt_dev, targets // col_count)
    innovation = reduced * (1.0 / math.sqrt(PARAMS))
    return (sensitivity, innovation)


def solution(mesh):
    return jax.shard_map(
        body,
        mesh=mesh,
        in_specs=(P("row", "col"), P("row", "col"), P("row", "col")),
        out_specs=(P("row", "col"), P("row", "col")),
        check_vma=False,
    )
```

profile of v0, /device:TPU:4, one launch (start us, length us, event | category | flops | bytes accessed | tf_op | source)
XLA Modules:
  0.0 542.6 jit_solution(16983160504591682633)
XLA Ops:
  8.0 0.0 copy-start.1
  8.0 0.0 all-reduce.4.cloned.1.call-start
  8.1 1.7 slice_select_fusion
  9.7 0.0 all-reduce.4.cloned.1.call-update
  9.7 0.0 all-gather.2.cloned.1.call-start
  9.8 0.5 all-gather.2.cloned.1.call-update
  10.3 2.3 copy.20
  12.6 7.4 %all-to-all-start.1 = ((bf16[128,8,512]{2,0,1:T(8,128)(2,1)}), bf16[128,8,512]{2,0,1:T(8,128)(2,1)S(1)}, u32[]{:S(2)}, u32[]{:S(2)}) async-start(bf16[128,8,512]{2,0,1:T(8,128)(2,1)} %bitcast.25), calls=%async_computation.1 | async-start | bytes 2097152 | tf_op jit(solution)/shard_map/all_to_all | solution.py:36
  20.1 0.0 all-reduce.6.cloned.1.call-start
  20.1 195.5 %all-reduce.4.cloned.1.call-done = bf16[128,512]{1,0:T(8,128)(2,1)} async-done(((bf16[128,512]{1,0:T(8,128)(2,1)}), bf16[128,512]{1,0:T(8,128)(2,1)}) %all-reduce.4.cloned.1.call-update) | async-done | bytes 131088 | tf_op jit(solution)/shard_map/psum | solution.py:15
  215.6 3.0 fusion.1
  218.6 0.0 copy-start
  218.6 0.1 copy.21
  218.7 0.0 all-to-all-done.1
  218.7 22.2 %all_to_all.32 = bf16[128,8,512]{2,0,1:T(8,128)(2,1)S(1)} all-to-all(bf16[128,8,512]{2,0,1:T(8,128)(2,1)S(1)} %bitcast.28), channel_id=1, replica_groups=mesh['row'=8,'col'=32] {'row'}, dimensions={1} | all-to-all | bytes 2097152 | tf_op jit(solution)/shard_map/all_to_all | solution.py:35
  240.9 3.2 convolution_bitcast_fusion
  244.1 0.0 copy-done
  244.1 10.4 %copy.13 = f32[8,32,128,32]{3,2,1,0:T(8,128)} copy(f32[8,32,128,32]{2,3,1,0:T(8,128)} %convolution_bitcast_fusion) | data formatting | bytes 8388608 | tf_op jit(solution)/shard_map/rik,cjk->rcij/transpose | solution.py:40
  254.5 13.0 %reshape.23 = f32[256,4096]{1,0:T(8,128)} reshape(f32[8,32,128,32]{3,2,1,0:T(8,128)} %copy.13) | data formatting | bytes 8388608 | tf_op jit(solution)/shard_map/reshape | solution.py:43
  267.5 0.0 all-reduce.6.cloned.1.call-update
  267.6 265.9 %all-reduce.6.cloned.1.call-done = f32[256,4096]{1,0:T(8,128)} async-done(((f32[256,4096]{1,0:T(8,128)}), f32[256,4096]{1,0:T(8,128)}) %all-reduce.6.cloned.1.call-update) | async-done | bytes 4194320
  533.5 1.0 fusion.3
  534.4 0.1 mul.19
  534.5 0.7 copy.14
  (2 shorter events, 0.0 us)
Async XLA Ops:
  8.0 207.6 %copy-start.1 = (bf16[128,4096]{1,0:T(8,128)(2,1)S(1)}, bf16[128,4096]{1,0:T(8,128)(2,1)}, u32[]{:S(2)}) copy-start(bf16[128,4096]{1,0:T(8,128)(2,1)} %param.5) | copy-start | bytes 3145732
  8.0 207.6 %all-reduce.4.cloned.1.call-start = ((), (), s32[]{:S(2)}) async-start(), calls=%async_computation.2 | async-start | bytes 262144 | tf_op jit(solution)/shard_map/psum | solution.py:15
  9.7 205.8 %all-gather.2.cloned.1.call-start = ((), (), s32[]{:S(2)}) async-start(), calls=%async_computation.3 | async-start | bytes 4718592 | tf_op jit(solution)/shard_map/all_gather | solution.py:25
  12.6 206.1 %all-to-all-start.1 = ((bf16[128,8,512]{2,0,1:T(8,128)(2,1)}), bf16[128,8,512]{2,0,1:T(8,128)(2,1)S(1)}, u32[]{:S(2)}, u32[]{:S(2)}) async-start(bf16[128,8,512]{2,0,1:T(8,128)(2,1)} %bitcast.25), calls=%async_computation.1 | async-start | bytes 2097152 | tf_op jit(solution)/shard_map/all_to_all | solution.py:36
  20.1 513.4 %all-reduce.6.cloned.1.call-start = ((), (), s32[]{:S(2)}) async-start(), calls=%async_computation.4 | async-start | bytes 8388608
  218.6 25.5 %copy-start = (bf16[128,4096]{1,0:T(8,128)(2,1)}, bf16[128,4096]{1,0:T(8,128)(2,1)S(1)}, u32[]{:S(2)}) copy-start(bf16[128,4096]{1,0:T(8,128)(2,1)S(1)} %fusion.1) | copy-start | bytes 3145732
Sparse Core Ops, SparseCore 0:
  12.0 203.4 all-reduce.3
  267.7 265.7 all-reduce.5
Sparse Core Ops, SparseCore 1:
  13.2 80.4 all-gather.1
where the time goes:
time: 543 us
  waiting for transfers between devices  462 us (85%)
  local copies, waits for them, and re-layouts  26.6 us (5%)
  blocking collectives  22.2 us (4%)
  between operations  15.5 us (3%)
  starting transfers between devices  7.52 us (1%)
  matrix products  6.26 us (1%)
    unnamed x4, waiting for transfers between devices  266 us
    psum x1, waiting for transfers between devices, spread(): return lax.psum(jnp.where(mine, value, jnp.zeros_like(value)), axis)  196 us
    all_to_all x1, blocking collectives, body(): lax.all_to_all(sensitivity, 'row', split_axis=1, concat_axis=0, tiled=True)  22.2 us
    reshape x1, local copies, waits for them, and re-layouts, body(): partial_value.reshape(row_count * col_count, tgt_dev * (targets // col_co...  13 us
  transfers between devices with their start and end apart: 4, of which 2 were waited for; matrix products, arithmetic and copies ran while one was open for 1% of the time, Pallas kernels for 0%

commit v1 on v0

v1 whole, which is shorter than its diff:
```python
import math

import jax
import jax.numpy as jnp
from jax import lax
from jax.experimental import pallas as pl
from jax.experimental.pallas import tpu as pltpu
from jax.sharding import Mesh, PartitionSpec as P

PARAMS = 131072
WIDTH = 512
X, H, L, Z, C = 4, 2, 2, 8, 2
AXES = ("x", "h", "l", "z", "c")
ROWS = X * H
SHIFTS = [(dx, dh) for dx in range(X) for dh in range(H)]
ANY = pl.BlockSpec(memory_space=pl.ANY)
VMEM = pl.BlockSpec(memory_space=pltpu.VMEM)
BF16, F32 = jnp.bfloat16, jnp.float32


def pairs(shift, back=False):
    dx, dh = shift
    there = [(x * H + h, ((x + dx) % X) * H + (h ^ dh)) for x in range(X) for h in range(H)]
    return [(b, a) for a, b in there] if back else there


def target(shift):
    dx, dh = shift
    return lax.rem(lax.axis_index("x") + dx, X) * H + lax.rem(lax.axis_index("h") + dh, H)


def source(shift):
    dx, dh = shift
    return lax.rem(lax.axis_index("x") + X - dx, X) * H + lax.rem(lax.axis_index("h") + dh, H)


def call(kernel, outs, ins, out_spec, in_spec, scratch=(), flops=0, nbytes=0):
    return pl.pallas_call(
        kernel,
        out_shape=outs,
        in_specs=[in_spec] * len(ins),
        out_specs=jax.tree.map(lambda _: out_spec, outs),
        scratch_shapes=list(scratch),
        cost_estimate=pl.CostEstimate(flops=flops, bytes_accessed=nbytes, transcendentals=0),
        compiler_params=pltpu.CompilerParams(vmem_limit_bytes=40 * 2**20),
    )(*ins)


def pack_kernel(jac, carry, cov, *rest):
    outs, sems = rest[:ROWS], rest[ROWS]
    copies = []
    for d, shift in enumerate(SHIFTS):
        columns = pl.ds(pl.multiple_of(target(shift) * 512, 512), 512)
        for part, (ref, first, size) in enumerate(((jac, 0, 128), (carry, 128, 128), (cov, 256, 64))):
            copies.append(
                pltpu.make_async_copy(
                    ref.at[:, columns], outs[d].at[pl.ds(first, size), :], sems.at[d * 3 + part]
                )
            )
            copies[-1].start()
    for copy in copies:
        copy.wait()


def split_kernel(*refs):
    pieces, keep, give = refs[:ROWS], refs[ROWS], refs[ROWS + 1]
    core = lax.axis_index("c")
    for d, shift in enumerate(SHIFTS):
        row = source(shift) * 64
        for half in range(2):
            to = pl.ds(pl.multiple_of(row + half * 32, 32), 32)
            mine = pl.ds(pl.multiple_of(half * 64 + core * 32, 32), 32)
            other = pl.ds(pl.multiple_of(half * 64 + (1 - core) * 32, 32), 32)
            keep[to, :] = pieces[d][mine, :]
            give[to, :] = pieces[d][other, :]


def sens_kernel(*refs):
    pieces, panels = refs[:ROWS], refs[ROWS : 2 * ROWS]
    outs, whole, cov = refs[2 * ROWS : 3 * ROWS], refs[3 * ROWS], refs[3 * ROWS + 1]
    for d, shift in enumerate(SHIFTS):
        cov[pl.ds(pl.multiple_of(source(shift) * 64, 64), 64), :] = pieces[d][256:320, :]
    for d in range(ROWS):
        product = jnp.dot(panels[d][...], cov[...], preferred_element_type=F32)
        value = pieces[d][128:256, :].astype(F32) + product * (1.0 / math.sqrt(WIDTH))
        value = value.astype(BF16)
        outs[d][...] = value
        whole[d * 128 : (d + 1) * 128, :] = value


def innov_kernel(keep, got, sens, sens_got, own, *outs):
    dims = (((1,), (1,)), ((), ()))
    for block in range(4):
        rows = pl.ds(block * 128, 128)
        value = lax.dot_general(keep[rows, :], sens[...], dims, preferred_element_type=F32)
        value += lax.dot_general(got[rows, :], sens_got[...], dims, preferred_element_type=F32)
        own[rows, :] = value[:, :128]
        for d in range(1, ROWS):
            outs[d - 1][rows, :] = value[:, d * 128 : (d + 1) * 128].astype(BF16)


def sum_kernel(own, *refs):
    out = refs[-1]
    total = own[...]
    for ref in refs[:-1]:
        total += ref[...].astype(F32)
    out[...] = total.astype(BF16)


def final_kernel(got, out):
    total = got[0].astype(F32)
    for k in range(1, L * Z):
        total += got[k].astype(F32)
    out[...] = total * (1.0 / math.sqrt(PARAMS))


def assemble_kernel(*refs):
    pieces, out, sems = refs[:ROWS], refs[ROWS], refs[ROWS + 1]
    copies = []
    for d, shift in enumerate(SHIFTS):
        columns = pl.ds(pl.multiple_of(target(shift) * 512, 512), 512)
        copies.append(pltpu.make_async_copy(pieces[d], out.at[:, columns], sems.at[d]))
        copies[-1].start()
    for copy in copies:
        copy.wait()


FIRST = [[((0, 0), (0, 4))], [((0, 0), (1, 2))], [((0, 0), (1, 6))]]
SECOND = [
    [((0, 0), (0, 1)), ((0, 4), (0, 3)), ((1, 2), (1, 1)), ((1, 6), (1, 5))],
    [((0, 0), (0, 7)), ((0, 4), (0, 5)), ((1, 2), (1, 3)), ((1, 6), (1, 7))],
    [((0, 0), (1, 0)), ((0, 4), (1, 4)), ((1, 2), (0, 2)), ((1, 6), (0, 6))],
]


def spread_panel(value):
    at = lax.axis_index("l") * Z + lax.axis_index("z")
    for stage in (FIRST, SECOND):
        received = []
        for group in stage:
            perm = [(a[0] * Z + a[1], b[0] * Z + b[1]) for a, b in group]
            hit = jnp.zeros((), jnp.bool_)
            for _, b in perm:
                hit = hit | (at == b)
            received.append((hit, lax.ppermute(value, ("l", "z"), perm)))
        for hit, got in received:
            value = jnp.where(hit, got, value)
    got = lax.ppermute(value, "c", [(0, 1)])
    return jnp.where(lax.axis_index("c") == 1, got, value)


def body(jacobian, cov_rows, sens_carry):
    shape = jax.ShapeDtypeStruct
    panel = spread_panel(jacobian[:, :WIDTH])
    packed = call(
        pack_kernel,
        [shape((320, 512), BF16)] * ROWS,
        (jacobian, sens_carry, cov_rows),
        ANY,
        ANY,
        scratch=[pltpu.SemaphoreType.DMA((3 * ROWS,))],
        nbytes=5 * 2**20,
    )
    pieces = [packed[0]] + [
        lax.ppermute(packed[d], ("x", "h"), pairs(SHIFTS[d])) for d in range(1, ROWS)
    ]
    keep, give = call(
        split_kernel, [shape((512, 512), BF16)] * 2, pieces, VMEM, VMEM, nbytes=4 * 2**20
    )
    got = lax.ppermute(give, "c", [(0, 1), (1, 0)])
    panels = [panel] + [
        lax.ppermute(panel, ("x", "h"), pairs(SHIFTS[d])) for d in range(1, ROWS)
    ]
    *sens, whole = call(
        sens_kernel,
        [shape((128, 512), BF16)] * ROWS + [shape((1024, 512), BF16)],
        (*pieces, *panels),
        VMEM,
        VMEM,
        scratch=[pltpu.VMEM((512, 512), BF16)],
        flops=2 * 1024 * 512 * 512,
        nbytes=6 * 2**20,
    )
    whole_got = lax.ppermute(whole, "c", [(0, 1), (1, 0)])
    own, *parts = call(
        innov_kernel,
        [shape((512, 128), F32)] + [shape((512, 128), BF16)] * (ROWS - 1),
        (keep, got, whole, whole_got),
        VMEM,
        VMEM,
        flops=2 * 512 * 1024 * 1024,
        nbytes=4 * 2**20,
    )
    parts_got = [
        lax.ppermute(parts[d - 1], ("x", "h"), pairs(SHIFTS[d], True)) for d in range(1, ROWS)
    ]
    summed = call(
        sum_kernel, shape((512, 128), BF16), (own, *parts_got), VMEM, VMEM, nbytes=2**20
    )
    sens_got = [sens[0]] + [
        lax.ppermute(sens[d], ("x", "h"), pairs(SHIFTS[d], True)) for d in range(1, ROWS)
    ]
    shared = lax.all_to_all(
        summed.reshape(L * Z, 32, 128), ("l", "z"), split_axis=0, concat_axis=0, tiled=True
    )
    innovation = call(final_kernel, shape((32, 128), F32), (shared,), VMEM, VMEM, nbytes=2**17)
    sensitivity = call(
        assemble_kernel,
        shape((128, 4096), BF16),
        sens_got,
        ANY,
        ANY,
        scratch=[pltpu.SemaphoreType.DMA((ROWS,))],
        nbytes=2 * 2**20,
    )
    return (sensitivity, innovation.T)


def solution(mesh):
    fine = Mesh(mesh.devices.reshape(X, H, L, Z, C), AXES)
    spec = P(("x", "h"), ("l", "z", "c"))
    return jax.shard_map(
        body, mesh=fine, in_specs=(spec,) * 3, out_specs=(spec,) * 2, check_vma=False
    )
```

time: 543 us -> 140 us (0.26)
  waiting for transfers between devices: 462 us -> 47.5 us
  starting transfers between devices: 7.52 us -> 77.7 us
  local copies, waits for them, and re-layouts: 26.6 us -> 3.42 us
  blocking collectives: 22.2 us -> 0 us
  between operations: 15.5 us -> 0.84 us
  Pallas kernels: 0 us -> 7.19 us
  matrix products: 6.26 us -> 0 us
    unnamed x4 -> x0, waiting for transfers between devices: 266 us -> none
    psum x1 -> x0, waiting for transfers between devices: 196 us -> none  [spread(): return lax.psum(jnp.where(mine, value, jnp.zeros_like(value)), axis)]
    ppermute x0 -> x37, starting transfers between devices: none -> 69.9 us  [the longest x6 15.7 us: spread_panel(): received.append((hit, lax.ppermute(value, ('l', 'z'), perm)))]
    ppermute x0 -> x37, waiting for transfers between devices: none -> 47.5 us  [the longest x7 22.4 us: body(): lax.ppermute(packed[d], ('x', 'h'), pairs(SHIFTS[d]))]
    all_to_all x1 -> x0, blocking collectives: 22.2 us -> none  [body(): lax.all_to_all(sensitivity, 'row', split_axis=1, concat_axis=0, tiled=True)]
    reshape x1 -> x0, local copies, waits for them, and re-layouts: 13 us -> none  [body(): partial_value.reshape(row_count * col_count, tgt_dev * (targets // col_co...]
    transpose x1 -> x0, local copies, waits for them, and re-layouts: 10.4 us -> none  [body(): jnp.einsum('rik,cjk->rcij', sens_blocks, jac_blocks, preferred_element_ty...]
    pallas_call x0 -> x7, Pallas kernels: none -> 7.19 us  [call(): pl.pallas_call(kernel, out_shape=outs, in_specs=[in_spec] * len(ins), out...]
  transfers between devices with their start and end apart: 4 -> 38, of which waited for: 2 -> 17; matrix products, arithmetic and copies ran while one was open for 1% -> 0% of each run, Pallas kernels for 0% -> 2%
where the time goes in v1:
time: 140 us; the launch traced here: 138 us
  starting transfers between devices  77.7 us (56%)
  waiting for transfers between devices  47.5 us (34%)
  Pallas kernels  7.19 us (5%)
  local copies, waits for them, and re-layouts  3.42 us (2%)
    ppermute x7, waiting for transfers between devices, body(): lax.ppermute(packed[d], ('x', 'h'), pairs(SHIFTS[d]))  22.4 us
    ppermute x6, starting transfers between devices, spread_panel(): received.append((hit, lax.ppermute(value, ('l', 'z'), perm)))  15.7 us
    ppermute x7, starting transfers between devices, body(): lax.ppermute(parts[d - 1], ('x', 'h'), pairs(SHIFTS[d], True))  14.2 us
    ppermute x7, starting transfers between devices, body(): lax.ppermute(sens[d], ('x', 'h'), pairs(SHIFTS[d], True))  13.1 us
    ppermute x7, starting transfers between devices, body(): lax.ppermute(packed[d], ('x', 'h'), pairs(SHIFTS[d]))  12.5 us
    ppermute x7, starting transfers between devices, body(): lax.ppermute(panel, ('x', 'h'), pairs(SHIFTS[d]))  12.3 us
    all_to_all x1, starting transfers between devices, body(): lax.all_to_all(summed.reshape(L * Z, 32, 128), ('l', 'z'), split_axis=0,...  7.75 us
    pallas_call x7, Pallas kernels, call(): pl.pallas_call(kernel, out_shape=outs, in_specs=[in_spec] * len(ins), out...  7.19 us
  transfers between devices with their start and end apart: 38, of which 17 were waited for; matrix products, arithmetic and copies ran while one was open for 0% of the time, Pallas kernels for 2%

profile of v1, /device:TPU:4, one launch (start us, length us, event | category | flops | bytes accessed | tf_op | source)
XLA Modules:
  0.0 137.6 jit_solution(15177392145179307129)
XLA Ops:
  1.6 9.2 %collective-permute-start.7 = (bf16[128,512]{1,0:T(8,128)(2,1)S(1)}, bf16[128,512]{1,0:T(8,128)(2,1)S(1)}, u32[]{:S(2)}, u32[]{:S(2)}) collective-permute-start(bf16[128,512]{1,0:T(8,128)(2,1)S(1)} %slice.3), channel_id=1, source_target_pairs={{0,28},{1,29},{32,60},{33,61},{64,92},{65,93},{96,124},{97,125},{1... | collective-permute-start | bytes 393224 | tf_op jit(solution)/shard_map/ppermute | solution.py:145
  26.1 3.0 %collective-permute-start = (bf16[320,512]{1,0:T(8,128)(2,1)}, bf16[320,512]{1,0:T(8,128)(2,1)S(1)}, u32[]{:S(2)}, u32[]{:S(2)}) collective-permute-start(bf16[320,512]{1,0:T(8,128)(2,1)} %get-tuple-element.30), channel_id=1, source_target_pairs={{0,32},{32,0},{64,96},{96,64},{128,160},{160,128},{192,224},{224,1... | collective-permute-start | bytes 983048 | tf_op jit(solution)/shard_map/ppermute | solution.py:165
  34.1 3.6 %collective-permute-done.refs_1_ = bf16[320,512]{1,0:T(8,128)(2,1)S(1)} collective-permute-done((bf16[320,512]{1,0:T(8,128)(2,1)}, bf16[320,512]{1,0:T(8,128)(2,1)S(1)}, u32[]{:S(2)}, u32[]{:S(2)}) %collective-permute-start) | collective-permute-done | bytes 327712 | tf_op jit(solution)/shard_map/ppermute | solution.py:165
  40.0 2.7 %collective-permute-start.5 = (bf16[320,512]{1,0:T(8,128)(2,1)S(1)}, bf16[320,512]{1,0:T(8,128)(2,1)S(1)}, u32[]{:S(2)}, u32[]{:S(2)}) collective-permute-start(bf16[320,512]{1,0:T(8,128)(2,1)S(1)} %get-tuple-element.35), channel_id=1, source_target_pairs={{0,192},{32,224},{64,0},{96,32},{128,64},{160,96},{192,128},{224,1... | collective-permute-start | bytes 983048 | tf_op jit(solution)/shard_map/ppermute | solution.py:165
  44.2 2.8 %collective-permute-done.2.refs_3_ = bf16[320,512]{1,0:T(8,128)(2,1)S(1)} collective-permute-done((bf16[320,512]{1,0:T(8,128)(2,1)S(1)}, bf16[320,512]{1,0:T(8,128)(2,1)S(1)}, u32[]{:S(2)}, u32[]{:S(2)}) %collective-permute-start.2) | collective-permute-done | bytes 327712 | tf_op jit(solution)/shard_map/ppermute | solution.py:165
  47.0 2.9 %collective-permute-start.14 = (bf16[128,512]{1,0:T(8,128)(2,1)S(1)}, bf16[128,512]{1,0:T(8,128)(2,1)S(1)}, u32[]{:S(2)}, u32[]{:S(2)}) collective-permute-start(bf16[128,512]{1,0:T(8,128)(2,1)S(1)} %broadcast_select_fusion.refs_8_), channel_id=1, source_target_pairs={{0,32},{32,0},{64,96},{96,64},{128,160},{160,128},{192,224},{224,1... | collective-permute-start | bytes 393224 | tf_op jit(solution)/shard_map/ppermute | solution.py:172
  49.9 4.3 %collective-permute-done.3.refs_4_ = bf16[320,512]{1,0:T(8,128)(2,1)S(1)} collective-permute-done((bf16[320,512]{1,0:T(8,128)(2,1)S(1)}, bf16[320,512]{1,0:T(8,128)(2,1)S(1)}, u32[]{:S(2)}, u32[]{:S(2)}) %collective-permute-start.3) | collective-permute-done | bytes 327712 | tf_op jit(solution)/shard_map/ppermute | solution.py:165
  54.2 7.5 %collective-permute-done.4.refs_5_ = bf16[320,512]{1,0:T(8,128)(2,1)S(1)} collective-permute-done((bf16[320,512]{1,0:T(8,128)(2,1)S(1)}, bf16[320,512]{1,0:T(8,128)(2,1)S(1)}, u32[]{:S(2)}, u32[]{:S(2)}) %collective-permute-start.4) | collective-permute-done | bytes 327712 | tf_op jit(solution)/shard_map/ppermute | solution.py:165
  61.6 2.9 %collective-permute-start.17 = (bf16[128,512]{1,0:T(8,128)(2,1)S(1)}, bf16[128,512]{1,0:T(8,128)(2,1)S(1)}, u32[]{:S(2)}, u32[]{:S(2)}) collective-permute-start(bf16[128,512]{1,0:T(8,128)(2,1)S(1)} %broadcast_select_fusion.refs_8_), channel_id=1, source_target_pairs={{0,128},{32,160},{64,192},{96,224},{128,0},{160,32},{192,64},{224,... | collective-permute-start | bytes 393224 | tf_op jit(solution)/shard_map/ppermute | solution.py:172
  64.5 3.6 %collective-permute-done.6.refs_7_ = bf16[320,512]{1,0:T(8,128)(2,1)S(1)} collective-permute-done((bf16[320,512]{1,0:T(8,128)(2,1)S(1)}, bf16[320,512]{1,0:T(8,128)(2,1)S(1)}, u32[]{:S(2)}, u32[]{:S(2)}) %collective-permute-start.6) | collective-permute-done | bytes 327712 | tf_op jit(solution)/shard_map/ppermute | solution.py:165
  70.6 4.0 %collective-permute-start.20 = (bf16[128,512]{1,0:T(8,128)(2,1)S(1)}, bf16[128,512]{1,0:T(8,128)(2,1)S(1)}, u32[]{:S(2)}, u32[]{:S(2)}) collective-permute-start(bf16[128,512]{1,0:T(8,128)(2,1)S(1)} %broadcast_select_fusion.refs_8_), channel_id=1, source_target_pairs={{0,224},{32,192},{64,32},{96,0},{128,96},{160,64},{192,160},{224,1... | collective-permute-start | bytes 393224 | tf_op jit(solution)/shard_map/ppermute | solution.py:172
  74.6 3.7 %collective-permute-done.18.refs_13_ = bf16[128,512]{1,0:T(8,128)(2,1)S(1)} collective-permute-done((bf16[128,512]{1,0:T(8,128)(2,1)S(1)}, bf16[128,512]{1,0:T(8,128)(2,1)S(1)}, u32[]{:S(2)}, u32[]{:S(2)}) %collective-permute-start.18) | collective-permute-done | bytes 131104 | tf_op jit(solution)/shard_map/ppermute | solution.py:172
  78.3 2.9 %collective-permute-done.20.refs_15_ = bf16[128,512]{1,0:T(8,128)(2,1)S(1)} collective-permute-done((bf16[128,512]{1,0:T(8,128)(2,1)S(1)}, bf16[128,512]{1,0:T(8,128)(2,1)S(1)}, u32[]{:S(2)}, u32[]{:S(2)}) %collective-permute-start.20) | collective-permute-done | bytes 131104 | tf_op jit(solution)/shard_map/ppermute | solution.py:172
  82.9 2.5 %collective-permute-done.28.got = bf16[512,512]{1,0:T(8,128)(2,1)S(1)} collective-permute-done((bf16[512,512]{1,0:T(8,128)(2,1)S(1)}, bf16[512,512]{1,0:T(8,128)(2,1)S(1)}, u32[]{:S(2)}, u32[]{:S(2)}) %collective-permute-start.28) | collective-permute-done | bytes 524320 | tf_op jit(solution)/shard_map/ppermute | solution.py:170
  85.4 2.8 %shard_map.54 = (f32[512,128]{1,0:T(8,128)S(1)}, bf16[512,128]{1,0:T(8,128)(2,1)S(1)}, bf16[512,128]{1,0:T(8,128)(2,1)S(1)}, bf16[512,128]{1,0:T(8,128)(2,1)S(1)...) custom-call(bf16[512,512]{1,0:T(8,128)(2,1)S(1)} %get-tuple-element., ...), custom_call_target="tpu_custom_call" | custom-call | flops 1073741824 | bytes 4194304 | tf_op jit(solution)/shard_map/pallas_call | solution.py:38
  90.2 2.8 %collective-permute-start.32 = (bf16[512,128]{1,0:T(8,128)(2,1)S(1)}, bf16[512,128]{1,0:T(8,128)(2,1)S(1)}, u32[]{:S(2)}, u32[]{:S(2)}) collective-permute-start(bf16[512,128]{1,0:T(8,128)(2,1)S(1)} %get-tuple-element.51), channel_id=1, source_target_pairs={{96,0},{64,32},{160,64},{128,96},{224,128},{192,160},{32,192},{0,2... | collective-permute-start | bytes 393224 | tf_op jit(solution)/shard_map/ppermute | solution.py:195
  95.4 3.3 %collective-permute-start.34 = (bf16[512,128]{1,0:T(8,128)(2,1)S(1)}, bf16[512,128]{1,0:T(8,128)(2,1)S(1)}, u32[]{:S(2)}, u32[]{:S(2)}) collective-permute-start(bf16[512,128]{1,0:T(8,128)(2,1)S(1)} %get-tuple-element.53), channel_id=1, source_target_pairs={{160,0},{128,32},{224,64},{192,96},{32,128},{0,160},{96,192},{64,2... | collective-permute-start | bytes 393224 | tf_op jit(solution)/shard_map/ppermute | solution.py:195
  98.7 3.8 %collective-permute-start.36 = (bf16[512,128]{1,0:T(8,128)(2,1)S(1)}, bf16[512,128]{1,0:T(8,128)(2,1)S(1)}, u32[]{:S(2)}, u32[]{:S(2)}) collective-permute-start(bf16[512,128]{1,0:T(8,128)(2,1)S(1)} %get-tuple-element.55), channel_id=1, source_target_pairs={{224,0},{192,32},{32,64},{0,96},{96,128},{64,160},{160,192},{128,2... | collective-permute-start | bytes 393224 | tf_op jit(solution)/shard_map/ppermute | solution.py:195
  106.0 4.1 %collective-permute-done.36.refs_6_ = bf16[512,128]{1,0:T(8,128)(2,1)S(1)} collective-permute-done((bf16[512,128]{1,0:T(8,128)(2,1)S(1)}, bf16[512,128]{1,0:T(8,128)(2,1)S(1)}, u32[]{:S(2)}, u32[]{:S(2)}) %collective-permute-start.36) | collective-permute-done | bytes 131104 | tf_op jit(solution)/shard_map/ppermute | solution.py:195
  110.9 7.8 %all-to-all-start = ((bf16[16,32,128]{2,1,0:T(8,128)(2,1)}), bf16[16,32,128]{2,1,0:T(8,128)(2,1)S(1)}, u32[]{:S(2)}, u32[]{:S(2)}) async-start(bf16[16,32,128]{2,1,0:T(8,128)(2,1)} %bitcast), calls=%async_computation | async-start | bytes 262144 | tf_op jit(solution)/shard_map/all_to_all | solution.py:203
  119.6 3.8 %collective-permute-start.24 = (bf16[128,512]{1,0:T(8,128)(2,1)S(1)}, bf16[128,512]{1,0:T(8,128)(2,1)S(1)}, u32[]{:S(2)}, u32[]{:S(2)}) collective-permute-start(bf16[128,512]{1,0:T(8,128)(2,1)S(1)} %get-tuple-element.41), channel_id=1, source_target_pairs={{128,0},{160,32},{192,64},{224,96},{0,128},{32,160},{64,192},{96,2... | collective-permute-start | bytes 393224 | tf_op jit(solution)/shard_map/ppermute | solution.py:201
  126.7 3.8 %collective-permute-start.27 = (bf16[128,512]{1,0:T(8,128)(2,1)S(1)}, bf16[128,512]{1,0:T(8,128)(2,1)S(1)}, u32[]{:S(2)}, u32[]{:S(2)}) collective-permute-start(bf16[128,512]{1,0:T(8,128)(2,1)S(1)} %get-tuple-element.44), channel_id=1, source_target_pairs={{224,0},{192,32},{32,64},{0,96},{96,128},{64,160},{160,192},{128,2... | collective-permute-start | bytes 393224 | tf_op jit(solution)/shard_map/ppermute | solution.py:201
  130.5 2.7 %collective-permute-done.25.refs_5_ = bf16[128,512]{1,0:T(8,128)(2,1)S(1)} collective-permute-done((bf16[128,512]{1,0:T(8,128)(2,1)S(1)}, bf16[128,512]{1,0:T(8,128)(2,1)S(1)}, u32[]{:S(2)}, u32[]{:S(2)}) %collective-permute-start.25) | collective-permute-done | bytes 131104 | tf_op jit(solution)/shard_map/ppermute | solution.py:201
  133.2 2.7 %collective-permute-done.27.refs_7_ = bf16[128,512]{1,0:T(8,128)(2,1)S(1)} collective-permute-done((bf16[128,512]{1,0:T(8,128)(2,1)S(1)}, bf16[128,512]{1,0:T(8,128)(2,1)S(1)}, u32[]{:S(2)}, u32[]{:S(2)}) %collective-permute-start.27) | collective-permute-done | bytes 131104 | tf_op jit(solution)/shard_map/ppermute | solution.py:201
  (69 shorter events, 43.6 us)
Async XLA Ops:
  1.6 12.0 %collective-permute-start.7 = (bf16[128,512]{1,0:T(8,128)(2,1)S(1)}, bf16[128,512]{1,0:T(8,128)(2,1)S(1)}, u32[]{:S(2)}, u32[]{:S(2)}) collective-permute-start(bf16[128,512]{1,0:T(8,128)(2,1)S(1)} %slice.3), channel_id=1, source_target_pairs={{0,28},{1,29},{32,60},{33,61},{64,92},{65,93},{96,124},{97,125},{1... | collective-permute-start | bytes 393224 | tf_op jit(solution)/shard_map/ppermute | solution.py:145
  18.6 11.7 %collective-permute-start.10 = (bf16[128,512]{1,0:T(8,128)(2,1)S(1)}, bf16[128,512]{1,0:T(8,128)(2,1)S(1)}, u32[]{:S(2)}, u32[]{:S(2)}) collective-permute-start(bf16[128,512]{1,0:T(8,128)(2,1)S(1)} %select_select_fusion.1), channel_id=1, source_target_pairs={{0,16},{8,24},{20,4},{28,12},{1,17},{9,25},{21,5},{29,13},{32,48},... | collective-permute-start | bytes 393224 | tf_op jit(solution)/shard_map/ppermute | solution.py:145
  26.1 11.5 %collective-permute-start = (bf16[320,512]{1,0:T(8,128)(2,1)}, bf16[320,512]{1,0:T(8,128)(2,1)S(1)}, u32[]{:S(2)}, u32[]{:S(2)}) collective-permute-start(bf16[320,512]{1,0:T(8,128)(2,1)} %get-tuple-element.30), channel_id=1, source_target_pairs={{0,32},{32,0},{64,96},{96,64},{128,160},{160,128},{192,224},{224,1... | collective-permute-start | bytes 983048 | tf_op jit(solution)/shard_map/ppermute | solution.py:165
  29.1 10.9 %collective-permute-start.1 = (bf16[320,512]{1,0:T(8,128)(2,1)}, bf16[320,512]{1,0:T(8,128)(2,1)S(1)}, u32[]{:S(2)}, u32[]{:S(2)}) collective-permute-start(bf16[320,512]{1,0:T(8,128)(2,1)} %get-tuple-element.31), channel_id=1, source_target_pairs={{0,64},{32,96},{64,128},{96,160},{128,192},{160,224},{192,0},{224,... | collective-permute-start | bytes 983048 | tf_op jit(solution)/shard_map/ppermute | solution.py:165
  30.3 12.3 %collective-permute-start.13 = (bf16[128,512]{1,0:T(8,128)(2,1)S(1)}, bf16[128,512]{1,0:T(8,128)(2,1)S(1)}, u32[]{:S(2)}, u32[]{:S(2)}) collective-permute-start(bf16[128,512]{1,0:T(8,128)(2,1)S(1)} %select_select_fusion), channel_id=1, source_target_pairs={{0,1},{2,3},{4,5},{6,7},{8,9},{10,11},{12,13},{14,15},{16,17},{18,... | collective-permute-start | bytes 393224 | tf_op jit(solution)/shard_map/ppermute | solution.py:148
  31.6 15.3 %collective-permute-start.2 = (bf16[320,512]{1,0:T(8,128)(2,1)S(1)}, bf16[320,512]{1,0:T(8,128)(2,1)S(1)}, u32[]{:S(2)}, u32[]{:S(2)}) collective-permute-start(bf16[320,512]{1,0:T(8,128)(2,1)S(1)} %get-tuple-element.32), channel_id=1, source_target_pairs={{0,96},{32,64},{64,160},{96,128},{128,224},{160,192},{192,32},{224... | collective-permute-start | bytes 983048 | tf_op jit(solution)/shard_map/ppermute | solution.py:165
  32.3 21.9 %collective-permute-start.3 = (bf16[320,512]{1,0:T(8,128)(2,1)S(1)}, bf16[320,512]{1,0:T(8,128)(2,1)S(1)}, u32[]{:S(2)}, u32[]{:S(2)}) collective-permute-start(bf16[320,512]{1,0:T(8,128)(2,1)S(1)} %get-tuple-element.33), channel_id=1, source_target_pairs={{0,128},{32,160},{64,192},{96,224},{128,0},{160,32},{192,64},{224,... | collective-permute-start | bytes 983048 | tf_op jit(solution)/shard_map/ppermute | solution.py:165
  37.6 24.0 %collective-permute-start.4 = (bf16[320,512]{1,0:T(8,128)(2,1)S(1)}, bf16[320,512]{1,0:T(8,128)(2,1)S(1)}, u32[]{:S(2)}, u32[]{:S(2)}) collective-permute-start(bf16[320,512]{1,0:T(8,128)(2,1)S(1)} %get-tuple-element.34), channel_id=1, source_target_pairs={{0,160},{32,128},{64,224},{96,192},{128,32},{160,0},{192,96},{224,... | collective-permute-start | bytes 983048 | tf_op jit(solution)/shard_map/ppermute | solution.py:165
  40.0 21.7 %collective-permute-start.5 = (bf16[320,512]{1,0:T(8,128)(2,1)S(1)}, bf16[320,512]{1,0:T(8,128)(2,1)S(1)}, u32[]{:S(2)}, u32[]{:S(2)}) collective-permute-start(bf16[320,512]{1,0:T(8,128)(2,1)S(1)} %get-tuple-element.35), channel_id=1, source_target_pairs={{0,192},{32,224},{64,0},{96,32},{128,64},{160,96},{192,128},{224,1... | collective-permute-start | bytes 983048 | tf_op jit(solution)/shard_map/ppermute | solution.py:165
  42.7 25.4 %collective-permute-start.6 = (bf16[320,512]{1,0:T(8,128)(2,1)S(1)}, bf16[320,512]{1,0:T(8,128)(2,1)S(1)}, u32[]{:S(2)}, u32[]{:S(2)}) collective-permute-start(bf16[320,512]{1,0:T(8,128)(2,1)S(1)} %get-tuple-element.36), channel_id=1, source_target_pairs={{0,224},{32,192},{64,32},{96,0},{128,96},{160,64},{192,160},{224,1... | collective-permute-start | bytes 983048 | tf_op jit(solution)/shard_map/ppermute | solution.py:165
  47.0 22.7 %collective-permute-start.14 = (bf16[128,512]{1,0:T(8,128)(2,1)S(1)}, bf16[128,512]{1,0:T(8,128)(2,1)S(1)}, u32[]{:S(2)}, u32[]{:S(2)}) collective-permute-start(bf16[128,512]{1,0:T(8,128)(2,1)S(1)} %broadcast_select_fusion.refs_8_), channel_id=1, source_target_pairs={{0,32},{32,0},{64,96},{96,64},{128,160},{160,128},{192,224},{224,1... | collective-permute-start | bytes 393224 | tf_op jit(solution)/shard_map/ppermute | solution.py:172
  54.2 16.4 %collective-permute-start.15 = (bf16[128,512]{1,0:T(8,128)(2,1)S(1)}, bf16[128,512]{1,0:T(8,128)(2,1)S(1)}, u32[]{:S(2)}, u32[]{:S(2)}) collective-permute-start(bf16[128,512]{1,0:T(8,128)(2,1)S(1)} %broadcast_select_fusion.refs_8_), channel_id=1, source_target_pairs={{0,64},{32,96},{64,128},{96,160},{128,192},{160,224},{192,0},{224,... | collective-permute-start | bytes 393224 | tf_op jit(solution)/shard_map/ppermute | solution.py:172
  61.6 13.0 %collective-permute-start.16 = (bf16[128,512]{1,0:T(8,128)(2,1)S(1)}, bf16[128,512]{1,0:T(8,128)(2,1)S(1)}, u32[]{:S(2)}, u32[]{:S(2)}) collective-permute-start(bf16[128,512]{1,0:T(8,128)(2,1)S(1)} %broadcast_select_fusion.refs_8_), channel_id=1, source_target_pairs={{0,96},{32,64},{64,160},{96,128},{128,224},{160,192},{192,32},{224... | collective-permute-start | bytes 393224 | tf_op jit(solution)/shard_map/ppermute | solution.py:172
  61.6 13.0 %collective-permute-start.17 = (bf16[128,512]{1,0:T(8,128)(2,1)S(1)}, bf16[128,512]{1,0:T(8,128)(2,1)S(1)}, u32[]{:S(2)}, u32[]{:S(2)}) collective-permute-start(bf16[128,512]{1,0:T(8,128)(2,1)S(1)} %broadcast_select_fusion.refs_8_), channel_id=1, source_target_pairs={{0,128},{32,160},{64,192},{96,224},{128,0},{160,32},{192,64},{224,... | collective-permute-start | bytes 393224 | tf_op jit(solution)/shard_map/ppermute | solution.py:172
  70.6 10.6 %collective-permute-start.20 = (bf16[128,512]{1,0:T(8,128)(2,1)S(1)}, bf16[128,512]{1,0:T(8,128)(2,1)S(1)}, u32[]{:S(2)}, u32[]{:S(2)}) collective-permute-start(bf16[128,512]{1,0:T(8,128)(2,1)S(1)} %broadcast_select_fusion.refs_8_), channel_id=1, source_target_pairs={{0,224},{32,192},{64,32},{96,0},{128,96},{160,64},{192,160},{224,1... | collective-permute-start | bytes 393224 | tf_op jit(solution)/shard_map/ppermute | solution.py:172
  88.3 10.4 %collective-permute-start.30 = (bf16[512,128]{1,0:T(8,128)(2,1)S(1)}, bf16[512,128]{1,0:T(8,128)(2,1)S(1)}, u32[]{:S(2)}, u32[]{:S(2)}) collective-permute-start(bf16[512,128]{1,0:T(8,128)(2,1)S(1)} %get-tuple-element.49), channel_id=1, source_target_pairs={{32,0},{0,32},{96,64},{64,96},{160,128},{128,160},{224,192},{192,2... | collective-permute-start | bytes 393224 | tf_op jit(solution)/shard_map/ppermute | solution.py:195
  90.2 12.3 %collective-permute-start.32 = (bf16[512,128]{1,0:T(8,128)(2,1)S(1)}, bf16[512,128]{1,0:T(8,128)(2,1)S(1)}, u32[]{:S(2)}, u32[]{:S(2)}) collective-permute-start(bf16[512,128]{1,0:T(8,128)(2,1)S(1)} %get-tuple-element.51), channel_id=1, source_target_pairs={{96,0},{64,32},{160,64},{128,96},{224,128},{192,160},{32,192},{0,2... | collective-permute-start | bytes 393224 | tf_op jit(solution)/shard_map/ppermute | solution.py:195
  93.0 10.7 %collective-permute-start.33 = (bf16[512,128]{1,0:T(8,128)(2,1)S(1)}, bf16[512,128]{1,0:T(8,128)(2,1)S(1)}, u32[]{:S(2)}, u32[]{:S(2)}) collective-permute-start(bf16[512,128]{1,0:T(8,128)(2,1)S(1)} %get-tuple-element.52), channel_id=1, source_target_pairs={{128,0},{160,32},{192,64},{224,96},{0,128},{32,160},{64,192},{96,2... | collective-permute-start | bytes 393224 | tf_op jit(solution)/shard_map/ppermute | solution.py:195
  98.7 11.5 %collective-permute-start.36 = (bf16[512,128]{1,0:T(8,128)(2,1)S(1)}, bf16[512,128]{1,0:T(8,128)(2,1)S(1)}, u32[]{:S(2)}, u32[]{:S(2)}) collective-permute-start(bf16[512,128]{1,0:T(8,128)(2,1)S(1)} %get-tuple-element.55), channel_id=1, source_target_pairs={{224,0},{192,32},{32,64},{0,96},{96,128},{64,160},{160,192},{128,2... | collective-permute-start | bytes 393224 | tf_op jit(solution)/shard_map/ppermute | solution.py:195
  102.5 22.7 %collective-permute-start.21 = (bf16[128,512]{1,0:T(8,128)(2,1)S(1)}, bf16[128,512]{1,0:T(8,128)(2,1)S(1)}, u32[]{:S(2)}, u32[]{:S(2)}) collective-permute-start(bf16[128,512]{1,0:T(8,128)(2,1)S(1)} %get-tuple-element.38), channel_id=1, source_target_pairs={{32,0},{0,32},{96,64},{64,96},{160,128},{128,160},{224,192},{192,2... | collective-permute-start | bytes 393224 | tf_op jit(solution)/shard_map/ppermute | solution.py:201
  103.8 22.9 %collective-permute-start.22 = (bf16[128,512]{1,0:T(8,128)(2,1)S(1)}, bf16[128,512]{1,0:T(8,128)(2,1)S(1)}, u32[]{:S(2)}, u32[]{:S(2)}) collective-permute-start(bf16[128,512]{1,0:T(8,128)(2,1)S(1)} %get-tuple-element.39), channel_id=1, source_target_pairs={{64,0},{96,32},{128,64},{160,96},{192,128},{224,160},{0,192},{32,2... | collective-permute-start | bytes 393224 | tf_op jit(solution)/shard_map/ppermute | solution.py:201
  110.9 26.0 %all-to-all-start = ((bf16[16,32,128]{2,1,0:T(8,128)(2,1)}), bf16[16,32,128]{2,1,0:T(8,128)(2,1)S(1)}, u32[]{:S(2)}, u32[]{:S(2)}) async-start(bf16[16,32,128]{2,1,0:T(8,128)(2,1)} %bitcast), calls=%async_computation | async-start | bytes 262144 | tf_op jit(solution)/shard_map/all_to_all | solution.py:203
  118.7 11.8 %collective-permute-start.23 = (bf16[128,512]{1,0:T(8,128)(2,1)S(1)}, bf16[128,512]{1,0:T(8,128)(2,1)S(1)}, u32[]{:S(2)}, u32[]{:S(2)}) collective-permute-start(bf16[128,512]{1,0:T(8,128)(2,1)S(1)} %get-tuple-element.40), channel_id=1, source_target_pairs={{96,0},{64,32},{160,64},{128,96},{224,128},{192,160},{32,192},{0,2... | collective-permute-start | bytes 393224 | tf_op jit(solution)/shard_map/ppermute | solution.py:201
  119.6 10.9 %collective-permute-start.24 = (bf16[128,512]{1,0:T(8,128)(2,1)S(1)}, bf16[128,512]{1,0:T(8,128)(2,1)S(1)}, u32[]{:S(2)}, u32[]{:S(2)}) collective-permute-start(bf16[128,512]{1,0:T(8,128)(2,1)S(1)} %get-tuple-element.41), channel_id=1, source_target_pairs={{128,0},{160,32},{192,64},{224,96},{0,128},{32,160},{64,192},{96,2... | collective-permute-start | bytes 393224 | tf_op jit(solution)/shard_map/ppermute | solution.py:201
  (17 other events, 133.8 us)

commit v2 on v0

v2 whole, which is shorter than its diff:
```python
import math

import jax
import jax.numpy as jnp
from jax import lax
from jax.experimental import pallas as pl
from jax.experimental.pallas import tpu as pltpu
from jax.sharding import Mesh, PartitionSpec as P

PARAMS = 131072
WIDTH = 512
X, H, L, Z, C = 4, 2, 2, 8, 2
AXES = ("x", "h", "l", "z", "c")
ANY = pl.BlockSpec(memory_space=pl.ANY)
VMEM = pl.BlockSpec(memory_space=pltpu.VMEM)
BF16, F32 = jnp.bfloat16, jnp.float32
SWAP = [(0, 1), (1, 0)]
MIB = 2**20


def source(d):
    return lax.rem(lax.axis_index("x") + X - d, X)


def call(kernel, outs, ins, spec, scratch=(), flops=0, nbytes=0, vmem=4):
    return pl.pallas_call(
        kernel,
        out_shape=outs,
        in_specs=[spec] * len(ins),
        out_specs=jax.tree.map(lambda _: spec, outs),
        scratch_shapes=list(scratch),
        cost_estimate=pl.CostEstimate(flops=flops, bytes_accessed=nbytes, transcendentals=0),
        compiler_params=pltpu.CompilerParams(vmem_limit_bytes=vmem * MIB),
    )(*ins)


def shape(*dims, kind=BF16):
    return jax.ShapeDtypeStruct(dims, kind)


def run_copies(copies, sems):
    started = [pltpu.make_async_copy(a, b, sems.at[k]) for k, (a, b) in enumerate(copies)]
    for copy in started:
        copy.start()
    for copy in started:
        copy.wait()


def slab(half, core):
    return pl.ds(pl.multiple_of(half * 64 + core * 32, 32), 32)


def give_kernel(jac, give, sems):
    other = 1 - lax.axis_index("c")
    run_copies(
        [(jac.at[slab(k, other), :], give.at[pl.ds(k * 32, 32), :]) for k in range(2)], sems
    )


def pack_kernel(jac, got, cov, first, own, sems):
    core, x = lax.axis_index("c"), lax.axis_index("x")
    mine = pl.ds(pl.multiple_of(x * 1024, 1024), 1024)
    copies = []
    for k in range(X + 1):
        columns = pl.ds(k * 1024, 1024) if k < X else mine
        to = first.at[k] if k < X else own
        copies += [(jac.at[slab(n, core), columns], to.at[pl.ds(n * 32, 32), :]) for n in range(2)]
        copies.append((got.at[:, columns], to.at[pl.ds(64, 64), :]))
        copies.append((cov.at[:, columns], to.at[pl.ds(128, 64), :]))
    run_copies(copies, sems)


def carry_kernel(carry, out, sems):
    run_copies([(carry.at[:, pl.ds(k * 1024, 1024)], out.at[k]) for k in range(X)], sems)


def rest_kernel(first, own_got, cov, jac, sems):
    copies = []
    for d in range(1, X):
        at = source(d)
        copies.append((first.at[at, pl.ds(128, 64), :], cov.at[d - 1]))
        copies.append((first.at[at, pl.ds(0, 128), :], jac.at[d - 1]))
    run_copies(copies, sems)


def sens_kernel(first, own_got, cov_got, carry, *refs):
    panels, outs, cov = refs[:X], refs[X : 2 * X], refs[2 * X]
    h = lax.axis_index("h")

    def rows(x, side):
        return pl.ds(pl.multiple_of((x * H + side) * 64, 64), 64)

    for k in range(X):
        cov[rows(k, h), :] = first[k, 128:192, :]
    cov[rows(source(0), 1 - h), :] = own_got[128:192, :]
    for d in range(1, X):
        cov[rows(source(d), 1 - h), :] = cov_got[d - 1]
    for d in range(X):
        product = jnp.dot(panels[d][...], cov[...], preferred_element_type=F32)
        value = carry[source(d)].astype(F32) + product * (1.0 / math.sqrt(WIDTH))
        outs[d][...] = value.astype(BF16)


def innov_kernel(first, own_got, jac_got, *refs):
    sens, sens_got, own, parts = refs[:X], refs[X : 2 * X], refs[2 * X], refs[2 * X + 1]
    h, x = lax.axis_index("h"), lax.axis_index("x")
    dims = (((1,), (1,)), ((), ()))
    chunks = [(first.at[k], k * H + h) for k in range(X)]
    chunks.append((own_got, x * H + 1 - h))
    chunks += [(jac_got.at[d - 1], source(d) * H + 1 - h) for d in range(1, X)]
    for ref, row in chunks:
        to = pl.ds(pl.multiple_of(row * 64, 64), 64)
        for d in range(X):
            value = lax.dot_general(ref[0:64, :], sens[d][...], dims, preferred_element_type=F32)
            value += lax.dot_general(
                ref[64:128, :], sens_got[d][...], dims, preferred_element_type=F32
            )
            parts[source(d), to, :] = value.astype(BF16)
            if d == 0:
                own[to, :] = value


def sum_kernel(own, got, out):
    total = own[...]
    x = lax.axis_index("x")
    for k in range(X):
        total += jnp.where(x == k, 0.0, got[k].astype(F32))
    out[...] = total.astype(BF16)


def final_kernel(got, out):
    total = got[0].astype(F32)
    for k in range(1, L * Z):
        total += got[k].astype(F32)
    out[...] = total * (1.0 / math.sqrt(PARAMS))


def assemble_kernel(*refs):
    pieces, out, sems = refs[:X], refs[X], refs[X + 1]
    copies = []
    for d in range(X):
        at = lax.rem(lax.axis_index("x") + d, X)
        copies.append((pieces[d], out.at[:, pl.ds(pl.multiple_of(at * 1024, 1024), 1024)]))
    run_copies(copies, sems)


FIRST = [[((0, 0), (0, 4))], [((0, 0), (1, 2))], [((0, 0), (1, 6))]]
SECOND = [
    [((0, 0), (0, 1)), ((0, 4), (0, 3)), ((1, 2), (1, 1)), ((1, 6), (1, 5))],
    [((0, 0), (0, 7)), ((0, 4), (0, 5)), ((1, 2), (1, 3)), ((1, 6), (1, 7))],
    [((0, 0), (1, 0)), ((0, 4), (1, 4)), ((1, 2), (0, 2)), ((1, 6), (0, 6))],
]


def spread_panel(value):
    at = lax.axis_index("l") * Z + lax.axis_index("z")
    for stage in (FIRST, SECOND):
        received = []
        for group in stage:
            perm = [(a[0] * Z + a[1], b[0] * Z + b[1]) for a, b in group]
            hit = jnp.zeros((), jnp.bool_)
            for _, b in perm:
                hit = hit | (at == b)
            received.append((hit, lax.ppermute(value, ("l", "z"), perm)))
        for hit, got in received:
            value = jnp.where(hit, got, value)
    got = lax.ppermute(value, "c", [(0, 1)])
    return jnp.where(lax.axis_index("c") == 1, got, value)


def ring(d):
    return [(x, (x + d) % X) for x in range(X)]


def over(value, axes):
    return lax.all_to_all(value, axes, split_axis=0, concat_axis=0, tiled=True)


def dma(n):
    return [pltpu.SemaphoreType.DMA((n,))]


def body(jacobian, cov_rows, sens_carry):
    give = call(give_kernel, shape(64, 4096), (jacobian,), ANY, dma(2), nbytes=MIB)
    got = lax.ppermute(give, "c", SWAP)
    packed, own = call(
        pack_kernel,
        [shape(X, 192, 1024), shape(192, 1024)],
        (jacobian, got, cov_rows),
        ANY,
        dma(4 * (X + 1)),
        nbytes=4 * MIB,
    )
    own_got = lax.ppermute(own, "h", SWAP)
    panel = spread_panel(jacobian[:, :WIDTH])
    panels = [panel] + [lax.ppermute(panel, "x", ring(d)) for d in range(1, X)]
    first = over(packed, "x")
    cov_rest, jac_rest = call(
        rest_kernel,
        [shape(X - 1, 64, 1024), shape(X - 1, 128, 1024)],
        (first, own_got),
        ANY,
        dma(2 * X - 2),
        nbytes=2 * MIB,
    )
    cov_got = lax.ppermute(cov_rest, "h", SWAP)
    jac_got = lax.ppermute(jac_rest, "h", SWAP)
    carry = over(
        call(carry_kernel, shape(X, 128, 1024), (sens_carry,), ANY, dma(X), nbytes=2 * MIB), "x"
    )
    sens = call(
        sens_kernel,
        [shape(128, 1024)] * X,
        (first, own_got, cov_got, carry, *panels),
        VMEM,
        [pltpu.VMEM((512, 1024), BF16)],
        flops=2 * 512 * 512 * 1024,
        nbytes=2 * MIB,
        vmem=16,
    )
    sens_got = [lax.ppermute(part, "c", SWAP) for part in sens]
    own_sum, parts = call(
        innov_kernel,
        [shape(512, 128, kind=F32), shape(X, 512, 128)],
        (first, own_got, jac_got, *sens, *sens_got),
        VMEM,
        flops=2 * 512 * 512 * 2048,
        nbytes=2 * MIB,
        vmem=16,
    )
    summed = call(sum_kernel, shape(512, 128), (own_sum, over(parts, "x")), VMEM, nbytes=MIB)
    sens_back = [sens[0]] + [lax.ppermute(sens[d], "x", ring(-d)) for d in range(1, X)]
    shared = over(summed.reshape(L * Z, 32, 128), ("l", "z"))
    innovation = call(final_kernel, shape(32, 128, kind=F32), (shared,), VMEM, nbytes=2**17)
    sensitivity = call(
        assemble_kernel, shape(128, 4096), sens_back, ANY, dma(X), nbytes=2 * MIB
    )
    return (sensitivity, innovation.T)


def solution(mesh):
    fine = Mesh(mesh.devices.reshape(X, H, L, Z, C), AXES)
    spec = P(("x", "h"), ("l", "z", "c"))
    return jax.shard_map(
        body, mesh=fine, in_specs=(spec,) * 3, out_specs=(spec,) * 2, check_vma=False
    )
```

time: 543 us -> 124 us (0.23)
  waiting for transfers between devices: 462 us -> 42.6 us
  starting transfers between devices: 7.52 us -> 56.8 us
  blocking collectives: 22.2 us -> 0 us
  local copies, waits for them, and re-layouts: 26.6 us -> 5.26 us
  Pallas kernels: 0 us -> 15.5 us
  between operations: 15.5 us -> 0.85 us
  matrix products: 6.26 us -> 0 us
    unnamed x4 -> x0, waiting for transfers between devices: 266 us -> none
    psum x1 -> x0, waiting for transfers between devices: 196 us -> none  [spread(): return lax.psum(jnp.where(mine, value, jnp.zeros_like(value)), axis)]
    ppermute x0 -> x21, starting transfers between devices: none -> 33 us  [the longest x6 17.3 us: spread_panel(): received.append((hit, lax.ppermute(value, ('l', 'z'), perm)))]
    ppermute x0 -> x21, waiting for transfers between devices: none -> 26.1 us  [the longest x1 13.5 us: body(): cov_got = lax.ppermute(cov_rest, 'h', SWAP)]
    all_to_all x1 -> x0, blocking collectives: 22.2 us -> none  [body(): lax.all_to_all(sensitivity, 'row', split_axis=1, concat_axis=0, tiled=True)]
    all_to_all x1 -> x4, waiting for transfers between devices: 0.01 us -> 16.4 us  [over(): return lax.all_to_all(value, axes, split_axis=0, concat_axis=0, tiled=True)]
    all_to_all x1 -> x4, starting transfers between devices: 7.43 us -> 23.7 us  [over(): return lax.all_to_all(value, axes, split_axis=0, concat_axis=0, tiled=True)]
    pallas_call x0 -> x9, Pallas kernels: none -> 15.5 us  [call(): pl.pallas_call(kernel, out_shape=outs, in_specs=[spec] * len(ins), out_sp...]
  transfers between devices with their start and end apart: 4 -> 25, of which waited for: 2 -> 11; matrix products, arithmetic and copies ran while one was open for 1% -> 2% of each run, Pallas kernels for 0% -> 5%
where the time goes in v2:
time: 124 us; the launch traced here: 123 us
  starting transfers between devices  56.8 us (46%)
  waiting for transfers between devices  42.6 us (34%)
  Pallas kernels  15.5 us (12%)
  local copies, waits for them, and re-layouts  5.26 us (4%)
  other arithmetic  1.9 us (2%)
    all_to_all x4, starting transfers between devices, over(): return lax.all_to_all(value, axes, split_axis=0, concat_axis=0, tiled=True)  23.7 us
    ppermute x6, starting transfers between devices, spread_panel(): received.append((hit, lax.ppermute(value, ('l', 'z'), perm)))  17.3 us
    all_to_all x4, waiting for transfers between devices, over(): return lax.all_to_all(value, axes, split_axis=0, concat_axis=0, tiled=True)  16.4 us
    pallas_call x9, Pallas kernels, call(): pl.pallas_call(kernel, out_shape=outs, in_specs=[spec] * len(ins), out_sp...  15.5 us
    ppermute x1, waiting for transfers between devices, body(): cov_got = lax.ppermute(cov_rest, 'h', SWAP)  13.5 us
    ppermute x3, waiting for transfers between devices, body(): panels = [panel] + [lax.ppermute(panel, 'x', ring(d)) for d in range(1, X)]  5.8 us
    unnamed x22, local copies, waits for them, and re-layouts  4.35 us
    ppermute x6, waiting for transfers between devices, spread_panel(): received.append((hit, lax.ppermute(value, ('l', 'z'), perm)))  3.34 us
  transfers between devices with their start and end apart: 25, of which 11 were waited for; matrix products, arithmetic and copies ran while one was open for 2% of the time, Pallas kernels for 5%

profile of v2, /device:TPU:4, one launch (start us, length us, event | category | flops | bytes accessed | tf_op | source)
XLA Modules:
  0.0 122.8 jit_solution(6588321366858781789)
XLA Ops:
  2.0 1.9 %collective-permute-done.got = bf16[64,4096]{1,0:T(8,128)(2,1)S(1)} collective-permute-done((bf16[64,4096]{1,0:T(8,128)(2,1)S(1)}, bf16[64,4096]{1,0:T(8,128)(2,1)S(1)}, u32[]{:S(2)}, u32[]{:S(2)}) %collective-permute-start) | collective-permute-done | bytes 524320 | tf_op jit(solution)/shard_map/ppermute | solution.py:185
  3.9 1.4 %shard_map.51 = (bf16[4,192,1024]{2,1,0:T(8,128)(2,1)}, bf16[192,1024]{1,0:T(8,128)(2,1)S(1)}) custom-call(bf16[128,4096]{1,0:T(8,128)(2,1)S(1)} %copy-done, bf16[64,4096]{1,0:T(8,128)(2,1)S(1)} %collective-permute-done.got, bf16[64,4096]{1,0:T(8,128)(2,1)S(1)} %copy-done.2), custom_call_target="tpu_custom_call" | custom-call | bytes 4194304 | tf_op jit(solution)/shard_map/pallas_call | solution.py:26
  5.3 5.9 %all-to-all-start = ((bf16[4,192,1024]{2,1,0:T(8,128)(2,1)}), bf16[4,192,1024]{2,1,0:T(8,128)(2,1)S(1)}, u32[]{:S(2)}, u32[]{:S(2)}) async-start(bf16[4,192,1024]{2,1,0:T(8,128)(2,1)} %get-tuple-element.12), calls=%async_computation | async-start | bytes 3145728 | tf_op jit(solution)/shard_map/all_to_all | solution.py:176
  12.1 8.2 %collective-permute-start.3 = (bf16[128,512]{1,0:T(8,128)(2,1)S(1)}, bf16[128,512]{1,0:T(8,128)(2,1)S(1)}, u32[]{:S(2)}, u32[]{:S(2)}) collective-permute-start(bf16[128,512]{1,0:T(8,128)(2,1)S(1)} %slice.3), channel_id=1, source_target_pairs={{0,28},{1,29},{32,60},{33,61},{64,92},{65,93},{96,124},{97,125},{1... | collective-permute-start | bytes 393224 | tf_op jit(solution)/shard_map/ppermute | solution.py:164
  20.4 1.3 %collective-permute-start.4 = (bf16[128,512]{1,0:T(8,128)(2,1)S(1)}, bf16[128,512]{1,0:T(8,128)(2,1)S(1)}, u32[]{:S(2)}, u32[]{:S(2)}) collective-permute-start(bf16[128,512]{1,0:T(8,128)(2,1)S(1)} %slice.3), channel_id=1, source_target_pairs={{0,20},{1,21},{32,52},{33,53},{64,84},{65,85},{96,116},{97,117},{1... | collective-permute-start | bytes 393224 | tf_op jit(solution)/shard_map/ppermute | solution.py:164
  21.7 1.9 %collective-permute-start.5 = (bf16[128,512]{1,0:T(8,128)(2,1)S(1)}, bf16[128,512]{1,0:T(8,128)(2,1)}, u32[]{:S(2)}, u32[]{:S(2)}) collective-permute-start(bf16[128,512]{1,0:T(8,128)(2,1)S(1)} %slice.3), channel_id=1, source_target_pairs={{0,8},{1,9},{32,40},{33,41},{64,72},{65,73},{96,104},{97,105},{128... | collective-permute-start | bytes 393224 | tf_op jit(solution)/shard_map/ppermute | solution.py:164
  23.6 1.9 %collective-permute-done.4 = bf16[128,512]{1,0:T(8,128)(2,1)S(1)} collective-permute-done((bf16[128,512]{1,0:T(8,128)(2,1)S(1)}, bf16[128,512]{1,0:T(8,128)(2,1)S(1)}, u32[]{:S(2)}, u32[]{:S(2)}) %collective-permute-start.4) | collective-permute-done | bytes 131104 | tf_op jit(solution)/shard_map/ppermute | solution.py:164
  25.6 1.4 %collective-permute-done.5 = bf16[128,512]{1,0:T(8,128)(2,1)} collective-permute-done((bf16[128,512]{1,0:T(8,128)(2,1)S(1)}, bf16[128,512]{1,0:T(8,128)(2,1)}, u32[]{:S(2)}, u32[]{:S(2)}) %collective-permute-start.5) | collective-permute-done | bytes 131104 | tf_op jit(solution)/shard_map/ppermute | solution.py:164
  27.9 1.9 %collective-permute-start.6 = (bf16[128,512]{1,0:T(8,128)(2,1)S(1)}, bf16[128,512]{1,0:T(8,128)(2,1)}, u32[]{:S(2)}, u32[]{:S(2)}) collective-permute-start(bf16[128,512]{1,0:T(8,128)(2,1)S(1)} %select_select_fusion.1), channel_id=1, source_target_pairs={{0,16},{8,24},{20,4},{28,12},{1,17},{9,25},{21,5},{29,13},{32,48},... | collective-permute-start | bytes 393224 | tf_op jit(solution)/shard_map/ppermute | solution.py:164
  29.9 1.9 %collective-permute-start.7 = (bf16[128,512]{1,0:T(8,128)(2,1)S(1)}, bf16[128,512]{1,0:T(8,128)(2,1)}, u32[]{:S(2)}, u32[]{:S(2)}) collective-permute-start(bf16[128,512]{1,0:T(8,128)(2,1)S(1)} %select_select_fusion.1), channel_id=1, source_target_pairs={{0,14},{8,10},{20,22},{28,30},{1,15},{9,11},{21,23},{29,31},{32,46... | collective-permute-start | bytes 393224 | tf_op jit(solution)/shard_map/ppermute | solution.py:164
  31.8 1.9 %collective-permute-start.8 = (bf16[128,512]{1,0:T(8,128)(2,1)S(1)}, bf16[128,512]{1,0:T(8,128)(2,1)}, u32[]{:S(2)}, u32[]{:S(2)}) collective-permute-start(bf16[128,512]{1,0:T(8,128)(2,1)S(1)} %select_select_fusion.1), channel_id=1, source_target_pairs={{0,2},{8,6},{20,18},{28,26},{1,3},{9,7},{21,19},{29,27},{32,34},{4... | collective-permute-start | bytes 393224 | tf_op jit(solution)/shard_map/ppermute | solution.py:164
  33.7 2.9 %collective-permute-start.1 = (bf16[192,1024]{1,0:T(8,128)(2,1)S(1)}, bf16[192,1024]{1,0:T(8,128)(2,1)S(1)}, u32[]{:S(2)}, u32[]{:S(2)}) collective-permute-start(bf16[192,1024]{1,0:T(8,128)(2,1)S(1)} %get-tuple-element.13), channel_id=1, source_target_pairs={{0,32},{32,0},{1,33},{33,1},{2,34},{34,2},{3,35},{35,3},{4,36},{36... | collective-permute-start | bytes 1179656 | tf_op jit(solution)/shard_map/ppermute | solution.py:194
  37.6 4.8 %all-to-all-start.1 = ((bf16[4,128,1024]{2,1,0:T(8,128)(2,1)}), bf16[4,128,1024]{2,1,0:T(8,128)(2,1)S(1)}, u32[]{:S(2)}, u32[]{:S(2)}) async-start(bf16[4,128,1024]{2,1,0:T(8,128)(2,1)} %shard_map.53), calls=%async_computation.1 | async-start | bytes 2097152 | tf_op jit(solution)/shard_map/all_to_all | solution.py:176
  43.4 2.0 %collective-permute-start.9 = (bf16[128,512]{1,0:T(8,128)(2,1)S(1)}, bf16[128,512]{1,0:T(8,128)(2,1)}, u32[]{:S(2)}, u32[]{:S(2)}) collective-permute-start(bf16[128,512]{1,0:T(8,128)(2,1)S(1)} %select_select_fusion), channel_id=1, source_target_pairs={{0,1},{2,3},{4,5},{6,7},{8,9},{10,11},{12,13},{14,15},{16,17},{18,... | collective-permute-start | bytes 393224 | tf_op jit(solution)/shard_map/ppermute | solution.py:167
  46.5 2.5 %collective-permute-start.16 = (bf16[3,128,1024]{2,1,0:T(8,128)(2,1)}, bf16[3,128,1024]{2,1,0:T(8,128)(2,1)}, u32[]{:S(2)}, u32[]{:S(2)}) collective-permute-start(bf16[3,128,1024]{2,1,0:T(8,128)(2,1)} %get-tuple-element.19), channel_id=1, source_target_pairs={{0,32},{32,0},{1,33},{33,1},{2,34},{34,2},{3,35},{35,3},{4,36},{36... | collective-permute-start | bytes 2359304 | tf_op jit(solution)/shard_map/ppermute | solution.py:207
  53.0 5.8 %collective-permute-done.10.refs_1_ = bf16[128,512]{1,0:T(8,128)(2,1)S(1)} collective-permute-done((bf16[128,512]{1,0:T(8,128)(2,1)S(1)}, bf16[128,512]{1,0:T(8,128)(2,1)S(1)}, u32[]{:S(2)}, u32[]{:S(2)}) %collective-permute-start.10) | collective-permute-done | bytes 131104 | tf_op jit(solution)/shard_map/ppermute | solution.py:196
  60.1 13.5 %collective-permute-done.2.cov_got = bf16[3,64,1024]{2,1,0:T(8,128)(2,1)} collective-permute-done((bf16[3,64,1024]{2,1,0:T(8,128)(2,1)}, bf16[3,64,1024]{2,1,0:T(8,128)(2,1)}, u32[]{:S(2)}, u32[]{:S(2)}) %collective-permute-start.2) | collective-permute-done | bytes 393248 | tf_op jit(solution)/shard_map/ppermute | solution.py:206
  75.3 1.8 %shard_map.54 = (bf16[128,1024]{1,0:T(8,128)(2,1)S(1)}, bf16[128,1024]{1,0:T(8,128)(2,1)S(1)}, bf16[128,1024]{1,0:T(8,128)(2,1)S(1)}, bf16[128,1024]{1,0:T(8,128)(2,1)S(1)}) custom-call(bf16[4,192,1024]{2,1,0:T(8,128)(2,1)S(1)} %all-to-all-done.first, bf16[192,1024]{1,0:T(8,128)(2,1)S(1)} %collective-permute-done.1.own_got, ...), custom_call_target="tpu_custom_call" | custom-call | flops 536870912 | bytes 2097152 | tf_op jit(solution)/shard_map/pallas_call | solution.py:26
  79.9 7.8 %shard_map.56 = (f32[512,128]{1,0:T(8,128)S(1)}, bf16[4,512,128]{2,1,0:T(8,128)(2,1)}) custom-call(bf16[4,192,1024]{2,1,0:T(8,128)(2,1)S(1)} %all-to-all-done.first, bf16[192,1024]{1,0:T(8,128)(2,1)S(1)} %collective-permute-done.1.own_got, bf16[3,128,1024]{2,1,0:T(8,128)(2,1)} %collective-permute-done.16.jac_got, ...), custom_call_target="tpu_custom_call" | custom-call | flops 1073741824 | bytes 2097152 | tf_op jit(solution)/shard_map/pallas_call | solution.py:26
  87.7 4.8 %all-to-all-start.2 = ((bf16[4,512,128]{2,1,0:T(8,128)(2,1)}), bf16[4,512,128]{2,1,0:T(8,128)(2,1)S(1)}, u32[]{:S(2)}, u32[]{:S(2)}) async-start(bf16[4,512,128]{2,1,0:T(8,128)(2,1)} %get-tuple-element.21), calls=%async_computation.2 | async-start | bytes 1048576 | tf_op jit(solution)/shard_map/all_to_all | solution.py:176
  93.1 2.7 %collective-permute-start.14 = (bf16[128,1024]{1,0:T(8,128)(2,1)}, bf16[128,1024]{1,0:T(8,128)(2,1)S(1)}, u32[]{:S(2)}, u32[]{:S(2)}) collective-permute-start(bf16[128,1024]{1,0:T(8,128)(2,1)} %copy-done.4), channel_id=1, source_target_pairs={{0,128},{64,192},{128,0},{192,64},{1,129},{65,193},{129,1},{193,65... | collective-permute-start | bytes 786440 | tf_op jit(solution)/shard_map/ppermute | solution.py:232
  95.8 8.9 %all-to-all-done.2.got = bf16[4,512,128]{2,1,0:T(8,128)(2,1)S(1)} async-done(((bf16[4,512,128]{2,1,0:T(8,128)(2,1)}), bf16[4,512,128]{2,1,0:T(8,128)(2,1)S(1)}, u32[]{:S(2)}, u32[]{:S(2)}) %all-to-all-start.2) | async-done | bytes 524320 | tf_op jit(solution)/shard_map/all_to_all | solution.py:176
  105.4 8.2 %all-to-all-start.3 = ((bf16[16,32,128]{2,1,0:T(8,128)(2,1)}), bf16[16,32,128]{2,1,0:T(8,128)(2,1)S(1)}, u32[]{:S(2)}, u32[]{:S(2)}) async-start(bf16[16,32,128]{2,1,0:T(8,128)(2,1)} %bitcast), calls=%async_computation.3 | async-start | bytes 262144 | tf_op jit(solution)/shard_map/all_to_all | solution.py:176
  114.7 7.5 %all-to-all-done.3.got = bf16[16,32,128]{2,1,0:T(8,128)(2,1)S(1)} async-done(((bf16[16,32,128]{2,1,0:T(8,128)(2,1)}), bf16[16,32,128]{2,1,0:T(8,128)(2,1)S(1)}, u32[]{:S(2)}, u32[]{:S(2)}) %all-to-all-start.3) | async-done | bytes 131104 | tf_op jit(solution)/shard_map/all_to_all | solution.py:176
  (61 shorter events, 19.1 us)
Async XLA Ops:
  1.9 2.0 %collective-permute-start = (bf16[64,4096]{1,0:T(8,128)(2,1)S(1)}, bf16[64,4096]{1,0:T(8,128)(2,1)S(1)}, u32[]{:S(2)}, u32[]{:S(2)}) collective-permute-start(bf16[64,4096]{1,0:T(8,128)(2,1)S(1)} %shard_map.50), channel_id=1, source_target_pairs={{0,1},{1,0},{2,3},{3,2},{4,5},{5,4},{6,7},{7,6},{8,9},{9,8},{10,11... | collective-permute-start | bytes 1572872 | tf_op jit(solution)/shard_map/ppermute | solution.py:185
  5.3 32.3 %all-to-all-start = ((bf16[4,192,1024]{2,1,0:T(8,128)(2,1)}), bf16[4,192,1024]{2,1,0:T(8,128)(2,1)S(1)}, u32[]{:S(2)}, u32[]{:S(2)}) async-start(bf16[4,192,1024]{2,1,0:T(8,128)(2,1)} %get-tuple-element.12), calls=%async_computation | async-start | bytes 3145728 | tf_op jit(solution)/shard_map/all_to_all | solution.py:176
  12.1 11.5 %collective-permute-start.3 = (bf16[128,512]{1,0:T(8,128)(2,1)S(1)}, bf16[128,512]{1,0:T(8,128)(2,1)S(1)}, u32[]{:S(2)}, u32[]{:S(2)}) collective-permute-start(bf16[128,512]{1,0:T(8,128)(2,1)S(1)} %slice.3), channel_id=1, source_target_pairs={{0,28},{1,29},{32,60},{33,61},{64,92},{65,93},{96,124},{97,125},{1... | collective-permute-start | bytes 393224 | tf_op jit(solution)/shard_map/ppermute | solution.py:164
  20.4 5.2 %collective-permute-start.4 = (bf16[128,512]{1,0:T(8,128)(2,1)S(1)}, bf16[128,512]{1,0:T(8,128)(2,1)S(1)}, u32[]{:S(2)}, u32[]{:S(2)}) collective-permute-start(bf16[128,512]{1,0:T(8,128)(2,1)S(1)} %slice.3), channel_id=1, source_target_pairs={{0,20},{1,21},{32,52},{33,53},{64,84},{65,85},{96,116},{97,117},{1... | collective-permute-start | bytes 393224 | tf_op jit(solution)/shard_map/ppermute | solution.py:164
  21.7 5.3 %collective-permute-start.5 = (bf16[128,512]{1,0:T(8,128)(2,1)S(1)}, bf16[128,512]{1,0:T(8,128)(2,1)}, u32[]{:S(2)}, u32[]{:S(2)}) collective-permute-start(bf16[128,512]{1,0:T(8,128)(2,1)S(1)} %slice.3), channel_id=1, source_target_pairs={{0,8},{1,9},{32,40},{33,41},{64,72},{65,73},{96,104},{97,105},{128... | collective-permute-start | bytes 393224 | tf_op jit(solution)/shard_map/ppermute | solution.py:164
  27.9 14.5 %collective-permute-start.6 = (bf16[128,512]{1,0:T(8,128)(2,1)S(1)}, bf16[128,512]{1,0:T(8,128)(2,1)}, u32[]{:S(2)}, u32[]{:S(2)}) collective-permute-start(bf16[128,512]{1,0:T(8,128)(2,1)S(1)} %select_select_fusion.1), channel_id=1, source_target_pairs={{0,16},{8,24},{20,4},{28,12},{1,17},{9,25},{21,5},{29,13},{32,48},... | collective-permute-start | bytes 393224 | tf_op jit(solution)/shard_map/ppermute | solution.py:164
  29.9 12.6 %collective-permute-start.7 = (bf16[128,512]{1,0:T(8,128)(2,1)S(1)}, bf16[128,512]{1,0:T(8,128)(2,1)}, u32[]{:S(2)}, u32[]{:S(2)}) collective-permute-start(bf16[128,512]{1,0:T(8,128)(2,1)S(1)} %select_select_fusion.1), channel_id=1, source_target_pairs={{0,14},{8,10},{20,22},{28,30},{1,15},{9,11},{21,23},{29,31},{32,46... | collective-permute-start | bytes 393224 | tf_op jit(solution)/shard_map/ppermute | solution.py:164
  31.8 10.7 %collective-permute-start.8 = (bf16[128,512]{1,0:T(8,128)(2,1)S(1)}, bf16[128,512]{1,0:T(8,128)(2,1)}, u32[]{:S(2)}, u32[]{:S(2)}) collective-permute-start(bf16[128,512]{1,0:T(8,128)(2,1)S(1)} %select_select_fusion.1), channel_id=1, source_target_pairs={{0,2},{8,6},{20,18},{28,26},{1,3},{9,7},{21,19},{29,27},{32,34},{4... | collective-permute-start | bytes 393224 | tf_op jit(solution)/shard_map/ppermute | solution.py:164
  33.7 11.7 %collective-permute-start.1 = (bf16[192,1024]{1,0:T(8,128)(2,1)S(1)}, bf16[192,1024]{1,0:T(8,128)(2,1)S(1)}, u32[]{:S(2)}, u32[]{:S(2)}) collective-permute-start(bf16[192,1024]{1,0:T(8,128)(2,1)S(1)} %get-tuple-element.13), channel_id=1, source_target_pairs={{0,32},{32,0},{1,33},{33,1},{2,34},{34,2},{3,35},{35,3},{4,36},{36... | collective-permute-start | bytes 1179656 | tf_op jit(solution)/shard_map/ppermute | solution.py:194
  37.6 22.4 %all-to-all-start.1 = ((bf16[4,128,1024]{2,1,0:T(8,128)(2,1)}), bf16[4,128,1024]{2,1,0:T(8,128)(2,1)S(1)}, u32[]{:S(2)}, u32[]{:S(2)}) async-start(bf16[4,128,1024]{2,1,0:T(8,128)(2,1)} %shard_map.53), calls=%async_computation.1 | async-start | bytes 2097152 | tf_op jit(solution)/shard_map/all_to_all | solution.py:176
  43.4 6.7 %collective-permute-start.9 = (bf16[128,512]{1,0:T(8,128)(2,1)S(1)}, bf16[128,512]{1,0:T(8,128)(2,1)}, u32[]{:S(2)}, u32[]{:S(2)}) collective-permute-start(bf16[128,512]{1,0:T(8,128)(2,1)S(1)} %select_select_fusion), channel_id=1, source_target_pairs={{0,1},{2,3},{4,5},{6,7},{8,9},{10,11},{12,13},{14,15},{16,17},{18,... | collective-permute-start | bytes 393224 | tf_op jit(solution)/shard_map/ppermute | solution.py:167
  46.5 33.4 %collective-permute-start.16 = (bf16[3,128,1024]{2,1,0:T(8,128)(2,1)}, bf16[3,128,1024]{2,1,0:T(8,128)(2,1)}, u32[]{:S(2)}, u32[]{:S(2)}) collective-permute-start(bf16[3,128,1024]{2,1,0:T(8,128)(2,1)} %get-tuple-element.19), channel_id=1, source_target_pairs={{0,32},{32,0},{1,33},{33,1},{2,34},{34,2},{3,35},{35,3},{4,36},{36... | collective-permute-start | bytes 2359304 | tf_op jit(solution)/shard_map/ppermute | solution.py:207
  49.0 24.5 %collective-permute-start.2 = (bf16[3,64,1024]{2,1,0:T(8,128)(2,1)}, bf16[3,64,1024]{2,1,0:T(8,128)(2,1)}, u32[]{:S(2)}, u32[]{:S(2)}) collective-permute-start(bf16[3,64,1024]{2,1,0:T(8,128)(2,1)} %get-tuple-element.14), channel_id=1, source_target_pairs={{0,32},{32,0},{1,33},{33,1},{2,34},{34,2},{3,35},{35,3},{4,36},{36... | collective-permute-start | bytes 1179656 | tf_op jit(solution)/shard_map/ppermute | solution.py:206
  50.1 8.6 %collective-permute-start.10 = (bf16[128,512]{1,0:T(8,128)(2,1)S(1)}, bf16[128,512]{1,0:T(8,128)(2,1)S(1)}, u32[]{:S(2)}, u32[]{:S(2)}) collective-permute-start(bf16[128,512]{1,0:T(8,128)(2,1)S(1)} %broadcast_select_fusion.refs_0_), channel_id=1, source_target_pairs={{0,64},{64,128},{128,192},{192,0},{1,65},{65,129},{129,193},{193,1... | collective-permute-start | bytes 393224 | tf_op jit(solution)/shard_map/ppermute | solution.py:196
  51.4 7.4 %collective-permute-start.11 = (bf16[128,512]{1,0:T(8,128)(2,1)S(1)}, bf16[128,512]{1,0:T(8,128)(2,1)S(1)}, u32[]{:S(2)}, u32[]{:S(2)}) collective-permute-start(bf16[128,512]{1,0:T(8,128)(2,1)S(1)} %broadcast_select_fusion.refs_0_), channel_id=1, source_target_pairs={{0,128},{64,192},{128,0},{192,64},{1,129},{65,193},{129,1},{193,65... | collective-permute-start | bytes 393224 | tf_op jit(solution)/shard_map/ppermute | solution.py:196
  52.2 7.2 %collective-permute-start.12 = (bf16[128,512]{1,0:T(8,128)(2,1)S(1)}, bf16[128,512]{1,0:T(8,128)(2,1)S(1)}, u32[]{:S(2)}, u32[]{:S(2)}) collective-permute-start(bf16[128,512]{1,0:T(8,128)(2,1)S(1)} %broadcast_select_fusion.refs_0_), channel_id=1, source_target_pairs={{0,192},{64,0},{128,64},{192,128},{1,193},{65,1},{129,65},{193,129... | collective-permute-start | bytes 393224 | tf_op jit(solution)/shard_map/ppermute | solution.py:196
  77.3 1.9 %collective-permute-start.18 = (bf16[128,1024]{1,0:T(8,128)(2,1)S(1)}, bf16[128,1024]{1,0:T(8,128)(2,1)S(1)}, u32[]{:S(2)}, u32[]{:S(2)}) collective-permute-start(bf16[128,1024]{1,0:T(8,128)(2,1)S(1)} %get-tuple-element.16.refs_1_), channel_id=1, source_target_pairs={{0,1},{1,0},{2,3},{3,2},{4,5},{5,4},{6,7},{7,6},{8,9},{9,8},{10,11... | collective-permute-start | bytes 786440 | tf_op jit(solution)/shard_map/ppermute | solution.py:221
  77.8 1.8 %collective-permute-start.19 = (bf16[128,1024]{1,0:T(8,128)(2,1)S(1)}, bf16[128,1024]{1,0:T(8,128)(2,1)S(1)}, u32[]{:S(2)}, u32[]{:S(2)}) collective-permute-start(bf16[128,1024]{1,0:T(8,128)(2,1)S(1)} %get-tuple-element.17.refs_2_), channel_id=1, source_target_pairs={{0,1},{1,0},{2,3},{3,2},{4,5},{5,4},{6,7},{7,6},{8,9},{9,8},{10,11... | collective-permute-start | bytes 786440 | tf_op jit(solution)/shard_map/ppermute | solution.py:221
  77.9 2.0 %collective-permute-start.20 = (bf16[128,1024]{1,0:T(8,128)(2,1)S(1)}, bf16[128,1024]{1,0:T(8,128)(2,1)S(1)}, u32[]{:S(2)}, u32[]{:S(2)}) collective-permute-start(bf16[128,1024]{1,0:T(8,128)(2,1)S(1)} %get-tuple-element.18.refs_3_), channel_id=1, source_target_pairs={{0,1},{1,0},{2,3},{3,2},{4,5},{5,4},{6,7},{7,6},{8,9},{9,8},{10,11... | collective-permute-start | bytes 786440 | tf_op jit(solution)/shard_map/ppermute | solution.py:221
  87.7 16.9 %all-to-all-start.2 = ((bf16[4,512,128]{2,1,0:T(8,128)(2,1)}), bf16[4,512,128]{2,1,0:T(8,128)(2,1)S(1)}, u32[]{:S(2)}, u32[]{:S(2)}) async-start(bf16[4,512,128]{2,1,0:T(8,128)(2,1)} %get-tuple-element.21), calls=%async_computation.2 | async-start | bytes 1048576 | tf_op jit(solution)/shard_map/all_to_all | solution.py:176
  92.5 21.1 %collective-permute-start.13 = (bf16[128,1024]{1,0:T(8,128)(2,1)}, bf16[128,1024]{1,0:T(8,128)(2,1)S(1)}, u32[]{:S(2)}, u32[]{:S(2)}) collective-permute-start(bf16[128,1024]{1,0:T(8,128)(2,1)} %copy-done.5), channel_id=1, source_target_pairs={{0,192},{64,0},{128,64},{192,128},{1,193},{65,1},{129,65},{193,129... | collective-permute-start | bytes 786440 | tf_op jit(solution)/shard_map/ppermute | solution.py:232
  93.1 20.6 %collective-permute-start.14 = (bf16[128,1024]{1,0:T(8,128)(2,1)}, bf16[128,1024]{1,0:T(8,128)(2,1)S(1)}, u32[]{:S(2)}, u32[]{:S(2)}) collective-permute-start(bf16[128,1024]{1,0:T(8,128)(2,1)} %copy-done.4), channel_id=1, source_target_pairs={{0,128},{64,192},{128,0},{192,64},{1,129},{65,193},{129,1},{193,65... | collective-permute-start | bytes 786440 | tf_op jit(solution)/shard_map/ppermute | solution.py:232
  95.8 17.9 %collective-permute-start.15 = (bf16[128,1024]{1,0:T(8,128)(2,1)}, bf16[128,1024]{1,0:T(8,128)(2,1)S(1)}, u32[]{:S(2)}, u32[]{:S(2)}) collective-permute-start(bf16[128,1024]{1,0:T(8,128)(2,1)} %copy-done.3), channel_id=1, source_target_pairs={{0,64},{64,128},{128,192},{192,0},{1,65},{65,129},{129,193},{193,1... | collective-permute-start | bytes 786440 | tf_op jit(solution)/shard_map/ppermute | solution.py:232
  105.4 16.8 %all-to-all-start.3 = ((bf16[16,32,128]{2,1,0:T(8,128)(2,1)}), bf16[16,32,128]{2,1,0:T(8,128)(2,1)S(1)}, u32[]{:S(2)}, u32[]{:S(2)}) async-start(bf16[16,32,128]{2,1,0:T(8,128)(2,1)} %bitcast), calls=%async_computation.3 | async-start | bytes 262144 | tf_op jit(solution)/shard_map/all_to_all | solution.py:176
  (12 other events, 80.8 us)

commit v3 on v2

--- a/solution.py
+++ b/solution.py
@@ -1,3 +1,4 @@
+import functools
 import math
 
 import jax
@@ -22,16 +23,16 @@
     return lax.rem(lax.axis_index("x") + X - d, X)
 
 
-def call(kernel, outs, ins, spec, scratch=(), flops=0, nbytes=0, vmem=4):
+def call(kernel, outs, ins, spec, scratch=(), flops=0, nbytes=0, vmem=1, behind=()):
     return pl.pallas_call(
         kernel,
         out_shape=outs,
-        in_specs=[spec] * len(ins),
+        in_specs=[spec] * len(ins) + [ANY] * len(behind),
         out_specs=jax.tree.map(lambda _: spec, outs),
         scratch_shapes=list(scratch),
         cost_estimate=pl.CostEstimate(flops=flops, bytes_accessed=nbytes, transcendentals=0),
         compiler_params=pltpu.CompilerParams(vmem_limit_bytes=vmem * MIB),
-    )(*ins)
+    )(*ins, *behind)
 
 
 def shape(*dims, kind=BF16):
@@ -70,8 +71,18 @@
     run_copies(copies, sems)
 
 
-def carry_kernel(carry, out, sems):
-    run_copies([(carry.at[:, pl.ds(k * 1024, 1024)], out.at[k]) for k in range(X)], sems)
+def carry_kernel(carry, panel, out, sems):
+    copies = []
+    for k in range(X):
+        copies.append((carry.at[:, pl.ds(k * 1024, 1024)], out.at[k, pl.ds(0, 128), :]))
+        for n in range(2):
+            copies.append(
+                (
+                    panel.at[pl.ds(n * 64, 64), :],
+                    out.at[k, pl.ds(128, 64), pl.ds(n * WIDTH, WIDTH)],
+                )
+            )
+    run_copies(copies, sems)
 
 
 def rest_kernel(first, own_got, cov, jac, sems):
@@ -83,8 +94,8 @@
     run_copies(copies, sems)
 
 
-def sens_kernel(first, own_got, cov_got, carry, *refs):
-    panels, outs, cov = refs[:X], refs[X : 2 * X], refs[2 * X]
+def sens_kernel(first, own_got, cov_got, second, *refs):
+    outs, cov, panel = refs[:X], refs[X], refs[X + 1]
     h = lax.axis_index("h")
 
     def rows(x, side):
@@ -96,28 +107,39 @@
     for d in range(1, X):
         cov[rows(source(d), 1 - h), :] = cov_got[d - 1]
     for d in range(X):
-        product = jnp.dot(panels[d][...], cov[...], preferred_element_type=F32)
-        value = carry[source(d)].astype(F32) + product * (1.0 / math.sqrt(WIDTH))
+        at = source(d)
+        for n in range(2):
+            panel[d * 128 + n * 64 : d * 128 + n * 64 + 64, :] = second[
+                at, 128:192, n * WIDTH : (n + 1) * WIDTH
+            ]
+    for d in range(X):
+        rows = slice(d * 128, (d + 1) * 128)
+        product = jnp.dot(panel[rows, :], cov[...], preferred_element_type=F32)
+        value = second[source(d), 0:128, :].astype(F32) + product * (1.0 / math.sqrt(WIDTH))
         outs[d][...] = value.astype(BF16)
 
 
 def innov_kernel(first, own_got, jac_got, *refs):
-    sens, sens_got, own, parts = refs[:X], refs[X : 2 * X], refs[2 * X], refs[2 * X + 1]
+    sens, sens_got, (own, parts, jac, both) = refs[:X], refs[X : 2 * X], refs[-4:]
     h, x = lax.axis_index("h"), lax.axis_index("x")
-    dims = (((1,), (1,)), ((), ()))
     chunks = [(first.at[k], k * H + h) for k in range(X)]
     chunks.append((own_got, x * H + 1 - h))
     chunks += [(jac_got.at[d - 1], source(d) * H + 1 - h) for d in range(1, X)]
     for ref, row in chunks:
         to = pl.ds(pl.multiple_of(row * 64, 64), 64)
+        jac[to, 0:1024] = ref[0:64, :]
+        jac[to, 1024:2048] = ref[64:128, :]
+    for d in range(X):
+        both[d * 128 : (d + 1) * 128, 0:1024] = sens[d][...]
+        both[d * 128 : (d + 1) * 128, 1024:2048] = sens_got[d][...]
+    for block in range(4):
+        to = slice(block * 128, (block + 1) * 128)
+        value = lax.dot_general(
+            jac[to, :], both[...], (((1,), (1,)), ((), ())), preferred_element_type=F32
+        )
+        own[to, :] = value[:, 0:128]
         for d in range(X):
-            value = lax.dot_general(ref[0:64, :], sens[d][...], dims, preferred_element_type=F32)
-            value += lax.dot_general(
-                ref[64:128, :], sens_got[d][...], dims, preferred_element_type=F32
-            )
-            parts[source(d), to, :] = value.astype(BF16)
-            if d == 0:
-                own[to, :] = value
+            parts[source(d), to, :] = value[:, d * 128 : (d + 1) * 128].astype(BF16)
 
 
 def sum_kernel(own, got, out):
@@ -152,20 +174,51 @@
 ]
 
 
-def spread_panel(value):
+def choose_kernel(groups, value, *refs):
+    received, out = refs[: len(groups)], refs[-1]
     at = lax.axis_index("l") * Z + lax.axis_index("z")
-    for stage in (FIRST, SECOND):
-        received = []
-        for group in stage:
-            perm = [(a[0] * Z + a[1], b[0] * Z + b[1]) for a, b in group]
-            hit = jnp.zeros((), jnp.bool_)
-            for _, b in perm:
-                hit = hit | (at == b)
-            received.append((hit, lax.ppermute(value, ("l", "z"), perm)))
-        for hit, got in received:
-            value = jnp.where(hit, got, value)
-    got = lax.ppermute(value, "c", [(0, 1)])
-    return jnp.where(lax.axis_index("c") == 1, got, value)
+    out[...] = value[...]
+    for perm, ref in zip(groups, received):
+        hit = at == perm[0][1]
+        for _, b in perm[1:]:
+            hit = hit | (at == b)
+
+        @pl.when(hit)
+        def _():
+            out[...] = ref[...]
+
+
+def core_kernel(value, got, out):
+    core = lax.axis_index("c")
+
+    @pl.when(core == 0)
+    def _():
+        out[...] = value[...]
+
+    @pl.when(core == 1)
+    def _():
+        out[...] = got[...]
+
+
+def panel_call(kernel, ins, behind=()):
+    return pl.pallas_call(
+        kernel,
+        out_shape=shape(128, WIDTH),
+        in_specs=[VMEM] * len(ins) + [ANY] * len(behind),
+        out_specs=VMEM,
+        cost_estimate=pl.CostEstimate(flops=0, bytes_accessed=2**18, transcendentals=0),
+        compiler_params=pltpu.CompilerParams(vmem_limit_bytes=2 * MIB),
+    )(*ins, *behind)
+
+
+def spread_panel(value, behind):
+    for number, stage in enumerate((FIRST, SECOND)):
+        groups = [[(a[0] * Z + a[1], b[0] * Z + b[1]) for a, b in group] for group in stage]
+        received = [lax.ppermute(value, ("l", "z"), perm) for perm in groups]
+        value = panel_call(
+            functools.partial(choose_kernel, groups), (value, *received), behind if number else ()
+        )
+    return panel_call(core_kernel, (value, lax.ppermute(value, "c", [(0, 1)])))
 
 
 def ring(d):
@@ -192,8 +245,7 @@
         nbytes=4 * MIB,
     )
     own_got = lax.ppermute(own, "h", SWAP)
-    panel = spread_panel(jacobian[:, :WIDTH])
-    panels = [panel] + [lax.ppermute(panel, "x", ring(d)) for d in range(1, X)]
+    panel = spread_panel(jacobian[:, :WIDTH], (own_got,))
     first = over(packed, "x")
     cov_rest, jac_rest = call(
         rest_kernel,
@@ -205,33 +257,36 @@
     )
     cov_got = lax.ppermute(cov_rest, "h", SWAP)
     jac_got = lax.ppermute(jac_rest, "h", SWAP)
-    carry = over(
-        call(carry_kernel, shape(X, 128, 1024), (sens_carry,), ANY, dma(X), nbytes=2 * MIB), "x"
-    )
+    packed = call(
+        carry_kernel, shape(X, 192, 1024), (sens_carry, panel), ANY, dma(3 * X), nbytes=2 * MIB
+    )
+    second = over(packed, "x")
     sens = call(
         sens_kernel,
         [shape(128, 1024)] * X,
-        (first, own_got, cov_got, carry, *panels),
+        (first, own_got, cov_got, second),
         VMEM,
-        [pltpu.VMEM((512, 1024), BF16)],
+        [pltpu.VMEM((512, 1024), BF16), pltpu.VMEM((512, WIDTH), BF16)],
         flops=2 * 512 * 512 * 1024,
         nbytes=2 * MIB,
-        vmem=16,
-    )
+        vmem=12,
+    )
+    sens_back = [sens[0]] + [lax.ppermute(sens[d], "x", ring(-d)) for d in range(1, X)]
     sens_got = [lax.ppermute(part, "c", SWAP) for part in sens]
     own_sum, parts = call(
         innov_kernel,
         [shape(512, 128, kind=F32), shape(X, 512, 128)],
         (first, own_got, jac_got, *sens, *sens_got),
         VMEM,
+        [pltpu.VMEM((512, 2048), BF16)] * 2,
         flops=2 * 512 * 512 * 2048,
         nbytes=2 * MIB,
         vmem=16,
-    )
-    summed = call(sum_kernel, shape(512, 128), (own_sum, over(parts, "x")), VMEM, nbytes=MIB)
-    sens_back = [sens[0]] + [lax.ppermute(sens[d], "x", ring(-d)) for d in range(1, X)]
+        behind=(sens_back[1], sens_back[3]),
+    )
+    summed = call(sum_kernel, shape(512, 128), (own_sum, over(parts, "x")), VMEM, nbytes=MIB, vmem=4)
     shared = over(summed.reshape(L * Z, 32, 128), ("l", "z"))
-    innovation = call(final_kernel, shape(32, 128, kind=F32), (shared,), VMEM, nbytes=2**17)
+    innovation = call(final_kernel, shape(32, 128, kind=F32), (shared,), VMEM, nbytes=2**17, vmem=4)
     sensitivity = call(
         assemble_kernel, shape(128, 4096), sens_back, ANY, dma(X), nbytes=2 * MIB
     )

time: 124 us -> 117 us (0.944)
  waiting for transfers between devices: 42.6 us -> 48.8 us
  starting transfers between devices: 56.8 us -> 51.2 us
  Pallas kernels: 15.5 us -> 10.3 us
  other arithmetic: 1.9 us -> 0 us
    ppermute x3, waiting for transfers between devices: 0.01 us -> 6.65 us  [body(): lax.ppermute(sens[d], 'x', ring(-d))]
    all_to_all x4, waiting for transfers between devices: 16.4 us -> 22.8 us  [over(): return lax.all_to_all(value, axes, split_axis=0, concat_axis=0, tiled=True)]
    ppermute x10 -> x7, starting transfers between devices: 22.1 us -> 16.9 us  [the longest x6 15.6 us: spread_panel(): received = [lax.ppermute(value, ('l', 'z'), perm) for perm in groups]]
    pallas_call x9 -> x12, Pallas kernels: 15.5 us -> 10.3 us  [the longest x9 10.2 us: call(): pl.pallas_call(kernel, out_shape=outs, in_specs=[spec] * len(ins) + [ANY]...]
    ppermute x1, waiting for transfers between devices: 13.5 us -> 9.98 us  [body(): cov_got = lax.ppermute(cov_rest, 'h', SWAP)]
    ppermute x10 -> x7, waiting for transfers between devices: 9.14 us -> 5.94 us  [the longest x6 4.98 us: spread_panel(): received = [lax.ppermute(value, ('l', 'z'), perm) for perm in groups]]
    select_n x3 -> x0, other arithmetic: 1.9 us -> none  [the longest x2 1.89 us: spread_panel(): value = jnp.where(hit, got, value)]
    all_to_all x4, starting transfers between devices: 23.7 us -> 25.5 us  [over(): return lax.all_to_all(value, axes, split_axis=0, concat_axis=0, tiled=True)]
  transfers between devices with their start and end apart: 25 -> 22, of which waited for: 11 -> 15; matrix products, arithmetic and copies ran while one was open for 2% -> 0% of each run, Pallas kernels for 5% -> 4%
where the time goes in v3:
time: 117 us; the launch traced here: 116 us
  starting transfers between devices  51.2 us (44%)
  waiting for transfers between devices  48.8 us (42%)
  Pallas kernels  10.3 us (9%)
  local copies, waits for them, and re-layouts  5.33 us (5%)
    all_to_all x4, starting transfers between devices, over(): return lax.all_to_all(value, axes, split_axis=0, concat_axis=0, tiled=True)  25.5 us
    all_to_all x4, waiting for transfers between devices, over(): return lax.all_to_all(value, axes, split_axis=0, concat_axis=0, tiled=True)  22.8 us
    ppermute x6, starting transfers between devices, spread_panel(): received = [lax.ppermute(value, ('l', 'z'), perm) for perm in groups]  15.6 us
    pallas_call x9, Pallas kernels, call(): pl.pallas_call(kernel, out_shape=outs, in_specs=[spec] * len(ins) + [ANY]...  10.2 us
    ppermute x1, waiting for transfers between devices, body(): cov_got = lax.ppermute(cov_rest, 'h', SWAP)  9.98 us
    ppermute x3, waiting for transfers between devices, body(): lax.ppermute(sens[d], 'x', ring(-d))  6.65 us
    unnamed x22, local copies, waits for them, and re-layouts  5.32 us
    ppermute x6, waiting for transfers between devices, spread_panel(): received = [lax.ppermute(value, ('l', 'z'), perm) for perm in groups]  4.98 us
  transfers between devices with their start and end apart: 22, of which 15 were waited for; matrix products, arithmetic and copies ran while one was open for 0% of the time, Pallas kernels for 4%

profile of v3, /device:TPU:4, one launch (start us, length us, event | category | flops | bytes accessed | tf_op | source)
XLA Modules:
  0.0 116.5 jit_solution(17446672552250767323)
XLA Ops:
  2.0 1.9 %collective-permute-done.got = bf16[64,4096]{1,0:T(8,128)(2,1)S(1)} collective-permute-done((bf16[64,4096]{1,0:T(8,128)(2,1)S(1)}, bf16[64,4096]{1,0:T(8,128)(2,1)S(1)}, u32[]{:S(2)}, u32[]{:S(2)}) %collective-permute-start) | collective-permute-done | bytes 524320 | tf_op jit(solution)/shard_map/ppermute | solution.py:238
  5.7 5.8 %all-to-all-start = ((bf16[4,192,1024]{2,1,0:T(8,128)(2,1)}), bf16[4,192,1024]{2,1,0:T(8,128)(2,1)S(1)}, u32[]{:S(2)}, u32[]{:S(2)}) async-start(bf16[4,192,1024]{2,1,0:T(8,128)(2,1)} %copy-done.3), calls=%async_computation | async-start | bytes 3145728 | tf_op jit(solution)/shard_map/all_to_all | solution.py:229
  11.5 2.2 %collective-permute-start.1 = (bf16[192,1024]{1,0:T(8,128)(2,1)S(1)}, bf16[192,1024]{1,0:T(8,128)(2,1)S(1)}, u32[]{:S(2)}, u32[]{:S(2)}) collective-permute-start(bf16[192,1024]{1,0:T(8,128)(2,1)S(1)} %get-tuple-element.13), channel_id=1, source_target_pairs={{0,32},{32,0},{1,33},{33,1},{2,34},{34,2},{3,35},{35,3},{4,36},{36... | collective-permute-start | bytes 1179656 | tf_op jit(solution)/shard_map/ppermute | solution.py:247
  13.7 9.1 %collective-permute-start.3 = (bf16[128,512]{1,0:T(8,128)(2,1)S(1)}, bf16[128,512]{1,0:T(8,128)(2,1)S(1)}, u32[]{:S(2)}, u32[]{:S(2)}) collective-permute-start(bf16[128,512]{1,0:T(8,128)(2,1)S(1)} %slice.3.value), channel_id=1, source_target_pairs={{0,8},{1,9},{32,40},{33,41},{64,72},{65,73},{96,104},{97,105},{128... | collective-permute-start | bytes 393224 | tf_op jit(solution)/shard_map/ppermute | solution.py:217
  22.8 1.3 %collective-permute-start.4 = (bf16[128,512]{1,0:T(8,128)(2,1)S(1)}, bf16[128,512]{1,0:T(8,128)(2,1)S(1)}, u32[]{:S(2)}, u32[]{:S(2)}) collective-permute-start(bf16[128,512]{1,0:T(8,128)(2,1)S(1)} %slice.3.value), channel_id=1, source_target_pairs={{0,20},{1,21},{32,52},{33,53},{64,84},{65,85},{96,116},{97,117},{1... | collective-permute-start | bytes 393224 | tf_op jit(solution)/shard_map/ppermute | solution.py:217
  24.1 1.3 %collective-permute-start.5 = (bf16[128,512]{1,0:T(8,128)(2,1)S(1)}, bf16[128,512]{1,0:T(8,128)(2,1)S(1)}, u32[]{:S(2)}, u32[]{:S(2)}) collective-permute-start(bf16[128,512]{1,0:T(8,128)(2,1)S(1)} %slice.3.value), channel_id=1, source_target_pairs={{0,28},{1,29},{32,60},{33,61},{64,92},{65,93},{96,124},{97,125},{1... | collective-permute-start | bytes 393224 | tf_op jit(solution)/shard_map/ppermute | solution.py:217
  26.4 1.4 %collective-permute-done.4.refs_1_ = bf16[128,512]{1,0:T(8,128)(2,1)S(1)} collective-permute-done((bf16[128,512]{1,0:T(8,128)(2,1)S(1)}, bf16[128,512]{1,0:T(8,128)(2,1)S(1)}, u32[]{:S(2)}, u32[]{:S(2)}) %collective-permute-start.4) | collective-permute-done | bytes 131104 | tf_op jit(solution)/shard_map/ppermute | solution.py:217
  29.3 1.3 %collective-permute-start.7 = (bf16[128,512]{1,0:T(8,128)(2,1)S(1)}, bf16[128,512]{1,0:T(8,128)(2,1)S(1)}, u32[]{:S(2)}, u32[]{:S(2)}) collective-permute-start(bf16[128,512]{1,0:T(8,128)(2,1)S(1)} %shard_map.53.value), channel_id=1, source_target_pairs={{0,14},{8,10},{20,22},{28,30},{1,15},{9,11},{21,23},{29,31},{32,46... | collective-permute-start | bytes 393224 | tf_op jit(solution)/shard_map/ppermute | solution.py:217
  30.6 1.3 %collective-permute-start.8 = (bf16[128,512]{1,0:T(8,128)(2,1)S(1)}, bf16[128,512]{1,0:T(8,128)(2,1)S(1)}, u32[]{:S(2)}, u32[]{:S(2)}) collective-permute-start(bf16[128,512]{1,0:T(8,128)(2,1)S(1)} %shard_map.53.value), channel_id=1, source_target_pairs={{0,16},{8,24},{20,4},{28,12},{1,17},{9,25},{21,5},{29,13},{32,48},... | collective-permute-start | bytes 393224 | tf_op jit(solution)/shard_map/ppermute | solution.py:217
  33.1 1.3 %collective-permute-done.8.refs_2_ = bf16[128,512]{1,0:T(8,128)(2,1)S(1)} collective-permute-done((bf16[128,512]{1,0:T(8,128)(2,1)S(1)}, bf16[128,512]{1,0:T(8,128)(2,1)S(1)}, u32[]{:S(2)}, u32[]{:S(2)}) %collective-permute-start.8) | collective-permute-done | bytes 131104 | tf_op jit(solution)/shard_map/ppermute | solution.py:217
  34.4 1.3 %collective-permute-start.9 = (bf16[128,512]{1,0:T(8,128)(2,1)S(1)}, bf16[128,512]{1,0:T(8,128)(2,1)S(1)}, u32[]{:S(2)}, u32[]{:S(2)}) collective-permute-start(bf16[128,512]{1,0:T(8,128)(2,1)S(1)} %shard_map.54.value), channel_id=1, source_target_pairs={{0,1},{2,3},{4,5},{6,7},{8,9},{10,11},{12,13},{14,15},{16,17},{18,... | collective-permute-start | bytes 393224 | tf_op jit(solution)/shard_map/ppermute | solution.py:221
  38.2 4.8 %all-to-all-start.1 = ((bf16[4,192,1024]{2,1,0:T(8,128)(2,1)}), bf16[4,192,1024]{2,1,0:T(8,128)(2,1)S(1)}, u32[]{:S(2)}, u32[]{:S(2)}) async-start(bf16[4,192,1024]{2,1,0:T(8,128)(2,1)} %copy-done), calls=%async_computation.1 | async-start | bytes 3145728 | tf_op jit(solution)/shard_map/all_to_all | solution.py:229
  44.7 3.2 %collective-permute-start.13 = (bf16[3,128,1024]{2,1,0:T(8,128)(2,1)}, bf16[3,128,1024]{2,1,0:T(8,128)(2,1)}, u32[]{:S(2)}, u32[]{:S(2)}) collective-permute-start(bf16[3,128,1024]{2,1,0:T(8,128)(2,1)} %get-tuple-element.19), channel_id=1, source_target_pairs={{0,32},{32,0},{1,33},{33,1},{2,34},{34,2},{3,35},{35,3},{4,36},{36... | collective-permute-start | bytes 2359304 | tf_op jit(solution)/shard_map/ppermute | solution.py:259
  47.9 10.0 %collective-permute-done.2.cov_got = bf16[3,64,1024]{2,1,0:T(8,128)(2,1)S(1)} collective-permute-done((bf16[3,64,1024]{2,1,0:T(8,128)(2,1)S(1)}, bf16[3,64,1024]{2,1,0:T(8,128)(2,1)S(1)}, u32[]{:S(2)}, u32[]{:S(2)}) %collective-permute-start.2) | collective-permute-done | bytes 393248 | tf_op jit(solution)/shard_map/ppermute | solution.py:258
  58.6 2.6 %all-to-all-done.1.second = bf16[4,192,1024]{2,1,0:T(8,128)(2,1)S(1)} async-done(((bf16[4,192,1024]{2,1,0:T(8,128)(2,1)}), bf16[4,192,1024]{2,1,0:T(8,128)(2,1)S(1)}, u32[]{:S(2)}, u32[]{:S(2)}) %all-to-all-start.1) | async-done | bytes 1572896 | tf_op jit(solution)/shard_map/all_to_all | solution.py:229
  63.1 2.1 %collective-permute-start.10 = (bf16[128,1024]{1,0:T(8,128)(2,1)S(1)}, bf16[128,1024]{1,0:T(8,128)(2,1)S(1)}, u32[]{:S(2)}, u32[]{:S(2)}) collective-permute-start(bf16[128,1024]{1,0:T(8,128)(2,1)S(1)} %get-tuple-element.16.refs_1_), channel_id=1, source_target_pairs={{0,192},{64,0},{128,64},{192,128},{1,193},{65,1},{129,65},{193,129... | collective-permute-start | bytes 786440 | tf_op jit(solution)/shard_map/ppermute | solution.py:274
  65.9 5.2 %collective-permute-done.10.refs_1_.refs_8_ = bf16[128,1024]{1,0:T(8,128)(2,1)S(1)} collective-permute-done((bf16[128,1024]{1,0:T(8,128)(2,1)S(1)}, bf16[128,1024]{1,0:T(8,128)(2,1)S(1)}, u32[]{:S(2)}, u32[]{:S(2)}) %collective-permute-start.10) | collective-permute-done | bytes 262176 | tf_op jit(solution)/shard_map/ppermute | solution.py:274
  71.1 1.5 %collective-permute-done.12.refs_3_.refs_9_ = bf16[128,1024]{1,0:T(8,128)(2,1)S(1)} collective-permute-done((bf16[128,1024]{1,0:T(8,128)(2,1)S(1)}, bf16[128,1024]{1,0:T(8,128)(2,1)S(1)}, u32[]{:S(2)}, u32[]{:S(2)}) %collective-permute-start.12) | collective-permute-done | bytes 262176 | tf_op jit(solution)/shard_map/ppermute | solution.py:274
  72.6 1.5 %collective-permute-done.17.refs_7_ = bf16[128,1024]{1,0:T(8,128)(2,1)S(1)} collective-permute-done((bf16[128,1024]{1,0:T(8,128)(2,1)S(1)}, bf16[128,1024]{1,0:T(8,128)(2,1)S(1)}, u32[]{:S(2)}, u32[]{:S(2)}) %collective-permute-start.17) | collective-permute-done | bytes 262176 | tf_op jit(solution)/shard_map/ppermute | solution.py:275
  74.1 4.8 %shard_map.59 = (f32[512,128]{1,0:T(8,128)S(1)}, bf16[4,512,128]{2,1,0:T(8,128)(2,1)}) custom-call(bf16[4,192,1024]{2,1,0:T(8,128)(2,1)S(1)} %all-to-all-done.first, bf16[192,1024]{1,0:T(8,128)(2,1)S(1)} %collective-permute-done.1.own_got.refs_3_, bf16[3,128,1024]{2,1,0:T(8,128)(2,1)} %collective-permute-done.13.jac_got, ...), custom_call_target="tpu_custom_call" | custom-call | flops 1073741824 | bytes 2097152 | tf_op jit(solution)/shard_map/pallas_call | solution.py:27
  78.8 6.9 %all-to-all-start.2 = ((bf16[4,512,128]{2,1,0:T(8,128)(2,1)}), bf16[4,512,128]{2,1,0:T(8,128)(2,1)S(1)}, u32[]{:S(2)}, u32[]{:S(2)}) async-start(bf16[4,512,128]{2,1,0:T(8,128)(2,1)} %get-tuple-element.21), calls=%async_computation.2 | async-start | bytes 1048576 | tf_op jit(solution)/shard_map/all_to_all | solution.py:229
  85.8 12.6 %all-to-all-done.2.got = bf16[4,512,128]{2,1,0:T(8,128)(2,1)S(1)} async-done(((bf16[4,512,128]{2,1,0:T(8,128)(2,1)}), bf16[4,512,128]{2,1,0:T(8,128)(2,1)S(1)}, u32[]{:S(2)}, u32[]{:S(2)}) %all-to-all-start.2) | async-done | bytes 524320 | tf_op jit(solution)/shard_map/all_to_all | solution.py:229
  99.2 8.1 %all-to-all-start.3 = ((bf16[16,32,128]{2,1,0:T(8,128)(2,1)}), bf16[16,32,128]{2,1,0:T(8,128)(2,1)S(1)}, u32[]{:S(2)}, u32[]{:S(2)}) async-start(bf16[16,32,128]{2,1,0:T(8,128)(2,1)} %bitcast), calls=%async_computation.3 | async-start | bytes 262144 | tf_op jit(solution)/shard_map/all_to_all | solution.py:229
  108.3 7.5 %all-to-all-done.3.got = bf16[16,32,128]{2,1,0:T(8,128)(2,1)S(1)} async-done(((bf16[16,32,128]{2,1,0:T(8,128)(2,1)}), bf16[16,32,128]{2,1,0:T(8,128)(2,1)S(1)}, u32[]{:S(2)}, u32[]{:S(2)}) %all-to-all-start.3) | async-done | bytes 131104 | tf_op jit(solution)/shard_map/all_to_all | solution.py:229
  (55 shorter events, 16.7 us)
Async XLA Ops:
  1.9 2.0 %collective-permute-start = (bf16[64,4096]{1,0:T(8,128)(2,1)S(1)}, bf16[64,4096]{1,0:T(8,128)(2,1)S(1)}, u32[]{:S(2)}, u32[]{:S(2)}) collective-permute-start(bf16[64,4096]{1,0:T(8,128)(2,1)S(1)} %shard_map.50), channel_id=1, source_target_pairs={{0,1},{1,0},{2,3},{3,2},{4,5},{5,4},{6,7},{7,6},{8,9},{9,8},{10,11... | collective-permute-start | bytes 1572872 | tf_op jit(solution)/shard_map/ppermute | solution.py:238
  5.7 32.5 %all-to-all-start = ((bf16[4,192,1024]{2,1,0:T(8,128)(2,1)}), bf16[4,192,1024]{2,1,0:T(8,128)(2,1)S(1)}, u32[]{:S(2)}, u32[]{:S(2)}) async-start(bf16[4,192,1024]{2,1,0:T(8,128)(2,1)} %copy-done.3), calls=%async_computation | async-start | bytes 3145728 | tf_op jit(solution)/shard_map/all_to_all | solution.py:229
  11.5 25.2 %copy-start.4 = (bf16[128,4096]{1,0:T(8,128)(2,1)S(1)}, bf16[128,4096]{1,0:T(8,128)(2,1)}, u32[]{:S(2)}) copy-start(bf16[128,4096]{1,0:T(8,128)(2,1)} %carry.1) | copy-start | bytes 3145732
  11.5 22.9 %collective-permute-start.1 = (bf16[192,1024]{1,0:T(8,128)(2,1)S(1)}, bf16[192,1024]{1,0:T(8,128)(2,1)S(1)}, u32[]{:S(2)}, u32[]{:S(2)}) collective-permute-start(bf16[192,1024]{1,0:T(8,128)(2,1)S(1)} %get-tuple-element.13), channel_id=1, source_target_pairs={{0,32},{32,0},{1,33},{33,1},{2,34},{34,2},{3,35},{35,3},{4,36},{36... | collective-permute-start | bytes 1179656 | tf_op jit(solution)/shard_map/ppermute | solution.py:247
  13.7 12.7 %collective-permute-start.3 = (bf16[128,512]{1,0:T(8,128)(2,1)S(1)}, bf16[128,512]{1,0:T(8,128)(2,1)S(1)}, u32[]{:S(2)}, u32[]{:S(2)}) collective-permute-start(bf16[128,512]{1,0:T(8,128)(2,1)S(1)} %slice.3.value), channel_id=1, source_target_pairs={{0,8},{1,9},{32,40},{33,41},{64,72},{65,73},{96,104},{97,105},{128... | collective-permute-start | bytes 393224 | tf_op jit(solution)/shard_map/ppermute | solution.py:217
  22.8 5.0 %collective-permute-start.4 = (bf16[128,512]{1,0:T(8,128)(2,1)S(1)}, bf16[128,512]{1,0:T(8,128)(2,1)S(1)}, u32[]{:S(2)}, u32[]{:S(2)}) collective-permute-start(bf16[128,512]{1,0:T(8,128)(2,1)S(1)} %slice.3.value), channel_id=1, source_target_pairs={{0,20},{1,21},{32,52},{33,53},{64,84},{65,85},{96,116},{97,117},{1... | collective-permute-start | bytes 393224 | tf_op jit(solution)/shard_map/ppermute | solution.py:217
  24.1 3.8 %collective-permute-start.5 = (bf16[128,512]{1,0:T(8,128)(2,1)S(1)}, bf16[128,512]{1,0:T(8,128)(2,1)S(1)}, u32[]{:S(2)}, u32[]{:S(2)}) collective-permute-start(bf16[128,512]{1,0:T(8,128)(2,1)S(1)} %slice.3.value), channel_id=1, source_target_pairs={{0,28},{1,29},{32,60},{33,61},{64,92},{65,93},{96,124},{97,125},{1... | collective-permute-start | bytes 393224 | tf_op jit(solution)/shard_map/ppermute | solution.py:217
  28.0 3.9 %collective-permute-start.6 = (bf16[128,512]{1,0:T(8,128)(2,1)S(1)}, bf16[128,512]{1,0:T(8,128)(2,1)S(1)}, u32[]{:S(2)}, u32[]{:S(2)}) collective-permute-start(bf16[128,512]{1,0:T(8,128)(2,1)S(1)} %shard_map.53.value), channel_id=1, source_target_pairs={{0,2},{8,6},{20,18},{28,26},{1,3},{9,7},{21,19},{29,27},{32,34},{4... | collective-permute-start | bytes 393224 | tf_op jit(solution)/shard_map/ppermute | solution.py:217
  29.3 3.8 %collective-permute-start.7 = (bf16[128,512]{1,0:T(8,128)(2,1)S(1)}, bf16[128,512]{1,0:T(8,128)(2,1)S(1)}, u32[]{:S(2)}, u32[]{:S(2)}) collective-permute-start(bf16[128,512]{1,0:T(8,128)(2,1)S(1)} %shard_map.53.value), channel_id=1, source_target_pairs={{0,14},{8,10},{20,22},{28,30},{1,15},{9,11},{21,23},{29,31},{32,46... | collective-permute-start | bytes 393224 | tf_op jit(solution)/shard_map/ppermute | solution.py:217
  30.6 3.8 %collective-permute-start.8 = (bf16[128,512]{1,0:T(8,128)(2,1)S(1)}, bf16[128,512]{1,0:T(8,128)(2,1)S(1)}, u32[]{:S(2)}, u32[]{:S(2)}) collective-permute-start(bf16[128,512]{1,0:T(8,128)(2,1)S(1)} %shard_map.53.value), channel_id=1, source_target_pairs={{0,16},{8,24},{20,4},{28,12},{1,17},{9,25},{21,5},{29,13},{32,48},... | collective-permute-start | bytes 393224 | tf_op jit(solution)/shard_map/ppermute | solution.py:217
  34.4 2.3 %collective-permute-start.9 = (bf16[128,512]{1,0:T(8,128)(2,1)S(1)}, bf16[128,512]{1,0:T(8,128)(2,1)S(1)}, u32[]{:S(2)}, u32[]{:S(2)}) collective-permute-start(bf16[128,512]{1,0:T(8,128)(2,1)S(1)} %shard_map.54.value), channel_id=1, source_target_pairs={{0,1},{2,3},{4,5},{6,7},{8,9},{10,11},{12,13},{14,15},{16,17},{18,... | collective-permute-start | bytes 393224 | tf_op jit(solution)/shard_map/ppermute | solution.py:221
  38.2 23.1 %all-to-all-start.1 = ((bf16[4,192,1024]{2,1,0:T(8,128)(2,1)}), bf16[4,192,1024]{2,1,0:T(8,128)(2,1)S(1)}, u32[]{:S(2)}, u32[]{:S(2)}) async-start(bf16[4,192,1024]{2,1,0:T(8,128)(2,1)} %copy-done), calls=%async_computation.1 | async-start | bytes 3145728 | tf_op jit(solution)/shard_map/all_to_all | solution.py:229
  44.3 13.6 %collective-permute-start.2 = (bf16[3,64,1024]{2,1,0:T(8,128)(2,1)S(1)}, bf16[3,64,1024]{2,1,0:T(8,128)(2,1)S(1)}, u32[]{:S(2)}, u32[]{:S(2)}) collective-permute-start(bf16[3,64,1024]{2,1,0:T(8,128)(2,1)S(1)} %get-tuple-element.14), channel_id=1, source_target_pairs={{0,32},{32,0},{1,33},{33,1},{2,34},{34,2},{3,35},{35,3},{4,36},{36... | collective-permute-start | bytes 1179656 | tf_op jit(solution)/shard_map/ppermute | solution.py:258
  44.7 29.4 %collective-permute-start.13 = (bf16[3,128,1024]{2,1,0:T(8,128)(2,1)}, bf16[3,128,1024]{2,1,0:T(8,128)(2,1)}, u32[]{:S(2)}, u32[]{:S(2)}) collective-permute-start(bf16[3,128,1024]{2,1,0:T(8,128)(2,1)} %get-tuple-element.19), channel_id=1, source_target_pairs={{0,32},{32,0},{1,33},{33,1},{2,34},{34,2},{3,35},{35,3},{4,36},{36... | collective-permute-start | bytes 2359304 | tf_op jit(solution)/shard_map/ppermute | solution.py:259
  63.1 7.9 %collective-permute-start.10 = (bf16[128,1024]{1,0:T(8,128)(2,1)S(1)}, bf16[128,1024]{1,0:T(8,128)(2,1)S(1)}, u32[]{:S(2)}, u32[]{:S(2)}) collective-permute-start(bf16[128,1024]{1,0:T(8,128)(2,1)S(1)} %get-tuple-element.16.refs_1_), channel_id=1, source_target_pairs={{0,192},{64,0},{128,64},{192,128},{1,193},{65,1},{129,65},{193,129... | collective-permute-start | bytes 786440 | tf_op jit(solution)/shard_map/ppermute | solution.py:274
  65.3 7.3 %collective-permute-start.12 = (bf16[128,1024]{1,0:T(8,128)(2,1)S(1)}, bf16[128,1024]{1,0:T(8,128)(2,1)S(1)}, u32[]{:S(2)}, u32[]{:S(2)}) collective-permute-start(bf16[128,1024]{1,0:T(8,128)(2,1)S(1)} %get-tuple-element.18.refs_3_), channel_id=1, source_target_pairs={{0,64},{64,128},{128,192},{192,0},{1,65},{65,129},{129,193},{193,1... | collective-permute-start | bytes 786440 | tf_op jit(solution)/shard_map/ppermute | solution.py:274
  65.4 7.2 %collective-permute-start.15 = (bf16[128,1024]{1,0:T(8,128)(2,1)S(1)}, bf16[128,1024]{1,0:T(8,128)(2,1)S(1)}, u32[]{:S(2)}, u32[]{:S(2)}) collective-permute-start(bf16[128,1024]{1,0:T(8,128)(2,1)S(1)} %get-tuple-element.16.refs_1_), channel_id=1, source_target_pairs={{0,1},{1,0},{2,3},{3,2},{4,5},{5,4},{6,7},{7,6},{8,9},{9,8},{10,11... | collective-permute-start | bytes 786440 | tf_op jit(solution)/shard_map/ppermute | solution.py:275
  65.4 7.2 %collective-permute-start.14 = (bf16[128,1024]{1,0:T(8,128)(2,1)S(1)}, bf16[128,1024]{1,0:T(8,128)(2,1)S(1)}, u32[]{:S(2)}, u32[]{:S(2)}) collective-permute-start(bf16[128,1024]{1,0:T(8,128)(2,1)S(1)} %get-tuple-element.15.refs_0_), channel_id=1, source_target_pairs={{0,1},{1,0},{2,3},{3,2},{4,5},{5,4},{6,7},{7,6},{8,9},{9,8},{10,11... | collective-permute-start | bytes 786440 | tf_op jit(solution)/shard_map/ppermute | solution.py:275
  71.1 1.5 %collective-permute-start.16 = (bf16[128,1024]{1,0:T(8,128)(2,1)S(1)}, bf16[128,1024]{1,0:T(8,128)(2,1)S(1)}, u32[]{:S(2)}, u32[]{:S(2)}) collective-permute-start(bf16[128,1024]{1,0:T(8,128)(2,1)S(1)} %get-tuple-element.17.refs_2_), channel_id=1, source_target_pairs={{0,1},{1,0},{2,3},{3,2},{4,5},{5,4},{6,7},{7,6},{8,9},{9,8},{10,11... | collective-permute-start | bytes 786440 | tf_op jit(solution)/shard_map/ppermute | solution.py:275
  72.5 1.5 %collective-permute-start.17 = (bf16[128,1024]{1,0:T(8,128)(2,1)S(1)}, bf16[128,1024]{1,0:T(8,128)(2,1)S(1)}, u32[]{:S(2)}, u32[]{:S(2)}) collective-permute-start(bf16[128,1024]{1,0:T(8,128)(2,1)S(1)} %get-tuple-element.18.refs_3_), channel_id=1, source_target_pairs={{0,1},{1,0},{2,3},{3,2},{4,5},{5,4},{6,7},{7,6},{8,9},{9,8},{10,11... | collective-permute-start | bytes 786440 | tf_op jit(solution)/shard_map/ppermute | solution.py:275
  78.8 28.4 %copy-start.6 = (bf16[128,1024]{1,0:T(8,128)(2,1)S(1)}, bf16[128,1024]{1,0:T(8,128)(2,1)}, u32[]{:S(2)}) copy-start(bf16[128,1024]{1,0:T(8,128)(2,1)} %copy-done.5) | copy-start | bytes 786436
  78.8 19.6 %all-to-all-start.2 = ((bf16[4,512,128]{2,1,0:T(8,128)(2,1)}), bf16[4,512,128]{2,1,0:T(8,128)(2,1)S(1)}, u32[]{:S(2)}, u32[]{:S(2)}) async-start(bf16[4,512,128]{2,1,0:T(8,128)(2,1)} %get-tuple-element.21), calls=%async_computation.2 | async-start | bytes 1048576 | tf_op jit(solution)/shard_map/all_to_all | solution.py:229
  85.7 21.6 %collective-permute-start.11 = (bf16[128,1024]{1,0:T(8,128)(2,1)}, bf16[128,1024]{1,0:T(8,128)(2,1)S(1)}, u32[]{:S(2)}, u32[]{:S(2)}) collective-permute-start(bf16[128,1024]{1,0:T(8,128)(2,1)} %copy-done.10), channel_id=1, source_target_pairs={{0,128},{64,192},{128,0},{192,64},{1,129},{65,193},{129,1},{193,65... | collective-permute-start | bytes 786440 | tf_op jit(solution)/shard_map/ppermute | solution.py:274
  99.2 16.7 %all-to-all-start.3 = ((bf16[16,32,128]{2,1,0:T(8,128)(2,1)}), bf16[16,32,128]{2,1,0:T(8,128)(2,1)S(1)}, u32[]{:S(2)}, u32[]{:S(2)}) async-start(bf16[16,32,128]{2,1,0:T(8,128)(2,1)} %bitcast), calls=%async_computation.3 | async-start | bytes 262144 | tf_op jit(solution)/shard_map/all_to_all | solution.py:229
  (9 other events, 40.9 us)

commit v4 on v2

v4 whole, which is shorter than its diff:
```python
import math

import jax
import jax.numpy as jnp
from jax import lax
from jax.experimental import pallas as pl
from jax.experimental.pallas import tpu as pltpu
from jax.sharding import Mesh, PartitionSpec as P

PARAMS = 131072
WIDTH = 512
X, H, L, Z, C = 4, 2, 2, 8, 2
AXES = ("x", "h", "l", "z", "c")
ANY = pl.BlockSpec(memory_space=pl.ANY)
VMEM = pl.BlockSpec(memory_space=pltpu.VMEM)
BF16, F32 = jnp.bfloat16, jnp.float32
SWAP = [(0, 1), (1, 0)]
MIB = 2**20


def source(d):
    return lax.rem(lax.axis_index("x") + X - d, X)


def call(kernel, outs, ins, spec, scratch=(), flops=0, nbytes=0, vmem=1, behind=()):
    return pl.pallas_call(
        kernel,
        out_shape=outs,
        in_specs=[spec] * len(ins) + [ANY] * len(behind),
        out_specs=jax.tree.map(lambda _: spec, outs),
        scratch_shapes=list(scratch),
        cost_estimate=pl.CostEstimate(flops=flops, bytes_accessed=nbytes, transcendentals=0),
        compiler_params=pltpu.CompilerParams(vmem_limit_bytes=vmem * MIB),
    )(*ins, *behind)


def shape(*dims, kind=BF16):
    return jax.ShapeDtypeStruct(dims, kind)


def run_copies(copies, sems):
    started = [pltpu.make_async_copy(a, b, sems.at[k]) for k, (a, b) in enumerate(copies)]
    for copy in started:
        copy.start()
    for copy in started:
        copy.wait()


def slab(half, core):
    return pl.ds(pl.multiple_of(half * 64 + core * 32, 32), 32)


def give_kernel(jac, give, sems):
    other = 1 - lax.axis_index("c")
    run_copies(
        [(jac.at[slab(k, other), :], give.at[pl.ds(k * 32, 32), :]) for k in range(2)], sems
    )


def part(d):
    at = lax.rem(lax.axis_index("x") + d, X)
    return pl.ds(pl.multiple_of(at * 1024, 1024), 1024)


def pack_kernel(jac, got, cov, *refs):
    outs, panel, sems, panel_sems = refs[:X], refs[X], refs[X + 1], refs[X + 2]
    core = lax.axis_index("c")

    def pieces(ref, rows):
        return [
            pltpu.make_async_copy(
                ref.at[rows(k), pl.ds(n * 128, 128)], panel.at[k * 4 + n], panel_sems.at[k * 4 + n]
            )
            for k in range(4)
            for n in range(4)
        ]

    @pl.when(core == 0)
    def _():
        for copy in pieces(jac, lambda k: pl.ds(k // 2 * 64 + k % 2 * 16, 16)):
            copy.start()

    @pl.when(core == 1)
    def _():
        for copy in pieces(got, lambda k: pl.ds(k * 16, 16)):
            copy.start()

    copies = []
    for d in range(X):
        copies += [(jac.at[slab(n, core), part(d)], outs[d].at[pl.ds(n * 32, 32), :]) for n in range(2)]
        copies.append((got.at[:, part(d)], outs[d].at[pl.ds(64, 64), :]))
        copies.append((cov.at[:, part(d)], outs[d].at[pl.ds(128, 64), :]))
    run_copies(copies, sems)
    for copy in pieces(got, lambda k: pl.ds(k * 16, 16)):
        copy.wait()


def carry_kernel(carry, *refs):
    run_copies([(carry.at[:, part(d)], refs[d]) for d in range(X)], refs[X])


def rest_kernel(*refs):
    first, cov, jac, sems = refs[: X - 1], refs[-3], refs[-2], refs[-1]
    copies = []
    for d in range(1, X):
        copies.append((first[d - 1].at[pl.ds(128, 64), :], cov.at[d - 1]))
        copies.append((first[d - 1].at[pl.ds(0, 128), :], jac.at[d - 1]))
    run_copies(copies, sems)


def sens_kernel(*refs):
    first, carry, panels, (own_got, cov_got) = refs[:4], refs[4:8], refs[8:12], refs[12:14]
    outs, cov, panel = refs[14:18], refs[18], refs[19]
    h = lax.axis_index("h")

    def rows(d, side):
        return pl.ds(pl.multiple_of((source(d) * H + side) * 64, 64), 64)

    for d in range(X):
        cov[rows(d, h), :] = first[d][128:192, :]
        cov[rows(d, 1 - h), :] = cov_got[d - 1] if d else own_got[128:192, :]
    for d in range(X):
        for k in range(4):
            for n in range(4):
                for core in range(C):
                    at = d * 128 + k // 2 * 64 + core * 32 + k % 2 * 16
                    panel[at : at + 16, n * 128 : n * 128 + 128] = panels[d][(k * 4 + n) * C + core]
    for d in range(X):
        product = jnp.dot(
            panel[d * 128 : (d + 1) * 128, :], cov[...], preferred_element_type=F32
        )
        value = carry[d][...].astype(F32) + product * (1.0 / math.sqrt(WIDTH))
        outs[d][...] = value.astype(BF16)


def innov_kernel(own_got, jac_got, *refs):
    first, sens, sens_got = refs[:X], refs[X : 2 * X], refs[2 * X : 3 * X]
    own, parts, jac, both = refs[-4:]
    h = lax.axis_index("h")
    for d in range(X):
        for side, ref in ((h, first[d]), (1 - h, jac_got.at[d - 1] if d else own_got)):
            to = pl.ds(pl.multiple_of((source(d) * H + side) * 64, 64), 64)
            jac[to, 0:1024] = ref[0:64, :]
            jac[to, 1024:2048] = ref[64:128, :]
        both[d * 128 : (d + 1) * 128, 0:1024] = sens[d][...]
        both[d * 128 : (d + 1) * 128, 1024:2048] = sens_got[d][...]
    value = lax.dot_general(
        jac[...], both[...], (((1,), (1,)), ((), ())), preferred_element_type=F32
    )
    own[...] = value[:, 0:128]
    for d in range(X):
        parts[source(d)] = value[:, d * 128 : (d + 1) * 128].astype(BF16)


def sum_kernel(own, got, out):
    total = own[...]
    x = lax.axis_index("x")
    for k in range(X):
        total += jnp.where(x == k, 0.0, got[k].astype(F32))
    out[...] = total.astype(BF16)


def final_kernel(got, out):
    total = got[0].astype(F32)
    for k in range(1, L * Z):
        total += got[k].astype(F32)
    out[...] = total * (1.0 / math.sqrt(PARAMS))


def assemble_kernel(*refs):
    pieces, out, sems = refs[:X], refs[X], refs[X + 1]
    copies = []
    for d in range(X):
        at = lax.rem(lax.axis_index("x") + d, X)
        copies.append((pieces[d], out.at[:, pl.ds(pl.multiple_of(at * 1024, 1024), 1024)]))
    run_copies(copies, sems)


def ring(d):
    return [(x, (x + d) % X) for x in range(X)]


def over(value, axes):
    return lax.all_to_all(value, axes, split_axis=0, concat_axis=0, tiled=True)


def dma(n):
    return [pltpu.SemaphoreType.DMA((n,))]


def body(jacobian, cov_rows, sens_carry):
    give = call(give_kernel, shape(64, 4096), (jacobian,), ANY, dma(2), nbytes=MIB)
    got = lax.ppermute(give, "c", SWAP)
    *packed, panel = call(
        pack_kernel,
        [shape(192, 1024)] * X + [shape(16, 16, 128)],
        (jacobian, got, cov_rows),
        ANY,
        dma(4 * X) + dma(16),
        nbytes=4 * MIB,
    )
    own_got = lax.ppermute(packed[0], "h", SWAP)
    first = [packed[0]] + [lax.ppermute(packed[d], "x", ring(d)) for d in range(1, X)]
    cov_rest, jac_rest = call(
        rest_kernel,
        [shape(X - 1, 64, 1024), shape(X - 1, 128, 1024)],
        first[1:],
        ANY,
        dma(2 * X - 2),
        nbytes=2 * MIB,
        behind=(own_got,),
    )
    cov_got = lax.ppermute(cov_rest, "h", SWAP)
    jac_got = lax.ppermute(jac_rest, "h", SWAP)
    mine = over(panel, ("l", "z"))[0]
    panel = over(jnp.broadcast_to(mine, (32, 16, 128)), ("l", "z", "c"))
    panels = [panel] + [lax.ppermute(panel, "x", ring(d)) for d in range(1, X)]
    packed = call(
        carry_kernel, [shape(128, 1024)] * X, (sens_carry,), ANY, dma(X), nbytes=2 * MIB
    )
    carry = [packed[0]] + [lax.ppermute(packed[d], "x", ring(d)) for d in range(1, X)]
    sens = call(
        sens_kernel,
        [shape(128, 1024)] * X,
        (*first, *carry, *panels, own_got, cov_got),
        VMEM,
        [pltpu.VMEM((512, 1024), BF16), pltpu.VMEM((512, WIDTH), BF16)],
        flops=2 * 512 * 512 * 1024,
        nbytes=2 * MIB,
        vmem=12,
    )
    sens_back = [sens[0]] + [lax.ppermute(sens[d], "x", ring(-d)) for d in range(1, X)]
    sens_got = [lax.ppermute(part, "c", SWAP) for part in sens]
    own_sum, parts = call(
        innov_kernel,
        [shape(512, 128, kind=F32), shape(X, 512, 128)],
        (own_got, jac_got, *first, *sens, *sens_got),
        VMEM,
        [pltpu.VMEM((512, 2048), BF16)] * 2,
        flops=2 * 512 * 512 * 2048,
        nbytes=2 * MIB,
        vmem=16,
        behind=(sens_back[1], sens_back[3]),
    )
    summed = call(sum_kernel, shape(512, 128), (own_sum, over(parts, "x")), VMEM, nbytes=MIB, vmem=4)
    shared = over(summed.reshape(L * Z, 32, 128), ("l", "z"))
    innovation = call(final_kernel, shape(32, 128, kind=F32), (shared,), VMEM, nbytes=2**17, vmem=4)
    sensitivity = call(
        assemble_kernel, shape(128, 4096), sens_back, ANY, dma(X), nbytes=2 * MIB
    )
    return (sensitivity, innovation.T)


def solution(mesh):
    fine = Mesh(mesh.devices.reshape(X, H, L, Z, C), AXES)
    spec = P(("x", "h"), ("l", "z", "c"))
    return jax.shard_map(
        body, mesh=fine, in_specs=(spec,) * 3, out_specs=(spec,) * 2, check_vma=False
    )
```

time: 124 us -> 115 us (0.927)
  Pallas kernels: 15.5 us -> 8.76 us
  starting transfers between devices: 56.8 us -> 53.3 us
  local copies, waits for them, and re-layouts: 5.26 us -> 7.61 us
  other arithmetic: 1.9 us -> 0 us
  waiting for transfers between devices: 42.6 us -> 44.5 us
    ppermute x1, waiting for transfers between devices: 13.5 us -> 0.01 us  [body(): cov_got = lax.ppermute(cov_rest, 'h', SWAP)]
    all_to_all x4, waiting for transfers between devices: 16.4 us -> 26.8 us  [over(): return lax.all_to_all(value, axes, split_axis=0, concat_axis=0, tiled=True)]
    ppermute x8 -> x7, starting transfers between devices: 22.1 us -> 12.1 us  [the longest x6 8.79 us: body(): lax.ppermute(packed[d], 'x', ring(d))]
    pallas_call x9, Pallas kernels: 15.5 us -> 8.76 us  [call(): pl.pallas_call(kernel, out_shape=outs, in_specs=[spec] * len(ins) + [ANY]...]
    all_to_all x4, starting transfers between devices: 23.7 us -> 29.1 us  [over(): return lax.all_to_all(value, axes, split_axis=0, concat_axis=0, tiled=True)]
    ppermute x3, waiting for transfers between devices: 0.01 us -> 4.93 us  [body(): lax.ppermute(sens[d], 'x', ring(-d))]
    ppermute x3, starting transfers between devices: 2.84 us -> 5.87 us  [body(): panels = [panel] + [lax.ppermute(panel, 'x', ring(d)) for d in range(1, X)]]
    unnamed x22 -> x28, local copies, waits for them, and re-layouts: 4.35 us -> 6.92 us
  transfers between devices with their start and end apart: 25 -> 24, of which waited for: 11 -> 13; matrix products, arithmetic and copies ran while one was open for 2% -> 1% of each run, Pallas kernels for 5% -> 5%
where the time goes in v4:
time: 115 us
  starting transfers between devices  53.3 us (46%)
  waiting for transfers between devices  44.5 us (39%)
  Pallas kernels  8.76 us (8%)
  local copies, waits for them, and re-layouts  7.61 us (7%)
    all_to_all x4, starting transfers between devices, over(): return lax.all_to_all(value, axes, split_axis=0, concat_axis=0, tiled=True)  29.1 us
    all_to_all x4, waiting for transfers between devices, over(): return lax.all_to_all(value, axes, split_axis=0, concat_axis=0, tiled=True)  26.8 us
    ppermute x6, starting transfers between devices, body(): lax.ppermute(packed[d], 'x', ring(d))  8.79 us
    pallas_call x9, Pallas kernels, call(): pl.pallas_call(kernel, out_shape=outs, in_specs=[spec] * len(ins) + [ANY]...  8.76 us
    unnamed x28, local copies, waits for them, and re-layouts  6.92 us
    ppermute x3, starting transfers between devices, body(): panels = [panel] + [lax.ppermute(panel, 'x', ring(d)) for d in range(1, X)]  5.87 us
    ppermute x3, waiting for transfers between devices, body(): panels = [panel] + [lax.ppermute(panel, 'x', ring(d)) for d in range(1, X)]  5.7 us
    ppermute x3, waiting for transfers between devices, body(): lax.ppermute(sens[d], 'x', ring(-d))  4.93 us
  transfers between devices with their start and end apart: 24, of which 13 were waited for; matrix products, arithmetic and copies ran while one was open for 1% of the time, Pallas kernels for 5%

profile of v4, /device:TPU:4, one launch (start us, length us, event | category | flops | bytes accessed | tf_op | source)
XLA Modules:
  0.0 115.0 jit_solution(1325400338774191608)
XLA Ops:
  0.6 1.2 %copy-done = bf16[128,4096]{1,0:T(8,128)(2,1)S(1)} copy-done((bf16[128,4096]{1,0:T(8,128)(2,1)S(1)}, bf16[128,4096]{1,0:T(8,128)(2,1)}, u32[]{:S(2)}) %copy-start) | copy-done | bytes 1048600
  2.0 1.9 %collective-permute-done.got = bf16[64,4096]{1,0:T(8,128)(2,1)S(1)} collective-permute-done((bf16[64,4096]{1,0:T(8,128)(2,1)S(1)}, bf16[64,4096]{1,0:T(8,128)(2,1)S(1)}, u32[]{:S(2)}, u32[]{:S(2)}) %collective-permute-start) | collective-permute-done | bytes 524320 | tf_op jit(solution)/shard_map/ppermute | solution.py:193
  3.9 1.3 %shard_map.51 = (bf16[192,1024]{1,0:T(8,128)(2,1)S(1)}, bf16[192,1024]{1,0:T(8,128)(2,1)}, bf16[192,1024]{1,0:T(8,128)(2,1)}, bf16[192,1024]{1,0:T(8,128)(2,1)S(1)}, bf16[16,16,128]{2,1,0:T(8,128)(2,1)}) custom-call(bf16[128,4096]{1,0:T(8,128)(2,1)S(1)} %copy-done.1, bf16[64,4096]{1,0:T(8,128)(2,1)S(1)} %collective-permute-done.got, ...), custom_call_target="tpu_custom_call" | custom-call | bytes 4194304 | tf_op jit(solution)/shard_map/pallas_call | solution.py:26
  5.3 3.3 %collective-permute-start.10 = (bf16[192,1024]{1,0:T(8,128)(2,1)S(1)}, bf16[192,1024]{1,0:T(8,128)(2,1)S(1)}, u32[]{:S(2)}, u32[]{:S(2)}) collective-permute-start(bf16[192,1024]{1,0:T(8,128)(2,1)S(1)} %get-tuple-element.19.refs_0_), channel_id=1, source_target_pairs={{0,32},{32,0},{1,33},{33,1},{2,34},{34,2},{3,35},{35,3},{4,36},{36... | collective-permute-start | bytes 1179656 | tf_op jit(solution)/shard_map/ppermute | solution.py:202
  8.5 1.2 %collective-permute-start.1 = (bf16[192,1024]{1,0:T(8,128)(2,1)}, bf16[192,1024]{1,0:T(8,128)(2,1)S(1)}, u32[]{:S(2)}, u32[]{:S(2)}) collective-permute-start(bf16[192,1024]{1,0:T(8,128)(2,1)} %get-tuple-element.20), channel_id=1, source_target_pairs={{0,64},{64,128},{128,192},{192,0},{1,65},{65,129},{129,193},{193,1... | collective-permute-start | bytes 1179656 | tf_op jit(solution)/shard_map/ppermute | solution.py:203
  11.7 8.7 %all-to-all-start = ((bf16[16,16,128]{2,1,0:T(8,128)(2,1)}), bf16[16,16,128]{2,1,0:T(8,128)(2,1)S(1)}, u32[]{:S(2)}, u32[]{:S(2)}) async-start(bf16[16,16,128]{2,1,0:T(8,128)(2,1)} %get-tuple-element.27), calls=%async_computation | async-start | bytes 131072 | tf_op jit(solution)/shard_map/all_to_all | solution.py:184
  23.0 2.7 %collective-permute-start.5 = (bf16[128,1024]{1,0:T(8,128)(2,1)}, bf16[128,1024]{1,0:T(8,128)(2,1)}, u32[]{:S(2)}, u32[]{:S(2)}) collective-permute-start(bf16[128,1024]{1,0:T(8,128)(2,1)} %get-tuple-element.25), channel_id=1, source_target_pairs={{0,128},{64,192},{128,0},{192,64},{1,129},{65,193},{129,1},{193,65... | collective-permute-start | bytes 786440 | tf_op jit(solution)/shard_map/ppermute | solution.py:221
  25.7 2.0 %collective-permute-start.6 = (bf16[128,1024]{1,0:T(8,128)(2,1)}, bf16[128,1024]{1,0:T(8,128)(2,1)}, u32[]{:S(2)}, u32[]{:S(2)}) collective-permute-start(bf16[128,1024]{1,0:T(8,128)(2,1)} %get-tuple-element.26), channel_id=1, source_target_pairs={{0,192},{64,0},{128,64},{192,128},{1,193},{65,1},{129,65},{193,129... | collective-permute-start | bytes 786440 | tf_op jit(solution)/shard_map/ppermute | solution.py:221
  27.7 1.5 %collective-permute-done.2.refs_1_.refs_2_ = bf16[192,1024]{1,0:T(8,128)(2,1)S(1)} collective-permute-done((bf16[192,1024]{1,0:T(8,128)(2,1)}, bf16[192,1024]{1,0:T(8,128)(2,1)S(1)}, u32[]{:S(2)}, u32[]{:S(2)}) %collective-permute-start.2) | collective-permute-done | bytes 393248 | tf_op jit(solution)/shard_map/ppermute | solution.py:203
  29.2 2.1 %collective-permute-done.3.refs_2_.refs_3_ = bf16[192,1024]{1,0:T(8,128)(2,1)S(1)} collective-permute-done((bf16[192,1024]{1,0:T(8,128)(2,1)S(1)}, bf16[192,1024]{1,0:T(8,128)(2,1)S(1)}, u32[]{:S(2)}, u32[]{:S(2)}) %collective-permute-start.3) | collective-permute-done | bytes 393248 | tf_op jit(solution)/shard_map/ppermute | solution.py:203
  34.0 9.8 %all-to-all-start.1 = ((bf16[32,16,128]{2,1,0:T(8,128)(2,1)}), bf16[32,16,128]{2,1,0:T(8,128)(2,1)S(1)}, u32[]{:S(2)}, u32[]{:S(2)}) async-start(bf16[32,16,128]{2,1,0:T(8,128)(2,1)} %broadcast_in_dim.3), calls=%async_computation.1 | async-start | bytes 262144 | tf_op jit(solution)/shard_map/all_to_all | solution.py:184
  43.9 3.0 %collective-permute-start.15 = (bf16[3,128,1024]{2,1,0:T(8,128)(2,1)}, bf16[3,128,1024]{2,1,0:T(8,128)(2,1)S(1)}, u32[]{:S(2)}, u32[]{:S(2)}) collective-permute-start(bf16[3,128,1024]{2,1,0:T(8,128)(2,1)} %copy-done.13), channel_id=1, source_target_pairs={{0,32},{32,0},{1,33},{33,1},{2,34},{34,2},{3,35},{35,3},{4,36},{36... | collective-permute-start | bytes 2359304 | tf_op jit(solution)/shard_map/ppermute | solution.py:214
  47.6 6.8 %all-to-all-done.1.refs_8_ = bf16[32,16,128]{2,1,0:T(8,128)(2,1)S(1)} async-done(((bf16[32,16,128]{2,1,0:T(8,128)(2,1)}), bf16[32,16,128]{2,1,0:T(8,128)(2,1)S(1)}, u32[]{:S(2)}, u32[]{:S(2)}) %all-to-all-start.1) | async-done | bytes 131104 | tf_op jit(solution)/shard_map/all_to_all | solution.py:184
  54.4 1.2 %collective-permute-start.7 = (bf16[32,16,128]{2,1,0:T(8,128)(2,1)S(1)}, bf16[32,16,128]{2,1,0:T(8,128)(2,1)S(1)}, u32[]{:S(2)}, u32[]{:S(2)}) collective-permute-start(bf16[32,16,128]{2,1,0:T(8,128)(2,1)S(1)} %all-to-all-done.1.refs_8_), channel_id=1, source_target_pairs={{0,64},{64,128},{128,192},{192,0},{1,65},{65,129},{129,193},{193,1... | collective-permute-start | bytes 393224 | tf_op jit(solution)/shard_map/ppermute | solution.py:217
  55.6 4.7 %collective-permute-start.8 = (bf16[32,16,128]{2,1,0:T(8,128)(2,1)S(1)}, bf16[32,16,128]{2,1,0:T(8,128)(2,1)S(1)}, u32[]{:S(2)}, u32[]{:S(2)}) collective-permute-start(bf16[32,16,128]{2,1,0:T(8,128)(2,1)S(1)} %all-to-all-done.1.refs_8_), channel_id=1, source_target_pairs={{0,128},{64,192},{128,0},{192,64},{1,129},{65,193},{129,1},{193,65... | collective-permute-start | bytes 393224 | tf_op jit(solution)/shard_map/ppermute | solution.py:217
  60.2 2.9 %collective-permute-done.7.refs_9_ = bf16[32,16,128]{2,1,0:T(8,128)(2,1)S(1)} collective-permute-done((bf16[32,16,128]{2,1,0:T(8,128)(2,1)S(1)}, bf16[32,16,128]{2,1,0:T(8,128)(2,1)S(1)}, u32[]{:S(2)}, u32[]{:S(2)}) %collective-permute-start.7) | collective-permute-done | bytes 131104 | tf_op jit(solution)/shard_map/ppermute | solution.py:217
  63.1 2.2 %collective-permute-done.8.refs_10_ = bf16[32,16,128]{2,1,0:T(8,128)(2,1)S(1)} collective-permute-done((bf16[32,16,128]{2,1,0:T(8,128)(2,1)S(1)}, bf16[32,16,128]{2,1,0:T(8,128)(2,1)S(1)}, u32[]{:S(2)}, u32[]{:S(2)}) %collective-permute-start.8) | collective-permute-done | bytes 131104 | tf_op jit(solution)/shard_map/ppermute | solution.py:217
  67.8 1.9 %shard_map.54 = (bf16[128,1024]{1,0:T(8,128)(2,1)S(1)}, bf16[128,1024]{1,0:T(8,128)(2,1)S(1)}, bf16[128,1024]{1,0:T(8,128)(2,1)S(1)}, bf16[128,1024]{1,0:T(8,128)(2,1)S(1)}) custom-call(bf16[192,1024]{1,0:T(8,128)(2,1)S(1)} %get-tuple-element.19.refs_0_, bf16[192,1024]{1,0:T(8,128)(2,1)S(1)} %collective-permute-done.1.refs_0_.refs_1_, ...), custom_call_target="tpu_custom_call" | custom-call | flops 536870912 | bytes 2097152 | tf_op jit(solution)/shard_map/pallas_call | solution.py:26
  72.3 3.8 %collective-permute-done.12.refs_1_.refs_12_ = bf16[128,1024]{1,0:T(8,128)(2,1)S(1)} collective-permute-done((bf16[128,1024]{1,0:T(8,128)(2,1)S(1)}, bf16[128,1024]{1,0:T(8,128)(2,1)S(1)}, u32[]{:S(2)}, u32[]{:S(2)}) %collective-permute-start.12) | collective-permute-done | bytes 262176 | tf_op jit(solution)/shard_map/ppermute | solution.py:232
  78.8 1.4 %shard_map.56 = (f32[512,128]{1,0:T(8,128)S(1)}, bf16[4,512,128]{2,1,0:T(8,128)(2,1)S(1)}) custom-call(bf16[192,1024]{1,0:T(8,128)(2,1)S(1)} %collective-permute-done.10.refs_3_.refs_12_.own_got, bf16[3,128,1024]{2,1,0:T(8,128)(2,1)S(1)} %collective-permute-done.15.jac_got, bf16[192,1024]{1,0:T(8,128)(2,1)S(1)} %get-tuple-element.19.refs_0_, ...), custom_call_target="tpu_custom_call" | custom-call | flops 1073741824 | bytes 2097152 | tf_op jit(solution)/shard_map/pallas_call | solution.py:26
  81.7 7.1 %all-to-all-start.2 = ((bf16[4,512,128]{2,1,0:T(8,128)(2,1)}), bf16[4,512,128]{2,1,0:T(8,128)(2,1)S(1)}, u32[]{:S(2)}, u32[]{:S(2)}) async-start(bf16[4,512,128]{2,1,0:T(8,128)(2,1)} %copy-done.3), calls=%async_computation.2 | async-start | bytes 1048576 | tf_op jit(solution)/shard_map/all_to_all | solution.py:184
  89.0 12.6 %all-to-all-done.2.got = bf16[4,512,128]{2,1,0:T(8,128)(2,1)S(1)} async-done(((bf16[4,512,128]{2,1,0:T(8,128)(2,1)}), bf16[4,512,128]{2,1,0:T(8,128)(2,1)S(1)}, u32[]{:S(2)}, u32[]{:S(2)}) %all-to-all-start.2) | async-done | bytes 524320 | tf_op jit(solution)/shard_map/all_to_all | solution.py:184
  102.3 3.5 %all-to-all-start.3 = ((bf16[16,32,128]{2,1,0:T(8,128)(2,1)}), bf16[16,32,128]{2,1,0:T(8,128)(2,1)S(1)}, u32[]{:S(2)}, u32[]{:S(2)}) async-start(bf16[16,32,128]{2,1,0:T(8,128)(2,1)} %bitcast.1), calls=%async_computation.3 | async-start | bytes 262144 | tf_op jit(solution)/shard_map/all_to_all | solution.py:184
  106.8 7.5 %all-to-all-done.3.got = bf16[16,32,128]{2,1,0:T(8,128)(2,1)S(1)} async-done(((bf16[16,32,128]{2,1,0:T(8,128)(2,1)}), bf16[16,32,128]{2,1,0:T(8,128)(2,1)S(1)}, u32[]{:S(2)}, u32[]{:S(2)}) %all-to-all-start.3) | async-done | bytes 131104 | tf_op jit(solution)/shard_map/all_to_all | solution.py:184
  (63 shorter events, 20.0 us)
Async XLA Ops:
  1.9 2.0 %collective-permute-start = (bf16[64,4096]{1,0:T(8,128)(2,1)S(1)}, bf16[64,4096]{1,0:T(8,128)(2,1)S(1)}, u32[]{:S(2)}, u32[]{:S(2)}) collective-permute-start(bf16[64,4096]{1,0:T(8,128)(2,1)S(1)} %shard_map.50), channel_id=1, source_target_pairs={{0,1},{1,0},{2,3},{3,2},{4,5},{5,4},{6,7},{7,6},{8,9},{9,8},{10,11... | collective-permute-start | bytes 1572872 | tf_op jit(solution)/shard_map/ppermute | solution.py:193
  5.3 17.8 %collective-permute-start.10 = (bf16[192,1024]{1,0:T(8,128)(2,1)S(1)}, bf16[192,1024]{1,0:T(8,128)(2,1)S(1)}, u32[]{:S(2)}, u32[]{:S(2)}) collective-permute-start(bf16[192,1024]{1,0:T(8,128)(2,1)S(1)} %get-tuple-element.19.refs_0_), channel_id=1, source_target_pairs={{0,32},{32,0},{1,33},{33,1},{2,34},{34,2},{3,35},{35,3},{4,36},{36... | collective-permute-start | bytes 1179656 | tf_op jit(solution)/shard_map/ppermute | solution.py:202
  8.5 17.1 %collective-permute-start.1 = (bf16[192,1024]{1,0:T(8,128)(2,1)}, bf16[192,1024]{1,0:T(8,128)(2,1)S(1)}, u32[]{:S(2)}, u32[]{:S(2)}) collective-permute-start(bf16[192,1024]{1,0:T(8,128)(2,1)} %get-tuple-element.20), channel_id=1, source_target_pairs={{0,64},{64,128},{128,192},{192,0},{1,65},{65,129},{129,193},{193,1... | collective-permute-start | bytes 1179656 | tf_op jit(solution)/shard_map/ppermute | solution.py:203
  9.7 19.5 %collective-permute-start.2 = (bf16[192,1024]{1,0:T(8,128)(2,1)}, bf16[192,1024]{1,0:T(8,128)(2,1)S(1)}, u32[]{:S(2)}, u32[]{:S(2)}) collective-permute-start(bf16[192,1024]{1,0:T(8,128)(2,1)} %get-tuple-element.21), channel_id=1, source_target_pairs={{0,128},{64,192},{128,0},{192,64},{1,129},{65,193},{129,1},{193,65... | collective-permute-start | bytes 1179656 | tf_op jit(solution)/shard_map/ppermute | solution.py:203
  10.5 20.8 %collective-permute-start.3 = (bf16[192,1024]{1,0:T(8,128)(2,1)S(1)}, bf16[192,1024]{1,0:T(8,128)(2,1)S(1)}, u32[]{:S(2)}, u32[]{:S(2)}) collective-permute-start(bf16[192,1024]{1,0:T(8,128)(2,1)S(1)} %get-tuple-element.22), channel_id=1, source_target_pairs={{0,192},{64,0},{128,64},{192,128},{1,193},{65,1},{129,65},{193,129... | collective-permute-start | bytes 1179656 | tf_op jit(solution)/shard_map/ppermute | solution.py:203
  11.7 21.7 %all-to-all-start = ((bf16[16,16,128]{2,1,0:T(8,128)(2,1)}), bf16[16,16,128]{2,1,0:T(8,128)(2,1)S(1)}, u32[]{:S(2)}, u32[]{:S(2)}) async-start(bf16[16,16,128]{2,1,0:T(8,128)(2,1)} %get-tuple-element.27), calls=%async_computation | async-start | bytes 131072 | tf_op jit(solution)/shard_map/all_to_all | solution.py:184
  22.0 24.8 %collective-permute-start.4 = (bf16[128,1024]{1,0:T(8,128)(2,1)}, bf16[128,1024]{1,0:T(8,128)(2,1)S(1)}, u32[]{:S(2)}, u32[]{:S(2)}) collective-permute-start(bf16[128,1024]{1,0:T(8,128)(2,1)} %get-tuple-element.24), channel_id=1, source_target_pairs={{0,64},{64,128},{128,192},{192,0},{1,65},{65,129},{129,193},{193,1... | collective-permute-start | bytes 786440 | tf_op jit(solution)/shard_map/ppermute | solution.py:221
  23.0 32.6 %collective-permute-start.5 = (bf16[128,1024]{1,0:T(8,128)(2,1)}, bf16[128,1024]{1,0:T(8,128)(2,1)}, u32[]{:S(2)}, u32[]{:S(2)}) collective-permute-start(bf16[128,1024]{1,0:T(8,128)(2,1)} %get-tuple-element.25), channel_id=1, source_target_pairs={{0,128},{64,192},{128,0},{192,64},{1,129},{65,193},{129,1},{193,65... | collective-permute-start | bytes 786440 | tf_op jit(solution)/shard_map/ppermute | solution.py:221
  25.7 34.6 %collective-permute-start.6 = (bf16[128,1024]{1,0:T(8,128)(2,1)}, bf16[128,1024]{1,0:T(8,128)(2,1)}, u32[]{:S(2)}, u32[]{:S(2)}) collective-permute-start(bf16[128,1024]{1,0:T(8,128)(2,1)} %get-tuple-element.26), channel_id=1, source_target_pairs={{0,192},{64,0},{128,64},{192,128},{1,193},{65,1},{129,65},{193,129... | collective-permute-start | bytes 786440 | tf_op jit(solution)/shard_map/ppermute | solution.py:221
  33.0 33.0 %collective-permute-start.11 = (bf16[3,64,1024]{2,1,0:T(8,128)(2,1)}, bf16[3,64,1024]{2,1,0:T(8,128)(2,1)S(1)}, u32[]{:S(2)}, u32[]{:S(2)}) collective-permute-start(bf16[3,64,1024]{2,1,0:T(8,128)(2,1)} %get-tuple-element.28), channel_id=1, source_target_pairs={{0,32},{32,0},{1,33},{33,1},{2,34},{34,2},{3,35},{35,3},{4,36},{36... | collective-permute-start | bytes 1179656 | tf_op jit(solution)/shard_map/ppermute | solution.py:213
  34.0 20.3 %all-to-all-start.1 = ((bf16[32,16,128]{2,1,0:T(8,128)(2,1)}), bf16[32,16,128]{2,1,0:T(8,128)(2,1)S(1)}, u32[]{:S(2)}, u32[]{:S(2)}) async-start(bf16[32,16,128]{2,1,0:T(8,128)(2,1)} %broadcast_in_dim.3), calls=%async_computation.1 | async-start | bytes 262144 | tf_op jit(solution)/shard_map/all_to_all | solution.py:184
  43.9 34.9 %collective-permute-start.15 = (bf16[3,128,1024]{2,1,0:T(8,128)(2,1)}, bf16[3,128,1024]{2,1,0:T(8,128)(2,1)S(1)}, u32[]{:S(2)}, u32[]{:S(2)}) collective-permute-start(bf16[3,128,1024]{2,1,0:T(8,128)(2,1)} %copy-done.13), channel_id=1, source_target_pairs={{0,32},{32,0},{1,33},{33,1},{2,34},{34,2},{3,35},{35,3},{4,36},{36... | collective-permute-start | bytes 2359304 | tf_op jit(solution)/shard_map/ppermute | solution.py:214
  54.4 8.7 %collective-permute-start.7 = (bf16[32,16,128]{2,1,0:T(8,128)(2,1)S(1)}, bf16[32,16,128]{2,1,0:T(8,128)(2,1)S(1)}, u32[]{:S(2)}, u32[]{:S(2)}) collective-permute-start(bf16[32,16,128]{2,1,0:T(8,128)(2,1)S(1)} %all-to-all-done.1.refs_8_), channel_id=1, source_target_pairs={{0,64},{64,128},{128,192},{192,0},{1,65},{65,129},{129,193},{193,1... | collective-permute-start | bytes 393224 | tf_op jit(solution)/shard_map/ppermute | solution.py:217
  55.6 9.7 %collective-permute-start.8 = (bf16[32,16,128]{2,1,0:T(8,128)(2,1)S(1)}, bf16[32,16,128]{2,1,0:T(8,128)(2,1)S(1)}, u32[]{:S(2)}, u32[]{:S(2)}) collective-permute-start(bf16[32,16,128]{2,1,0:T(8,128)(2,1)S(1)} %all-to-all-done.1.refs_8_), channel_id=1, source_target_pairs={{0,128},{64,192},{128,0},{192,64},{1,129},{65,193},{129,1},{193,65... | collective-permute-start | bytes 393224 | tf_op jit(solution)/shard_map/ppermute | solution.py:217
  60.2 5.7 %collective-permute-start.9 = (bf16[32,16,128]{2,1,0:T(8,128)(2,1)S(1)}, bf16[32,16,128]{2,1,0:T(8,128)(2,1)S(1)}, u32[]{:S(2)}, u32[]{:S(2)}) collective-permute-start(bf16[32,16,128]{2,1,0:T(8,128)(2,1)S(1)} %all-to-all-done.1.refs_8_), channel_id=1, source_target_pairs={{0,192},{64,0},{128,64},{192,128},{1,193},{65,1},{129,65},{193,129... | collective-permute-start | bytes 393224 | tf_op jit(solution)/shard_map/ppermute | solution.py:217
  69.7 6.4 %collective-permute-start.12 = (bf16[128,1024]{1,0:T(8,128)(2,1)S(1)}, bf16[128,1024]{1,0:T(8,128)(2,1)S(1)}, u32[]{:S(2)}, u32[]{:S(2)}) collective-permute-start(bf16[128,1024]{1,0:T(8,128)(2,1)S(1)} %get-tuple-element.30.refs_5_), channel_id=1, source_target_pairs={{0,192},{64,0},{128,64},{192,128},{1,193},{65,1},{129,65},{193,129... | collective-permute-start | bytes 786440 | tf_op jit(solution)/shard_map/ppermute | solution.py:232
  70.9 6.4 %collective-permute-start.14 = (bf16[128,1024]{1,0:T(8,128)(2,1)S(1)}, bf16[128,1024]{1,0:T(8,128)(2,1)S(1)}, u32[]{:S(2)}, u32[]{:S(2)}) collective-permute-start(bf16[128,1024]{1,0:T(8,128)(2,1)S(1)} %get-tuple-element.32.refs_7_), channel_id=1, source_target_pairs={{0,64},{64,128},{128,192},{192,0},{1,65},{65,129},{129,193},{193,1... | collective-permute-start | bytes 786440 | tf_op jit(solution)/shard_map/ppermute | solution.py:232
  71.8 5.5 %collective-permute-start.17 = (bf16[128,1024]{1,0:T(8,128)(2,1)S(1)}, bf16[128,1024]{1,0:T(8,128)(2,1)S(1)}, u32[]{:S(2)}, u32[]{:S(2)}) collective-permute-start(bf16[128,1024]{1,0:T(8,128)(2,1)S(1)} %get-tuple-element.30.refs_5_), channel_id=1, source_target_pairs={{0,1},{1,0},{2,3},{3,2},{4,5},{5,4},{6,7},{7,6},{8,9},{9,8},{10,11... | collective-permute-start | bytes 786440 | tf_op jit(solution)/shard_map/ppermute | solution.py:233
  71.8 5.4 %collective-permute-start.16 = (bf16[128,1024]{1,0:T(8,128)(2,1)S(1)}, bf16[128,1024]{1,0:T(8,128)(2,1)S(1)}, u32[]{:S(2)}, u32[]{:S(2)}) collective-permute-start(bf16[128,1024]{1,0:T(8,128)(2,1)S(1)} %get-tuple-element.29.refs_0_.refs_4_), channel_id=1, source_target_pairs={{0,1},{1,0},{2,3},{3,2},{4,5},{5,4},{6,7},{7,6},{8,9},{9,8},{10,11... | collective-permute-start | bytes 786440 | tf_op jit(solution)/shard_map/ppermute | solution.py:233
  76.2 1.5 %collective-permute-start.18 = (bf16[128,1024]{1,0:T(8,128)(2,1)S(1)}, bf16[128,1024]{1,0:T(8,128)(2,1)S(1)}, u32[]{:S(2)}, u32[]{:S(2)}) collective-permute-start(bf16[128,1024]{1,0:T(8,128)(2,1)S(1)} %get-tuple-element.31.refs_6_), channel_id=1, source_target_pairs={{0,1},{1,0},{2,3},{3,2},{4,5},{5,4},{6,7},{7,6},{8,9},{9,8},{10,11... | collective-permute-start | bytes 786440 | tf_op jit(solution)/shard_map/ppermute | solution.py:233
  77.3 1.5 %collective-permute-start.19 = (bf16[128,1024]{1,0:T(8,128)(2,1)S(1)}, bf16[128,1024]{1,0:T(8,128)(2,1)S(1)}, u32[]{:S(2)}, u32[]{:S(2)}) collective-permute-start(bf16[128,1024]{1,0:T(8,128)(2,1)S(1)} %get-tuple-element.32.refs_7_), channel_id=1, source_target_pairs={{0,1},{1,0},{2,3},{3,2},{4,5},{5,4},{6,7},{7,6},{8,9},{9,8},{10,11... | collective-permute-start | bytes 786440 | tf_op jit(solution)/shard_map/ppermute | solution.py:233
  81.7 19.8 %all-to-all-start.2 = ((bf16[4,512,128]{2,1,0:T(8,128)(2,1)}), bf16[4,512,128]{2,1,0:T(8,128)(2,1)S(1)}, u32[]{:S(2)}, u32[]{:S(2)}) async-start(bf16[4,512,128]{2,1,0:T(8,128)(2,1)} %copy-done.3), calls=%async_computation.2 | async-start | bytes 1048576 | tf_op jit(solution)/shard_map/all_to_all | solution.py:184
  88.8 17.0 %collective-permute-start.13 = (bf16[128,1024]{1,0:T(8,128)(2,1)S(1)}, bf16[128,1024]{1,0:T(8,128)(2,1)S(1)}, u32[]{:S(2)}, u32[]{:S(2)}) collective-permute-start(bf16[128,1024]{1,0:T(8,128)(2,1)S(1)} %copy-done.12), channel_id=1, source_target_pairs={{0,128},{64,192},{128,0},{192,64},{1,129},{65,193},{129,1},{193,65... | collective-permute-start | bytes 786440 | tf_op jit(solution)/shard_map/ppermute | solution.py:232
  102.3 12.0 %all-to-all-start.3 = ((bf16[16,32,128]{2,1,0:T(8,128)(2,1)}), bf16[16,32,128]{2,1,0:T(8,128)(2,1)S(1)}, u32[]{:S(2)}, u32[]{:S(2)}) async-start(bf16[16,32,128]{2,1,0:T(8,128)(2,1)} %bitcast.1), calls=%async_computation.3 | async-start | bytes 262144 | tf_op jit(solution)/shard_map/all_to_all | solution.py:184
  (14 other events, 66.9 us)

commit v5 on v4

--- a/solution.py
+++ b/solution.py
@@ -66,23 +66,24 @@
     outs, panel, sems, panel_sems = refs[:X], refs[X], refs[X + 1], refs[X + 2]
     core = lax.axis_index("c")
 
-    def pieces(ref, rows):
+    def halves(ref, step):
         return [
             pltpu.make_async_copy(
-                ref.at[rows(k), pl.ds(n * 128, 128)], panel.at[k * 4 + n], panel_sems.at[k * 4 + n]
+                ref.at[pl.ds(n * step, 32), pl.ds(0, WIDTH)],
+                panel.at[pl.ds(n * 32, 32), :],
+                panel_sems.at[n],
             )
-            for k in range(4)
-            for n in range(4)
+            for n in range(2)
         ]
 
     @pl.when(core == 0)
     def _():
-        for copy in pieces(jac, lambda k: pl.ds(k // 2 * 64 + k % 2 * 16, 16)):
+        for copy in halves(jac, 64):
             copy.start()
 
     @pl.when(core == 1)
     def _():
-        for copy in pieces(got, lambda k: pl.ds(k * 16, 16)):
+        for copy in halves(got, 32):
             copy.start()
 
     copies = []
@@ -91,12 +92,24 @@
         copies.append((got.at[:, part(d)], outs[d].at[pl.ds(64, 64), :]))
         copies.append((cov.at[:, part(d)], outs[d].at[pl.ds(128, 64), :]))
     run_copies(copies, sems)
-    for copy in pieces(got, lambda k: pl.ds(k * 16, 16)):
+    for copy in halves(got, 32):
         copy.wait()
 
 
+def merge_kernel(mine, swapped, near, cross, out):
+    core = lax.axis_index("c")
+    for here, own, other in ((0, mine, swapped), (1, near, cross)):
+
+        @pl.when(lax.axis_index("l") == here)
+        def _():
+            for n in range(2):
+                out[slab(n, core), :] = own[n * 32 : n * 32 + 32, :]
+                out[slab(n, 1 - core), :] = other[n * 32 : n * 32 + 32, :]
+
+
 def carry_kernel(carry, *refs):
-    run_copies([(carry.at[:, part(d)], refs[d]) for d in range(X)], refs[X])
+    out, sems = refs[-2:]
+    run_copies([(carry.at[:, pl.ds(k * 1024, 1024)], out.at[k]) for k in range(X)], sems)
 
 
 def rest_kernel(*refs):
@@ -109,8 +122,8 @@
 
 
 def sens_kernel(*refs):
-    first, carry, panels, (own_got, cov_got) = refs[:4], refs[4:8], refs[8:12], refs[12:14]
-    outs, cov, panel = refs[14:18], refs[18], refs[19]
+    first, panels, (carry, own_got, cov_got) = refs[:4], refs[4:8], refs[8:11]
+    outs, pairs, cov = refs[11:15], refs[15:17], refs[17]
     h = lax.axis_index("h")
 
     def rows(d, side):
@@ -120,49 +133,35 @@
         cov[rows(d, h), :] = first[d][128:192, :]
         cov[rows(d, 1 - h), :] = cov_got[d - 1] if d else own_got[128:192, :]
     for d in range(X):
-        for k in range(4):
-            for n in range(4):
-                for core in range(C):
-                    at = d * 128 + k // 2 * 64 + core * 32 + k % 2 * 16
-                    panel[at : at + 16, n * 128 : n * 128 + 128] = panels[d][(k * 4 + n) * C + core]
-    for d in range(X):
-        product = jnp.dot(
-            panel[d * 128 : (d + 1) * 128, :], cov[...], preferred_element_type=F32
-        )
-        value = carry[d][...].astype(F32) + product * (1.0 / math.sqrt(WIDTH))
-        outs[d][...] = value.astype(BF16)
+        product = jnp.dot(panels[d][...], cov[...], preferred_element_type=F32)
+        value = carry[source(d)].astype(F32) + product * (1.0 / math.sqrt(WIDTH))
+        value = value.astype(BF16)
+        outs[d][...] = value
+        pairs[d // 2][d % 2 * 128 : d % 2 * 128 + 128, :] = value
 
 
 def innov_kernel(own_got, jac_got, *refs):
-    first, sens, sens_got = refs[:X], refs[X : 2 * X], refs[2 * X : 3 * X]
-    own, parts, jac, both = refs[-4:]
+    first, sens, sens_got = refs[:X], refs[X : X + 2], refs[X + 2 : X + 4]
+    parts, jac, both = refs[-3:]
     h = lax.axis_index("h")
     for d in range(X):
         for side, ref in ((h, first[d]), (1 - h, jac_got.at[d - 1] if d else own_got)):
             to = pl.ds(pl.multiple_of((source(d) * H + side) * 64, 64), 64)
             jac[to, 0:1024] = ref[0:64, :]
             jac[to, 1024:2048] = ref[64:128, :]
-        both[d * 128 : (d + 1) * 128, 0:1024] = sens[d][...]
-        both[d * 128 : (d + 1) * 128, 1024:2048] = sens_got[d][...]
+    for k in range(2):
+        both[k * 256 : (k + 1) * 256, 0:1024] = sens[k][...]
+        both[k * 256 : (k + 1) * 256, 1024:2048] = sens_got[k][...]
     value = lax.dot_general(
         jac[...], both[...], (((1,), (1,)), ((), ())), preferred_element_type=F32
     )
-    own[...] = value[:, 0:128]
     for d in range(X):
         parts[source(d)] = value[:, d * 128 : (d + 1) * 128].astype(BF16)
-
-
-def sum_kernel(own, got, out):
-    total = own[...]
-    x = lax.axis_index("x")
-    for k in range(X):
-        total += jnp.where(x == k, 0.0, got[k].astype(F32))
-    out[...] = total.astype(BF16)
 
 
 def final_kernel(got, out):
     total = got[0].astype(F32)
-    for k in range(1, L * Z):
+    for k in range(1, X * L * Z):
         total += got[k].astype(F32)
     out[...] = total * (1.0 / math.sqrt(PARAMS))
 
@@ -193,10 +192,10 @@
     got = lax.ppermute(give, "c", SWAP)
     *packed, panel = call(
         pack_kernel,
-        [shape(192, 1024)] * X + [shape(16, 16, 128)],
+        [shape(192, 1024)] * X + [shape(64, WIDTH)],
         (jacobian, got, cov_rows),
         ANY,
-        dma(4 * X) + dma(16),
+        dma(4 * X) + dma(2),
         nbytes=4 * MIB,
     )
     own_got = lax.ppermute(packed[0], "h", SWAP)
@@ -212,29 +211,40 @@
     )
     cov_got = lax.ppermute(cov_rest, "h", SWAP)
     jac_got = lax.ppermute(jac_rest, "h", SWAP)
-    mine = over(panel, ("l", "z"))[0]
-    panel = over(jnp.broadcast_to(mine, (32, 16, 128)), ("l", "z", "c"))
+    mine = over(jnp.broadcast_to(panel, (Z, 64, WIDTH)), "z")[0]
+    swapped = lax.ppermute(mine, ("l", "c"), [(0, 1), (1, 0)])
+    near = lax.ppermute(mine, ("l", "c"), [(0, 2), (1, 3)])
+    cross = lax.ppermute(mine, ("l", "c"), [(0, 3), (1, 2)])
+    panel = call(
+        merge_kernel, shape(128, WIDTH), (mine, swapped, near, cross), VMEM, nbytes=2**18
+    )
     panels = [panel] + [lax.ppermute(panel, "x", ring(d)) for d in range(1, X)]
     packed = call(
-        carry_kernel, [shape(128, 1024)] * X, (sens_carry,), ANY, dma(X), nbytes=2 * MIB
-    )
-    carry = [packed[0]] + [lax.ppermute(packed[d], "x", ring(d)) for d in range(1, X)]
-    sens = call(
+        carry_kernel,
+        shape(X, 128, 1024),
+        (sens_carry,),
+        ANY,
+        dma(X),
+        nbytes=2 * MIB,
+        behind=(mine,),
+    )
+    carry = over(packed, "x")
+    *sens, low, high = call(
         sens_kernel,
-        [shape(128, 1024)] * X,
-        (*first, *carry, *panels, own_got, cov_got),
+        [shape(128, 1024)] * X + [shape(256, 1024)] * 2,
+        (*first, *panels, carry, own_got, cov_got),
         VMEM,
-        [pltpu.VMEM((512, 1024), BF16), pltpu.VMEM((512, WIDTH), BF16)],
+        [pltpu.VMEM((512, 1024), BF16)],
         flops=2 * 512 * 512 * 1024,
         nbytes=2 * MIB,
         vmem=12,
     )
     sens_back = [sens[0]] + [lax.ppermute(sens[d], "x", ring(-d)) for d in range(1, X)]
-    sens_got = [lax.ppermute(part, "c", SWAP) for part in sens]
-    own_sum, parts = call(
+    sens_got = [lax.ppermute(pair, "c", SWAP) for pair in (low, high)]
+    parts = call(
         innov_kernel,
-        [shape(512, 128, kind=F32), shape(X, 512, 128)],
-        (own_got, jac_got, *first, *sens, *sens_got),
+        shape(X, 512, 128),
+        (own_got, jac_got, *first, low, high, *sens_got),
         VMEM,
         [pltpu.VMEM((512, 2048), BF16)] * 2,
         flops=2 * 512 * 512 * 2048,
@@ -242,9 +252,8 @@
         vmem=16,
         behind=(sens_back[1], sens_back[3]),
     )
-    summed = call(sum_kernel, shape(512, 128), (own_sum, over(parts, "x")), VMEM, nbytes=MIB, vmem=4)
-    shared = over(summed.reshape(L * Z, 32, 128), ("l", "z"))
-    innovation = call(final_kernel, shape(32, 128, kind=F32), (shared,), VMEM, nbytes=2**17, vmem=4)
+    shared = over(parts.reshape(X * L * Z, 32, 128), ("x", "l", "z"))
+    innovation = call(final_kernel, shape(32, 128, kind=F32), (shared,), VMEM, nbytes=2**19, vmem=4)
     sensitivity = call(
         assemble_kernel, shape(128, 4096), sens_back, ANY, dma(X), nbytes=2 * MIB
     )

time: 115 us -> 129 us (1.12); the launches traced: 115 us -> 127 us
  waiting for transfers between devices: 44.5 us -> 60.3 us
  starting transfers between devices: 53.3 us -> 46.3 us
  local copies, waits for them, and re-layouts: 7.61 us -> 10 us
    ppermute x4 -> x5, waiting for transfers between devices: 1.53 us -> 21.9 us  [the longest x1 21.2 us: body(): near = lax.ppermute(mine, ('l', 'c'), [(0, 2), (1, 3)])]
    ppermute x3, waiting for transfers between devices: 4.93 us -> 18.7 us  [body(): lax.ppermute(sens[d], 'x', ring(-d))]
    all_to_all x4 -> x3, waiting for transfers between devices: 26.8 us -> 14.2 us  [over(): return lax.all_to_all(value, axes, split_axis=0, concat_axis=0, tiled=True)]
    ppermute x6 -> x3, starting transfers between devices: 8.79 us -> 3.14 us  [body(): lax.ppermute(packed[d], 'x', ring(d))]
    ppermute x4 -> x5, starting transfers between devices: 0.52 us -> 5.94 us  [the longest x1 2.23 us: body(): near = lax.ppermute(mine, ('l', 'c'), [(0, 2), (1, 3)])]
    all_to_all x4 -> x3, starting transfers between devices: 29.1 us -> 24.9 us  [over(): return lax.all_to_all(value, axes, split_axis=0, concat_axis=0, tiled=True)]
    ppermute x6 -> x3, waiting for transfers between devices: 3.59 us -> 0.01 us  [body(): lax.ppermute(packed[d], 'x', ring(d))]
    ppermute x1, starting transfers between devices: 0.37 us -> 3.28 us  [body(): cov_got = lax.ppermute(cov_rest, 'h', SWAP)]
  transfers between devices with their start and end apart: 24 -> 21, of which waited for: 13 -> 11; matrix products, arithmetic and copies ran while one was open for 1% -> 1% of each run, Pallas kernels for 5% -> 3%
where the time goes in v5:
time: 129 us; the launch traced here: 127 us
  waiting for transfers between devices  60.3 us (47%)
  starting transfers between devices  46.3 us (36%)
  local copies, waits for them, and re-layouts  10 us (8%)
  Pallas kernels  9.35 us (7%)
    all_to_all x3, starting transfers between devices, over(): return lax.all_to_all(value, axes, split_axis=0, concat_axis=0, tiled=True)  24.9 us
    ppermute x1, waiting for transfers between devices, body(): near = lax.ppermute(mine, ('l', 'c'), [(0, 2), (1, 3)])  21.2 us
    ppermute x3, waiting for transfers between devices, body(): lax.ppermute(sens[d], 'x', ring(-d))  18.7 us
    all_to_all x3, waiting for transfers between devices, over(): return lax.all_to_all(value, axes, split_axis=0, concat_axis=0, tiled=True)  14.2 us
    pallas_call x9, Pallas kernels, call(): pl.pallas_call(kernel, out_shape=outs, in_specs=[spec] * len(ins) + [ANY]...  9.35 us
    unnamed x28, local copies, waits for them, and re-layouts  8.33 us
    ppermute x3, waiting for transfers between devices, body(): panels = [panel] + [lax.ppermute(panel, 'x', ring(d)) for d in range(1, X)]  3.65 us
    ppermute x1, starting transfers between devices, body(): cov_got = lax.ppermute(cov_rest, 'h', SWAP)  3.28 us
  transfers between devices with their start and end apart: 21, of which 11 were waited for; matrix products, arithmetic and copies ran while one was open for 1% of the time, Pallas kernels for 3%

profile of v5, /device:TPU:4, one launch (start us, length us, event | category | flops | bytes accessed | tf_op | source)
XLA Modules:
  0.0 126.8 jit_solution(14255668038426017319)
XLA Ops:
  0.6 1.2 copy-done
  2.0 1.9 %collective-permute-done.got = bf16[64,4096]{1,0:T(8,128)(2,1)S(1)} collective-permute-done((bf16[64,4096]{1,0:T(8,128)(2,1)S(1)}, bf16[64,4096]{1,0:T(8,128)(2,1)S(1)}, u32[]{:S(2)}, u32[]{:S(2)}) %collective-permute-start) | collective-permute-done | bytes 524320 | tf_op jit(solution)/shard_map/ppermute | solution.py:192
  3.9 1.2 shard_map.51
  6.0 8.5 %all-to-all-start = ((bf16[8,64,512]{2,1,0:T(8,128)(2,1)}), bf16[8,64,512]{2,1,0:T(8,128)(2,1)}, u32[]{:S(2)}, u32[]{:S(2)}) async-start(bf16[8,64,512]{2,1,0:T(8,128)(2,1)} %broadcast_in_dim.3), calls=%async_computation | async-start | bytes 1048576 | tf_op jit(solution)/shard_map/all_to_all | solution.py:183
  14.5 3.2 %collective-permute-start.10 = (bf16[192,1024]{1,0:T(8,128)(2,1)S(1)}, bf16[192,1024]{1,0:T(8,128)(2,1)S(1)}, u32[]{:S(2)}, u32[]{:S(2)}) collective-permute-start(bf16[192,1024]{1,0:T(8,128)(2,1)S(1)} %get-tuple-element.15.refs_0_), channel_id=1, source_target_pairs={{0,32},{32,0},{1,33},{33,1},{2,34},{34,2},{3,35},{35,3},{4,36},{36... | collective-permute-start | bytes 1179656 | tf_op jit(solution)/shard_map/ppermute | solution.py:201
  17.7 1.2 collective-permute-start.1
  19.7 1.1 collective-permute-start.3
  20.8 11.6 %all-to-all-done = bf16[8,64,512]{2,1,0:T(8,128)(2,1)} async-done(((bf16[8,64,512]{2,1,0:T(8,128)(2,1)}), bf16[8,64,512]{2,1,0:T(8,128)(2,1)}, u32[]{:S(2)}, u32[]{:S(2)}) %all-to-all-start) | async-done | bytes 524320 | tf_op jit(solution)/shard_map/all_to_all | solution.py:183
  34.2 4.8 %all-to-all-start.1 = ((bf16[4,128,1024]{2,1,0:T(8,128)(2,1)}), bf16[4,128,1024]{2,1,0:T(8,128)(2,1)S(1)}, u32[]{:S(2)}, u32[]{:S(2)}) async-start(bf16[4,128,1024]{2,1,0:T(8,128)(2,1)} %shard_map.53), calls=%async_computation.1 | async-start | bytes 2097152 | tf_op jit(solution)/shard_map/all_to_all | solution.py:183
  39.0 1.3 %shard_map.54 = (bf16[3,64,1024]{2,1,0:T(8,128)(2,1)S(1)}, bf16[3,128,1024]{2,1,0:T(8,128)(2,1)}) custom-call(bf16[192,1024]{1,0:T(8,128)(2,1)S(1)} %collective-permute-done.1.refs_0_.refs_1_, bf16[192,1024]{1,0:T(8,128)(2,1)S(1)} %collective-permute-done.2.refs_1_.refs_2_, bf16[192,1024]{1,0:T(8,128)(2,1)S(1)} %collective-permute-done.3.refs_2_.refs_3_, ...), custom_call_target="tpu_custom_call" | custom-call | bytes 2097152 | tf_op jit(solution)/shard_map/pallas_call | solution.py:26
  40.3 3.3 %collective-permute-start.11 = (bf16[3,64,1024]{2,1,0:T(8,128)(2,1)S(1)}, bf16[3,64,1024]{2,1,0:T(8,128)(2,1)S(1)}, u32[]{:S(2)}, u32[]{:S(2)}) collective-permute-start(bf16[3,64,1024]{2,1,0:T(8,128)(2,1)S(1)} %get-tuple-element.20), channel_id=1, source_target_pairs={{0,32},{32,0},{1,33},{33,1},{2,34},{34,2},{3,35},{35,3},{4,36},{36... | collective-permute-start | bytes 1179656 | tf_op jit(solution)/shard_map/ppermute | solution.py:212
  43.9 1.9 %collective-permute-start.4 = (bf16[64,512]{1,0:T(8,128)(2,1)S(1)}, bf16[64,512]{1,0:T(8,128)(2,1)S(1)}, u32[]{:S(2)}, u32[]{:S(2)}) collective-permute-start(bf16[64,512]{1,0:T(8,128)(2,1)S(1)} %slice_bitcast_fusion.mine.refs_0_), channel_id=1, source_target_pairs={{0,1},{1,0},{2,3},{3,2},{4,5},{5,4},{6,7},{7,6},{8,9},{9,8},{10,11... | collective-permute-start | bytes 196616 | tf_op jit(solution)/shard_map/ppermute | solution.py:215
  45.9 2.2 %collective-permute-start.5 = (bf16[64,512]{1,0:T(8,128)(2,1)S(1)}, bf16[64,512]{1,0:T(8,128)(2,1)S(1)}, u32[]{:S(2)}, u32[]{:S(2)}) collective-permute-start(bf16[64,512]{1,0:T(8,128)(2,1)S(1)} %slice_bitcast_fusion.mine.refs_0_), channel_id=1, source_target_pairs={{0,16},{1,17},{2,18},{3,19},{4,20},{5,21},{6,22},{7,23},{8,24},{9,... | collective-permute-start | bytes 196616 | tf_op jit(solution)/shard_map/ppermute | solution.py:216
  48.1 1.3 %collective-permute-start.6 = (bf16[64,512]{1,0:T(8,128)(2,1)S(1)}, bf16[64,512]{1,0:T(8,128)(2,1)S(1)}, u32[]{:S(2)}, u32[]{:S(2)}) collective-permute-start(bf16[64,512]{1,0:T(8,128)(2,1)S(1)} %slice_bitcast_fusion.mine.refs_0_), channel_id=1, source_target_pairs={{0,17},{1,16},{2,19},{3,18},{4,21},{5,20},{6,23},{7,22},{8,25},{9,... | collective-permute-start | bytes 196616 | tf_op jit(solution)/shard_map/ppermute | solution.py:217
  49.4 21.2 %collective-permute-done.5.near = bf16[64,512]{1,0:T(8,128)(2,1)S(1)} collective-permute-done((bf16[64,512]{1,0:T(8,128)(2,1)S(1)}, bf16[64,512]{1,0:T(8,128)(2,1)S(1)}, u32[]{:S(2)}, u32[]{:S(2)}) %collective-permute-start.5) | collective-permute-done | bytes 65568 | tf_op jit(solution)/shard_map/ppermute | solution.py:216
  71.3 1.2 collective-permute-start.7
  75.0 2.6 %collective-permute-done.7.refs_5_ = bf16[128,512]{1,0:T(8,128)(2,1)S(1)} collective-permute-done((bf16[128,512]{1,0:T(8,128)(2,1)S(1)}, bf16[128,512]{1,0:T(8,128)(2,1)S(1)}, u32[]{:S(2)}, u32[]{:S(2)}) %collective-permute-start.7) | collective-permute-done | bytes 131104 | tf_op jit(solution)/shard_map/ppermute | solution.py:221
  80.6 1.0 copy-done.5
  87.2 1.2 collective-permute-start.14
  88.4 6.2 %collective-permute-done.12.refs_1_.refs_8_ = bf16[128,1024]{1,0:T(8,128)(2,1)S(1)} collective-permute-done((bf16[128,1024]{1,0:T(8,128)(2,1)S(1)}, bf16[128,1024]{1,0:T(8,128)(2,1)S(1)}, u32[]{:S(2)}, u32[]{:S(2)}) %collective-permute-start.12) | collective-permute-done | bytes 262176 | tf_op jit(solution)/shard_map/ppermute | solution.py:242
  95.1 3.3 %shard_map.57 = bf16[4,512,128]{2,1,0:T(8,128)(2,1)} custom-call(bf16[192,1024]{1,0:T(8,128)(2,1)S(1)} %collective-permute-done.10.refs_3_.refs_9_.own_got, bf16[3,128,1024]{2,1,0:T(8,128)(2,1)} %collective-permute-done.15.jac_got, bf16[192,1024]{1,0:T(8,128)(2,1)S(1)} %get-tuple-element.15.refs_0_, ...), custom_call_target="tpu_custom_call" | custom-call | flops 1073741824 | bytes 2097152 | tf_op jit(solution)/shard_map/pallas_call | solution.py:26
  98.4 11.6 %all-to-all-start.2 = ((bf16[64,32,128]{2,1,0:T(8,128)(2,1)}), bf16[64,32,128]{2,1,0:T(8,128)(2,1)S(1)}, u32[]{:S(2)}, u32[]{:S(2)}) async-start(bf16[64,32,128]{2,1,0:T(8,128)(2,1)} %bitcast.1), calls=%async_computation.2 | async-start | bytes 1048576 | tf_op jit(solution)/shard_map/all_to_all | solution.py:183
  110.5 12.0 %collective-permute-done.13.refs_2_ = bf16[128,1024]{1,0:T(8,128)(2,1)S(1)} collective-permute-done((bf16[128,1024]{1,0:T(8,128)(2,1)S(1)}, bf16[128,1024]{1,0:T(8,128)(2,1)S(1)}, u32[]{:S(2)}, u32[]{:S(2)}) %collective-permute-start.13) | collective-permute-done | bytes 262176 | tf_op jit(solution)/shard_map/ppermute | solution.py:242
  123.4 2.6 %all-to-all-done.2.got = bf16[64,32,128]{2,1,0:T(8,128)(2,1)S(1)} async-done(((bf16[64,32,128]{2,1,0:T(8,128)(2,1)}), bf16[64,32,128]{2,1,0:T(8,128)(2,1)S(1)}, u32[]{:S(2)}, u32[]{:S(2)}) %all-to-all-start.2) | async-done | bytes 524320 | tf_op jit(solution)/shard_map/all_to_all | solution.py:183
  (57 shorter events, 18.3 us)
Async XLA Ops:
  1.9 2.1 %copy-start.3 = (bf16[64,4096]{1,0:T(8,128)(2,1)S(1)}, bf16[64,4096]{1,0:T(8,128)(2,1)}, u32[]{:S(2)}) copy-start(bf16[64,4096]{1,0:T(8,128)(2,1)} %cov.1) | copy-start | bytes 1572868
  1.9 2.0 %collective-permute-start = (bf16[64,4096]{1,0:T(8,128)(2,1)S(1)}, bf16[64,4096]{1,0:T(8,128)(2,1)S(1)}, u32[]{:S(2)}, u32[]{:S(2)}) collective-permute-start(bf16[64,4096]{1,0:T(8,128)(2,1)S(1)} %shard_map.50), channel_id=1, source_target_pairs={{0,1},{1,0},{2,3},{3,2},{4,5},{5,4},{6,7},{7,6},{8,9},{9,8},{10,11... | collective-permute-start | bytes 1572872 | tf_op jit(solution)/shard_map/ppermute | solution.py:192
  5.1 28.1 %copy-start.2 = (bf16[128,4096]{1,0:T(8,128)(2,1)S(1)}, bf16[128,4096]{1,0:T(8,128)(2,1)}, u32[]{:S(2)}) copy-start(bf16[128,4096]{1,0:T(8,128)(2,1)} %carry.1) | copy-start | bytes 3145732
  6.0 26.4 %all-to-all-start = ((bf16[8,64,512]{2,1,0:T(8,128)(2,1)}), bf16[8,64,512]{2,1,0:T(8,128)(2,1)}, u32[]{:S(2)}, u32[]{:S(2)}) async-start(bf16[8,64,512]{2,1,0:T(8,128)(2,1)} %broadcast_in_dim.3), calls=%async_computation | async-start | bytes 1048576 | tf_op jit(solution)/shard_map/all_to_all | solution.py:183
  14.5 24.6 %collective-permute-start.10 = (bf16[192,1024]{1,0:T(8,128)(2,1)S(1)}, bf16[192,1024]{1,0:T(8,128)(2,1)S(1)}, u32[]{:S(2)}, u32[]{:S(2)}) collective-permute-start(bf16[192,1024]{1,0:T(8,128)(2,1)S(1)} %get-tuple-element.15.refs_0_), channel_id=1, source_target_pairs={{0,32},{32,0},{1,33},{33,1},{2,34},{34,2},{3,35},{35,3},{4,36},{36... | collective-permute-start | bytes 1179656 | tf_op jit(solution)/shard_map/ppermute | solution.py:201
  17.7 21.4 %collective-permute-start.1 = (bf16[192,1024]{1,0:T(8,128)(2,1)}, bf16[192,1024]{1,0:T(8,128)(2,1)S(1)}, u32[]{:S(2)}, u32[]{:S(2)}) collective-permute-start(bf16[192,1024]{1,0:T(8,128)(2,1)} %get-tuple-element.16), channel_id=1, source_target_pairs={{0,64},{64,128},{128,192},{192,0},{1,65},{65,129},{129,193},{193,1... | collective-permute-start | bytes 1179656 | tf_op jit(solution)/shard_map/ppermute | solution.py:202
  18.9 20.2 %collective-permute-start.2 = (bf16[192,1024]{1,0:T(8,128)(2,1)}, bf16[192,1024]{1,0:T(8,128)(2,1)S(1)}, u32[]{:S(2)}, u32[]{:S(2)}) collective-permute-start(bf16[192,1024]{1,0:T(8,128)(2,1)} %get-tuple-element.17), channel_id=1, source_target_pairs={{0,128},{64,192},{128,0},{192,64},{1,129},{65,193},{129,1},{193,65... | collective-permute-start | bytes 1179656 | tf_op jit(solution)/shard_map/ppermute | solution.py:202
  19.7 19.4 %collective-permute-start.3 = (bf16[192,1024]{1,0:T(8,128)(2,1)S(1)}, bf16[192,1024]{1,0:T(8,128)(2,1)S(1)}, u32[]{:S(2)}, u32[]{:S(2)}) collective-permute-start(bf16[192,1024]{1,0:T(8,128)(2,1)S(1)} %get-tuple-element.18), channel_id=1, source_target_pairs={{0,192},{64,0},{128,64},{192,128},{1,193},{65,1},{129,65},{193,129... | collective-permute-start | bytes 1179656 | tf_op jit(solution)/shard_map/ppermute | solution.py:202
  34.2 46.4 %all-to-all-start.1 = ((bf16[4,128,1024]{2,1,0:T(8,128)(2,1)}), bf16[4,128,1024]{2,1,0:T(8,128)(2,1)S(1)}, u32[]{:S(2)}, u32[]{:S(2)}) async-start(bf16[4,128,1024]{2,1,0:T(8,128)(2,1)} %shard_map.53), calls=%async_computation.1 | async-start | bytes 2097152 | tf_op jit(solution)/shard_map/all_to_all | solution.py:183
  40.3 34.0 %collective-permute-start.11 = (bf16[3,64,1024]{2,1,0:T(8,128)(2,1)S(1)}, bf16[3,64,1024]{2,1,0:T(8,128)(2,1)S(1)}, u32[]{:S(2)}, u32[]{:S(2)}) collective-permute-start(bf16[3,64,1024]{2,1,0:T(8,128)(2,1)S(1)} %get-tuple-element.20), channel_id=1, source_target_pairs={{0,32},{32,0},{1,33},{33,1},{2,34},{34,2},{3,35},{35,3},{4,36},{36... | collective-permute-start | bytes 1179656 | tf_op jit(solution)/shard_map/ppermute | solution.py:212
  43.6 44.8 %collective-permute-start.15 = (bf16[3,128,1024]{2,1,0:T(8,128)(2,1)}, bf16[3,128,1024]{2,1,0:T(8,128)(2,1)}, u32[]{:S(2)}, u32[]{:S(2)}) collective-permute-start(bf16[3,128,1024]{2,1,0:T(8,128)(2,1)} %get-tuple-element.25), channel_id=1, source_target_pairs={{0,32},{32,0},{1,33},{33,1},{2,34},{34,2},{3,35},{35,3},{4,36},{36... | collective-permute-start | bytes 2359304 | tf_op jit(solution)/shard_map/ppermute | solution.py:213
  43.9 5.5 %collective-permute-start.4 = (bf16[64,512]{1,0:T(8,128)(2,1)S(1)}, bf16[64,512]{1,0:T(8,128)(2,1)S(1)}, u32[]{:S(2)}, u32[]{:S(2)}) collective-permute-start(bf16[64,512]{1,0:T(8,128)(2,1)S(1)} %slice_bitcast_fusion.mine.refs_0_), channel_id=1, source_target_pairs={{0,1},{1,0},{2,3},{3,2},{4,5},{5,4},{6,7},{7,6},{8,9},{9,8},{10,11... | collective-permute-start | bytes 196616 | tf_op jit(solution)/shard_map/ppermute | solution.py:215
  45.9 24.7 %collective-permute-start.5 = (bf16[64,512]{1,0:T(8,128)(2,1)S(1)}, bf16[64,512]{1,0:T(8,128)(2,1)S(1)}, u32[]{:S(2)}, u32[]{:S(2)}) collective-permute-start(bf16[64,512]{1,0:T(8,128)(2,1)S(1)} %slice_bitcast_fusion.mine.refs_0_), channel_id=1, source_target_pairs={{0,16},{1,17},{2,18},{3,19},{4,20},{5,21},{6,22},{7,23},{8,24},{9,... | collective-permute-start | bytes 196616 | tf_op jit(solution)/shard_map/ppermute | solution.py:216
  48.1 23.2 %collective-permute-start.6 = (bf16[64,512]{1,0:T(8,128)(2,1)S(1)}, bf16[64,512]{1,0:T(8,128)(2,1)S(1)}, u32[]{:S(2)}, u32[]{:S(2)}) collective-permute-start(bf16[64,512]{1,0:T(8,128)(2,1)S(1)} %slice_bitcast_fusion.mine.refs_0_), channel_id=1, source_target_pairs={{0,17},{1,16},{2,19},{3,18},{4,21},{5,20},{6,23},{7,22},{8,25},{9,... | collective-permute-start | bytes 196616 | tf_op jit(solution)/shard_map/ppermute | solution.py:217
  71.3 6.4 %collective-permute-start.7 = (bf16[128,512]{1,0:T(8,128)(2,1)S(1)}, bf16[128,512]{1,0:T(8,128)(2,1)S(1)}, u32[]{:S(2)}, u32[]{:S(2)}) collective-permute-start(bf16[128,512]{1,0:T(8,128)(2,1)S(1)} %shard_map.52.refs_4_), channel_id=1, source_target_pairs={{0,64},{64,128},{128,192},{192,0},{1,65},{65,129},{129,193},{193,1... | collective-permute-start | bytes 393224 | tf_op jit(solution)/shard_map/ppermute | solution.py:221
  72.5 6.6 %collective-permute-start.8 = (bf16[128,512]{1,0:T(8,128)(2,1)S(1)}, bf16[128,512]{1,0:T(8,128)(2,1)S(1)}, u32[]{:S(2)}, u32[]{:S(2)}) collective-permute-start(bf16[128,512]{1,0:T(8,128)(2,1)S(1)} %shard_map.52.refs_4_), channel_id=1, source_target_pairs={{0,128},{64,192},{128,0},{192,64},{1,129},{65,193},{129,1},{193,65... | collective-permute-start | bytes 393224 | tf_op jit(solution)/shard_map/ppermute | solution.py:221
  73.4 6.6 %collective-permute-start.9 = (bf16[128,512]{1,0:T(8,128)(2,1)S(1)}, bf16[128,512]{1,0:T(8,128)(2,1)S(1)}, u32[]{:S(2)}, u32[]{:S(2)}) collective-permute-start(bf16[128,512]{1,0:T(8,128)(2,1)S(1)} %shard_map.52.refs_4_), channel_id=1, source_target_pairs={{0,192},{64,0},{128,64},{192,128},{1,193},{65,1},{129,65},{193,129... | collective-permute-start | bytes 393224 | tf_op jit(solution)/shard_map/ppermute | solution.py:221
  85.9 9.2 %collective-permute-start.16 = (bf16[256,1024]{1,0:T(8,128)(2,1)S(1)}, bf16[256,1024]{1,0:T(8,128)(2,1)S(1)}, u32[]{:S(2)}, u32[]{:S(2)}) collective-permute-start(bf16[256,1024]{1,0:T(8,128)(2,1)S(1)} %get-tuple-element.26.refs_4_), channel_id=1, source_target_pairs={{0,1},{1,0},{2,3},{3,2},{4,5},{5,4},{6,7},{7,6},{8,9},{9,8},{10,11... | collective-permute-start | bytes 1572872 | tf_op jit(solution)/shard_map/ppermute | solution.py:243
  85.9 9.2 %collective-permute-start.17 = (bf16[256,1024]{1,0:T(8,128)(2,1)S(1)}, bf16[256,1024]{1,0:T(8,128)(2,1)S(1)}, u32[]{:S(2)}, u32[]{:S(2)}) collective-permute-start(bf16[256,1024]{1,0:T(8,128)(2,1)S(1)} %get-tuple-element.27.refs_5_), channel_id=1, source_target_pairs={{0,1},{1,0},{2,3},{3,2},{4,5},{5,4},{6,7},{7,6},{8,9},{9,8},{10,11... | collective-permute-start | bytes 1572872 | tf_op jit(solution)/shard_map/ppermute | solution.py:243
  86.4 8.2 %collective-permute-start.12 = (bf16[128,1024]{1,0:T(8,128)(2,1)S(1)}, bf16[128,1024]{1,0:T(8,128)(2,1)S(1)}, u32[]{:S(2)}, u32[]{:S(2)}) collective-permute-start(bf16[128,1024]{1,0:T(8,128)(2,1)S(1)} %get-tuple-element.22), channel_id=1, source_target_pairs={{0,192},{64,0},{128,64},{192,128},{1,193},{65,1},{129,65},{193,129... | collective-permute-start | bytes 786440 | tf_op jit(solution)/shard_map/ppermute | solution.py:242
  87.2 7.9 %collective-permute-start.14 = (bf16[128,1024]{1,0:T(8,128)(2,1)S(1)}, bf16[128,1024]{1,0:T(8,128)(2,1)S(1)}, u32[]{:S(2)}, u32[]{:S(2)}) collective-permute-start(bf16[128,1024]{1,0:T(8,128)(2,1)S(1)} %get-tuple-element.24), channel_id=1, source_target_pairs={{0,64},{64,128},{128,192},{192,0},{1,65},{65,129},{129,193},{193,1... | collective-permute-start | bytes 786440 | tf_op jit(solution)/shard_map/ppermute | solution.py:242
  98.4 11.6 %copy-start.13 = (bf16[128,1024]{1,0:T(8,128)(2,1)S(1)}, bf16[128,1024]{1,0:T(8,128)(2,1)}, u32[]{:S(2)}) copy-start(bf16[128,1024]{1,0:T(8,128)(2,1)} %copy-done.12) | copy-start | bytes 786436
  98.4 27.7 %all-to-all-start.2 = ((bf16[64,32,128]{2,1,0:T(8,128)(2,1)}), bf16[64,32,128]{2,1,0:T(8,128)(2,1)S(1)}, u32[]{:S(2)}, u32[]{:S(2)}) async-start(bf16[64,32,128]{2,1,0:T(8,128)(2,1)} %bitcast.1), calls=%async_computation.2 | async-start | bytes 1048576 | tf_op jit(solution)/shard_map/all_to_all | solution.py:183
  110.0 12.4 %collective-permute-start.13 = (bf16[128,1024]{1,0:T(8,128)(2,1)S(1)}, bf16[128,1024]{1,0:T(8,128)(2,1)S(1)}, u32[]{:S(2)}, u32[]{:S(2)}) collective-permute-start(bf16[128,1024]{1,0:T(8,128)(2,1)S(1)} %copy-done.13), channel_id=1, source_target_pairs={{0,128},{64,192},{128,0},{192,64},{1,129},{65,193},{129,1},{193,65... | collective-permute-start | bytes 786440 | tf_op jit(solution)/shard_map/ppermute | solution.py:242
  (11 other events, 10.4 us)

commit v6 on v4

--- a/solution.py
+++ b/solution.py
@@ -1,3 +1,4 @@
+import functools
 import math
 
 import jax
@@ -99,18 +100,16 @@
     run_copies([(carry.at[:, part(d)], refs[d]) for d in range(X)], refs[X])
 
 
-def rest_kernel(*refs):
-    first, cov, jac, sems = refs[: X - 1], refs[-3], refs[-2], refs[-1]
-    copies = []
-    for d in range(1, X):
-        copies.append((first[d - 1].at[pl.ds(128, 64), :], cov.at[d - 1]))
-        copies.append((first[d - 1].at[pl.ds(0, 128), :], jac.at[d - 1]))
-    run_copies(copies, sems)
+def join_kernel(first_row, rows, *refs):
+    pieces, out, sems = refs[: X - 1], refs[-2], refs[-1]
+    run_copies(
+        [(pieces[d].at[pl.ds(first_row, rows), :], out.at[d]) for d in range(X - 1)], sems
+    )
 
 
 def sens_kernel(*refs):
     first, carry, panels, (own_got, cov_got) = refs[:4], refs[4:8], refs[8:12], refs[12:14]
-    outs, cov, panel = refs[14:18], refs[18], refs[19]
+    outs, pairs, cov, panel = refs[14:18], refs[18:20], refs[20], refs[21]
     h = lax.axis_index("h")
 
     def rows(d, side):
@@ -130,39 +129,33 @@
             panel[d * 128 : (d + 1) * 128, :], cov[...], preferred_element_type=F32
         )
         value = carry[d][...].astype(F32) + product * (1.0 / math.sqrt(WIDTH))
-        outs[d][...] = value.astype(BF16)
+        value = value.astype(BF16)
+        outs[d][...] = value
+        pairs[d // 2][d % 2 * 128 : d % 2 * 128 + 128, :] = value
 
 
 def innov_kernel(own_got, jac_got, *refs):
-    first, sens, sens_got = refs[:X], refs[X : 2 * X], refs[2 * X : 3 * X]
-    own, parts, jac, both = refs[-4:]
+    first, sens, sens_got = refs[:X], refs[X : X + 2], refs[X + 2 : X + 4]
+    parts, jac, both = refs[-3:]
     h = lax.axis_index("h")
     for d in range(X):
         for side, ref in ((h, first[d]), (1 - h, jac_got.at[d - 1] if d else own_got)):
             to = pl.ds(pl.multiple_of((source(d) * H + side) * 64, 64), 64)
             jac[to, 0:1024] = ref[0:64, :]
             jac[to, 1024:2048] = ref[64:128, :]
-        both[d * 128 : (d + 1) * 128, 0:1024] = sens[d][...]
-        both[d * 128 : (d + 1) * 128, 1024:2048] = sens_got[d][...]
+    for k in range(2):
+        both[k * 256 : (k + 1) * 256, 0:1024] = sens[k][...]
+        both[k * 256 : (k + 1) * 256, 1024:2048] = sens_got[k][...]
     value = lax.dot_general(
         jac[...], both[...], (((1,), (1,)), ((), ())), preferred_element_type=F32
     )
-    own[...] = value[:, 0:128]
     for d in range(X):
         parts[source(d)] = value[:, d * 128 : (d + 1) * 128].astype(BF16)
-
-
-def sum_kernel(own, got, out):
-    total = own[...]
-    x = lax.axis_index("x")
-    for k in range(X):
-        total += jnp.where(x == k, 0.0, got[k].astype(F32))
-    out[...] = total.astype(BF16)
 
 
 def final_kernel(got, out):
     total = got[0].astype(F32)
-    for k in range(1, L * Z):
+    for k in range(1, X * L * Z):
         total += got[k].astype(F32)
     out[...] = total * (1.0 / math.sqrt(PARAMS))
 
@@ -186,6 +179,19 @@
 
 def dma(n):
     return [pltpu.SemaphoreType.DMA((n,))]
+
+
+def swap_rest(first, first_row, rows, behind):
+    joined = call(
+        functools.partial(join_kernel, first_row, rows),
+        shape(X - 1, rows, 1024),
+        first[1:],
+        ANY,
+        dma(X - 1),
+        nbytes=2 * MIB,
+        behind=behind,
+    )
+    return lax.ppermute(joined, "h", SWAP)
 
 
 def body(jacobian, cov_rows, sens_carry):
@@ -201,17 +207,6 @@
     )
     own_got = lax.ppermute(packed[0], "h", SWAP)
     first = [packed[0]] + [lax.ppermute(packed[d], "x", ring(d)) for d in range(1, X)]
-    cov_rest, jac_rest = call(
-        rest_kernel,
-        [shape(X - 1, 64, 1024), shape(X - 1, 128, 1024)],
-        first[1:],
-        ANY,
-        dma(2 * X - 2),
-        nbytes=2 * MIB,
-        behind=(own_got,),
-    )
-    cov_got = lax.ppermute(cov_rest, "h", SWAP)
-    jac_got = lax.ppermute(jac_rest, "h", SWAP)
     mine = over(panel, ("l", "z"))[0]
     panel = over(jnp.broadcast_to(mine, (32, 16, 128)), ("l", "z", "c"))
     panels = [panel] + [lax.ppermute(panel, "x", ring(d)) for d in range(1, X)]
@@ -219,9 +214,11 @@
         carry_kernel, [shape(128, 1024)] * X, (sens_carry,), ANY, dma(X), nbytes=2 * MIB
     )
     carry = [packed[0]] + [lax.ppermute(packed[d], "x", ring(d)) for d in range(1, X)]
-    sens = call(
+    cov_got = swap_rest(first, 128, 64, (own_got, panel))
+    jac_got = swap_rest(first, 0, 128, (cov_got,))
+    *sens, low, high = call(
         sens_kernel,
-        [shape(128, 1024)] * X,
+        [shape(128, 1024)] * X + [shape(256, 1024)] * 2,
         (*first, *carry, *panels, own_got, cov_got),
         VMEM,
         [pltpu.VMEM((512, 1024), BF16), pltpu.VMEM((512, WIDTH), BF16)],
@@ -230,21 +227,20 @@
         vmem=12,
     )
     sens_back = [sens[0]] + [lax.ppermute(sens[d], "x", ring(-d)) for d in range(1, X)]
-    sens_got = [lax.ppermute(part, "c", SWAP) for part in sens]
-    own_sum, parts = call(
+    sens_got = [lax.ppermute(pair, "c", SWAP) for pair in (low, high)]
+    parts = call(
         innov_kernel,
-        [shape(512, 128, kind=F32), shape(X, 512, 128)],
-        (own_got, jac_got, *first, *sens, *sens_got),
+        shape(X, 512, 128),
+        (own_got, jac_got, *first, low, high, *sens_got),
         VMEM,
         [pltpu.VMEM((512, 2048), BF16)] * 2,
         flops=2 * 512 * 512 * 2048,
         nbytes=2 * MIB,
         vmem=16,
-        behind=(sens_back[1], sens_back[3]),
-    )
-    summed = call(sum_kernel, shape(512, 128), (own_sum, over(parts, "x")), VMEM, nbytes=MIB, vmem=4)
-    shared = over(summed.reshape(L * Z, 32, 128), ("l", "z"))
-    innovation = call(final_kernel, shape(32, 128, kind=F32), (shared,), VMEM, nbytes=2**17, vmem=4)
+        behind=sens_back[1:],
+    )
+    shared = over(parts.reshape(X * L * Z, 32, 128), ("x", "l", "z"))
+    innovation = call(final_kernel, shape(32, 128, kind=F32), (shared,), VMEM, nbytes=2**19, vmem=4)
     sensitivity = call(
         assemble_kernel, shape(128, 4096), sens_back, ANY, dma(X), nbytes=2 * MIB
     )

time: 115 us -> 112 us (0.974); the launches traced: 115 us -> 111 us
  blocking collectives: 0 us -> 15.5 us
  starting transfers between devices: 53.3 us -> 44.7 us
  local copies, waits for them, and re-layouts: 7.61 us -> 1.25 us
  waiting for transfers between devices: 44.5 us -> 42 us
  Pallas kernels: 8.76 us -> 6.45 us
    all_to_all x0 -> x1, blocking collectives: none -> 15.5 us  [over(): return lax.all_to_all(value, axes, split_axis=0, concat_axis=0, tiled=True)]
    all_to_all x4 -> x2, waiting for transfers between devices: 26.8 us -> 16.4 us  [over(): return lax.all_to_all(value, axes, split_axis=0, concat_axis=0, tiled=True)]
    all_to_all x4 -> x2, starting transfers between devices: 29.1 us -> 19.3 us  [over(): return lax.all_to_all(value, axes, split_axis=0, concat_axis=0, tiled=True)]
    ppermute x3, waiting for transfers between devices: 4.93 us -> 13.7 us  [body(): lax.ppermute(sens[d], 'x', ring(-d))]
    unnamed x28 -> x8, local copies, waits for them, and re-layouts: 6.92 us -> 1.23 us
    ppermute x6, waiting for transfers between devices: 3.59 us -> 0.02 us  [body(): lax.ppermute(packed[d], 'x', ring(d))]
    pallas_call x9, Pallas kernels: 8.76 us -> 6.45 us  [call(): pl.pallas_call(kernel, out_shape=outs, in_specs=[spec] * len(ins) + [ANY]...]
    ppermute x6 -> x4, waiting for transfers between devices: 1.53 us -> 3.71 us  [the longest x2 3.71 us: swap_rest(): return lax.ppermute(joined, 'h', SWAP)]
  transfers between devices with their start and end apart: 24 -> 20, of which waited for: 13 -> 9; matrix products, arithmetic and copies ran while one was open for 1% -> 0% of each run, Pallas kernels for 5% -> 2%
where the time goes in v6:
time: 112 us; the launch traced here: 111 us
  starting transfers between devices  44.7 us (40%)
  waiting for transfers between devices  42 us (38%)
  blocking collectives  15.5 us (14%)
  Pallas kernels  6.45 us (6%)
  local copies, waits for them, and re-layouts  1.25 us (1%)
    all_to_all x2, starting transfers between devices, over(): return lax.all_to_all(value, axes, split_axis=0, concat_axis=0, tiled=True)  19.3 us
    all_to_all x2, waiting for transfers between devices, over(): return lax.all_to_all(value, axes, split_axis=0, concat_axis=0, tiled=True)  16.4 us
    all_to_all x1, blocking collectives, over(): return lax.all_to_all(value, axes, split_axis=0, concat_axis=0, tiled=True)  15.5 us
    ppermute x3, waiting for transfers between devices, body(): lax.ppermute(sens[d], 'x', ring(-d))  13.7 us
    ppermute x6, starting transfers between devices, body(): lax.ppermute(packed[d], 'x', ring(d))  8.87 us
    ppermute x3, starting transfers between devices, body(): panels = [panel] + [lax.ppermute(panel, 'x', ring(d)) for d in range(1, X)]  7.39 us
    pallas_call x9, Pallas kernels, call(): pl.pallas_call(kernel, out_shape=outs, in_specs=[spec] * len(ins) + [ANY]...  6.45 us
    ppermute x3, waiting for transfers between devices, body(): panels = [panel] + [lax.ppermute(panel, 'x', ring(d)) for d in range(1, X)]  6.32 us
  transfers between devices with their start and end apart: 20, of which 9 were waited for; matrix products, arithmetic and copies ran while one was open for 0% of the time, Pallas kernels for 2%

profile of v6, /device:TPU:4, one launch (start us, length us, event | category | flops | bytes accessed | tf_op | source)
XLA Modules:
  0.0 110.7 jit_solution(2920945514674428264)
XLA Ops:
  0.6 1.2 %copy-done = bf16[128,4096]{1,0:T(8,128)(2,1)S(1)} copy-done((bf16[128,4096]{1,0:T(8,128)(2,1)S(1)}, bf16[128,4096]{1,0:T(8,128)(2,1)}, u32[]{:S(2)}) %copy-start) | copy-done | bytes 1048600
  2.0 1.9 %collective-permute-done.got = bf16[64,4096]{1,0:T(8,128)(2,1)S(1)} collective-permute-done((bf16[64,4096]{1,0:T(8,128)(2,1)S(1)}, bf16[64,4096]{1,0:T(8,128)(2,1)S(1)}, u32[]{:S(2)}, u32[]{:S(2)}) %collective-permute-start) | collective-permute-done | bytes 524320 | tf_op jit(solution)/shard_map/ppermute | solution.py:199
  4.9 9.6 %all-to-all-start = ((bf16[16,16,128]{2,1,0:T(8,128)(2,1)}), bf16[16,16,128]{2,1,0:T(8,128)(2,1)S(1)}, u32[]{:S(2)}, u32[]{:S(2)}) async-start(bf16[16,16,128]{2,1,0:T(8,128)(2,1)} %get-tuple-element.25), calls=%async_computation | async-start | bytes 131072 | tf_op jit(solution)/shard_map/all_to_all | solution.py:177
  14.5 3.0 %collective-permute-start.10 = (bf16[192,1024]{1,0:T(8,128)(2,1)S(1)}, bf16[192,1024]{1,0:T(8,128)(2,1)S(1)}, u32[]{:S(2)}, u32[]{:S(2)}) collective-permute-start(bf16[192,1024]{1,0:T(8,128)(2,1)S(1)} %get-tuple-element.17.refs_0_), channel_id=1, source_target_pairs={{0,32},{32,0},{1,33},{33,1},{2,34},{34,2},{3,35},{35,3},{4,36},{36... | collective-permute-start | bytes 1179656 | tf_op jit(solution)/shard_map/ppermute | solution.py:208
  17.5 1.2 %collective-permute-start.1 = (bf16[192,1024]{1,0:T(8,128)(2,1)S(1)}, bf16[192,1024]{1,0:T(8,128)(2,1)S(1)}, u32[]{:S(2)}, u32[]{:S(2)}) collective-permute-start(bf16[192,1024]{1,0:T(8,128)(2,1)S(1)} %get-tuple-element.18), channel_id=1, source_target_pairs={{0,64},{64,128},{128,192},{192,0},{1,65},{65,129},{129,193},{193,1... | collective-permute-start | bytes 1179656 | tf_op jit(solution)/shard_map/ppermute | solution.py:209
  19.5 1.1 %collective-permute-start.3 = (bf16[192,1024]{1,0:T(8,128)(2,1)S(1)}, bf16[192,1024]{1,0:T(8,128)(2,1)S(1)}, u32[]{:S(2)}, u32[]{:S(2)}) collective-permute-start(bf16[192,1024]{1,0:T(8,128)(2,1)S(1)} %get-tuple-element.20), channel_id=1, source_target_pairs={{0,192},{64,0},{128,64},{192,128},{1,193},{65,1},{129,65},{193,129... | collective-permute-start | bytes 1179656 | tf_op jit(solution)/shard_map/ppermute | solution.py:209
  20.6 2.5 %all-to-all-done = bf16[16,16,128]{2,1,0:T(8,128)(2,1)S(1)} async-done(((bf16[16,16,128]{2,1,0:T(8,128)(2,1)}), bf16[16,16,128]{2,1,0:T(8,128)(2,1)S(1)}, u32[]{:S(2)}, u32[]{:S(2)}) %all-to-all-start) | async-done | bytes 65568 | tf_op jit(solution)/shard_map/all_to_all | solution.py:177
  23.1 15.5 %all_to_all.15.refs_4_.refs_8_ = bf16[32,16,128]{2,1,0:T(8,128)(2,1)S(1)} all-to-all(bf16[32,16,128]{2,1,0:T(8,128)(2,1)S(1)} %broadcast_in_dim.3), channel_id=1, replica_groups=mesh['x'=4,'h'=2,'l'=2,'z'=8,'c'=2] {'l','z','c'}, dimensions={0} | all-to-all | bytes 262144 | tf_op jit(solution)/shard_map/all_to_all | solution.py:177
  39.2 1.9 %collective-permute-start.11 = (bf16[3,64,1024]{2,1,0:T(8,128)(2,1)S(1)}, bf16[3,64,1024]{2,1,0:T(8,128)(2,1)S(1)}, u32[]{:S(2)}, u32[]{:S(2)}) collective-permute-start(bf16[3,64,1024]{2,1,0:T(8,128)(2,1)S(1)} %shard_map.53), channel_id=1, source_target_pairs={{0,32},{32,0},{1,33},{33,1},{2,34},{34,2},{3,35},{35,3},{4,36},{36... | collective-permute-start | bytes 1179656 | tf_op jit(solution)/shard_map/ppermute | solution.py:194
  41.2 1.0 collective-permute-start.4
  42.3 2.7 %collective-permute-start.5 = (bf16[128,1024]{1,0:T(8,128)(2,1)S(1)}, bf16[128,1024]{1,0:T(8,128)(2,1)S(1)}, u32[]{:S(2)}, u32[]{:S(2)}) collective-permute-start(bf16[128,1024]{1,0:T(8,128)(2,1)S(1)} %get-tuple-element.23), channel_id=1, source_target_pairs={{0,128},{64,192},{128,0},{192,64},{1,129},{65,193},{129,1},{193,65... | collective-permute-start | bytes 786440 | tf_op jit(solution)/shard_map/ppermute | solution.py:216
  44.9 2.0 %collective-permute-start.6 = (bf16[128,1024]{1,0:T(8,128)(2,1)S(1)}, bf16[128,1024]{1,0:T(8,128)(2,1)S(1)}, u32[]{:S(2)}, u32[]{:S(2)}) collective-permute-start(bf16[128,1024]{1,0:T(8,128)(2,1)S(1)} %get-tuple-element.24), channel_id=1, source_target_pairs={{0,192},{64,0},{128,64},{192,128},{1,193},{65,1},{129,65},{193,129... | collective-permute-start | bytes 786440 | tf_op jit(solution)/shard_map/ppermute | solution.py:216
  47.0 3.7 %collective-permute-done.11.refs_13_.refs_3_ = bf16[3,64,1024]{2,1,0:T(8,128)(2,1)S(1)} collective-permute-done((bf16[3,64,1024]{2,1,0:T(8,128)(2,1)S(1)}, bf16[3,64,1024]{2,1,0:T(8,128)(2,1)S(1)}, u32[]{:S(2)}, u32[]{:S(2)}) %collective-permute-start.11) | collective-permute-done | bytes 393248 | tf_op jit(solution)/shard_map/ppermute | solution.py:194
  50.8 1.9 %collective-permute-start.15 = (bf16[3,128,1024]{2,1,0:T(8,128)(2,1)S(1)}, bf16[3,128,1024]{2,1,0:T(8,128)(2,1)S(1)}, u32[]{:S(2)}, u32[]{:S(2)}) collective-permute-start(bf16[3,128,1024]{2,1,0:T(8,128)(2,1)S(1)} %shard_map.56), channel_id=1, source_target_pairs={{0,32},{32,0},{1,33},{33,1},{2,34},{34,2},{3,35},{35,3},{4,36},{36... | collective-permute-start | bytes 2359304 | tf_op jit(solution)/shard_map/ppermute | solution.py:194
  53.7 6.4 %collective-permute-start.8 = (bf16[32,16,128]{2,1,0:T(8,128)(2,1)S(1)}, bf16[32,16,128]{2,1,0:T(8,128)(2,1)S(1)}, u32[]{:S(2)}, u32[]{:S(2)}) collective-permute-start(bf16[32,16,128]{2,1,0:T(8,128)(2,1)S(1)} %all_to_all.15.refs_4_.refs_8_), channel_id=1, source_target_pairs={{0,128},{64,192},{128,0},{192,64},{1,129},{65,193},{129,1},{193,65... | collective-permute-start | bytes 393224 | tf_op jit(solution)/shard_map/ppermute | solution.py:212
  60.1 2.9 %collective-permute-done.8.refs_10_ = bf16[32,16,128]{2,1,0:T(8,128)(2,1)S(1)} collective-permute-done((bf16[32,16,128]{2,1,0:T(8,128)(2,1)S(1)}, bf16[32,16,128]{2,1,0:T(8,128)(2,1)S(1)}, u32[]{:S(2)}, u32[]{:S(2)}) %collective-permute-start.8) | collective-permute-done | bytes 131104 | tf_op jit(solution)/shard_map/ppermute | solution.py:212
  63.0 3.4 %collective-permute-done.9.refs_11_ = bf16[32,16,128]{2,1,0:T(8,128)(2,1)S(1)} collective-permute-done((bf16[32,16,128]{2,1,0:T(8,128)(2,1)S(1)}, bf16[32,16,128]{2,1,0:T(8,128)(2,1)S(1)}, u32[]{:S(2)}, u32[]{:S(2)}) %collective-permute-start.9) | collective-permute-done | bytes 131104 | tf_op jit(solution)/shard_map/ppermute | solution.py:212
  67.9 1.5 %collective-permute-start.13 = (bf16[128,1024]{1,0:T(8,128)(2,1)S(1)}, bf16[128,1024]{1,0:T(8,128)(2,1)S(1)}, u32[]{:S(2)}, u32[]{:S(2)}) collective-permute-start(bf16[128,1024]{1,0:T(8,128)(2,1)S(1)} %get-tuple-element.28), channel_id=1, source_target_pairs={{0,128},{64,192},{128,0},{192,64},{1,129},{65,193},{129,1},{193,65... | collective-permute-start | bytes 786440 | tf_op jit(solution)/shard_map/ppermute | solution.py:229
  69.5 6.8 %collective-permute-done.12.refs_1_.refs_8_ = bf16[128,1024]{1,0:T(8,128)(2,1)S(1)} collective-permute-done((bf16[128,1024]{1,0:T(8,128)(2,1)S(1)}, bf16[128,1024]{1,0:T(8,128)(2,1)S(1)}, u32[]{:S(2)}, u32[]{:S(2)}) %collective-permute-start.12) | collective-permute-done | bytes 262176 | tf_op jit(solution)/shard_map/ppermute | solution.py:229
  76.2 2.4 %collective-permute-done.13.refs_2_.refs_9_ = bf16[128,1024]{1,0:T(8,128)(2,1)S(1)} collective-permute-done((bf16[128,1024]{1,0:T(8,128)(2,1)S(1)}, bf16[128,1024]{1,0:T(8,128)(2,1)S(1)}, u32[]{:S(2)}, u32[]{:S(2)}) %collective-permute-start.13) | collective-permute-done | bytes 262176 | tf_op jit(solution)/shard_map/ppermute | solution.py:229
  78.6 4.5 %collective-permute-done.14.refs_3_.refs_10_ = bf16[128,1024]{1,0:T(8,128)(2,1)S(1)} collective-permute-done((bf16[128,1024]{1,0:T(8,128)(2,1)S(1)}, bf16[128,1024]{1,0:T(8,128)(2,1)S(1)}, u32[]{:S(2)}, u32[]{:S(2)}) %collective-permute-start.14) | collective-permute-done | bytes 262176 | tf_op jit(solution)/shard_map/ppermute | solution.py:229
  83.2 2.2 %shard_map.57 = bf16[4,512,128]{2,1,0:T(8,128)(2,1)} custom-call(bf16[192,1024]{1,0:T(8,128)(2,1)S(1)} %collective-permute-done.10.refs_3_.refs_12_.own_got, bf16[3,128,1024]{2,1,0:T(8,128)(2,1)S(1)} %collective-permute-done.15.jac_got, bf16[192,1024]{1,0:T(8,128)(2,1)S(1)} %get-tuple-element.17.refs_0_, ...), custom_call_target="tpu_custom_call" | custom-call | flops 1073741824 | bytes 2097152 | tf_op jit(solution)/shard_map/pallas_call | solution.py:27
  85.3 9.7 %all-to-all-start.2 = ((bf16[64,32,128]{2,1,0:T(8,128)(2,1)}), bf16[64,32,128]{2,1,0:T(8,128)(2,1)S(1)}, u32[]{:S(2)}, u32[]{:S(2)}) async-start(bf16[64,32,128]{2,1,0:T(8,128)(2,1)} %bitcast.1), calls=%async_computation.2 | async-start | bytes 1048576 | tf_op jit(solution)/shard_map/all_to_all | solution.py:177
  96.1 13.9 %all-to-all-done.2.got = bf16[64,32,128]{2,1,0:T(8,128)(2,1)S(1)} async-done(((bf16[64,32,128]{2,1,0:T(8,128)(2,1)}), bf16[64,32,128]{2,1,0:T(8,128)(2,1)S(1)}, u32[]{:S(2)}, u32[]{:S(2)}) %all-to-all-start.2) | async-done | bytes 524320 | tf_op jit(solution)/shard_map/all_to_all | solution.py:177
  (36 shorter events, 6.9 us)
Async XLA Ops:
  0.6 1.2 %copy-start = (bf16[128,4096]{1,0:T(8,128)(2,1)S(1)}, bf16[128,4096]{1,0:T(8,128)(2,1)}, u32[]{:S(2)}) copy-start(bf16[128,4096]{1,0:T(8,128)(2,1)} %jac.3) | copy-start | bytes 3145732
  1.9 2.1 %copy-start.1 = (bf16[128,4096]{1,0:T(8,128)(2,1)S(1)}, bf16[128,4096]{1,0:T(8,128)(2,1)}, u32[]{:S(2)}) copy-start(bf16[128,4096]{1,0:T(8,128)(2,1)} %jac.3) | copy-start | bytes 3145732
  1.9 2.1 %copy-start.3 = (bf16[64,4096]{1,0:T(8,128)(2,1)S(1)}, bf16[64,4096]{1,0:T(8,128)(2,1)}, u32[]{:S(2)}) copy-start(bf16[64,4096]{1,0:T(8,128)(2,1)} %cov.1) | copy-start | bytes 1572868
  1.9 2.0 %collective-permute-start = (bf16[64,4096]{1,0:T(8,128)(2,1)S(1)}, bf16[64,4096]{1,0:T(8,128)(2,1)S(1)}, u32[]{:S(2)}, u32[]{:S(2)}) collective-permute-start(bf16[64,4096]{1,0:T(8,128)(2,1)S(1)} %shard_map.50), channel_id=1, source_target_pairs={{0,1},{1,0},{2,3},{3,2},{4,5},{5,4},{6,7},{7,6},{8,9},{9,8},{10,11... | collective-permute-start | bytes 1572872 | tf_op jit(solution)/shard_map/ppermute | solution.py:199
  4.9 18.2 %all-to-all-start = ((bf16[16,16,128]{2,1,0:T(8,128)(2,1)}), bf16[16,16,128]{2,1,0:T(8,128)(2,1)S(1)}, u32[]{:S(2)}, u32[]{:S(2)}) async-start(bf16[16,16,128]{2,1,0:T(8,128)(2,1)} %get-tuple-element.25), calls=%async_computation | async-start | bytes 131072 | tf_op jit(solution)/shard_map/all_to_all | solution.py:177
  14.5 24.1 %collective-permute-start.10 = (bf16[192,1024]{1,0:T(8,128)(2,1)S(1)}, bf16[192,1024]{1,0:T(8,128)(2,1)S(1)}, u32[]{:S(2)}, u32[]{:S(2)}) collective-permute-start(bf16[192,1024]{1,0:T(8,128)(2,1)S(1)} %get-tuple-element.17.refs_0_), channel_id=1, source_target_pairs={{0,32},{32,0},{1,33},{33,1},{2,34},{34,2},{3,35},{35,3},{4,36},{36... | collective-permute-start | bytes 1179656 | tf_op jit(solution)/shard_map/ppermute | solution.py:208
  17.5 21.1 %collective-permute-start.1 = (bf16[192,1024]{1,0:T(8,128)(2,1)S(1)}, bf16[192,1024]{1,0:T(8,128)(2,1)S(1)}, u32[]{:S(2)}, u32[]{:S(2)}) collective-permute-start(bf16[192,1024]{1,0:T(8,128)(2,1)S(1)} %get-tuple-element.18), channel_id=1, source_target_pairs={{0,64},{64,128},{128,192},{192,0},{1,65},{65,129},{129,193},{193,1... | collective-permute-start | bytes 1179656 | tf_op jit(solution)/shard_map/ppermute | solution.py:209
  18.7 20.0 %collective-permute-start.2 = (bf16[192,1024]{1,0:T(8,128)(2,1)S(1)}, bf16[192,1024]{1,0:T(8,128)(2,1)S(1)}, u32[]{:S(2)}, u32[]{:S(2)}) collective-permute-start(bf16[192,1024]{1,0:T(8,128)(2,1)S(1)} %get-tuple-element.19), channel_id=1, source_target_pairs={{0,128},{64,192},{128,0},{192,64},{1,129},{65,193},{129,1},{193,65... | collective-permute-start | bytes 1179656 | tf_op jit(solution)/shard_map/ppermute | solution.py:209
  19.5 19.2 %collective-permute-start.3 = (bf16[192,1024]{1,0:T(8,128)(2,1)S(1)}, bf16[192,1024]{1,0:T(8,128)(2,1)S(1)}, u32[]{:S(2)}, u32[]{:S(2)}) collective-permute-start(bf16[192,1024]{1,0:T(8,128)(2,1)S(1)} %get-tuple-element.20), channel_id=1, source_target_pairs={{0,192},{64,0},{128,64},{192,128},{1,193},{65,1},{129,65},{193,129... | collective-permute-start | bytes 1179656 | tf_op jit(solution)/shard_map/ppermute | solution.py:209
  38.6 2.5 %copy-start.2 = (bf16[128,4096]{1,0:T(8,128)(2,1)S(1)}, bf16[128,4096]{1,0:T(8,128)(2,1)}, u32[]{:S(2)}) copy-start(bf16[128,4096]{1,0:T(8,128)(2,1)} %carry.1) | copy-start | bytes 3145732
  39.2 11.5 %collective-permute-start.11 = (bf16[3,64,1024]{2,1,0:T(8,128)(2,1)S(1)}, bf16[3,64,1024]{2,1,0:T(8,128)(2,1)S(1)}, u32[]{:S(2)}, u32[]{:S(2)}) collective-permute-start(bf16[3,64,1024]{2,1,0:T(8,128)(2,1)S(1)} %shard_map.53), channel_id=1, source_target_pairs={{0,32},{32,0},{1,33},{33,1},{2,34},{34,2},{3,35},{35,3},{4,36},{36... | collective-permute-start | bytes 1179656 | tf_op jit(solution)/shard_map/ppermute | solution.py:194
  41.2 12.4 %collective-permute-start.4 = (bf16[128,1024]{1,0:T(8,128)(2,1)S(1)}, bf16[128,1024]{1,0:T(8,128)(2,1)S(1)}, u32[]{:S(2)}, u32[]{:S(2)}) collective-permute-start(bf16[128,1024]{1,0:T(8,128)(2,1)S(1)} %get-tuple-element.22), channel_id=1, source_target_pairs={{0,64},{64,128},{128,192},{192,0},{1,65},{65,129},{129,193},{193,1... | collective-permute-start | bytes 786440 | tf_op jit(solution)/shard_map/ppermute | solution.py:216
  42.3 17.8 %collective-permute-start.5 = (bf16[128,1024]{1,0:T(8,128)(2,1)S(1)}, bf16[128,1024]{1,0:T(8,128)(2,1)S(1)}, u32[]{:S(2)}, u32[]{:S(2)}) collective-permute-start(bf16[128,1024]{1,0:T(8,128)(2,1)S(1)} %get-tuple-element.23), channel_id=1, source_target_pairs={{0,128},{64,192},{128,0},{192,64},{1,129},{65,193},{129,1},{193,65... | collective-permute-start | bytes 786440 | tf_op jit(solution)/shard_map/ppermute | solution.py:216
  44.9 15.2 %collective-permute-start.6 = (bf16[128,1024]{1,0:T(8,128)(2,1)S(1)}, bf16[128,1024]{1,0:T(8,128)(2,1)S(1)}, u32[]{:S(2)}, u32[]{:S(2)}) collective-permute-start(bf16[128,1024]{1,0:T(8,128)(2,1)S(1)} %get-tuple-element.24), channel_id=1, source_target_pairs={{0,192},{64,0},{128,64},{192,128},{1,193},{65,1},{129,65},{193,129... | collective-permute-start | bytes 786440 | tf_op jit(solution)/shard_map/ppermute | solution.py:216
  50.8 32.4 %collective-permute-start.15 = (bf16[3,128,1024]{2,1,0:T(8,128)(2,1)S(1)}, bf16[3,128,1024]{2,1,0:T(8,128)(2,1)S(1)}, u32[]{:S(2)}, u32[]{:S(2)}) collective-permute-start(bf16[3,128,1024]{2,1,0:T(8,128)(2,1)S(1)} %shard_map.56), channel_id=1, source_target_pairs={{0,32},{32,0},{1,33},{33,1},{2,34},{34,2},{3,35},{35,3},{4,36},{36... | collective-permute-start | bytes 2359304 | tf_op jit(solution)/shard_map/ppermute | solution.py:194
  52.7 7.4 %collective-permute-start.7 = (bf16[32,16,128]{2,1,0:T(8,128)(2,1)S(1)}, bf16[32,16,128]{2,1,0:T(8,128)(2,1)S(1)}, u32[]{:S(2)}, u32[]{:S(2)}) collective-permute-start(bf16[32,16,128]{2,1,0:T(8,128)(2,1)S(1)} %all_to_all.15.refs_4_.refs_8_), channel_id=1, source_target_pairs={{0,64},{64,128},{128,192},{192,0},{1,65},{65,129},{129,193},{193,1... | collective-permute-start | bytes 393224 | tf_op jit(solution)/shard_map/ppermute | solution.py:212
  53.7 9.4 %collective-permute-start.8 = (bf16[32,16,128]{2,1,0:T(8,128)(2,1)S(1)}, bf16[32,16,128]{2,1,0:T(8,128)(2,1)S(1)}, u32[]{:S(2)}, u32[]{:S(2)}) collective-permute-start(bf16[32,16,128]{2,1,0:T(8,128)(2,1)S(1)} %all_to_all.15.refs_4_.refs_8_), channel_id=1, source_target_pairs={{0,128},{64,192},{128,0},{192,64},{1,129},{65,193},{129,1},{193,65... | collective-permute-start | bytes 393224 | tf_op jit(solution)/shard_map/ppermute | solution.py:212
  60.1 6.3 %collective-permute-start.9 = (bf16[32,16,128]{2,1,0:T(8,128)(2,1)S(1)}, bf16[32,16,128]{2,1,0:T(8,128)(2,1)S(1)}, u32[]{:S(2)}, u32[]{:S(2)}) collective-permute-start(bf16[32,16,128]{2,1,0:T(8,128)(2,1)S(1)} %all_to_all.15.refs_4_.refs_8_), channel_id=1, source_target_pairs={{0,192},{64,0},{128,64},{192,128},{1,193},{65,1},{129,65},{193,129... | collective-permute-start | bytes 393224 | tf_op jit(solution)/shard_map/ppermute | solution.py:212
  67.3 9.0 %collective-permute-start.12 = (bf16[128,1024]{1,0:T(8,128)(2,1)S(1)}, bf16[128,1024]{1,0:T(8,128)(2,1)S(1)}, u32[]{:S(2)}, u32[]{:S(2)}) collective-permute-start(bf16[128,1024]{1,0:T(8,128)(2,1)S(1)} %get-tuple-element.27), channel_id=1, source_target_pairs={{0,192},{64,0},{128,64},{192,128},{1,193},{65,1},{129,65},{193,129... | collective-permute-start | bytes 786440 | tf_op jit(solution)/shard_map/ppermute | solution.py:229
  67.3 15.8 %collective-permute-start.16 = (bf16[256,1024]{1,0:T(8,128)(2,1)S(1)}, bf16[256,1024]{1,0:T(8,128)(2,1)S(1)}, u32[]{:S(2)}, u32[]{:S(2)}) collective-permute-start(bf16[256,1024]{1,0:T(8,128)(2,1)S(1)} %get-tuple-element.30.refs_4_), channel_id=1, source_target_pairs={{0,1},{1,0},{2,3},{3,2},{4,5},{5,4},{6,7},{7,6},{8,9},{9,8},{10,11... | collective-permute-start | bytes 1572872 | tf_op jit(solution)/shard_map/ppermute | solution.py:230
  67.4 15.7 %collective-permute-start.17 = (bf16[256,1024]{1,0:T(8,128)(2,1)S(1)}, bf16[256,1024]{1,0:T(8,128)(2,1)S(1)}, u32[]{:S(2)}, u32[]{:S(2)}) collective-permute-start(bf16[256,1024]{1,0:T(8,128)(2,1)S(1)} %get-tuple-element.31.refs_5_), channel_id=1, source_target_pairs={{0,1},{1,0},{2,3},{3,2},{4,5},{5,4},{6,7},{7,6},{8,9},{9,8},{10,11... | collective-permute-start | bytes 1572872 | tf_op jit(solution)/shard_map/ppermute | solution.py:230
  67.9 10.7 %collective-permute-start.13 = (bf16[128,1024]{1,0:T(8,128)(2,1)S(1)}, bf16[128,1024]{1,0:T(8,128)(2,1)S(1)}, u32[]{:S(2)}, u32[]{:S(2)}) collective-permute-start(bf16[128,1024]{1,0:T(8,128)(2,1)S(1)} %get-tuple-element.28), channel_id=1, source_target_pairs={{0,128},{64,192},{128,0},{192,64},{1,129},{65,193},{129,1},{193,65... | collective-permute-start | bytes 786440 | tf_op jit(solution)/shard_map/ppermute | solution.py:229
  76.2 6.9 %collective-permute-start.14 = (bf16[128,1024]{1,0:T(8,128)(2,1)S(1)}, bf16[128,1024]{1,0:T(8,128)(2,1)S(1)}, u32[]{:S(2)}, u32[]{:S(2)}) collective-permute-start(bf16[128,1024]{1,0:T(8,128)(2,1)S(1)} %get-tuple-element.29), channel_id=1, source_target_pairs={{0,64},{64,128},{128,192},{192,0},{1,65},{65,129},{129,193},{193,1... | collective-permute-start | bytes 786440 | tf_op jit(solution)/shard_map/ppermute | solution.py:229
  85.3 24.6 %all-to-all-start.2 = ((bf16[64,32,128]{2,1,0:T(8,128)(2,1)}), bf16[64,32,128]{2,1,0:T(8,128)(2,1)S(1)}, u32[]{:S(2)}, u32[]{:S(2)}) async-start(bf16[64,32,128]{2,1,0:T(8,128)(2,1)} %bitcast.1), calls=%async_computation.2 | async-start | bytes 1048576 | tf_op jit(solution)/shard_map/all_to_all | solution.py:177

commit v7 on v6

--- a/solution.py
+++ b/solution.py
@@ -51,11 +51,13 @@
     return pl.ds(pl.multiple_of(half * 64 + core * 32, 32), 32)
 
 
-def give_kernel(jac, give, sems):
+def give_kernel(jac, give, panel, sems):
     other = 1 - lax.axis_index("c")
-    run_copies(
-        [(jac.at[slab(k, other), :], give.at[pl.ds(k * 32, 32), :]) for k in range(2)], sems
-    )
+    copies = [(jac.at[slab(k, other), :], give.at[pl.ds(k * 32, 32), :]) for k in range(2)]
+    for k in range(8):
+        for n in range(4):
+            copies.append((jac.at[pl.ds(k * 16, 16), pl.ds(n * 128, 128)], panel.at[k * 4 + n]))
+    run_copies(copies, sems)
 
 
 def part(d):
@@ -63,41 +65,16 @@
     return pl.ds(pl.multiple_of(at * 1024, 1024), 1024)
 
 
-def pack_kernel(jac, got, cov, *refs):
-    outs, panel, sems, panel_sems = refs[:X], refs[X], refs[X + 1], refs[X + 2]
+def pack_kernel(jac, got, cov, carry, *refs):
+    outs, sems = refs[:X], refs[X]
     core = lax.axis_index("c")
-
-    def pieces(ref, rows):
-        return [
-            pltpu.make_async_copy(
-                ref.at[rows(k), pl.ds(n * 128, 128)], panel.at[k * 4 + n], panel_sems.at[k * 4 + n]
-            )
-            for k in range(4)
-            for n in range(4)
-        ]
-
-    @pl.when(core == 0)
-    def _():
-        for copy in pieces(jac, lambda k: pl.ds(k // 2 * 64 + k % 2 * 16, 16)):
-            copy.start()
-
-    @pl.when(core == 1)
-    def _():
-        for copy in pieces(got, lambda k: pl.ds(k * 16, 16)):
-            copy.start()
-
     copies = []
     for d in range(X):
         copies += [(jac.at[slab(n, core), part(d)], outs[d].at[pl.ds(n * 32, 32), :]) for n in range(2)]
         copies.append((got.at[:, part(d)], outs[d].at[pl.ds(64, 64), :]))
         copies.append((cov.at[:, part(d)], outs[d].at[pl.ds(128, 64), :]))
+        copies.append((carry.at[:, part(d)], outs[d].at[pl.ds(192, 128), :]))
     run_copies(copies, sems)
-    for copy in pieces(got, lambda k: pl.ds(k * 16, 16)):
-        copy.wait()
-
-
-def carry_kernel(carry, *refs):
-    run_copies([(carry.at[:, part(d)], refs[d]) for d in range(X)], refs[X])
 
 
 def join_kernel(first_row, rows, *refs):
@@ -108,8 +85,8 @@
 
 
 def sens_kernel(*refs):
-    first, carry, panels, (own_got, cov_got) = refs[:4], refs[4:8], refs[8:12], refs[12:14]
-    outs, pairs, cov, panel = refs[14:18], refs[18:20], refs[20], refs[21]
+    first, panels, (own_got, cov_got) = refs[:4], refs[4:8], refs[8:10]
+    outs, pairs, cov, panel = refs[10:14], refs[14:16], refs[16], refs[17]
     h = lax.axis_index("h")
 
     def rows(d, side):
@@ -119,16 +96,15 @@
         cov[rows(d, h), :] = first[d][128:192, :]
         cov[rows(d, 1 - h), :] = cov_got[d - 1] if d else own_got[128:192, :]
     for d in range(X):
-        for k in range(4):
+        for k in range(8):
             for n in range(4):
-                for core in range(C):
-                    at = d * 128 + k // 2 * 64 + core * 32 + k % 2 * 16
-                    panel[at : at + 16, n * 128 : n * 128 + 128] = panels[d][(k * 4 + n) * C + core]
+                at = d * 128 + k * 16
+                panel[at : at + 16, n * 128 : n * 128 + 128] = panels[d][k * 4 + n]
     for d in range(X):
         product = jnp.dot(
             panel[d * 128 : (d + 1) * 128, :], cov[...], preferred_element_type=F32
         )
-        value = carry[d][...].astype(F32) + product * (1.0 / math.sqrt(WIDTH))
+        value = first[d][192:320, :].astype(F32) + product * (1.0 / math.sqrt(WIDTH))
         value = value.astype(BF16)
         outs[d][...] = value
         pairs[d // 2][d % 2 * 128 : d % 2 * 128 + 128, :] = value
@@ -195,31 +171,34 @@
 
 
 def body(jacobian, cov_rows, sens_carry):
-    give = call(give_kernel, shape(64, 4096), (jacobian,), ANY, dma(2), nbytes=MIB)
+    give, panel = call(
+        give_kernel,
+        [shape(64, 4096), shape(32, 16, 128)],
+        (jacobian,),
+        ANY,
+        dma(34),
+        nbytes=MIB,
+    )
     got = lax.ppermute(give, "c", SWAP)
-    *packed, panel = call(
+    mine = over(panel, ("l", "z", "c"))[0]
+    panel = over(jnp.broadcast_to(mine, (32, 16, 128)), ("l", "z", "c"))
+    packed = call(
         pack_kernel,
-        [shape(192, 1024)] * X + [shape(16, 16, 128)],
-        (jacobian, got, cov_rows),
+        [shape(320, 1024)] * X,
+        (jacobian, got, cov_rows, sens_carry),
         ANY,
-        dma(4 * X) + dma(16),
-        nbytes=4 * MIB,
-    )
-    own_got = lax.ppermute(packed[0], "h", SWAP)
+        dma(5 * X),
+        nbytes=5 * MIB,
+    )
+    own_got = lax.ppermute(packed[0][:192], "h", SWAP)
     first = [packed[0]] + [lax.ppermute(packed[d], "x", ring(d)) for d in range(1, X)]
-    mine = over(panel, ("l", "z"))[0]
-    panel = over(jnp.broadcast_to(mine, (32, 16, 128)), ("l", "z", "c"))
     panels = [panel] + [lax.ppermute(panel, "x", ring(d)) for d in range(1, X)]
-    packed = call(
-        carry_kernel, [shape(128, 1024)] * X, (sens_carry,), ANY, dma(X), nbytes=2 * MIB
-    )
-    carry = [packed[0]] + [lax.ppermute(packed[d], "x", ring(d)) for d in range(1, X)]
     cov_got = swap_rest(first, 128, 64, (own_got, panel))
-    jac_got = swap_rest(first, 0, 128, (cov_got,))
+    jac_got = swap_rest(first, 0, 128, (cov_got, *panels[1:]))
     *sens, low, high = call(
         sens_kernel,
         [shape(128, 1024)] * X + [shape(256, 1024)] * 2,
-        (*first, *carry, *panels, own_got, cov_got),
+        (*first, *panels, own_got, cov_got),
         VMEM,
         [pltpu.VMEM((512, 1024), BF16), pltpu.VMEM((512, WIDTH), BF16)],
         flops=2 * 512 * 512 * 1024,

time: 112 us -> 116 us (1.036)
  waiting for transfers between devices: 42 us -> 35.3 us
  starting transfers between devices: 44.7 us -> 48.4 us
  local copies, waits for them, and re-layouts: 1.25 us -> 4.24 us
  blocking collectives: 15.5 us -> 17.6 us
  Pallas kernels: 6.45 us -> 7.9 us
    ppermute x3, starting transfers between devices: 1.6 us -> 10.6 us  [body(): lax.ppermute(sens[d], 'x', ring(-d))]
    ppermute x6 -> x3, waiting for transfers between devices: 0.02 us -> 8.85 us  [body(): lax.ppermute(packed[d], 'x', ring(d))]
    ppermute x6 -> x3, starting transfers between devices: 8.87 us -> 3.21 us  [body(): lax.ppermute(packed[d], 'x', ring(d))]
    ppermute x3, waiting for transfers between devices: 13.7 us -> 8.63 us  [body(): lax.ppermute(sens[d], 'x', ring(-d))]
    all_to_all x2, waiting for transfers between devices: 16.4 us -> 12.1 us  [over(): return lax.all_to_all(value, axes, split_axis=0, concat_axis=0, tiled=True)]
    ppermute x3, starting transfers between devices: 7.39 us -> 3.51 us  [body(): panels = [panel] + [lax.ppermute(panel, 'x', ring(d)) for d in range(1, X)]]
    ppermute x2, waiting for transfers between devices: 3.71 us -> 0.01 us  [swap_rest(): return lax.ppermute(joined, 'h', SWAP)]
    unnamed x8 -> x16, local copies, waits for them, and re-layouts: 1.23 us -> 4.19 us
  transfers between devices with their start and end apart: 20 -> 17, of which waited for: 9 -> 9; matrix products, arithmetic and copies ran while one was open for 0% -> 0% of each run, Pallas kernels for 2% -> 3%
where the time goes in v7:
time: 116 us; the launch traced here: 114 us
  starting transfers between devices  48.4 us (42%)
  waiting for transfers between devices  35.3 us (30%)
  blocking collectives  17.6 us (15%)
  Pallas kernels  7.9 us (7%)
  local copies, waits for them, and re-layouts  4.24 us (4%)
    all_to_all x2, starting transfers between devices, over(): return lax.all_to_all(value, axes, split_axis=0, concat_axis=0, tiled=True)  21.9 us
    all_to_all x1, blocking collectives, over(): return lax.all_to_all(value, axes, split_axis=0, concat_axis=0, tiled=True)  17.6 us
    all_to_all x2, waiting for transfers between devices, over(): return lax.all_to_all(value, axes, split_axis=0, concat_axis=0, tiled=True)  12.1 us
    ppermute x3, starting transfers between devices, body(): lax.ppermute(sens[d], 'x', ring(-d))  10.6 us
    ppermute x3, waiting for transfers between devices, body(): lax.ppermute(packed[d], 'x', ring(d))  8.85 us
    ppermute x3, waiting for transfers between devices, body(): lax.ppermute(sens[d], 'x', ring(-d))  8.63 us
    pallas_call x8, Pallas kernels, call(): pl.pallas_call(kernel, out_shape=outs, in_specs=[spec] * len(ins) + [ANY]...  7.9 us
    ppermute x3, waiting for transfers between devices, body(): panels = [panel] + [lax.ppermute(panel, 'x', ring(d)) for d in range(1, X)]  5.69 us
  transfers between devices with their start and end apart: 17, of which 9 were waited for; matrix products, arithmetic and copies ran while one was open for 0% of the time, Pallas kernels for 3%

profile of v7, /device:TPU:4, one launch (start us, length us, event | category | flops | bytes accessed | tf_op | source)
XLA Modules:
  0.0 114.2 jit_solution(391578224298463709)
XLA Ops:
  0.6 1.2 %copy-done = bf16[128,4096]{1,0:T(8,128)(2,1)S(1)} copy-done((bf16[128,4096]{1,0:T(8,128)(2,1)S(1)}, bf16[128,4096]{1,0:T(8,128)(2,1)}, u32[]{:S(2)}) %copy-start) | copy-done | bytes 1048600
  1.9 1.0 shard_map.50
  3.0 10.0 %all-to-all-start = ((bf16[32,16,128]{2,1,0:T(8,128)(2,1)}), bf16[32,16,128]{2,1,0:T(8,128)(2,1)S(1)}, u32[]{:S(2)}, u32[]{:S(2)}) async-start(bf16[32,16,128]{2,1,0:T(8,128)(2,1)} %get-tuple-element.19), calls=%async_computation | async-start | bytes 262144 | tf_op jit(solution)/shard_map/all_to_all | solution.py:153
  13.0 1.2 %copy-done.4 = bf16[128,4096]{1,0:T(8,128)(2,1)S(1)} copy-done((bf16[128,4096]{1,0:T(8,128)(2,1)S(1)}, bf16[128,4096]{1,0:T(8,128)(2,1)}, u32[]{:S(2)}) %copy-start.4) | copy-done | bytes 1048600
  15.3 1.5 %shard_map.51 = (bf16[320,1024]{1,0:T(8,128)(2,1)S(1)}, bf16[320,1024]{1,0:T(8,128)(2,1)}, bf16[320,1024]{1,0:T(8,128)(2,1)}, bf16[320,1024]{1,0:T(8,128)(2,1)}) custom-call(bf16[128,4096]{1,0:T(8,128)(2,1)S(1)} %copy-done.1, bf16[64,4096]{1,0:T(8,128)(2,1)S(1)} %collective-permute-done.got, bf16[64,4096]{1,0:T(8,128)(2,1)S(1)} %copy-done.5, ...), custom_call_target="tpu_custom_call" | custom-call | bytes 5242880 | tf_op jit(solution)/shard_map/pallas_call | solution.py:27
  16.8 1.3 %collective-permute-start.1 = (bf16[320,1024]{1,0:T(8,128)(2,1)}, bf16[320,1024]{1,0:T(8,128)(2,1)S(1)}, u32[]{:S(2)}, u32[]{:S(2)}) collective-permute-start(bf16[320,1024]{1,0:T(8,128)(2,1)} %get-tuple-element.16), channel_id=1, source_target_pairs={{0,64},{64,128},{128,192},{192,0},{1,65},{65,129},{129,193},{193,1... | collective-permute-start | bytes 1966088 | tf_op jit(solution)/shard_map/ppermute | solution.py:194
  18.9 1.1 collective-permute-start.3
  20.1 3.0 %collective-permute-start.7 = (bf16[192,1024]{1,0:T(8,128)(2,1)S(1)}, bf16[192,1024]{1,0:T(8,128)(2,1)S(1)}, u32[]{:S(2)}, u32[]{:S(2)}) collective-permute-start(bf16[192,1024]{1,0:T(8,128)(2,1)S(1)} %slice.7), channel_id=1, source_target_pairs={{0,32},{32,0},{1,33},{33,1},{2,34},{34,2},{3,35},{35,3},{4,36},{36... | collective-permute-start | bytes 1179656 | tf_op jit(solution)/shard_map/ppermute | solution.py:193
  23.5 17.6 %all_to_all.15.refs_4_ = bf16[32,16,128]{2,1,0:T(8,128)(2,1)S(1)} all-to-all(bf16[32,16,128]{2,1,0:T(8,128)(2,1)S(1)} %broadcast_in_dim.3), channel_id=1, replica_groups=mesh['x'=4,'h'=2,'l'=2,'z'=8,'c'=2] {'l','z','c'}, dimensions={0} | all-to-all | bytes 262144 | tf_op jit(solution)/shard_map/all_to_all | solution.py:153
  41.0 7.0 %collective-permute-done.2.refs_1_.refs_2_ = bf16[320,1024]{1,0:T(8,128)(2,1)S(1)} collective-permute-done((bf16[320,1024]{1,0:T(8,128)(2,1)}, bf16[320,1024]{1,0:T(8,128)(2,1)S(1)}, u32[]{:S(2)}, u32[]{:S(2)}) %collective-permute-start.2) | collective-permute-done | bytes 655392 | tf_op jit(solution)/shard_map/ppermute | solution.py:194
  48.1 1.8 %collective-permute-done.3.refs_2_.refs_3_ = bf16[320,1024]{1,0:T(8,128)(2,1)S(1)} collective-permute-done((bf16[320,1024]{1,0:T(8,128)(2,1)}, bf16[320,1024]{1,0:T(8,128)(2,1)S(1)}, u32[]{:S(2)}, u32[]{:S(2)}) %collective-permute-start.3) | collective-permute-done | bytes 655392 | tf_op jit(solution)/shard_map/ppermute | solution.py:194
  50.4 3.0 %collective-permute-start.8 = (bf16[3,64,1024]{2,1,0:T(8,128)(2,1)S(1)}, bf16[3,64,1024]{2,1,0:T(8,128)(2,1)S(1)}, u32[]{:S(2)}, u32[]{:S(2)}) collective-permute-start(bf16[3,64,1024]{2,1,0:T(8,128)(2,1)S(1)} %shard_map.52), channel_id=1, source_target_pairs={{0,32},{32,0},{1,33},{33,1},{2,34},{34,2},{3,35},{35,3},{4,36},{36... | collective-permute-start | bytes 1179656 | tf_op jit(solution)/shard_map/ppermute | solution.py:170
  54.1 2.4 %collective-permute-start.5 = (bf16[32,16,128]{2,1,0:T(8,128)(2,1)S(1)}, bf16[32,16,128]{2,1,0:T(8,128)(2,1)S(1)}, u32[]{:S(2)}, u32[]{:S(2)}) collective-permute-start(bf16[32,16,128]{2,1,0:T(8,128)(2,1)S(1)} %all_to_all.15.refs_4_), channel_id=1, source_target_pairs={{0,128},{64,192},{128,0},{192,64},{1,129},{65,193},{129,1},{193,65... | collective-permute-start | bytes 393224 | tf_op jit(solution)/shard_map/ppermute | solution.py:195
  56.9 2.4 %collective-permute-done.6.refs_7_.refs_6_ = bf16[32,16,128]{2,1,0:T(8,128)(2,1)S(1)} collective-permute-done((bf16[32,16,128]{2,1,0:T(8,128)(2,1)S(1)}, bf16[32,16,128]{2,1,0:T(8,128)(2,1)S(1)}, u32[]{:S(2)}, u32[]{:S(2)}) %collective-permute-start.6) | collective-permute-done | bytes 131104 | tf_op jit(solution)/shard_map/ppermute | solution.py:195
  59.3 2.0 %collective-permute-done.5.refs_6_.refs_5_ = bf16[32,16,128]{2,1,0:T(8,128)(2,1)S(1)} collective-permute-done((bf16[32,16,128]{2,1,0:T(8,128)(2,1)S(1)}, bf16[32,16,128]{2,1,0:T(8,128)(2,1)S(1)}, u32[]{:S(2)}, u32[]{:S(2)}) %collective-permute-start.5) | collective-permute-done | bytes 131104 | tf_op jit(solution)/shard_map/ppermute | solution.py:195
  61.3 1.3 %collective-permute-done.4.refs_5_.refs_4_ = bf16[32,16,128]{2,1,0:T(8,128)(2,1)S(1)} collective-permute-done((bf16[32,16,128]{2,1,0:T(8,128)(2,1)S(1)}, bf16[32,16,128]{2,1,0:T(8,128)(2,1)S(1)}, u32[]{:S(2)}, u32[]{:S(2)}) %collective-permute-start.4) | collective-permute-done | bytes 131104 | tf_op jit(solution)/shard_map/ppermute | solution.py:195
  62.7 2.6 %collective-permute-start.12 = (bf16[3,128,1024]{2,1,0:T(8,128)(2,1)S(1)}, bf16[3,128,1024]{2,1,0:T(8,128)(2,1)S(1)}, u32[]{:S(2)}, u32[]{:S(2)}) collective-permute-start(bf16[3,128,1024]{2,1,0:T(8,128)(2,1)S(1)} %shard_map.55), channel_id=1, source_target_pairs={{0,32},{32,0},{1,33},{33,1},{2,34},{34,2},{3,35},{35,3},{4,36},{36... | collective-permute-start | bytes 2359304 | tf_op jit(solution)/shard_map/ppermute | solution.py:170
  68.2 3.1 %collective-permute-start.10 = (bf16[128,1024]{1,0:T(8,128)(2,1)S(1)}, bf16[128,1024]{1,0:T(8,128)(2,1)S(1)}, u32[]{:S(2)}, u32[]{:S(2)}) collective-permute-start(bf16[128,1024]{1,0:T(8,128)(2,1)S(1)} %get-tuple-element.22), channel_id=1, source_target_pairs={{0,128},{64,192},{128,0},{192,64},{1,129},{65,193},{129,1},{193,65... | collective-permute-start | bytes 786440 | tf_op jit(solution)/shard_map/ppermute | solution.py:208
  71.3 4.7 %collective-permute-done.9.refs_1_.refs_8_ = bf16[128,1024]{1,0:T(8,128)(2,1)S(1)} collective-permute-done((bf16[128,1024]{1,0:T(8,128)(2,1)S(1)}, bf16[128,1024]{1,0:T(8,128)(2,1)S(1)}, u32[]{:S(2)}, u32[]{:S(2)}) %collective-permute-start.9) | collective-permute-done | bytes 262176 | tf_op jit(solution)/shard_map/ppermute | solution.py:208
  76.0 6.6 %collective-permute-start.11 = (bf16[128,1024]{1,0:T(8,128)(2,1)S(1)}, bf16[128,1024]{1,0:T(8,128)(2,1)S(1)}, u32[]{:S(2)}, u32[]{:S(2)}) collective-permute-start(bf16[128,1024]{1,0:T(8,128)(2,1)S(1)} %get-tuple-element.23), channel_id=1, source_target_pairs={{0,64},{64,128},{128,192},{192,0},{1,65},{65,129},{129,193},{193,1... | collective-permute-start | bytes 786440 | tf_op jit(solution)/shard_map/ppermute | solution.py:208
  82.7 3.9 %collective-permute-done.11.refs_3_.refs_10_ = bf16[128,1024]{1,0:T(8,128)(2,1)S(1)} collective-permute-done((bf16[128,1024]{1,0:T(8,128)(2,1)S(1)}, bf16[128,1024]{1,0:T(8,128)(2,1)S(1)}, u32[]{:S(2)}, u32[]{:S(2)}) %collective-permute-start.11) | collective-permute-done | bytes 262176 | tf_op jit(solution)/shard_map/ppermute | solution.py:208
  86.6 2.2 %shard_map.56 = bf16[4,512,128]{2,1,0:T(8,128)(2,1)} custom-call(bf16[192,1024]{1,0:T(8,128)(2,1)S(1)} %collective-permute-done.7.refs_3_.refs_8_.own_got, bf16[3,128,1024]{2,1,0:T(8,128)(2,1)S(1)} %collective-permute-done.12.jac_got, bf16[320,1024]{1,0:T(8,128)(2,1)S(1)} %get-tuple-element.15.refs_0_, ...), custom_call_target="tpu_custom_call" | custom-call | flops 1073741824 | bytes 2097152 | tf_op jit(solution)/shard_map/pallas_call | solution.py:27
  88.8 12.0 %all-to-all-start.2 = ((bf16[64,32,128]{2,1,0:T(8,128)(2,1)}), bf16[64,32,128]{2,1,0:T(8,128)(2,1)S(1)}, u32[]{:S(2)}, u32[]{:S(2)}) async-start(bf16[64,32,128]{2,1,0:T(8,128)(2,1)} %bitcast.1), calls=%async_computation.2 | async-start | bytes 1048576 | tf_op jit(solution)/shard_map/all_to_all | solution.py:153
  101.8 11.7 %all-to-all-done.2.got = bf16[64,32,128]{2,1,0:T(8,128)(2,1)S(1)} async-done(((bf16[64,32,128]{2,1,0:T(8,128)(2,1)}), bf16[64,32,128]{2,1,0:T(8,128)(2,1)S(1)}, u32[]{:S(2)}, u32[]{:S(2)}) %all-to-all-start.2) | async-done | bytes 524320 | tf_op jit(solution)/shard_map/all_to_all | solution.py:153
  (38 shorter events, 8.8 us)
Async XLA Ops:
  0.6 1.2 %copy-start = (bf16[128,4096]{1,0:T(8,128)(2,1)S(1)}, bf16[128,4096]{1,0:T(8,128)(2,1)}, u32[]{:S(2)}) copy-start(bf16[128,4096]{1,0:T(8,128)(2,1)} %jac.3) | copy-start | bytes 3145732
  1.9 11.1 %copy-start.1 = (bf16[128,4096]{1,0:T(8,128)(2,1)S(1)}, bf16[128,4096]{1,0:T(8,128)(2,1)}, u32[]{:S(2)}) copy-start(bf16[128,4096]{1,0:T(8,128)(2,1)} %jac.3) | copy-start | bytes 3145732
  2.9 10.1 %collective-permute-start = (bf16[64,4096]{1,0:T(8,128)(2,1)S(1)}, bf16[64,4096]{1,0:T(8,128)(2,1)S(1)}, u32[]{:S(2)}, u32[]{:S(2)}) collective-permute-start(bf16[64,4096]{1,0:T(8,128)(2,1)S(1)} %get-tuple-element.14), channel_id=1, source_target_pairs={{0,1},{1,0},{2,3},{3,2},{4,5},{5,4},{6,7},{7,6},{8,9},{9,8},{10,11... | collective-permute-start | bytes 1572872 | tf_op jit(solution)/shard_map/ppermute | solution.py:182
  3.0 20.4 %all-to-all-start = ((bf16[32,16,128]{2,1,0:T(8,128)(2,1)}), bf16[32,16,128]{2,1,0:T(8,128)(2,1)S(1)}, u32[]{:S(2)}, u32[]{:S(2)}) async-start(bf16[32,16,128]{2,1,0:T(8,128)(2,1)} %get-tuple-element.19), calls=%async_computation | async-start | bytes 262144 | tf_op jit(solution)/shard_map/all_to_all | solution.py:153
  13.0 1.2 %copy-start.4 = (bf16[128,4096]{1,0:T(8,128)(2,1)S(1)}, bf16[128,4096]{1,0:T(8,128)(2,1)}, u32[]{:S(2)}) copy-start(bf16[128,4096]{1,0:T(8,128)(2,1)} %carry.1) | copy-start | bytes 3145732
  14.2 1.0 copy-start.5
  16.8 24.2 %collective-permute-start.1 = (bf16[320,1024]{1,0:T(8,128)(2,1)}, bf16[320,1024]{1,0:T(8,128)(2,1)S(1)}, u32[]{:S(2)}, u32[]{:S(2)}) collective-permute-start(bf16[320,1024]{1,0:T(8,128)(2,1)} %get-tuple-element.16), channel_id=1, source_target_pairs={{0,64},{64,128},{128,192},{192,0},{1,65},{65,129},{129,193},{193,1... | collective-permute-start | bytes 1966088 | tf_op jit(solution)/shard_map/ppermute | solution.py:194
  18.1 30.0 %collective-permute-start.2 = (bf16[320,1024]{1,0:T(8,128)(2,1)}, bf16[320,1024]{1,0:T(8,128)(2,1)S(1)}, u32[]{:S(2)}, u32[]{:S(2)}) collective-permute-start(bf16[320,1024]{1,0:T(8,128)(2,1)} %get-tuple-element.17), channel_id=1, source_target_pairs={{0,128},{64,192},{128,0},{192,64},{1,129},{65,193},{129,1},{193,65... | collective-permute-start | bytes 1966088 | tf_op jit(solution)/shard_map/ppermute | solution.py:194
  18.9 31.0 %collective-permute-start.3 = (bf16[320,1024]{1,0:T(8,128)(2,1)}, bf16[320,1024]{1,0:T(8,128)(2,1)S(1)}, u32[]{:S(2)}, u32[]{:S(2)}) collective-permute-start(bf16[320,1024]{1,0:T(8,128)(2,1)} %get-tuple-element.18), channel_id=1, source_target_pairs={{0,192},{64,0},{128,64},{192,128},{1,193},{65,1},{129,65},{193,129... | collective-permute-start | bytes 1966088 | tf_op jit(solution)/shard_map/ppermute | solution.py:194
  20.1 21.0 %collective-permute-start.7 = (bf16[192,1024]{1,0:T(8,128)(2,1)S(1)}, bf16[192,1024]{1,0:T(8,128)(2,1)S(1)}, u32[]{:S(2)}, u32[]{:S(2)}) collective-permute-start(bf16[192,1024]{1,0:T(8,128)(2,1)S(1)} %slice.7), channel_id=1, source_target_pairs={{0,32},{32,0},{1,33},{33,1},{2,34},{34,2},{3,35},{35,3},{4,36},{36... | collective-permute-start | bytes 1179656 | tf_op jit(solution)/shard_map/ppermute | solution.py:193
  50.4 12.2 %collective-permute-start.8 = (bf16[3,64,1024]{2,1,0:T(8,128)(2,1)S(1)}, bf16[3,64,1024]{2,1,0:T(8,128)(2,1)S(1)}, u32[]{:S(2)}, u32[]{:S(2)}) collective-permute-start(bf16[3,64,1024]{2,1,0:T(8,128)(2,1)S(1)} %shard_map.52), channel_id=1, source_target_pairs={{0,32},{32,0},{1,33},{33,1},{2,34},{34,2},{3,35},{35,3},{4,36},{36... | collective-permute-start | bytes 1179656 | tf_op jit(solution)/shard_map/ppermute | solution.py:170
  53.4 5.9 %collective-permute-start.6 = (bf16[32,16,128]{2,1,0:T(8,128)(2,1)S(1)}, bf16[32,16,128]{2,1,0:T(8,128)(2,1)S(1)}, u32[]{:S(2)}, u32[]{:S(2)}) collective-permute-start(bf16[32,16,128]{2,1,0:T(8,128)(2,1)S(1)} %all_to_all.15.refs_4_), channel_id=1, source_target_pairs={{0,192},{64,0},{128,64},{192,128},{1,193},{65,1},{129,65},{193,129... | collective-permute-start | bytes 393224 | tf_op jit(solution)/shard_map/ppermute | solution.py:195
  54.1 7.2 %collective-permute-start.5 = (bf16[32,16,128]{2,1,0:T(8,128)(2,1)S(1)}, bf16[32,16,128]{2,1,0:T(8,128)(2,1)S(1)}, u32[]{:S(2)}, u32[]{:S(2)}) collective-permute-start(bf16[32,16,128]{2,1,0:T(8,128)(2,1)S(1)} %all_to_all.15.refs_4_), channel_id=1, source_target_pairs={{0,128},{64,192},{128,0},{192,64},{1,129},{65,193},{129,1},{193,65... | collective-permute-start | bytes 393224 | tf_op jit(solution)/shard_map/ppermute | solution.py:195
  56.5 6.1 %collective-permute-start.4 = (bf16[32,16,128]{2,1,0:T(8,128)(2,1)S(1)}, bf16[32,16,128]{2,1,0:T(8,128)(2,1)S(1)}, u32[]{:S(2)}, u32[]{:S(2)}) collective-permute-start(bf16[32,16,128]{2,1,0:T(8,128)(2,1)S(1)} %all_to_all.15.refs_4_), channel_id=1, source_target_pairs={{0,64},{64,128},{128,192},{192,0},{1,65},{65,129},{129,193},{193,1... | collective-permute-start | bytes 393224 | tf_op jit(solution)/shard_map/ppermute | solution.py:195
  62.7 23.9 %collective-permute-start.12 = (bf16[3,128,1024]{2,1,0:T(8,128)(2,1)S(1)}, bf16[3,128,1024]{2,1,0:T(8,128)(2,1)S(1)}, u32[]{:S(2)}, u32[]{:S(2)}) collective-permute-start(bf16[3,128,1024]{2,1,0:T(8,128)(2,1)S(1)} %shard_map.55), channel_id=1, source_target_pairs={{0,32},{32,0},{1,33},{33,1},{2,34},{34,2},{3,35},{35,3},{4,36},{36... | collective-permute-start | bytes 2359304 | tf_op jit(solution)/shard_map/ppermute | solution.py:170
  66.8 9.2 %collective-permute-start.9 = (bf16[128,1024]{1,0:T(8,128)(2,1)S(1)}, bf16[128,1024]{1,0:T(8,128)(2,1)S(1)}, u32[]{:S(2)}, u32[]{:S(2)}) collective-permute-start(bf16[128,1024]{1,0:T(8,128)(2,1)S(1)} %get-tuple-element.21), channel_id=1, source_target_pairs={{0,192},{64,0},{128,64},{192,128},{1,193},{65,1},{129,65},{193,129... | collective-permute-start | bytes 786440 | tf_op jit(solution)/shard_map/ppermute | solution.py:208
  67.7 18.9 %collective-permute-start.13 = (bf16[256,1024]{1,0:T(8,128)(2,1)S(1)}, bf16[256,1024]{1,0:T(8,128)(2,1)S(1)}, u32[]{:S(2)}, u32[]{:S(2)}) collective-permute-start(bf16[256,1024]{1,0:T(8,128)(2,1)S(1)} %get-tuple-element.24.refs_4_), channel_id=1, source_target_pairs={{0,1},{1,0},{2,3},{3,2},{4,5},{5,4},{6,7},{7,6},{8,9},{9,8},{10,11... | collective-permute-start | bytes 1572872 | tf_op jit(solution)/shard_map/ppermute | solution.py:209
  67.7 18.9 %collective-permute-start.14 = (bf16[256,1024]{1,0:T(8,128)(2,1)S(1)}, bf16[256,1024]{1,0:T(8,128)(2,1)S(1)}, u32[]{:S(2)}, u32[]{:S(2)}) collective-permute-start(bf16[256,1024]{1,0:T(8,128)(2,1)S(1)} %get-tuple-element.25.refs_5_), channel_id=1, source_target_pairs={{0,1},{1,0},{2,3},{3,2},{4,5},{5,4},{6,7},{7,6},{8,9},{9,8},{10,11... | collective-permute-start | bytes 1572872 | tf_op jit(solution)/shard_map/ppermute | solution.py:209
  68.2 14.5 %collective-permute-start.10 = (bf16[128,1024]{1,0:T(8,128)(2,1)S(1)}, bf16[128,1024]{1,0:T(8,128)(2,1)S(1)}, u32[]{:S(2)}, u32[]{:S(2)}) collective-permute-start(bf16[128,1024]{1,0:T(8,128)(2,1)S(1)} %get-tuple-element.22), channel_id=1, source_target_pairs={{0,128},{64,192},{128,0},{192,64},{1,129},{65,193},{129,1},{193,65... | collective-permute-start | bytes 786440 | tf_op jit(solution)/shard_map/ppermute | solution.py:208
  76.0 10.5 %collective-permute-start.11 = (bf16[128,1024]{1,0:T(8,128)(2,1)S(1)}, bf16[128,1024]{1,0:T(8,128)(2,1)S(1)}, u32[]{:S(2)}, u32[]{:S(2)}) collective-permute-start(bf16[128,1024]{1,0:T(8,128)(2,1)S(1)} %get-tuple-element.23), channel_id=1, source_target_pairs={{0,64},{64,128},{128,192},{192,0},{1,65},{65,129},{129,193},{193,1... | collective-permute-start | bytes 786440 | tf_op jit(solution)/shard_map/ppermute | solution.py:208
  86.5 2.2 %copy-start.2 = (bf16[128,1024]{1,0:T(8,128)(2,1)}, bf16[128,1024]{1,0:T(8,128)(2,1)S(1)}, u32[]{:S(2)}) copy-start(bf16[128,1024]{1,0:T(8,128)(2,1)S(1)} %collective-permute-done.11.refs_3_.refs_10_) | copy-start | bytes 786436
  88.8 12.0 %copy-start.3 = (bf16[128,1024]{1,0:T(8,128)(2,1)S(1)}, bf16[128,1024]{1,0:T(8,128)(2,1)}, u32[]{:S(2)}) copy-start(bf16[128,1024]{1,0:T(8,128)(2,1)} %copy-done.2) | copy-start | bytes 786436
  88.8 12.0 %copy-start.7 = (bf16[128,1024]{1,0:T(8,128)(2,1)S(1)}, bf16[128,1024]{1,0:T(8,128)(2,1)}, u32[]{:S(2)}) copy-start(bf16[128,1024]{1,0:T(8,128)(2,1)} %copy-done.6) | copy-start | bytes 786436
  88.8 24.7 %all-to-all-start.2 = ((bf16[64,32,128]{2,1,0:T(8,128)(2,1)}), bf16[64,32,128]{2,1,0:T(8,128)(2,1)S(1)}, u32[]{:S(2)}, u32[]{:S(2)}) async-start(bf16[64,32,128]{2,1,0:T(8,128)(2,1)} %bitcast.1), calls=%async_computation.2 | async-start | bytes 1048576 | tf_op jit(solution)/shard_map/all_to_all | solution.py:153
  (1 other events, 0.7 us)

commit v8 on v7

--- a/solution.py
+++ b/solution.py
@@ -65,7 +65,7 @@
     return pl.ds(pl.multiple_of(at * 1024, 1024), 1024)
 
 
-def pack_kernel(jac, got, cov, carry, *refs):
+def pack_kernel(jac, got, cov, *refs):
     outs, sems = refs[:X], refs[X]
     core = lax.axis_index("c")
     copies = []
@@ -73,8 +73,11 @@
         copies += [(jac.at[slab(n, core), part(d)], outs[d].at[pl.ds(n * 32, 32), :]) for n in range(2)]
         copies.append((got.at[:, part(d)], outs[d].at[pl.ds(64, 64), :]))
         copies.append((cov.at[:, part(d)], outs[d].at[pl.ds(128, 64), :]))
-        copies.append((carry.at[:, part(d)], outs[d].at[pl.ds(192, 128), :]))
     run_copies(copies, sems)
+
+
+def carry_kernel(carry, *refs):
+    run_copies([(carry.at[:, part(d)], refs[d]) for d in range(X)], refs[X])
 
 
 def join_kernel(first_row, rows, *refs):
@@ -85,8 +88,8 @@
 
 
 def sens_kernel(*refs):
-    first, panels, (own_got, cov_got) = refs[:4], refs[4:8], refs[8:10]
-    outs, pairs, cov, panel = refs[10:14], refs[14:16], refs[16], refs[17]
+    first, carry, panels, (own_got, cov_got) = refs[:4], refs[4:8], refs[8:12], refs[12:14]
+    outs, pairs, cov, panel = refs[14:18], refs[18:20], refs[20], refs[21]
     h = lax.axis_index("h")
 
     def rows(d, side):
@@ -104,7 +107,7 @@
         product = jnp.dot(
             panel[d * 128 : (d + 1) * 128, :], cov[...], preferred_element_type=F32
         )
-        value = first[d][192:320, :].astype(F32) + product * (1.0 / math.sqrt(WIDTH))
+        value = carry[d][...].astype(F32) + product * (1.0 / math.sqrt(WIDTH))
         value = value.astype(BF16)
         outs[d][...] = value
         pairs[d // 2][d % 2 * 128 : d % 2 * 128 + 128, :] = value
@@ -157,8 +160,8 @@
     return [pltpu.SemaphoreType.DMA((n,))]
 
 
-def swap_rest(first, first_row, rows, behind):
-    joined = call(
+def join(first, first_row, rows, behind):
+    return call(
         functools.partial(join_kernel, first_row, rows),
         shape(X - 1, rows, 1024),
         first[1:],
@@ -167,8 +170,6 @@
         nbytes=2 * MIB,
         behind=behind,
     )
-    return lax.ppermute(joined, "h", SWAP)
-
 
 def body(jacobian, cov_rows, sens_carry):
     give, panel = call(
@@ -184,21 +185,27 @@
     panel = over(jnp.broadcast_to(mine, (32, 16, 128)), ("l", "z", "c"))
     packed = call(
         pack_kernel,
-        [shape(320, 1024)] * X,
-        (jacobian, got, cov_rows, sens_carry),
+        [shape(192, 1024)] * X,
+        (jacobian, got, cov_rows),
         ANY,
-        dma(5 * X),
-        nbytes=5 * MIB,
-    )
-    own_got = lax.ppermute(packed[0][:192], "h", SWAP)
+        dma(4 * X),
+        nbytes=4 * MIB,
+    )
+    own_got = lax.ppermute(packed[0], "h", SWAP)
     first = [packed[0]] + [lax.ppermute(packed[d], "x", ring(d)) for d in range(1, X)]
     panels = [panel] + [lax.ppermute(panel, "x", ring(d)) for d in range(1, X)]
-    cov_got = swap_rest(first, 128, 64, (own_got, panel))
-    jac_got = swap_rest(first, 0, 128, (cov_got, *panels[1:]))
+    packed = call(
+        carry_kernel, [shape(128, 1024)] * X, (sens_carry,), ANY, dma(X), nbytes=2 * MIB
+    )
+    carry = [packed[0]] + [lax.ppermute(packed[d], "x", ring(d)) for d in range(1, X)]
+    cov_rest = join(first, 128, 64, (own_got, panel))
+    jac_rest = join(first, 0, 128, (cov_rest,))
+    cov_got = lax.ppermute(cov_rest, "h", SWAP)
+    jac_got = lax.ppermute(jac_rest, "h", SWAP)
     *sens, low, high = call(
         sens_kernel,
         [shape(128, 1024)] * X + [shape(256, 1024)] * 2,
-        (*first, *panels, own_got, cov_got),
+        (*first, *carry, *panels, own_got, cov_got),
         VMEM,
         [pltpu.VMEM((512, 1024), BF16), pltpu.VMEM((512, WIDTH), BF16)],
         flops=2 * 512 * 512 * 1024,
@@ -216,7 +223,6 @@
         flops=2 * 512 * 512 * 2048,
         nbytes=2 * MIB,
         vmem=16,
-        behind=sens_back[1:],
     )
     shared = over(parts.reshape(X * L * Z, 32, 128), ("x", "l", "z"))
     innovation = call(final_kernel, shape(32, 128, kind=F32), (shared,), VMEM, nbytes=2**19, vmem=4)

time: 116 us -> 107 us (0.922)
  the two profiles are of different devices: /device:TPU:4 before, /device:TPU:1 now
where the time goes in v8:
time: 107 us; the launch traced here: 106 us
  starting transfers between devices  49.1 us (46%)
  waiting for transfers between devices  41.4 us (39%)
  Pallas kernels  8.57 us (8%)
  local copies, waits for them, and re-layouts  6.18 us (6%)
    all_to_all x3, starting transfers between devices, over(): return lax.all_to_all(value, axes, split_axis=0, concat_axis=0, tiled=True)  24.3 us
    ppermute x3, waiting for transfers between devices, body(): lax.ppermute(sens[d], 'x', ring(-d))  18.7 us
    ppermute x1, waiting for transfers between devices, body(): jac_got = lax.ppermute(jac_rest, 'h', SWAP)  9.51 us
    pallas_call x9, Pallas kernels, call(): pl.pallas_call(kernel, out_shape=outs, in_specs=[spec] * len(ins) + [ANY]...  8.57 us
    ppermute x6, starting transfers between devices, body(): lax.ppermute(packed[d], 'x', ring(d))  5.88 us
    unnamed x24, local copies, waits for them, and re-layouts  5.51 us
    ppermute x6, waiting for transfers between devices, body(): lax.ppermute(packed[d], 'x', ring(d))  4.89 us
    all_to_all x3, waiting for transfers between devices, over(): return lax.all_to_all(value, axes, split_axis=0, concat_axis=0, tiled=True)  4.69 us
  transfers between devices with their start and end apart: 21, of which 9 were waited for; matrix products, arithmetic and copies ran while one was open for 1% of the time, Pallas kernels for 4%

profile of v8, /device:TPU:1, one launch (start us, length us, event | category | flops | bytes accessed | tf_op | source)
XLA Modules:
  0.0 106.1 jit_solution(4192817859884390141)
XLA Ops:
  0.6 1.2 %copy-done = bf16[128,4096]{1,0:T(8,128)(2,1)S(1)} copy-done((bf16[128,4096]{1,0:T(8,128)(2,1)S(1)}, bf16[128,4096]{1,0:T(8,128)(2,1)}, u32[]{:S(2)}) %copy-start) | copy-done | bytes 1048600
  2.9 3.3 %collective-permute-start = (bf16[64,4096]{1,0:T(8,128)(2,1)S(1)}, bf16[64,4096]{1,0:T(8,128)(2,1)S(1)}, u32[]{:S(2)}, u32[]{:S(2)}) collective-permute-start(bf16[64,4096]{1,0:T(8,128)(2,1)S(1)} %get-tuple-element.18), channel_id=1, source_target_pairs={{0,1},{1,0},{2,3},{3,2},{4,5},{5,4},{6,7},{7,6},{8,9},{9,8},{10,11... | collective-permute-start | bytes 1572872 | tf_op jit(solution)/shard_map/ppermute | solution.py:183
  6.2 8.0 %all-to-all-start = ((bf16[32,16,128]{2,1,0:T(8,128)(2,1)}), bf16[32,16,128]{2,1,0:T(8,128)(2,1)S(1)}, u32[]{:S(2)}, u32[]{:S(2)}) async-start(bf16[32,16,128]{2,1,0:T(8,128)(2,1)} %get-tuple-element.27), calls=%async_computation | async-start | bytes 262144 | tf_op jit(solution)/shard_map/all_to_all | solution.py:156
  17.2 1.2 %shard_map.51 = (bf16[192,1024]{1,0:T(8,128)(2,1)S(1)}, bf16[192,1024]{1,0:T(8,128)(2,1)}, bf16[192,1024]{1,0:T(8,128)(2,1)}, bf16[192,1024]{1,0:T(8,128)(2,1)}) custom-call(bf16[128,4096]{1,0:T(8,128)(2,1)S(1)} %copy-done.1, bf16[64,4096]{1,0:T(8,128)(2,1)S(1)} %copy-done.5, bf16[64,4096]{1,0:T(8,128)(2,1)S(1)} %copy-done.3), custom_call_target="tpu_custom_call" | custom-call | bytes 4194304 | tf_op jit(solution)/shard_map/pallas_call | solution.py:27
  18.4 1.3 %collective-permute-start.1 = (bf16[192,1024]{1,0:T(8,128)(2,1)}, bf16[192,1024]{1,0:T(8,128)(2,1)S(1)}, u32[]{:S(2)}, u32[]{:S(2)}) collective-permute-start(bf16[192,1024]{1,0:T(8,128)(2,1)} %get-tuple-element.20), channel_id=1, source_target_pairs={{0,64},{64,128},{128,192},{192,0},{1,65},{65,129},{129,193},{193,1... | collective-permute-start | bytes 1179656 | tf_op jit(solution)/shard_map/ppermute | solution.py:195
  19.7 2.5 %collective-permute-start.2 = (bf16[192,1024]{1,0:T(8,128)(2,1)}, bf16[192,1024]{1,0:T(8,128)(2,1)S(1)}, u32[]{:S(2)}, u32[]{:S(2)}) collective-permute-start(bf16[192,1024]{1,0:T(8,128)(2,1)} %get-tuple-element.21), channel_id=1, source_target_pairs={{0,128},{64,192},{128,0},{192,64},{1,129},{65,193},{129,1},{193,65... | collective-permute-start | bytes 1179656 | tf_op jit(solution)/shard_map/ppermute | solution.py:195
  23.3 2.6 %collective-permute-start.10 = (bf16[192,1024]{1,0:T(8,128)(2,1)S(1)}, bf16[192,1024]{1,0:T(8,128)(2,1)S(1)}, u32[]{:S(2)}, u32[]{:S(2)}) collective-permute-start(bf16[192,1024]{1,0:T(8,128)(2,1)S(1)} %get-tuple-element.19.refs_0_), channel_id=1, source_target_pairs={{0,32},{32,0},{1,33},{33,1},{2,34},{34,2},{3,35},{35,3},{4,36},{36... | collective-permute-start | bytes 1179656 | tf_op jit(solution)/shard_map/ppermute | solution.py:194
  26.6 8.8 %all-to-all-start.1 = ((bf16[32,16,128]{2,1,0:T(8,128)(2,1)}), bf16[32,16,128]{2,1,0:T(8,128)(2,1)S(1)}, u32[]{:S(2)}, u32[]{:S(2)}) async-start(bf16[32,16,128]{2,1,0:T(8,128)(2,1)} %broadcast_in_dim.3), calls=%async_computation.1 | async-start | bytes 262144 | tf_op jit(solution)/shard_map/all_to_all | solution.py:156
  37.4 2.4 %collective-permute-done.2.refs_1_.refs_2_ = bf16[192,1024]{1,0:T(8,128)(2,1)S(1)} collective-permute-done((bf16[192,1024]{1,0:T(8,128)(2,1)}, bf16[192,1024]{1,0:T(8,128)(2,1)S(1)}, u32[]{:S(2)}, u32[]{:S(2)}) %collective-permute-start.2) | collective-permute-done | bytes 393248 | tf_op jit(solution)/shard_map/ppermute | solution.py:195
  39.8 4.7 %all-to-all-done.1.refs_4_.refs_8_ = bf16[32,16,128]{2,1,0:T(8,128)(2,1)S(1)} async-done(((bf16[32,16,128]{2,1,0:T(8,128)(2,1)}), bf16[32,16,128]{2,1,0:T(8,128)(2,1)S(1)}, u32[]{:S(2)}, u32[]{:S(2)}) %all-to-all-start.1) | async-done | bytes 131104 | tf_op jit(solution)/shard_map/all_to_all | solution.py:156
  45.0 1.6 %collective-permute-start.11 = (bf16[3,64,1024]{2,1,0:T(8,128)(2,1)S(1)}, bf16[3,64,1024]{2,1,0:T(8,128)(2,1)S(1)}, u32[]{:S(2)}, u32[]{:S(2)}) collective-permute-start(bf16[3,64,1024]{2,1,0:T(8,128)(2,1)S(1)} %shard_map.53.refs_3_), channel_id=1, source_target_pairs={{0,32},{32,0},{1,33},{33,1},{2,34},{34,2},{3,35},{35,3},{4,36},{36... | collective-permute-start | bytes 1179656 | tf_op jit(solution)/shard_map/ppermute | solution.py:203
  46.8 1.5 %collective-permute-start.15 = (bf16[3,128,1024]{2,1,0:T(8,128)(2,1)S(1)}, bf16[3,128,1024]{2,1,0:T(8,128)(2,1)S(1)}, u32[]{:S(2)}, u32[]{:S(2)}) collective-permute-start(bf16[3,128,1024]{2,1,0:T(8,128)(2,1)S(1)} %shard_map.56), channel_id=1, source_target_pairs={{0,32},{32,0},{1,33},{33,1},{2,34},{34,2},{3,35},{35,3},{4,36},{36... | collective-permute-start | bytes 2359304 | tf_op jit(solution)/shard_map/ppermute | solution.py:204
  48.6 2.5 %collective-permute-done.5.refs_6_ = bf16[128,1024]{1,0:T(8,128)(2,1)S(1)} collective-permute-done((bf16[128,1024]{1,0:T(8,128)(2,1)}, bf16[128,1024]{1,0:T(8,128)(2,1)S(1)}, u32[]{:S(2)}, u32[]{:S(2)}) %collective-permute-start.5) | collective-permute-done | bytes 262176 | tf_op jit(solution)/shard_map/ppermute | solution.py:200
  51.8 2.9 %collective-permute-start.9 = (bf16[32,16,128]{2,1,0:T(8,128)(2,1)S(1)}, bf16[32,16,128]{2,1,0:T(8,128)(2,1)S(1)}, u32[]{:S(2)}, u32[]{:S(2)}) collective-permute-start(bf16[32,16,128]{2,1,0:T(8,128)(2,1)S(1)} %all-to-all-done.1.refs_4_.refs_8_), channel_id=1, source_target_pairs={{0,192},{64,0},{128,64},{192,128},{1,193},{65,1},{129,65},{193,129... | collective-permute-start | bytes 393224 | tf_op jit(solution)/shard_map/ppermute | solution.py:196
  54.7 2.4 %collective-permute-done.8.refs_10_ = bf16[32,16,128]{2,1,0:T(8,128)(2,1)S(1)} collective-permute-done((bf16[32,16,128]{2,1,0:T(8,128)(2,1)S(1)}, bf16[32,16,128]{2,1,0:T(8,128)(2,1)S(1)}, u32[]{:S(2)}, u32[]{:S(2)}) %collective-permute-start.8) | collective-permute-done | bytes 131104 | tf_op jit(solution)/shard_map/ppermute | solution.py:196
  57.1 1.2 %collective-permute-done.9.refs_11_ = bf16[32,16,128]{2,1,0:T(8,128)(2,1)S(1)} collective-permute-done((bf16[32,16,128]{2,1,0:T(8,128)(2,1)S(1)}, bf16[32,16,128]{2,1,0:T(8,128)(2,1)S(1)}, u32[]{:S(2)}, u32[]{:S(2)}) %collective-permute-start.9) | collective-permute-done | bytes 131104 | tf_op jit(solution)/shard_map/ppermute | solution.py:196
  60.6 2.3 %collective-permute-start.16 = (bf16[256,1024]{1,0:T(8,128)(2,1)S(1)}, bf16[256,1024]{1,0:T(8,128)(2,1)S(1)}, u32[]{:S(2)}, u32[]{:S(2)}) collective-permute-start(bf16[256,1024]{1,0:T(8,128)(2,1)S(1)} %get-tuple-element.32.refs_4_), channel_id=1, source_target_pairs={{0,1},{1,0},{2,3},{3,2},{4,5},{5,4},{6,7},{7,6},{8,9},{9,8},{10,11... | collective-permute-start | bytes 1572872 | tf_op jit(solution)/shard_map/ppermute | solution.py:216
  62.9 9.5 %collective-permute-done.15.jac_got = bf16[3,128,1024]{2,1,0:T(8,128)(2,1)S(1)} collective-permute-done((bf16[3,128,1024]{2,1,0:T(8,128)(2,1)S(1)}, bf16[3,128,1024]{2,1,0:T(8,128)(2,1)S(1)}, u32[]{:S(2)}, u32[]{:S(2)}) %collective-permute-start.15) | collective-permute-done | bytes 786464 | tf_op jit(solution)/shard_map/ppermute | solution.py:204
  72.5 2.2 %shard_map.57 = bf16[4,512,128]{2,1,0:T(8,128)(2,1)} custom-call(bf16[192,1024]{1,0:T(8,128)(2,1)S(1)} %collective-permute-done.10.refs_3_.refs_12_.own_got, bf16[3,128,1024]{2,1,0:T(8,128)(2,1)S(1)} %collective-permute-done.15.jac_got, bf16[192,1024]{1,0:T(8,128)(2,1)S(1)} %get-tuple-element.19.refs_0_, ...), custom_call_target="tpu_custom_call" | custom-call | flops 1073741824 | bytes 2097152 | tf_op jit(solution)/shard_map/pallas_call | solution.py:27
  74.6 7.4 %all-to-all-start.2 = ((bf16[64,32,128]{2,1,0:T(8,128)(2,1)}), bf16[64,32,128]{2,1,0:T(8,128)(2,1)S(1)}, u32[]{:S(2)}, u32[]{:S(2)}) async-start(bf16[64,32,128]{2,1,0:T(8,128)(2,1)} %bitcast.1), calls=%async_computation.2 | async-start | bytes 1048576 | tf_op jit(solution)/shard_map/all_to_all | solution.py:156
  82.1 2.5 %collective-permute-start.12 = (bf16[128,1024]{1,0:T(8,128)(2,1)S(1)}, bf16[128,1024]{1,0:T(8,128)(2,1)S(1)}, u32[]{:S(2)}, u32[]{:S(2)}) collective-permute-start(bf16[128,1024]{1,0:T(8,128)(2,1)S(1)} %copy-done.11), channel_id=1, source_target_pairs={{0,192},{64,0},{128,64},{192,128},{1,193},{65,1},{129,65},{193,129... | collective-permute-start | bytes 786440 | tf_op jit(solution)/shard_map/ppermute | solution.py:215
  85.6 8.6 %collective-permute-done.12.refs_1_ = bf16[128,1024]{1,0:T(8,128)(2,1)S(1)} collective-permute-done((bf16[128,1024]{1,0:T(8,128)(2,1)S(1)}, bf16[128,1024]{1,0:T(8,128)(2,1)S(1)}, u32[]{:S(2)}, u32[]{:S(2)}) %collective-permute-start.12) | collective-permute-done | bytes 262176 | tf_op jit(solution)/shard_map/ppermute | solution.py:215
  94.2 2.4 %collective-permute-done.13.refs_2_ = bf16[128,1024]{1,0:T(8,128)(2,1)S(1)} collective-permute-done((bf16[128,1024]{1,0:T(8,128)(2,1)S(1)}, bf16[128,1024]{1,0:T(8,128)(2,1)S(1)}, u32[]{:S(2)}, u32[]{:S(2)}) %collective-permute-start.13) | collective-permute-done | bytes 262176 | tf_op jit(solution)/shard_map/ppermute | solution.py:215
  96.7 7.7 %collective-permute-done.14.refs_3_ = bf16[128,1024]{1,0:T(8,128)(2,1)S(1)} collective-permute-done((bf16[128,1024]{1,0:T(8,128)(2,1)S(1)}, bf16[128,1024]{1,0:T(8,128)(2,1)S(1)}, u32[]{:S(2)}, u32[]{:S(2)}) %collective-permute-start.14) | collective-permute-done | bytes 262176 | tf_op jit(solution)/shard_map/ppermute | solution.py:215
  (53 shorter events, 14.4 us)
Async XLA Ops:
  1.9 13.2 %copy-start.1 = (bf16[128,4096]{1,0:T(8,128)(2,1)S(1)}, bf16[128,4096]{1,0:T(8,128)(2,1)}, u32[]{:S(2)}) copy-start(bf16[128,4096]{1,0:T(8,128)(2,1)} %jac.3) | copy-start | bytes 3145732
  2.9 11.4 %collective-permute-start = (bf16[64,4096]{1,0:T(8,128)(2,1)S(1)}, bf16[64,4096]{1,0:T(8,128)(2,1)S(1)}, u32[]{:S(2)}, u32[]{:S(2)}) collective-permute-start(bf16[64,4096]{1,0:T(8,128)(2,1)S(1)} %get-tuple-element.18), channel_id=1, source_target_pairs={{0,1},{1,0},{2,3},{3,2},{4,5},{5,4},{6,7},{7,6},{8,9},{9,8},{10,11... | collective-permute-start | bytes 1572872 | tf_op jit(solution)/shard_map/ppermute | solution.py:183
  6.2 19.7 %all-to-all-start = ((bf16[32,16,128]{2,1,0:T(8,128)(2,1)}), bf16[32,16,128]{2,1,0:T(8,128)(2,1)S(1)}, u32[]{:S(2)}, u32[]{:S(2)}) async-start(bf16[32,16,128]{2,1,0:T(8,128)(2,1)} %get-tuple-element.27), calls=%async_computation | async-start | bytes 262144 | tf_op jit(solution)/shard_map/all_to_all | solution.py:156
  14.3 21.2 %copy-start.2 = (bf16[128,4096]{1,0:T(8,128)(2,1)S(1)}, bf16[128,4096]{1,0:T(8,128)(2,1)}, u32[]{:S(2)}) copy-start(bf16[128,4096]{1,0:T(8,128)(2,1)} %carry.1) | copy-start | bytes 3145732
  18.4 18.4 %collective-permute-start.1 = (bf16[192,1024]{1,0:T(8,128)(2,1)}, bf16[192,1024]{1,0:T(8,128)(2,1)S(1)}, u32[]{:S(2)}, u32[]{:S(2)}) collective-permute-start(bf16[192,1024]{1,0:T(8,128)(2,1)} %get-tuple-element.20), channel_id=1, source_target_pairs={{0,64},{64,128},{128,192},{192,0},{1,65},{65,129},{129,193},{193,1... | collective-permute-start | bytes 1179656 | tf_op jit(solution)/shard_map/ppermute | solution.py:195
  19.7 20.1 %collective-permute-start.2 = (bf16[192,1024]{1,0:T(8,128)(2,1)}, bf16[192,1024]{1,0:T(8,128)(2,1)S(1)}, u32[]{:S(2)}, u32[]{:S(2)}) collective-permute-start(bf16[192,1024]{1,0:T(8,128)(2,1)} %get-tuple-element.21), channel_id=1, source_target_pairs={{0,128},{64,192},{128,0},{192,64},{1,129},{65,193},{129,1},{193,65... | collective-permute-start | bytes 1179656 | tf_op jit(solution)/shard_map/ppermute | solution.py:195
  22.1 22.3 %collective-permute-start.3 = (bf16[192,1024]{1,0:T(8,128)(2,1)}, bf16[192,1024]{1,0:T(8,128)(2,1)S(1)}, u32[]{:S(2)}, u32[]{:S(2)}) collective-permute-start(bf16[192,1024]{1,0:T(8,128)(2,1)} %get-tuple-element.22), channel_id=1, source_target_pairs={{0,192},{64,0},{128,64},{192,128},{1,193},{65,1},{129,65},{193,129... | collective-permute-start | bytes 1179656 | tf_op jit(solution)/shard_map/ppermute | solution.py:195
  23.3 21.2 %collective-permute-start.10 = (bf16[192,1024]{1,0:T(8,128)(2,1)S(1)}, bf16[192,1024]{1,0:T(8,128)(2,1)S(1)}, u32[]{:S(2)}, u32[]{:S(2)}) collective-permute-start(bf16[192,1024]{1,0:T(8,128)(2,1)S(1)} %get-tuple-element.19.refs_0_), channel_id=1, source_target_pairs={{0,32},{32,0},{1,33},{33,1},{2,34},{34,2},{3,35},{35,3},{4,36},{36... | collective-permute-start | bytes 1179656 | tf_op jit(solution)/shard_map/ppermute | solution.py:194
  26.6 17.9 %all-to-all-start.1 = ((bf16[32,16,128]{2,1,0:T(8,128)(2,1)}), bf16[32,16,128]{2,1,0:T(8,128)(2,1)S(1)}, u32[]{:S(2)}, u32[]{:S(2)}) async-start(bf16[32,16,128]{2,1,0:T(8,128)(2,1)} %broadcast_in_dim.3), calls=%async_computation.1 | async-start | bytes 262144 | tf_op jit(solution)/shard_map/all_to_all | solution.py:156
  36.4 11.8 %collective-permute-start.4 = (bf16[128,1024]{1,0:T(8,128)(2,1)}, bf16[128,1024]{1,0:T(8,128)(2,1)S(1)}, u32[]{:S(2)}, u32[]{:S(2)}) collective-permute-start(bf16[128,1024]{1,0:T(8,128)(2,1)} %get-tuple-element.24), channel_id=1, source_target_pairs={{0,64},{64,128},{128,192},{192,0},{1,65},{65,129},{129,193},{193,1... | collective-permute-start | bytes 786440 | tf_op jit(solution)/shard_map/ppermute | solution.py:200
  36.8 14.3 %collective-permute-start.5 = (bf16[128,1024]{1,0:T(8,128)(2,1)}, bf16[128,1024]{1,0:T(8,128)(2,1)S(1)}, u32[]{:S(2)}, u32[]{:S(2)}) collective-permute-start(bf16[128,1024]{1,0:T(8,128)(2,1)} %get-tuple-element.25), channel_id=1, source_target_pairs={{0,128},{64,192},{128,0},{192,64},{1,129},{65,193},{129,1},{193,65... | collective-permute-start | bytes 786440 | tf_op jit(solution)/shard_map/ppermute | solution.py:200
  39.8 12.0 %collective-permute-start.6 = (bf16[128,1024]{1,0:T(8,128)(2,1)}, bf16[128,1024]{1,0:T(8,128)(2,1)S(1)}, u32[]{:S(2)}, u32[]{:S(2)}) collective-permute-start(bf16[128,1024]{1,0:T(8,128)(2,1)} %get-tuple-element.26), channel_id=1, source_target_pairs={{0,192},{64,0},{128,64},{192,128},{1,193},{65,1},{129,65},{193,129... | collective-permute-start | bytes 786440 | tf_op jit(solution)/shard_map/ppermute | solution.py:200
  45.0 13.3 %collective-permute-start.11 = (bf16[3,64,1024]{2,1,0:T(8,128)(2,1)S(1)}, bf16[3,64,1024]{2,1,0:T(8,128)(2,1)S(1)}, u32[]{:S(2)}, u32[]{:S(2)}) collective-permute-start(bf16[3,64,1024]{2,1,0:T(8,128)(2,1)S(1)} %shard_map.53.refs_3_), channel_id=1, source_target_pairs={{0,32},{32,0},{1,33},{33,1},{2,34},{34,2},{3,35},{35,3},{4,36},{36... | collective-permute-start | bytes 1179656 | tf_op jit(solution)/shard_map/ppermute | solution.py:203
  46.8 25.7 %collective-permute-start.15 = (bf16[3,128,1024]{2,1,0:T(8,128)(2,1)S(1)}, bf16[3,128,1024]{2,1,0:T(8,128)(2,1)S(1)}, u32[]{:S(2)}, u32[]{:S(2)}) collective-permute-start(bf16[3,128,1024]{2,1,0:T(8,128)(2,1)S(1)} %shard_map.56), channel_id=1, source_target_pairs={{0,32},{32,0},{1,33},{33,1},{2,34},{34,2},{3,35},{35,3},{4,36},{36... | collective-permute-start | bytes 2359304 | tf_op jit(solution)/shard_map/ppermute | solution.py:204
  48.3 6.5 %collective-permute-start.7 = (bf16[32,16,128]{2,1,0:T(8,128)(2,1)S(1)}, bf16[32,16,128]{2,1,0:T(8,128)(2,1)S(1)}, u32[]{:S(2)}, u32[]{:S(2)}) collective-permute-start(bf16[32,16,128]{2,1,0:T(8,128)(2,1)S(1)} %all-to-all-done.1.refs_4_.refs_8_), channel_id=1, source_target_pairs={{0,64},{64,128},{128,192},{192,0},{1,65},{65,129},{129,193},{193,1... | collective-permute-start | bytes 393224 | tf_op jit(solution)/shard_map/ppermute | solution.py:196
  51.1 6.1 %collective-permute-start.8 = (bf16[32,16,128]{2,1,0:T(8,128)(2,1)S(1)}, bf16[32,16,128]{2,1,0:T(8,128)(2,1)S(1)}, u32[]{:S(2)}, u32[]{:S(2)}) collective-permute-start(bf16[32,16,128]{2,1,0:T(8,128)(2,1)S(1)} %all-to-all-done.1.refs_4_.refs_8_), channel_id=1, source_target_pairs={{0,128},{64,192},{128,0},{192,64},{1,129},{65,193},{129,1},{193,65... | collective-permute-start | bytes 393224 | tf_op jit(solution)/shard_map/ppermute | solution.py:196
  51.8 6.5 %collective-permute-start.9 = (bf16[32,16,128]{2,1,0:T(8,128)(2,1)S(1)}, bf16[32,16,128]{2,1,0:T(8,128)(2,1)S(1)}, u32[]{:S(2)}, u32[]{:S(2)}) collective-permute-start(bf16[32,16,128]{2,1,0:T(8,128)(2,1)S(1)} %all-to-all-done.1.refs_4_.refs_8_), channel_id=1, source_target_pairs={{0,192},{64,0},{128,64},{192,128},{1,193},{65,1},{129,65},{193,129... | collective-permute-start | bytes 393224 | tf_op jit(solution)/shard_map/ppermute | solution.py:196
  60.6 14.0 %copy-start.6 = (bf16[128,1024]{1,0:T(8,128)(2,1)}, bf16[128,1024]{1,0:T(8,128)(2,1)S(1)}, u32[]{:S(2)}) copy-start(bf16[128,1024]{1,0:T(8,128)(2,1)S(1)} %get-tuple-element.31) | copy-start | bytes 786436
  60.6 11.9 %collective-permute-start.16 = (bf16[256,1024]{1,0:T(8,128)(2,1)S(1)}, bf16[256,1024]{1,0:T(8,128)(2,1)S(1)}, u32[]{:S(2)}, u32[]{:S(2)}) collective-permute-start(bf16[256,1024]{1,0:T(8,128)(2,1)S(1)} %get-tuple-element.32.refs_4_), channel_id=1, source_target_pairs={{0,1},{1,0},{2,3},{3,2},{4,5},{5,4},{6,7},{7,6},{8,9},{9,8},{10,11... | collective-permute-start | bytes 1572872 | tf_op jit(solution)/shard_map/ppermute | solution.py:216
  62.9 9.5 %collective-permute-start.17 = (bf16[256,1024]{1,0:T(8,128)(2,1)S(1)}, bf16[256,1024]{1,0:T(8,128)(2,1)S(1)}, u32[]{:S(2)}, u32[]{:S(2)}) collective-permute-start(bf16[256,1024]{1,0:T(8,128)(2,1)S(1)} %get-tuple-element.33.refs_5_), channel_id=1, source_target_pairs={{0,1},{1,0},{2,3},{3,2},{4,5},{5,4},{6,7},{7,6},{8,9},{9,8},{10,11... | collective-permute-start | bytes 1572872 | tf_op jit(solution)/shard_map/ppermute | solution.py:216
  74.6 30.8 %all-to-all-start.2 = ((bf16[64,32,128]{2,1,0:T(8,128)(2,1)}), bf16[64,32,128]{2,1,0:T(8,128)(2,1)S(1)}, u32[]{:S(2)}, u32[]{:S(2)}) async-start(bf16[64,32,128]{2,1,0:T(8,128)(2,1)} %bitcast.1), calls=%async_computation.2 | async-start | bytes 1048576 | tf_op jit(solution)/shard_map/all_to_all | solution.py:156
  82.1 12.2 %collective-permute-start.12 = (bf16[128,1024]{1,0:T(8,128)(2,1)S(1)}, bf16[128,1024]{1,0:T(8,128)(2,1)S(1)}, u32[]{:S(2)}, u32[]{:S(2)}) collective-permute-start(bf16[128,1024]{1,0:T(8,128)(2,1)S(1)} %copy-done.11), channel_id=1, source_target_pairs={{0,192},{64,0},{128,64},{192,128},{1,193},{65,1},{129,65},{193,129... | collective-permute-start | bytes 786440 | tf_op jit(solution)/shard_map/ppermute | solution.py:215
  84.6 12.1 %collective-permute-start.13 = (bf16[128,1024]{1,0:T(8,128)(2,1)S(1)}, bf16[128,1024]{1,0:T(8,128)(2,1)S(1)}, u32[]{:S(2)}, u32[]{:S(2)}) collective-permute-start(bf16[128,1024]{1,0:T(8,128)(2,1)S(1)} %copy-done.9), channel_id=1, source_target_pairs={{0,128},{64,192},{128,0},{192,64},{1,129},{65,193},{129,1},{193,65... | collective-permute-start | bytes 786440 | tf_op jit(solution)/shard_map/ppermute | solution.py:215
  85.0 19.4 %collective-permute-start.14 = (bf16[128,1024]{1,0:T(8,128)(2,1)S(1)}, bf16[128,1024]{1,0:T(8,128)(2,1)S(1)}, u32[]{:S(2)}, u32[]{:S(2)}) collective-permute-start(bf16[128,1024]{1,0:T(8,128)(2,1)S(1)} %copy-done.7), channel_id=1, source_target_pairs={{0,64},{64,128},{128,192},{192,0},{1,65},{65,129},{129,193},{193,1... | collective-permute-start | bytes 786440 | tf_op jit(solution)/shard_map/ppermute | solution.py:215
  (9 other events, 33.3 us)

commit v9 on v8

--- a/solution.py
+++ b/solution.py
@@ -179,6 +179,7 @@
         ANY,
         dma(34),
         nbytes=MIB,
+        vmem=60,
     )
     got = lax.ppermute(give, "c", SWAP)
     mine = over(panel, ("l", "z", "c"))[0]
@@ -190,6 +191,7 @@
         ANY,
         dma(4 * X),
         nbytes=4 * MIB,
+        vmem=60,
     )
     own_got = lax.ppermute(packed[0], "h", SWAP)
     first = [packed[0]] + [lax.ppermute(packed[d], "x", ring(d)) for d in range(1, X)]
@@ -223,6 +225,7 @@
         flops=2 * 512 * 512 * 2048,
         nbytes=2 * MIB,
         vmem=16,
+        behind=(sens_back[1], sens_back[3]),
     )
     shared = over(parts.reshape(X * L * Z, 32, 128), ("x", "l", "z"))
     innovation = call(final_kernel, shape(32, 128, kind=F32), (shared,), VMEM, nbytes=2**19, vmem=4)

time: 107 us -> 168 us (1.57)
  the two profiles are of different devices: /device:TPU:1 before, /device:TPU:4 now
where the time goes in v9:
time: 168 us; the launch traced here: 166 us
  Pallas kernels  76.4 us (45%)
  starting transfers between devices  52.1 us (31%)
  waiting for transfers between devices  35.7 us (21%)
    pallas_call x9, Pallas kernels, call(): pl.pallas_call(kernel, out_shape=outs, in_specs=[spec] * len(ins) + [ANY]...  76.4 us
    all_to_all x3, starting transfers between devices, over(): return lax.all_to_all(value, axes, split_axis=0, concat_axis=0, tiled=True)  29.4 us
    ppermute x3, waiting for transfers between devices, body(): lax.ppermute(sens[d], 'x', ring(-d))  20 us
    ppermute x6, starting transfers between devices, body(): lax.ppermute(packed[d], 'x', ring(d))  8.87 us
    all_to_all x3, waiting for transfers between devices, over(): return lax.all_to_all(value, axes, split_axis=0, concat_axis=0, tiled=True)  6.44 us
    ppermute x3, waiting for transfers between devices, body(): panels = [panel] + [lax.ppermute(panel, 'x', ring(d)) for d in range(1, X)]  4.96 us
    ppermute x6, waiting for transfers between devices, body(): lax.ppermute(packed[d], 'x', ring(d))  4.35 us
    ppermute x3, starting transfers between devices, body(): panels = [panel] + [lax.ppermute(panel, 'x', ring(d)) for d in range(1, X)]  3.92 us
  transfers between devices with their start and end apart: 21, of which 10 were waited for; matrix products, arithmetic and copies ran while one was open for 0% of the time, Pallas kernels for 31%

profile of v9, /device:TPU:4, one launch (start us, length us, event | category | flops | bytes accessed | tf_op | source)
XLA Modules:
  0.0 166.5 jit_solution(3318576344669065976)
XLA Ops:
  0.6 21.3 %shard_map.50 = (bf16[64,4096]{1,0:T(8,128)(2,1)}, bf16[32,16,128]{2,1,0:T(8,128)(2,1)}) custom-call(bf16[128,4096]{1,0:T(8,128)(2,1)} %jac.3), custom_call_target="tpu_custom_call" | custom-call | bytes 1048576 | tf_op jit(solution)/shard_map/pallas_call | solution.py:27
  22.0 10.0 %all-to-all-start = ((bf16[32,16,128]{2,1,0:T(8,128)(2,1)}), bf16[32,16,128]{2,1,0:T(8,128)(2,1)S(1)}, u32[]{:S(2)}, u32[]{:S(2)}) async-start(bf16[32,16,128]{2,1,0:T(8,128)(2,1)} %get-tuple-element.27), calls=%async_computation | async-start | bytes 262144 | tf_op jit(solution)/shard_map/all_to_all | solution.py:156
  32.8 48.9 %shard_map.51 = (bf16[192,1024]{1,0:T(8,128)(2,1)}, bf16[192,1024]{1,0:T(8,128)(2,1)}, bf16[192,1024]{1,0:T(8,128)(2,1)}, bf16[192,1024]{1,0:T(8,128)(2,1)}) custom-call(bf16[128,4096]{1,0:T(8,128)(2,1)} %jac.3, bf16[64,4096]{1,0:T(8,128)(2,1)} %copy-done.2, bf16[64,4096]{1,0:T(8,128)(2,1)} %cov.1), custom_call_target="tpu_custom_call" | custom-call | bytes 4194304 | tf_op jit(solution)/shard_map/pallas_call | solution.py:27
  81.7 3.0 %collective-permute-start.10 = (bf16[192,1024]{1,0:T(8,128)(2,1)}, bf16[192,1024]{1,0:T(8,128)(2,1)S(1)}, u32[]{:S(2)}, u32[]{:S(2)}) collective-permute-start(bf16[192,1024]{1,0:T(8,128)(2,1)} %get-tuple-element.19.refs_0_), channel_id=1, source_target_pairs={{0,32},{32,0},{1,33},{33,1},{2,34},{34,2},{3,35},{35,3},{4,36},{36... | collective-permute-start | bytes 1179656 | tf_op jit(solution)/shard_map/ppermute | solution.py:196
  84.7 1.2 collective-permute-start.1
  88.5 7.7 %all-to-all-start.1 = ((bf16[32,16,128]{2,1,0:T(8,128)(2,1)}), bf16[32,16,128]{2,1,0:T(8,128)(2,1)S(1)}, u32[]{:S(2)}, u32[]{:S(2)}) async-start(bf16[32,16,128]{2,1,0:T(8,128)(2,1)} %broadcast_in_dim.3), calls=%async_computation.1 | async-start | bytes 262144 | tf_op jit(solution)/shard_map/all_to_all | solution.py:156
  98.2 2.7 %collective-permute-start.5 = (bf16[128,1024]{1,0:T(8,128)(2,1)}, bf16[128,1024]{1,0:T(8,128)(2,1)S(1)}, u32[]{:S(2)}, u32[]{:S(2)}) collective-permute-start(bf16[128,1024]{1,0:T(8,128)(2,1)} %get-tuple-element.25), channel_id=1, source_target_pairs={{0,128},{64,192},{128,0},{192,64},{1,129},{65,193},{129,1},{193,65... | collective-permute-start | bytes 786440 | tf_op jit(solution)/shard_map/ppermute | solution.py:202
  100.8 2.0 %collective-permute-start.6 = (bf16[128,1024]{1,0:T(8,128)(2,1)S(1)}, bf16[128,1024]{1,0:T(8,128)(2,1)S(1)}, u32[]{:S(2)}, u32[]{:S(2)}) collective-permute-start(bf16[128,1024]{1,0:T(8,128)(2,1)S(1)} %get-tuple-element.26), channel_id=1, source_target_pairs={{0,192},{64,0},{128,64},{192,128},{1,193},{65,1},{129,65},{193,129... | collective-permute-start | bytes 786440 | tf_op jit(solution)/shard_map/ppermute | solution.py:202
  102.9 3.8 %all-to-all-done.1.refs_4_.refs_8_ = bf16[32,16,128]{2,1,0:T(8,128)(2,1)S(1)} async-done(((bf16[32,16,128]{2,1,0:T(8,128)(2,1)}), bf16[32,16,128]{2,1,0:T(8,128)(2,1)S(1)}, u32[]{:S(2)}, u32[]{:S(2)}) %all-to-all-start.1) | async-done | bytes 131104 | tf_op jit(solution)/shard_map/all_to_all | solution.py:156
  107.9 1.2 collective-permute-start.11
  109.2 2.5 %collective-permute-start.15 = (bf16[3,128,1024]{2,1,0:T(8,128)(2,1)S(1)}, bf16[3,128,1024]{2,1,0:T(8,128)(2,1)S(1)}, u32[]{:S(2)}, u32[]{:S(2)}) collective-permute-start(bf16[3,128,1024]{2,1,0:T(8,128)(2,1)S(1)} %shard_map.56), channel_id=1, source_target_pairs={{0,32},{32,0},{1,33},{33,1},{2,34},{34,2},{3,35},{35,3},{4,36},{36... | collective-permute-start | bytes 2359304 | tf_op jit(solution)/shard_map/ppermute | solution.py:206
  111.7 1.2 collective-permute-start.7
  113.0 3.6 %collective-permute-done.5.refs_6_ = bf16[128,1024]{1,0:T(8,128)(2,1)S(1)} collective-permute-done((bf16[128,1024]{1,0:T(8,128)(2,1)}, bf16[128,1024]{1,0:T(8,128)(2,1)S(1)}, u32[]{:S(2)}, u32[]{:S(2)}) %collective-permute-start.5) | collective-permute-done | bytes 262176 | tf_op jit(solution)/shard_map/ppermute | solution.py:202
  116.6 2.7 %collective-permute-start.8 = (bf16[32,16,128]{2,1,0:T(8,128)(2,1)S(1)}, bf16[32,16,128]{2,1,0:T(8,128)(2,1)S(1)}, u32[]{:S(2)}, u32[]{:S(2)}) collective-permute-start(bf16[32,16,128]{2,1,0:T(8,128)(2,1)S(1)} %all-to-all-done.1.refs_4_.refs_8_), channel_id=1, source_target_pairs={{0,128},{64,192},{128,0},{192,64},{1,129},{65,193},{129,1},{193,65... | collective-permute-start | bytes 393224 | tf_op jit(solution)/shard_map/ppermute | solution.py:198
  119.3 1.5 collective-permute-done.7.refs_9_
  120.7 2.3 %collective-permute-done.8.refs_10_ = bf16[32,16,128]{2,1,0:T(8,128)(2,1)S(1)} collective-permute-done((bf16[32,16,128]{2,1,0:T(8,128)(2,1)S(1)}, bf16[32,16,128]{2,1,0:T(8,128)(2,1)S(1)}, u32[]{:S(2)}, u32[]{:S(2)}) %collective-permute-start.8) | collective-permute-done | bytes 131104 | tf_op jit(solution)/shard_map/ppermute | solution.py:198
  123.0 1.2 collective-permute-done.9.refs_11_
  125.7 2.1 %collective-permute-start.12 = (bf16[128,1024]{1,0:T(8,128)(2,1)S(1)}, bf16[128,1024]{1,0:T(8,128)(2,1)S(1)}, u32[]{:S(2)}, u32[]{:S(2)}) collective-permute-start(bf16[128,1024]{1,0:T(8,128)(2,1)S(1)} %get-tuple-element.29), channel_id=1, source_target_pairs={{0,192},{64,0},{128,64},{192,128},{1,193},{65,1},{129,65},{193,129... | collective-permute-start | bytes 786440 | tf_op jit(solution)/shard_map/ppermute | solution.py:217
  127.8 6.2 %collective-permute-done.12.refs_1_.refs_8_ = bf16[128,1024]{1,0:T(8,128)(2,1)S(1)} collective-permute-done((bf16[128,1024]{1,0:T(8,128)(2,1)S(1)}, bf16[128,1024]{1,0:T(8,128)(2,1)S(1)}, u32[]{:S(2)}, u32[]{:S(2)}) %collective-permute-start.12) | collective-permute-done | bytes 262176 | tf_op jit(solution)/shard_map/ppermute | solution.py:217
  134.0 1.9 %collective-permute-done.14.refs_3_.refs_9_ = bf16[128,1024]{1,0:T(8,128)(2,1)S(1)} collective-permute-done((bf16[128,1024]{1,0:T(8,128)(2,1)S(1)}, bf16[128,1024]{1,0:T(8,128)(2,1)S(1)}, u32[]{:S(2)}, u32[]{:S(2)}) %collective-permute-start.14) | collective-permute-done | bytes 262176 | tf_op jit(solution)/shard_map/ppermute | solution.py:217
  135.8 2.2 %shard_map.57 = bf16[4,512,128]{2,1,0:T(8,128)(2,1)} custom-call(bf16[192,1024]{1,0:T(8,128)(2,1)S(1)} %collective-permute-done.10.refs_3_.refs_12_.own_got, bf16[3,128,1024]{2,1,0:T(8,128)(2,1)S(1)} %collective-permute-done.15.jac_got, bf16[192,1024]{1,0:T(8,128)(2,1)S(1)} %copy-done, bf16[192,1024]{1,0:T(8,128)(2,1)S(1)} %collective-permute-done.1.refs_0_.refs_1_, ...), custom_call_target="tpu_custom_call" | custom-call | flops 1073741824 | bytes 2097152 | tf_op jit(solution)/shard_map/pallas_call | solution.py:27
  138.0 11.7 %all-to-all-start.2 = ((bf16[64,32,128]{2,1,0:T(8,128)(2,1)}), bf16[64,32,128]{2,1,0:T(8,128)(2,1)S(1)}, u32[]{:S(2)}, u32[]{:S(2)}) async-start(bf16[64,32,128]{2,1,0:T(8,128)(2,1)} %bitcast.1), calls=%async_computation.2 | async-start | bytes 1048576 | tf_op jit(solution)/shard_map/all_to_all | solution.py:156
  150.2 11.9 %collective-permute-done.13.refs_2_ = bf16[128,1024]{1,0:T(8,128)(2,1)S(1)} collective-permute-done((bf16[128,1024]{1,0:T(8,128)(2,1)S(1)}, bf16[128,1024]{1,0:T(8,128)(2,1)S(1)}, u32[]{:S(2)}, u32[]{:S(2)}) %collective-permute-start.13) | collective-permute-done | bytes 262176 | tf_op jit(solution)/shard_map/ppermute | solution.py:217
  163.1 2.6 %all-to-all-done.2.got = bf16[64,32,128]{2,1,0:T(8,128)(2,1)S(1)} async-done(((bf16[64,32,128]{2,1,0:T(8,128)(2,1)}), bf16[64,32,128]{2,1,0:T(8,128)(2,1)S(1)}, u32[]{:S(2)}, u32[]{:S(2)}) %all-to-all-start.2) | async-done | bytes 524320 | tf_op jit(solution)/shard_map/all_to_all | solution.py:156
  (35 shorter events, 10.3 us)
Async XLA Ops:
  21.9 10.1 %collective-permute-start = (bf16[64,4096]{1,0:T(8,128)(2,1)}, bf16[64,4096]{1,0:T(8,128)(2,1)S(1)}, u32[]{:S(2)}, u32[]{:S(2)}) collective-permute-start(bf16[64,4096]{1,0:T(8,128)(2,1)} %get-tuple-element.18), channel_id=1, source_target_pairs={{0,1},{1,0},{2,3},{3,2},{4,5},{5,4},{6,7},{7,6},{8,9},{9,8},{10,11... | collective-permute-start | bytes 1572872 | tf_op jit(solution)/shard_map/ppermute | solution.py:184
  22.0 65.8 %all-to-all-start = ((bf16[32,16,128]{2,1,0:T(8,128)(2,1)}), bf16[32,16,128]{2,1,0:T(8,128)(2,1)S(1)}, u32[]{:S(2)}, u32[]{:S(2)}) async-start(bf16[32,16,128]{2,1,0:T(8,128)(2,1)} %get-tuple-element.27), calls=%async_computation | async-start | bytes 262144 | tf_op jit(solution)/shard_map/all_to_all | solution.py:156
  32.0 64.2 %copy-start.1 = (bf16[128,4096]{1,0:T(8,128)(2,1)S(1)}, bf16[128,4096]{1,0:T(8,128)(2,1)}, u32[]{:S(2)}) copy-start(bf16[128,4096]{1,0:T(8,128)(2,1)} %carry.1) | copy-start | bytes 3145732
  32.0 0.8 copy-start.2
  81.7 16.5 %collective-permute-start.10 = (bf16[192,1024]{1,0:T(8,128)(2,1)}, bf16[192,1024]{1,0:T(8,128)(2,1)S(1)}, u32[]{:S(2)}, u32[]{:S(2)}) collective-permute-start(bf16[192,1024]{1,0:T(8,128)(2,1)} %get-tuple-element.19.refs_0_), channel_id=1, source_target_pairs={{0,32},{32,0},{1,33},{33,1},{2,34},{34,2},{3,35},{35,3},{4,36},{36... | collective-permute-start | bytes 1179656 | tf_op jit(solution)/shard_map/ppermute | solution.py:196
  84.7 16.1 %collective-permute-start.1 = (bf16[192,1024]{1,0:T(8,128)(2,1)}, bf16[192,1024]{1,0:T(8,128)(2,1)S(1)}, u32[]{:S(2)}, u32[]{:S(2)}) collective-permute-start(bf16[192,1024]{1,0:T(8,128)(2,1)} %get-tuple-element.20), channel_id=1, source_target_pairs={{0,64},{64,128},{128,192},{192,0},{1,65},{65,129},{129,193},{193,1... | collective-permute-start | bytes 1179656 | tf_op jit(solution)/shard_map/ppermute | solution.py:197
  85.9 20.8 %collective-permute-start.2 = (bf16[192,1024]{1,0:T(8,128)(2,1)}, bf16[192,1024]{1,0:T(8,128)(2,1)S(1)}, u32[]{:S(2)}, u32[]{:S(2)}) collective-permute-start(bf16[192,1024]{1,0:T(8,128)(2,1)} %get-tuple-element.21), channel_id=1, source_target_pairs={{0,128},{64,192},{128,0},{192,64},{1,129},{65,193},{129,1},{193,65... | collective-permute-start | bytes 1179656 | tf_op jit(solution)/shard_map/ppermute | solution.py:197
  86.7 20.7 %collective-permute-start.3 = (bf16[192,1024]{1,0:T(8,128)(2,1)}, bf16[192,1024]{1,0:T(8,128)(2,1)S(1)}, u32[]{:S(2)}, u32[]{:S(2)}) collective-permute-start(bf16[192,1024]{1,0:T(8,128)(2,1)} %get-tuple-element.22), channel_id=1, source_target_pairs={{0,192},{64,0},{128,64},{192,128},{1,193},{65,1},{129,65},{193,129... | collective-permute-start | bytes 1179656 | tf_op jit(solution)/shard_map/ppermute | solution.py:197
  88.5 18.2 %all-to-all-start.1 = ((bf16[32,16,128]{2,1,0:T(8,128)(2,1)}), bf16[32,16,128]{2,1,0:T(8,128)(2,1)S(1)}, u32[]{:S(2)}, u32[]{:S(2)}) async-start(bf16[32,16,128]{2,1,0:T(8,128)(2,1)} %broadcast_in_dim.3), calls=%async_computation.1 | async-start | bytes 262144 | tf_op jit(solution)/shard_map/all_to_all | solution.py:156
  97.1 14.6 %collective-permute-start.4 = (bf16[128,1024]{1,0:T(8,128)(2,1)}, bf16[128,1024]{1,0:T(8,128)(2,1)S(1)}, u32[]{:S(2)}, u32[]{:S(2)}) collective-permute-start(bf16[128,1024]{1,0:T(8,128)(2,1)} %get-tuple-element.24), channel_id=1, source_target_pairs={{0,64},{64,128},{128,192},{192,0},{1,65},{65,129},{129,193},{193,1... | collective-permute-start | bytes 786440 | tf_op jit(solution)/shard_map/ppermute | solution.py:202
  98.2 18.4 %collective-permute-start.5 = (bf16[128,1024]{1,0:T(8,128)(2,1)}, bf16[128,1024]{1,0:T(8,128)(2,1)S(1)}, u32[]{:S(2)}, u32[]{:S(2)}) collective-permute-start(bf16[128,1024]{1,0:T(8,128)(2,1)} %get-tuple-element.25), channel_id=1, source_target_pairs={{0,128},{64,192},{128,0},{192,64},{1,129},{65,193},{129,1},{193,65... | collective-permute-start | bytes 786440 | tf_op jit(solution)/shard_map/ppermute | solution.py:202
  100.8 18.4 %collective-permute-start.6 = (bf16[128,1024]{1,0:T(8,128)(2,1)S(1)}, bf16[128,1024]{1,0:T(8,128)(2,1)S(1)}, u32[]{:S(2)}, u32[]{:S(2)}) collective-permute-start(bf16[128,1024]{1,0:T(8,128)(2,1)S(1)} %get-tuple-element.26), channel_id=1, source_target_pairs={{0,192},{64,0},{128,64},{192,128},{1,193},{65,1},{129,65},{193,129... | collective-permute-start | bytes 786440 | tf_op jit(solution)/shard_map/ppermute | solution.py:202
  107.9 16.3 %copy-start = (bf16[192,1024]{1,0:T(8,128)(2,1)S(1)}, bf16[192,1024]{1,0:T(8,128)(2,1)}, u32[]{:S(2)}) copy-start(bf16[192,1024]{1,0:T(8,128)(2,1)} %get-tuple-element.19.refs_0_) | copy-start | bytes 1179652
  107.9 16.3 %collective-permute-start.11 = (bf16[3,64,1024]{2,1,0:T(8,128)(2,1)S(1)}, bf16[3,64,1024]{2,1,0:T(8,128)(2,1)S(1)}, u32[]{:S(2)}, u32[]{:S(2)}) collective-permute-start(bf16[3,64,1024]{2,1,0:T(8,128)(2,1)S(1)} %shard_map.53.refs_3_), channel_id=1, source_target_pairs={{0,32},{32,0},{1,33},{33,1},{2,34},{34,2},{3,35},{35,3},{4,36},{36... | collective-permute-start | bytes 1179656 | tf_op jit(solution)/shard_map/ppermute | solution.py:205
  109.2 26.6 %collective-permute-start.15 = (bf16[3,128,1024]{2,1,0:T(8,128)(2,1)S(1)}, bf16[3,128,1024]{2,1,0:T(8,128)(2,1)S(1)}, u32[]{:S(2)}, u32[]{:S(2)}) collective-permute-start(bf16[3,128,1024]{2,1,0:T(8,128)(2,1)S(1)} %shard_map.56), channel_id=1, source_target_pairs={{0,32},{32,0},{1,33},{33,1},{2,34},{34,2},{3,35},{35,3},{4,36},{36... | collective-permute-start | bytes 2359304 | tf_op jit(solution)/shard_map/ppermute | solution.py:206
  111.7 9.0 %collective-permute-start.7 = (bf16[32,16,128]{2,1,0:T(8,128)(2,1)S(1)}, bf16[32,16,128]{2,1,0:T(8,128)(2,1)S(1)}, u32[]{:S(2)}, u32[]{:S(2)}) collective-permute-start(bf16[32,16,128]{2,1,0:T(8,128)(2,1)S(1)} %all-to-all-done.1.refs_4_.refs_8_), channel_id=1, source_target_pairs={{0,64},{64,128},{128,192},{192,0},{1,65},{65,129},{129,193},{193,1... | collective-permute-start | bytes 393224 | tf_op jit(solution)/shard_map/ppermute | solution.py:198
  116.6 6.5 %collective-permute-start.8 = (bf16[32,16,128]{2,1,0:T(8,128)(2,1)S(1)}, bf16[32,16,128]{2,1,0:T(8,128)(2,1)S(1)}, u32[]{:S(2)}, u32[]{:S(2)}) collective-permute-start(bf16[32,16,128]{2,1,0:T(8,128)(2,1)S(1)} %all-to-all-done.1.refs_4_.refs_8_), channel_id=1, source_target_pairs={{0,128},{64,192},{128,0},{192,64},{1,129},{65,193},{129,1},{193,65... | collective-permute-start | bytes 393224 | tf_op jit(solution)/shard_map/ppermute | solution.py:198
  119.3 5.0 %collective-permute-start.9 = (bf16[32,16,128]{2,1,0:T(8,128)(2,1)S(1)}, bf16[32,16,128]{2,1,0:T(8,128)(2,1)S(1)}, u32[]{:S(2)}, u32[]{:S(2)}) collective-permute-start(bf16[32,16,128]{2,1,0:T(8,128)(2,1)S(1)} %all-to-all-done.1.refs_4_.refs_8_), channel_id=1, source_target_pairs={{0,192},{64,0},{128,64},{192,128},{1,193},{65,1},{129,65},{193,129... | collective-permute-start | bytes 393224 | tf_op jit(solution)/shard_map/ppermute | solution.py:198
  125.1 10.8 %collective-permute-start.16 = (bf16[256,1024]{1,0:T(8,128)(2,1)S(1)}, bf16[256,1024]{1,0:T(8,128)(2,1)S(1)}, u32[]{:S(2)}, u32[]{:S(2)}) collective-permute-start(bf16[256,1024]{1,0:T(8,128)(2,1)S(1)} %get-tuple-element.32.refs_4_), channel_id=1, source_target_pairs={{0,1},{1,0},{2,3},{3,2},{4,5},{5,4},{6,7},{7,6},{8,9},{9,8},{10,11... | collective-permute-start | bytes 1572872 | tf_op jit(solution)/shard_map/ppermute | solution.py:218
  125.2 10.7 %collective-permute-start.17 = (bf16[256,1024]{1,0:T(8,128)(2,1)S(1)}, bf16[256,1024]{1,0:T(8,128)(2,1)S(1)}, u32[]{:S(2)}, u32[]{:S(2)}) collective-permute-start(bf16[256,1024]{1,0:T(8,128)(2,1)S(1)} %get-tuple-element.33.refs_5_), channel_id=1, source_target_pairs={{0,1},{1,0},{2,3},{3,2},{4,5},{5,4},{6,7},{7,6},{8,9},{9,8},{10,11... | collective-permute-start | bytes 1572872 | tf_op jit(solution)/shard_map/ppermute | solution.py:218
  125.7 8.3 %collective-permute-start.12 = (bf16[128,1024]{1,0:T(8,128)(2,1)S(1)}, bf16[128,1024]{1,0:T(8,128)(2,1)S(1)}, u32[]{:S(2)}, u32[]{:S(2)}) collective-permute-start(bf16[128,1024]{1,0:T(8,128)(2,1)S(1)} %get-tuple-element.29), channel_id=1, source_target_pairs={{0,192},{64,0},{128,64},{192,128},{1,193},{65,1},{129,65},{193,129... | collective-permute-start | bytes 786440 | tf_op jit(solution)/shard_map/ppermute | solution.py:217
  127.8 8.0 %collective-permute-start.14 = (bf16[128,1024]{1,0:T(8,128)(2,1)S(1)}, bf16[128,1024]{1,0:T(8,128)(2,1)S(1)}, u32[]{:S(2)}, u32[]{:S(2)}) collective-permute-start(bf16[128,1024]{1,0:T(8,128)(2,1)S(1)} %get-tuple-element.31), channel_id=1, source_target_pairs={{0,64},{64,128},{128,192},{192,0},{1,65},{65,129},{129,193},{193,1... | collective-permute-start | bytes 786440 | tf_op jit(solution)/shard_map/ppermute | solution.py:217
  138.0 27.7 %all-to-all-start.2 = ((bf16[64,32,128]{2,1,0:T(8,128)(2,1)}), bf16[64,32,128]{2,1,0:T(8,128)(2,1)S(1)}, u32[]{:S(2)}, u32[]{:S(2)}) async-start(bf16[64,32,128]{2,1,0:T(8,128)(2,1)} %bitcast.1), calls=%async_computation.2 | async-start | bytes 1048576 | tf_op jit(solution)/shard_map/all_to_all | solution.py:156
  149.8 12.4 %collective-permute-start.13 = (bf16[128,1024]{1,0:T(8,128)(2,1)S(1)}, bf16[128,1024]{1,0:T(8,128)(2,1)S(1)}, u32[]{:S(2)}, u32[]{:S(2)}) collective-permute-start(bf16[128,1024]{1,0:T(8,128)(2,1)S(1)} %get-tuple-element.30), channel_id=1, source_target_pairs={{0,128},{64,192},{128,0},{192,64},{1,129},{65,193},{129,1},{193,65... | collective-permute-start | bytes 786440 | tf_op jit(solution)/shard_map/ppermute | solution.py:217

commit v10 on v9

--- a/solution.py
+++ b/solution.py
@@ -23,12 +23,12 @@
     return lax.rem(lax.axis_index("x") + X - d, X)
 
 
-def call(kernel, outs, ins, spec, scratch=(), flops=0, nbytes=0, vmem=1, behind=()):
+def call(kernel, outs, ins, spec, scratch=(), flops=0, nbytes=0, vmem=1, behind=(), outs_spec=None):
     return pl.pallas_call(
         kernel,
         out_shape=outs,
         in_specs=[spec] * len(ins) + [ANY] * len(behind),
-        out_specs=jax.tree.map(lambda _: spec, outs),
+        out_specs=jax.tree.map(lambda _: outs_spec or spec, outs),
         scratch_shapes=list(scratch),
         cost_estimate=pl.CostEstimate(flops=flops, bytes_accessed=nbytes, transcendentals=0),
         compiler_params=pltpu.CompilerParams(vmem_limit_bytes=vmem * MIB),
@@ -176,8 +176,9 @@
         give_kernel,
         [shape(64, 4096), shape(32, 16, 128)],
         (jacobian,),
-        ANY,
+        VMEM,
         dma(34),
+        outs_spec=ANY,
         nbytes=MIB,
         vmem=60,
     )
@@ -188,8 +189,9 @@
         pack_kernel,
         [shape(192, 1024)] * X,
         (jacobian, got, cov_rows),
-        ANY,
+        VMEM,
         dma(4 * X),
+        outs_spec=ANY,
         nbytes=4 * MIB,
         vmem=60,
     )
@@ -225,7 +227,7 @@
         flops=2 * 512 * 512 * 2048,
         nbytes=2 * MIB,
         vmem=16,
-        behind=(sens_back[1], sens_back[3]),
+        behind=(sens_back[1], sens_back[2]),
     )
     shared = over(parts.reshape(X * L * Z, 32, 128), ("x", "l", "z"))
     innovation = call(final_kernel, shape(32, 128, kind=F32), (shared,), VMEM, nbytes=2**19, vmem=4)

time: 168 us -> 107 us (0.64)
  Pallas kernels: 76.4 us -> 11.4 us
  waiting for transfers between devices: 35.7 us -> 38.6 us
    pallas_call x9, Pallas kernels: 76.4 us -> 11.4 us  [call(): pl.pallas_call(kernel, out_shape=outs, in_specs=[spec] * len(ins) + [ANY]...]
    ppermute x3, starting transfers between devices: 2.58 us -> 4.3 us  [body(): lax.ppermute(sens[d], 'x', ring(-d))]
  transfers between devices with their start and end apart: 21 -> 21, of which waited for: 10 -> 10; matrix products, arithmetic and copies ran while one was open for 0% -> 1% of each run, Pallas kernels for 31% -> 6%
where the time goes in v10:
time: 107 us; the launch traced here: 106 us
  starting transfers between devices  53.4 us (50%)
  waiting for transfers between devices  38.6 us (36%)
  Pallas kernels  11.4 us (11%)
  local copies, waits for them, and re-layouts  1.47 us (1%)
    all_to_all x3, starting transfers between devices, over(): return lax.all_to_all(value, axes, split_axis=0, concat_axis=0, tiled=True)  29 us
    ppermute x3, waiting for transfers between devices, body(): lax.ppermute(sens[d], 'x', ring(-d))  21.4 us
    pallas_call x9, Pallas kernels, call(): pl.pallas_call(kernel, out_shape=outs, in_specs=[spec] * len(ins) + [ANY]...  11.4 us
    ppermute x6, starting transfers between devices, body(): lax.ppermute(packed[d], 'x', ring(d))  8.87 us
    all_to_all x3, waiting for transfers between devices, over(): return lax.all_to_all(value, axes, split_axis=0, concat_axis=0, tiled=True)  7.89 us
    ppermute x3, waiting for transfers between devices, body(): panels = [panel] + [lax.ppermute(panel, 'x', ring(d)) for d in range(1, X)]  4.96 us
    ppermute x6, waiting for transfers between devices, body(): lax.ppermute(packed[d], 'x', ring(d))  4.35 us
    ppermute x3, starting transfers between devices, body(): lax.ppermute(sens[d], 'x', ring(-d))  4.3 us
  transfers between devices with their start and end apart: 21, of which 10 were waited for; matrix products, arithmetic and copies ran while one was open for 1% of the time, Pallas kernels for 6%

profile of v10, /device:TPU:4, one launch (start us, length us, event | category | flops | bytes accessed | tf_op | source)
XLA Modules:
  0.0 105.7 jit_solution(6678112855858547117)
XLA Ops:
  0.6 2.4 %shard_map.50 = (bf16[64,4096]{1,0:T(8,128)(2,1)}, bf16[32,16,128]{2,1,0:T(8,128)(2,1)}) custom-call(bf16[128,4096]{1,0:T(8,128)(2,1)} %jac.3), custom_call_target="tpu_custom_call" | custom-call | bytes 1048576 | tf_op jit(solution)/shard_map/pallas_call | solution.py:27
  3.1 10.0 %all-to-all-start = ((bf16[32,16,128]{2,1,0:T(8,128)(2,1)}), bf16[32,16,128]{2,1,0:T(8,128)(2,1)S(1)}, u32[]{:S(2)}, u32[]{:S(2)}) async-start(bf16[32,16,128]{2,1,0:T(8,128)(2,1)} %get-tuple-element.27), calls=%async_computation | async-start | bytes 262144 | tf_op jit(solution)/shard_map/all_to_all | solution.py:156
  13.9 2.8 %shard_map.51 = (bf16[192,1024]{1,0:T(8,128)(2,1)}, bf16[192,1024]{1,0:T(8,128)(2,1)}, bf16[192,1024]{1,0:T(8,128)(2,1)}, bf16[192,1024]{1,0:T(8,128)(2,1)}) custom-call(bf16[128,4096]{1,0:T(8,128)(2,1)} %jac.3, bf16[64,4096]{1,0:T(8,128)(2,1)} %copy-done.2, bf16[64,4096]{1,0:T(8,128)(2,1)} %cov.1), custom_call_target="tpu_custom_call" | custom-call | bytes 4194304 | tf_op jit(solution)/shard_map/pallas_call | solution.py:27
  16.8 3.0 %collective-permute-start.10 = (bf16[192,1024]{1,0:T(8,128)(2,1)}, bf16[192,1024]{1,0:T(8,128)(2,1)S(1)}, u32[]{:S(2)}, u32[]{:S(2)}) collective-permute-start(bf16[192,1024]{1,0:T(8,128)(2,1)} %get-tuple-element.19.refs_0_), channel_id=1, source_target_pairs={{0,32},{32,0},{1,33},{33,1},{2,34},{34,2},{3,35},{35,3},{4,36},{36... | collective-permute-start | bytes 1179656 | tf_op jit(solution)/shard_map/ppermute | solution.py:198
  19.8 1.2 %collective-permute-start.1 = (bf16[192,1024]{1,0:T(8,128)(2,1)}, bf16[192,1024]{1,0:T(8,128)(2,1)S(1)}, u32[]{:S(2)}, u32[]{:S(2)}) collective-permute-start(bf16[192,1024]{1,0:T(8,128)(2,1)} %get-tuple-element.20), channel_id=1, source_target_pairs={{0,64},{64,128},{128,192},{192,0},{1,65},{65,129},{129,193},{193,1... | collective-permute-start | bytes 1179656 | tf_op jit(solution)/shard_map/ppermute | solution.py:199
  24.3 7.0 %all-to-all-start.1 = ((bf16[32,16,128]{2,1,0:T(8,128)(2,1)}), bf16[32,16,128]{2,1,0:T(8,128)(2,1)S(1)}, u32[]{:S(2)}, u32[]{:S(2)}) async-start(bf16[32,16,128]{2,1,0:T(8,128)(2,1)} %broadcast_in_dim.3), calls=%async_computation.1 | async-start | bytes 262144 | tf_op jit(solution)/shard_map/all_to_all | solution.py:156
  33.2 2.7 %collective-permute-start.5 = (bf16[128,1024]{1,0:T(8,128)(2,1)}, bf16[128,1024]{1,0:T(8,128)(2,1)S(1)}, u32[]{:S(2)}, u32[]{:S(2)}) collective-permute-start(bf16[128,1024]{1,0:T(8,128)(2,1)} %get-tuple-element.25), channel_id=1, source_target_pairs={{0,128},{64,192},{128,0},{192,64},{1,129},{65,193},{129,1},{193,65... | collective-permute-start | bytes 786440 | tf_op jit(solution)/shard_map/ppermute | solution.py:204
  35.9 2.0 %collective-permute-start.6 = (bf16[128,1024]{1,0:T(8,128)(2,1)S(1)}, bf16[128,1024]{1,0:T(8,128)(2,1)S(1)}, u32[]{:S(2)}, u32[]{:S(2)}) collective-permute-start(bf16[128,1024]{1,0:T(8,128)(2,1)S(1)} %get-tuple-element.26), channel_id=1, source_target_pairs={{0,192},{64,0},{128,64},{192,128},{1,193},{65,1},{129,65},{193,129... | collective-permute-start | bytes 786440 | tf_op jit(solution)/shard_map/ppermute | solution.py:204
  37.9 3.8 %all-to-all-done.1.refs_4_.refs_8_ = bf16[32,16,128]{2,1,0:T(8,128)(2,1)S(1)} async-done(((bf16[32,16,128]{2,1,0:T(8,128)(2,1)}), bf16[32,16,128]{2,1,0:T(8,128)(2,1)S(1)}, u32[]{:S(2)}, u32[]{:S(2)}) %all-to-all-start.1) | async-done | bytes 131104 | tf_op jit(solution)/shard_map/all_to_all | solution.py:156
  43.0 1.2 %collective-permute-start.11 = (bf16[3,64,1024]{2,1,0:T(8,128)(2,1)S(1)}, bf16[3,64,1024]{2,1,0:T(8,128)(2,1)S(1)}, u32[]{:S(2)}, u32[]{:S(2)}) collective-permute-start(bf16[3,64,1024]{2,1,0:T(8,128)(2,1)S(1)} %shard_map.53.refs_3_), channel_id=1, source_target_pairs={{0,32},{32,0},{1,33},{33,1},{2,34},{34,2},{3,35},{35,3},{4,36},{36... | collective-permute-start | bytes 1179656 | tf_op jit(solution)/shard_map/ppermute | solution.py:207
  44.3 2.5 %collective-permute-start.15 = (bf16[3,128,1024]{2,1,0:T(8,128)(2,1)S(1)}, bf16[3,128,1024]{2,1,0:T(8,128)(2,1)S(1)}, u32[]{:S(2)}, u32[]{:S(2)}) collective-permute-start(bf16[3,128,1024]{2,1,0:T(8,128)(2,1)S(1)} %shard_map.56), channel_id=1, source_target_pairs={{0,32},{32,0},{1,33},{33,1},{2,34},{34,2},{3,35},{35,3},{4,36},{36... | collective-permute-start | bytes 2359304 | tf_op jit(solution)/shard_map/ppermute | solution.py:208
  46.8 1.2 %collective-permute-start.7 = (bf16[32,16,128]{2,1,0:T(8,128)(2,1)S(1)}, bf16[32,16,128]{2,1,0:T(8,128)(2,1)S(1)}, u32[]{:S(2)}, u32[]{:S(2)}) collective-permute-start(bf16[32,16,128]{2,1,0:T(8,128)(2,1)S(1)} %all-to-all-done.1.refs_4_.refs_8_), channel_id=1, source_target_pairs={{0,64},{64,128},{128,192},{192,0},{1,65},{65,129},{129,193},{193,1... | collective-permute-start | bytes 393224 | tf_op jit(solution)/shard_map/ppermute | solution.py:200
  48.0 3.6 %collective-permute-done.5.refs_6_ = bf16[128,1024]{1,0:T(8,128)(2,1)S(1)} collective-permute-done((bf16[128,1024]{1,0:T(8,128)(2,1)}, bf16[128,1024]{1,0:T(8,128)(2,1)S(1)}, u32[]{:S(2)}, u32[]{:S(2)}) %collective-permute-start.5) | collective-permute-done | bytes 262176 | tf_op jit(solution)/shard_map/ppermute | solution.py:204
  51.6 2.7 %collective-permute-start.8 = (bf16[32,16,128]{2,1,0:T(8,128)(2,1)S(1)}, bf16[32,16,128]{2,1,0:T(8,128)(2,1)S(1)}, u32[]{:S(2)}, u32[]{:S(2)}) collective-permute-start(bf16[32,16,128]{2,1,0:T(8,128)(2,1)S(1)} %all-to-all-done.1.refs_4_.refs_8_), channel_id=1, source_target_pairs={{0,128},{64,192},{128,0},{192,64},{1,129},{65,193},{129,1},{193,65... | collective-permute-start | bytes 393224 | tf_op jit(solution)/shard_map/ppermute | solution.py:200
  54.3 1.5 %collective-permute-done.7.refs_9_ = bf16[32,16,128]{2,1,0:T(8,128)(2,1)S(1)} collective-permute-done((bf16[32,16,128]{2,1,0:T(8,128)(2,1)S(1)}, bf16[32,16,128]{2,1,0:T(8,128)(2,1)S(1)}, u32[]{:S(2)}, u32[]{:S(2)}) %collective-permute-start.7) | collective-permute-done | bytes 131104 | tf_op jit(solution)/shard_map/ppermute | solution.py:200
  55.8 2.3 %collective-permute-done.8.refs_10_ = bf16[32,16,128]{2,1,0:T(8,128)(2,1)S(1)} collective-permute-done((bf16[32,16,128]{2,1,0:T(8,128)(2,1)S(1)}, bf16[32,16,128]{2,1,0:T(8,128)(2,1)S(1)}, u32[]{:S(2)}, u32[]{:S(2)}) %collective-permute-start.8) | collective-permute-done | bytes 131104 | tf_op jit(solution)/shard_map/ppermute | solution.py:200
  58.1 1.2 %collective-permute-done.9.refs_11_ = bf16[32,16,128]{2,1,0:T(8,128)(2,1)S(1)} collective-permute-done((bf16[32,16,128]{2,1,0:T(8,128)(2,1)S(1)}, bf16[32,16,128]{2,1,0:T(8,128)(2,1)S(1)}, u32[]{:S(2)}, u32[]{:S(2)}) %collective-permute-start.9) | collective-permute-done | bytes 131104 | tf_op jit(solution)/shard_map/ppermute | solution.py:200
  60.7 2.1 %collective-permute-start.12 = (bf16[128,1024]{1,0:T(8,128)(2,1)S(1)}, bf16[128,1024]{1,0:T(8,128)(2,1)S(1)}, u32[]{:S(2)}, u32[]{:S(2)}) collective-permute-start(bf16[128,1024]{1,0:T(8,128)(2,1)S(1)} %get-tuple-element.29), channel_id=1, source_target_pairs={{0,192},{64,0},{128,64},{192,128},{1,193},{65,1},{129,65},{193,129... | collective-permute-start | bytes 786440 | tf_op jit(solution)/shard_map/ppermute | solution.py:219
  63.7 10.7 %collective-permute-done.12.refs_1_.refs_8_ = bf16[128,1024]{1,0:T(8,128)(2,1)S(1)} collective-permute-done((bf16[128,1024]{1,0:T(8,128)(2,1)S(1)}, bf16[128,1024]{1,0:T(8,128)(2,1)S(1)}, u32[]{:S(2)}, u32[]{:S(2)}) %collective-permute-start.12) | collective-permute-done | bytes 262176 | tf_op jit(solution)/shard_map/ppermute | solution.py:219
  74.4 2.2 %shard_map.57 = bf16[4,512,128]{2,1,0:T(8,128)(2,1)} custom-call(bf16[192,1024]{1,0:T(8,128)(2,1)S(1)} %collective-permute-done.10.refs_3_.refs_12_.own_got, bf16[3,128,1024]{2,1,0:T(8,128)(2,1)S(1)} %collective-permute-done.15.jac_got, bf16[192,1024]{1,0:T(8,128)(2,1)S(1)} %copy-done, bf16[192,1024]{1,0:T(8,128)(2,1)S(1)} %collective-permute-done.1.refs_0_.refs_1_, ...), custom_call_target="tpu_custom_call" | custom-call | flops 1073741824 | bytes 2097152 | tf_op jit(solution)/shard_map/pallas_call | solution.py:27
  76.6 12.0 %all-to-all-start.2 = ((bf16[64,32,128]{2,1,0:T(8,128)(2,1)}), bf16[64,32,128]{2,1,0:T(8,128)(2,1)S(1)}, u32[]{:S(2)}, u32[]{:S(2)}) async-start(bf16[64,32,128]{2,1,0:T(8,128)(2,1)} %bitcast.1), calls=%async_computation.2 | async-start | bytes 1048576 | tf_op jit(solution)/shard_map/all_to_all | solution.py:156
  88.6 1.4 %collective-permute-start.14 = (bf16[128,1024]{1,0:T(8,128)(2,1)S(1)}, bf16[128,1024]{1,0:T(8,128)(2,1)S(1)}, u32[]{:S(2)}, u32[]{:S(2)}) collective-permute-start(bf16[128,1024]{1,0:T(8,128)(2,1)S(1)} %get-tuple-element.31), channel_id=1, source_target_pairs={{0,64},{64,128},{128,192},{192,0},{1,65},{65,129},{129,193},{193,1... | collective-permute-start | bytes 786440 | tf_op jit(solution)/shard_map/ppermute | solution.py:219
  89.9 10.7 %collective-permute-done.14.refs_3_ = bf16[128,1024]{1,0:T(8,128)(2,1)S(1)} collective-permute-done((bf16[128,1024]{1,0:T(8,128)(2,1)S(1)}, bf16[128,1024]{1,0:T(8,128)(2,1)S(1)}, u32[]{:S(2)}, u32[]{:S(2)}) %collective-permute-start.14) | collective-permute-done | bytes 262176 | tf_op jit(solution)/shard_map/ppermute | solution.py:219
  101.6 3.4 %all-to-all-done.2.got = bf16[64,32,128]{2,1,0:T(8,128)(2,1)S(1)} async-done(((bf16[64,32,128]{2,1,0:T(8,128)(2,1)}), bf16[64,32,128]{2,1,0:T(8,128)(2,1)S(1)}, u32[]{:S(2)}, u32[]{:S(2)}) %all-to-all-start.2) | async-done | bytes 524320 | tf_op jit(solution)/shard_map/all_to_all | solution.py:156
  (35 shorter events, 11.4 us)
Async XLA Ops:
  3.0 10.1 %collective-permute-start = (bf16[64,4096]{1,0:T(8,128)(2,1)}, bf16[64,4096]{1,0:T(8,128)(2,1)S(1)}, u32[]{:S(2)}, u32[]{:S(2)}) collective-permute-start(bf16[64,4096]{1,0:T(8,128)(2,1)} %get-tuple-element.18), channel_id=1, source_target_pairs={{0,1},{1,0},{2,3},{3,2},{4,5},{5,4},{6,7},{7,6},{8,9},{9,8},{10,11... | collective-permute-start | bytes 1572872 | tf_op jit(solution)/shard_map/ppermute | solution.py:185
  3.1 20.4 %all-to-all-start = ((bf16[32,16,128]{2,1,0:T(8,128)(2,1)}), bf16[32,16,128]{2,1,0:T(8,128)(2,1)S(1)}, u32[]{:S(2)}, u32[]{:S(2)}) async-start(bf16[32,16,128]{2,1,0:T(8,128)(2,1)} %get-tuple-element.27), calls=%async_computation | async-start | bytes 262144 | tf_op jit(solution)/shard_map/all_to_all | solution.py:156
  13.1 18.2 %copy-start.1 = (bf16[128,4096]{1,0:T(8,128)(2,1)S(1)}, bf16[128,4096]{1,0:T(8,128)(2,1)}, u32[]{:S(2)}) copy-start(bf16[128,4096]{1,0:T(8,128)(2,1)} %carry.1) | copy-start | bytes 3145732
  13.1 0.8 copy-start.2
  16.8 16.5 %collective-permute-start.10 = (bf16[192,1024]{1,0:T(8,128)(2,1)}, bf16[192,1024]{1,0:T(8,128)(2,1)S(1)}, u32[]{:S(2)}, u32[]{:S(2)}) collective-permute-start(bf16[192,1024]{1,0:T(8,128)(2,1)} %get-tuple-element.19.refs_0_), channel_id=1, source_target_pairs={{0,32},{32,0},{1,33},{33,1},{2,34},{34,2},{3,35},{35,3},{4,36},{36... | collective-permute-start | bytes 1179656 | tf_op jit(solution)/shard_map/ppermute | solution.py:198
  19.8 16.1 %collective-permute-start.1 = (bf16[192,1024]{1,0:T(8,128)(2,1)}, bf16[192,1024]{1,0:T(8,128)(2,1)S(1)}, u32[]{:S(2)}, u32[]{:S(2)}) collective-permute-start(bf16[192,1024]{1,0:T(8,128)(2,1)} %get-tuple-element.20), channel_id=1, source_target_pairs={{0,64},{64,128},{128,192},{192,0},{1,65},{65,129},{129,193},{193,1... | collective-permute-start | bytes 1179656 | tf_op jit(solution)/shard_map/ppermute | solution.py:199
  21.0 20.8 %collective-permute-start.2 = (bf16[192,1024]{1,0:T(8,128)(2,1)}, bf16[192,1024]{1,0:T(8,128)(2,1)S(1)}, u32[]{:S(2)}, u32[]{:S(2)}) collective-permute-start(bf16[192,1024]{1,0:T(8,128)(2,1)} %get-tuple-element.21), channel_id=1, source_target_pairs={{0,128},{64,192},{128,0},{192,64},{1,129},{65,193},{129,1},{193,65... | collective-permute-start | bytes 1179656 | tf_op jit(solution)/shard_map/ppermute | solution.py:199
  21.8 20.7 %collective-permute-start.3 = (bf16[192,1024]{1,0:T(8,128)(2,1)}, bf16[192,1024]{1,0:T(8,128)(2,1)S(1)}, u32[]{:S(2)}, u32[]{:S(2)}) collective-permute-start(bf16[192,1024]{1,0:T(8,128)(2,1)} %get-tuple-element.22), channel_id=1, source_target_pairs={{0,192},{64,0},{128,64},{192,128},{1,193},{65,1},{129,65},{193,129... | collective-permute-start | bytes 1179656 | tf_op jit(solution)/shard_map/ppermute | solution.py:199
  24.3 17.5 %all-to-all-start.1 = ((bf16[32,16,128]{2,1,0:T(8,128)(2,1)}), bf16[32,16,128]{2,1,0:T(8,128)(2,1)S(1)}, u32[]{:S(2)}, u32[]{:S(2)}) async-start(bf16[32,16,128]{2,1,0:T(8,128)(2,1)} %broadcast_in_dim.3), calls=%async_computation.1 | async-start | bytes 262144 | tf_op jit(solution)/shard_map/all_to_all | solution.py:156
  32.2 14.6 %collective-permute-start.4 = (bf16[128,1024]{1,0:T(8,128)(2,1)}, bf16[128,1024]{1,0:T(8,128)(2,1)S(1)}, u32[]{:S(2)}, u32[]{:S(2)}) collective-permute-start(bf16[128,1024]{1,0:T(8,128)(2,1)} %get-tuple-element.24), channel_id=1, source_target_pairs={{0,64},{64,128},{128,192},{192,0},{1,65},{65,129},{129,193},{193,1... | collective-permute-start | bytes 786440 | tf_op jit(solution)/shard_map/ppermute | solution.py:204
  33.2 18.4 %collective-permute-start.5 = (bf16[128,1024]{1,0:T(8,128)(2,1)}, bf16[128,1024]{1,0:T(8,128)(2,1)S(1)}, u32[]{:S(2)}, u32[]{:S(2)}) collective-permute-start(bf16[128,1024]{1,0:T(8,128)(2,1)} %get-tuple-element.25), channel_id=1, source_target_pairs={{0,128},{64,192},{128,0},{192,64},{1,129},{65,193},{129,1},{193,65... | collective-permute-start | bytes 786440 | tf_op jit(solution)/shard_map/ppermute | solution.py:204
  35.9 18.4 %collective-permute-start.6 = (bf16[128,1024]{1,0:T(8,128)(2,1)S(1)}, bf16[128,1024]{1,0:T(8,128)(2,1)S(1)}, u32[]{:S(2)}, u32[]{:S(2)}) collective-permute-start(bf16[128,1024]{1,0:T(8,128)(2,1)S(1)} %get-tuple-element.26), channel_id=1, source_target_pairs={{0,192},{64,0},{128,64},{192,128},{1,193},{65,1},{129,65},{193,129... | collective-permute-start | bytes 786440 | tf_op jit(solution)/shard_map/ppermute | solution.py:204
  43.0 16.3 %copy-start = (bf16[192,1024]{1,0:T(8,128)(2,1)S(1)}, bf16[192,1024]{1,0:T(8,128)(2,1)}, u32[]{:S(2)}) copy-start(bf16[192,1024]{1,0:T(8,128)(2,1)} %get-tuple-element.19.refs_0_) | copy-start | bytes 1179652
  43.0 16.3 %collective-permute-start.11 = (bf16[3,64,1024]{2,1,0:T(8,128)(2,1)S(1)}, bf16[3,64,1024]{2,1,0:T(8,128)(2,1)S(1)}, u32[]{:S(2)}, u32[]{:S(2)}) collective-permute-start(bf16[3,64,1024]{2,1,0:T(8,128)(2,1)S(1)} %shard_map.53.refs_3_), channel_id=1, source_target_pairs={{0,32},{32,0},{1,33},{33,1},{2,34},{34,2},{3,35},{35,3},{4,36},{36... | collective-permute-start | bytes 1179656 | tf_op jit(solution)/shard_map/ppermute | solution.py:207
  44.3 30.0 %collective-permute-start.15 = (bf16[3,128,1024]{2,1,0:T(8,128)(2,1)S(1)}, bf16[3,128,1024]{2,1,0:T(8,128)(2,1)S(1)}, u32[]{:S(2)}, u32[]{:S(2)}) collective-permute-start(bf16[3,128,1024]{2,1,0:T(8,128)(2,1)S(1)} %shard_map.56), channel_id=1, source_target_pairs={{0,32},{32,0},{1,33},{33,1},{2,34},{34,2},{3,35},{35,3},{4,36},{36... | collective-permute-start | bytes 2359304 | tf_op jit(solution)/shard_map/ppermute | solution.py:208
  46.8 9.0 %collective-permute-start.7 = (bf16[32,16,128]{2,1,0:T(8,128)(2,1)S(1)}, bf16[32,16,128]{2,1,0:T(8,128)(2,1)S(1)}, u32[]{:S(2)}, u32[]{:S(2)}) collective-permute-start(bf16[32,16,128]{2,1,0:T(8,128)(2,1)S(1)} %all-to-all-done.1.refs_4_.refs_8_), channel_id=1, source_target_pairs={{0,64},{64,128},{128,192},{192,0},{1,65},{65,129},{129,193},{193,1... | collective-permute-start | bytes 393224 | tf_op jit(solution)/shard_map/ppermute | solution.py:200
  51.6 6.5 %collective-permute-start.8 = (bf16[32,16,128]{2,1,0:T(8,128)(2,1)S(1)}, bf16[32,16,128]{2,1,0:T(8,128)(2,1)S(1)}, u32[]{:S(2)}, u32[]{:S(2)}) collective-permute-start(bf16[32,16,128]{2,1,0:T(8,128)(2,1)S(1)} %all-to-all-done.1.refs_4_.refs_8_), channel_id=1, source_target_pairs={{0,128},{64,192},{128,0},{192,64},{1,129},{65,193},{129,1},{193,65... | collective-permute-start | bytes 393224 | tf_op jit(solution)/shard_map/ppermute | solution.py:200
  54.3 5.0 %collective-permute-start.9 = (bf16[32,16,128]{2,1,0:T(8,128)(2,1)S(1)}, bf16[32,16,128]{2,1,0:T(8,128)(2,1)S(1)}, u32[]{:S(2)}, u32[]{:S(2)}) collective-permute-start(bf16[32,16,128]{2,1,0:T(8,128)(2,1)S(1)} %all-to-all-done.1.refs_4_.refs_8_), channel_id=1, source_target_pairs={{0,192},{64,0},{128,64},{192,128},{1,193},{65,1},{129,65},{193,129... | collective-permute-start | bytes 393224 | tf_op jit(solution)/shard_map/ppermute | solution.py:200
  60.1 14.2 %collective-permute-start.16 = (bf16[256,1024]{1,0:T(8,128)(2,1)S(1)}, bf16[256,1024]{1,0:T(8,128)(2,1)S(1)}, u32[]{:S(2)}, u32[]{:S(2)}) collective-permute-start(bf16[256,1024]{1,0:T(8,128)(2,1)S(1)} %get-tuple-element.32.refs_4_), channel_id=1, source_target_pairs={{0,1},{1,0},{2,3},{3,2},{4,5},{5,4},{6,7},{7,6},{8,9},{9,8},{10,11... | collective-permute-start | bytes 1572872 | tf_op jit(solution)/shard_map/ppermute | solution.py:220
  60.2 14.1 %collective-permute-start.17 = (bf16[256,1024]{1,0:T(8,128)(2,1)S(1)}, bf16[256,1024]{1,0:T(8,128)(2,1)S(1)}, u32[]{:S(2)}, u32[]{:S(2)}) collective-permute-start(bf16[256,1024]{1,0:T(8,128)(2,1)S(1)} %get-tuple-element.33.refs_5_), channel_id=1, source_target_pairs={{0,1},{1,0},{2,3},{3,2},{4,5},{5,4},{6,7},{7,6},{8,9},{9,8},{10,11... | collective-permute-start | bytes 1572872 | tf_op jit(solution)/shard_map/ppermute | solution.py:220
  60.7 13.6 %collective-permute-start.12 = (bf16[128,1024]{1,0:T(8,128)(2,1)S(1)}, bf16[128,1024]{1,0:T(8,128)(2,1)S(1)}, u32[]{:S(2)}, u32[]{:S(2)}) collective-permute-start(bf16[128,1024]{1,0:T(8,128)(2,1)S(1)} %get-tuple-element.29), channel_id=1, source_target_pairs={{0,192},{64,0},{128,64},{192,128},{1,193},{65,1},{129,65},{193,129... | collective-permute-start | bytes 786440 | tf_op jit(solution)/shard_map/ppermute | solution.py:219
  62.9 11.5 %collective-permute-start.13 = (bf16[128,1024]{1,0:T(8,128)(2,1)S(1)}, bf16[128,1024]{1,0:T(8,128)(2,1)S(1)}, u32[]{:S(2)}, u32[]{:S(2)}) collective-permute-start(bf16[128,1024]{1,0:T(8,128)(2,1)S(1)} %get-tuple-element.30), channel_id=1, source_target_pairs={{0,128},{64,192},{128,0},{192,64},{1,129},{65,193},{129,1},{193,65... | collective-permute-start | bytes 786440 | tf_op jit(solution)/shard_map/ppermute | solution.py:219
  76.6 28.4 %all-to-all-start.2 = ((bf16[64,32,128]{2,1,0:T(8,128)(2,1)}), bf16[64,32,128]{2,1,0:T(8,128)(2,1)S(1)}, u32[]{:S(2)}, u32[]{:S(2)}) async-start(bf16[64,32,128]{2,1,0:T(8,128)(2,1)} %bitcast.1), calls=%async_computation.2 | async-start | bytes 1048576 | tf_op jit(solution)/shard_map/all_to_all | solution.py:156
  88.6 12.1 %collective-permute-start.14 = (bf16[128,1024]{1,0:T(8,128)(2,1)S(1)}, bf16[128,1024]{1,0:T(8,128)(2,1)S(1)}, u32[]{:S(2)}, u32[]{:S(2)}) collective-permute-start(bf16[128,1024]{1,0:T(8,128)(2,1)S(1)} %get-tuple-element.31), channel_id=1, source_target_pairs={{0,64},{64,128},{128,192},{192,0},{1,65},{65,129},{129,193},{193,1... | collective-permute-start | bytes 786440 | tf_op jit(solution)/shard_map/ppermute | solution.py:219

commit v11 on v10

--- a/solution.py
+++ b/solution.py
@@ -115,7 +115,7 @@
 
 def innov_kernel(own_got, jac_got, *refs):
     first, sens, sens_got = refs[:X], refs[X : X + 2], refs[X + 2 : X + 4]
-    parts, jac, both = refs[-3:]
+    own, parts, jac, both = refs[-X - 2], refs[-X - 1 : -2], refs[-2], refs[-1]
     h = lax.axis_index("h")
     for d in range(X):
         for side, ref in ((h, first[d]), (1 - h, jac_got.at[d - 1] if d else own_got)):
@@ -128,13 +128,21 @@
     value = lax.dot_general(
         jac[...], both[...], (((1,), (1,)), ((), ())), preferred_element_type=F32
     )
-    for d in range(X):
-        parts[source(d)] = value[:, d * 128 : (d + 1) * 128].astype(BF16)
+    own[...] = value[:, 0:128]
+    for d in range(1, X):
+        parts[d - 1][...] = value[:, d * 128 : (d + 1) * 128].astype(BF16)
+
+
+def sum_kernel(own, *refs):
+    total = own[...]
+    for ref in refs[:-1]:
+        total += ref[...].astype(F32)
+    refs[-1][...] = total.astype(BF16)
 
 
 def final_kernel(got, out):
     total = got[0].astype(F32)
-    for k in range(1, X * L * Z):
+    for k in range(1, L * Z):
         total += got[k].astype(F32)
     out[...] = total * (1.0 / math.sqrt(PARAMS))
 
@@ -218,9 +226,9 @@
     )
     sens_back = [sens[0]] + [lax.ppermute(sens[d], "x", ring(-d)) for d in range(1, X)]
     sens_got = [lax.ppermute(pair, "c", SWAP) for pair in (low, high)]
-    parts = call(
+    own, *parts = call(
         innov_kernel,
-        shape(X, 512, 128),
+        [shape(512, 128, kind=F32)] + [shape(512, 128)] * (X - 1),
         (own_got, jac_got, *first, low, high, *sens_got),
         VMEM,
         [pltpu.VMEM((512, 2048), BF16)] * 2,
@@ -229,7 +237,9 @@
         vmem=16,
         behind=(sens_back[1], sens_back[2]),
     )
-    shared = over(parts.reshape(X * L * Z, 32, 128), ("x", "l", "z"))
+    parts = [lax.ppermute(parts[d - 1], "x", ring(-d)) for d in range(1, X)]
+    summed = call(sum_kernel, shape(512, 128), (own, *parts), VMEM, nbytes=MIB, vmem=4)
+    shared = over(summed.reshape(L * Z, 32, 128), ("l", "z"))
     innovation = call(final_kernel, shape(32, 128, kind=F32), (shared,), VMEM, nbytes=2**19, vmem=4)
     sensitivity = call(
         assemble_kernel, shape(128, 4096), sens_back, ANY, dma(X), nbytes=2 * MIB

time: 107 us -> 107 us (level)
  waiting for transfers between devices: 38.6 us -> 37.2 us
  starting transfers between devices: 53.4 us -> 54.5 us
    ppermute x3, waiting for transfers between devices: 21.4 us -> 10.7 us  [body(): lax.ppermute(sens[d], 'x', ring(-d))]
    ppermute x0 -> x3, waiting for transfers between devices: none -> 5.11 us  [body(): parts = [lax.ppermute(parts[d - 1], 'x', ring(-d)) for d in range(1, X)]]
    ppermute x0 -> x3, starting transfers between devices: none -> 4.9 us  [body(): parts = [lax.ppermute(parts[d - 1], 'x', ring(-d)) for d in range(1, X)]]
    all_to_all x3, starting transfers between devices: 29 us -> 24.1 us  [over(): return lax.all_to_all(value, axes, split_axis=0, concat_axis=0, tiled=True)]
    all_to_all x3, waiting for transfers between devices: 7.89 us -> 12 us  [over(): return lax.all_to_all(value, axes, split_axis=0, concat_axis=0, tiled=True)]
    pallas_call x9 -> x10, Pallas kernels: 11.4 us -> 11.3 us  [call(): pl.pallas_call(kernel, out_shape=outs, in_specs=[spec] * len(ins) + [ANY]...]
  transfers between devices with their start and end apart: 21 -> 24, of which waited for: 10 -> 11; matrix products, arithmetic and copies ran while one was open for 1% -> 1% of each run, Pallas kernels for 6% -> 7%
where the time goes in v11:
time: 107 us; the launch traced here: 105 us
  starting transfers between devices  54.5 us (51%)
  waiting for transfers between devices  37.2 us (35%)
  Pallas kernels  11.3 us (11%)
  local copies, waits for them, and re-layouts  1.47 us (1%)
    all_to_all x3, starting transfers between devices, over(): return lax.all_to_all(value, axes, split_axis=0, concat_axis=0, tiled=True)  24.1 us
    all_to_all x3, waiting for transfers between devices, over(): return lax.all_to_all(value, axes, split_axis=0, concat_axis=0, tiled=True)  12 us
    pallas_call x10, Pallas kernels, call(): pl.pallas_call(kernel, out_shape=outs, in_specs=[spec] * len(ins) + [ANY]...  11.3 us
    ppermute x3, waiting for transfers between devices, body(): lax.ppermute(sens[d], 'x', ring(-d))  10.7 us
    ppermute x6, starting transfers between devices, body(): lax.ppermute(packed[d], 'x', ring(d))  8.87 us
    ppermute x3, starting transfers between devices, body(): lax.ppermute(sens[d], 'x', ring(-d))  5.26 us
    ppermute x3, waiting for transfers between devices, body(): parts = [lax.ppermute(parts[d - 1], 'x', ring(-d)) for d in range(1, X)]  5.11 us
    ppermute x3, waiting for transfers between devices, body(): panels = [panel] + [lax.ppermute(panel, 'x', ring(d)) for d in range(1, X)]  4.96 us
  transfers between devices with their start and end apart: 24, of which 11 were waited for; matrix products, arithmetic and copies ran while one was open for 1% of the time, Pallas kernels for 7%

profile of v11, /device:TPU:4, one launch (start us, length us, event | category | flops | bytes accessed | tf_op | source)
XLA Modules:
  0.0 105.2 jit_solution(14327615370001207996)
XLA Ops:
  0.6 2.4 %shard_map.50 = (bf16[64,4096]{1,0:T(8,128)(2,1)}, bf16[32,16,128]{2,1,0:T(8,128)(2,1)}) custom-call(bf16[128,4096]{1,0:T(8,128)(2,1)} %jac.3), custom_call_target="tpu_custom_call" | custom-call | bytes 1048576 | tf_op jit(solution)/shard_map/pallas_call | solution.py:27
  3.1 10.0 %all-to-all-start = ((bf16[32,16,128]{2,1,0:T(8,128)(2,1)}), bf16[32,16,128]{2,1,0:T(8,128)(2,1)S(1)}, u32[]{:S(2)}, u32[]{:S(2)}) async-start(bf16[32,16,128]{2,1,0:T(8,128)(2,1)} %get-tuple-element.31), calls=%async_computation | async-start | bytes 262144 | tf_op jit(solution)/shard_map/all_to_all | solution.py:164
  13.9 2.8 %shard_map.51 = (bf16[192,1024]{1,0:T(8,128)(2,1)}, bf16[192,1024]{1,0:T(8,128)(2,1)}, bf16[192,1024]{1,0:T(8,128)(2,1)}, bf16[192,1024]{1,0:T(8,128)(2,1)}) custom-call(bf16[128,4096]{1,0:T(8,128)(2,1)} %jac.3, bf16[64,4096]{1,0:T(8,128)(2,1)} %copy-done.2, bf16[64,4096]{1,0:T(8,128)(2,1)} %cov.1), custom_call_target="tpu_custom_call" | custom-call | bytes 4194304 | tf_op jit(solution)/shard_map/pallas_call | solution.py:27
  16.8 3.0 %collective-permute-start.10 = (bf16[192,1024]{1,0:T(8,128)(2,1)}, bf16[192,1024]{1,0:T(8,128)(2,1)S(1)}, u32[]{:S(2)}, u32[]{:S(2)}) collective-permute-start(bf16[192,1024]{1,0:T(8,128)(2,1)} %get-tuple-element.23.refs_0_), channel_id=1, source_target_pairs={{0,32},{32,0},{1,33},{33,1},{2,34},{34,2},{3,35},{35,3},{4,36},{36... | collective-permute-start | bytes 1179656 | tf_op jit(solution)/shard_map/ppermute | solution.py:206
  24.3 7.0 %all-to-all-start.1 = ((bf16[32,16,128]{2,1,0:T(8,128)(2,1)}), bf16[32,16,128]{2,1,0:T(8,128)(2,1)S(1)}, u32[]{:S(2)}, u32[]{:S(2)}) async-start(bf16[32,16,128]{2,1,0:T(8,128)(2,1)} %broadcast_in_dim.3), calls=%async_computation.1 | async-start | bytes 262144 | tf_op jit(solution)/shard_map/all_to_all | solution.py:164
  33.2 2.7 %collective-permute-start.5 = (bf16[128,1024]{1,0:T(8,128)(2,1)}, bf16[128,1024]{1,0:T(8,128)(2,1)S(1)}, u32[]{:S(2)}, u32[]{:S(2)}) collective-permute-start(bf16[128,1024]{1,0:T(8,128)(2,1)} %get-tuple-element.29), channel_id=1, source_target_pairs={{0,128},{64,192},{128,0},{192,64},{1,129},{65,193},{129,1},{193,65... | collective-permute-start | bytes 786440 | tf_op jit(solution)/shard_map/ppermute | solution.py:212
  35.9 2.0 %collective-permute-start.6 = (bf16[128,1024]{1,0:T(8,128)(2,1)S(1)}, bf16[128,1024]{1,0:T(8,128)(2,1)S(1)}, u32[]{:S(2)}, u32[]{:S(2)}) collective-permute-start(bf16[128,1024]{1,0:T(8,128)(2,1)S(1)} %get-tuple-element.30), channel_id=1, source_target_pairs={{0,192},{64,0},{128,64},{192,128},{1,193},{65,1},{129,65},{193,129... | collective-permute-start | bytes 786440 | tf_op jit(solution)/shard_map/ppermute | solution.py:212
  37.9 3.8 %all-to-all-done.1.refs_4_.refs_8_ = bf16[32,16,128]{2,1,0:T(8,128)(2,1)S(1)} async-done(((bf16[32,16,128]{2,1,0:T(8,128)(2,1)}), bf16[32,16,128]{2,1,0:T(8,128)(2,1)S(1)}, u32[]{:S(2)}, u32[]{:S(2)}) %all-to-all-start.1) | async-done | bytes 131104 | tf_op jit(solution)/shard_map/all_to_all | solution.py:164
  43.0 1.2 %collective-permute-start.11 = (bf16[3,64,1024]{2,1,0:T(8,128)(2,1)S(1)}, bf16[3,64,1024]{2,1,0:T(8,128)(2,1)S(1)}, u32[]{:S(2)}, u32[]{:S(2)}) collective-permute-start(bf16[3,64,1024]{2,1,0:T(8,128)(2,1)S(1)} %shard_map.53.refs_3_), channel_id=1, source_target_pairs={{0,32},{32,0},{1,33},{33,1},{2,34},{34,2},{3,35},{35,3},{4,36},{36... | collective-permute-start | bytes 1179656 | tf_op jit(solution)/shard_map/ppermute | solution.py:215
  44.3 2.5 %collective-permute-start.15 = (bf16[3,128,1024]{2,1,0:T(8,128)(2,1)S(1)}, bf16[3,128,1024]{2,1,0:T(8,128)(2,1)S(1)}, u32[]{:S(2)}, u32[]{:S(2)}) collective-permute-start(bf16[3,128,1024]{2,1,0:T(8,128)(2,1)S(1)} %shard_map.56), channel_id=1, source_target_pairs={{0,32},{32,0},{1,33},{33,1},{2,34},{34,2},{3,35},{35,3},{4,36},{36... | collective-permute-start | bytes 2359304 | tf_op jit(solution)/shard_map/ppermute | solution.py:216
  48.0 3.6 %collective-permute-done.5.refs_6_ = bf16[128,1024]{1,0:T(8,128)(2,1)S(1)} collective-permute-done((bf16[128,1024]{1,0:T(8,128)(2,1)}, bf16[128,1024]{1,0:T(8,128)(2,1)S(1)}, u32[]{:S(2)}, u32[]{:S(2)}) %collective-permute-start.5) | collective-permute-done | bytes 262176 | tf_op jit(solution)/shard_map/ppermute | solution.py:212
  51.6 2.7 %collective-permute-start.8 = (bf16[32,16,128]{2,1,0:T(8,128)(2,1)S(1)}, bf16[32,16,128]{2,1,0:T(8,128)(2,1)S(1)}, u32[]{:S(2)}, u32[]{:S(2)}) collective-permute-start(bf16[32,16,128]{2,1,0:T(8,128)(2,1)S(1)} %all-to-all-done.1.refs_4_.refs_8_), channel_id=1, source_target_pairs={{0,128},{64,192},{128,0},{192,64},{1,129},{65,193},{129,1},{193,65... | collective-permute-start | bytes 393224 | tf_op jit(solution)/shard_map/ppermute | solution.py:208
  54.3 1.5 %collective-permute-done.7.refs_9_ = bf16[32,16,128]{2,1,0:T(8,128)(2,1)S(1)} collective-permute-done((bf16[32,16,128]{2,1,0:T(8,128)(2,1)S(1)}, bf16[32,16,128]{2,1,0:T(8,128)(2,1)S(1)}, u32[]{:S(2)}, u32[]{:S(2)}) %collective-permute-start.7) | collective-permute-done | bytes 131104 | tf_op jit(solution)/shard_map/ppermute | solution.py:208
  55.8 2.3 %collective-permute-done.8.refs_10_ = bf16[32,16,128]{2,1,0:T(8,128)(2,1)S(1)} collective-permute-done((bf16[32,16,128]{2,1,0:T(8,128)(2,1)S(1)}, bf16[32,16,128]{2,1,0:T(8,128)(2,1)S(1)}, u32[]{:S(2)}, u32[]{:S(2)}) %collective-permute-start.8) | collective-permute-done | bytes 131104 | tf_op jit(solution)/shard_map/ppermute | solution.py:208
  60.7 2.1 %collective-permute-start.12 = (bf16[128,1024]{1,0:T(8,128)(2,1)S(1)}, bf16[128,1024]{1,0:T(8,128)(2,1)S(1)}, u32[]{:S(2)}, u32[]{:S(2)}) collective-permute-start(bf16[128,1024]{1,0:T(8,128)(2,1)S(1)} %get-tuple-element.33), channel_id=1, source_target_pairs={{0,192},{64,0},{128,64},{192,128},{1,193},{65,1},{129,65},{193,129... | collective-permute-start | bytes 786440 | tf_op jit(solution)/shard_map/ppermute | solution.py:227
  63.7 10.7 %collective-permute-done.12.refs_1_.refs_8_ = bf16[128,1024]{1,0:T(8,128)(2,1)S(1)} collective-permute-done((bf16[128,1024]{1,0:T(8,128)(2,1)S(1)}, bf16[128,1024]{1,0:T(8,128)(2,1)S(1)}, u32[]{:S(2)}, u32[]{:S(2)}) %collective-permute-start.12) | collective-permute-done | bytes 262176 | tf_op jit(solution)/shard_map/ppermute | solution.py:227
  74.4 1.4 %shard_map.57 = (f32[512,128]{1,0:T(8,128)S(1)}, bf16[512,128]{1,0:T(8,128)(2,1)S(1)}, bf16[512,128]{1,0:T(8,128)(2,1)S(1)}, bf16[512,128]{1,0:T(8,128)(2,1)S(1)}) custom-call(bf16[192,1024]{1,0:T(8,128)(2,1)S(1)} %collective-permute-done.10.refs_3_.refs_12_.own_got, bf16[3,128,1024]{2,1,0:T(8,128)(2,1)S(1)} %collective-permute-done.15.jac_got, ...), custom_call_target="tpu_custom_call" | custom-call | flops 1073741824 | bytes 2097152 | tf_op jit(solution)/shard_map/pallas_call | solution.py:27
  75.8 2.5 %collective-permute-start.18 = (bf16[512,128]{1,0:T(8,128)(2,1)S(1)}, bf16[512,128]{1,0:T(8,128)(2,1)S(1)}, u32[]{:S(2)}, u32[]{:S(2)}) collective-permute-start(bf16[512,128]{1,0:T(8,128)(2,1)S(1)} %get-tuple-element.39), channel_id=1, source_target_pairs={{0,192},{64,0},{128,64},{192,128},{1,193},{65,1},{129,65},{193,129... | collective-permute-start | bytes 393224 | tf_op jit(solution)/shard_map/ppermute | solution.py:240
  78.3 2.4 %collective-permute-start.19 = (bf16[512,128]{1,0:T(8,128)(2,1)S(1)}, bf16[512,128]{1,0:T(8,128)(2,1)S(1)}, u32[]{:S(2)}, u32[]{:S(2)}) collective-permute-start(bf16[512,128]{1,0:T(8,128)(2,1)S(1)} %get-tuple-element.40), channel_id=1, source_target_pairs={{0,128},{64,192},{128,0},{192,64},{1,129},{65,193},{129,1},{193,65... | collective-permute-start | bytes 393224 | tf_op jit(solution)/shard_map/ppermute | solution.py:240
  80.7 2.3 %collective-permute-start.14 = (bf16[128,1024]{1,0:T(8,128)(2,1)S(1)}, bf16[128,1024]{1,0:T(8,128)(2,1)S(1)}, u32[]{:S(2)}, u32[]{:S(2)}) collective-permute-start(bf16[128,1024]{1,0:T(8,128)(2,1)S(1)} %get-tuple-element.35), channel_id=1, source_target_pairs={{0,64},{64,128},{128,192},{192,0},{1,65},{65,129},{129,193},{193,1... | collective-permute-start | bytes 786440 | tf_op jit(solution)/shard_map/ppermute | solution.py:227
  83.0 3.2 %collective-permute-done.19.refs_1_ = bf16[512,128]{1,0:T(8,128)(2,1)S(1)} collective-permute-done((bf16[512,128]{1,0:T(8,128)(2,1)S(1)}, bf16[512,128]{1,0:T(8,128)(2,1)S(1)}, u32[]{:S(2)}, u32[]{:S(2)}) %collective-permute-start.19) | collective-permute-done | bytes 131104 | tf_op jit(solution)/shard_map/ppermute | solution.py:240
  86.2 1.9 %collective-permute-done.20.refs_2_ = bf16[512,128]{1,0:T(8,128)(2,1)S(1)} collective-permute-done((bf16[512,128]{1,0:T(8,128)(2,1)S(1)}, bf16[512,128]{1,0:T(8,128)(2,1)S(1)}, u32[]{:S(2)}, u32[]{:S(2)}) %collective-permute-start.20) | collective-permute-done | bytes 131104 | tf_op jit(solution)/shard_map/ppermute | solution.py:240
  88.8 7.2 %all-to-all-start.2 = ((bf16[16,32,128]{2,1,0:T(8,128)(2,1)}), bf16[16,32,128]{2,1,0:T(8,128)(2,1)S(1)}, u32[]{:S(2)}, u32[]{:S(2)}) async-start(bf16[16,32,128]{2,1,0:T(8,128)(2,1)} %bitcast.1), calls=%async_computation.2 | async-start | bytes 262144 | tf_op jit(solution)/shard_map/all_to_all | solution.py:164
  97.0 7.5 %all-to-all-done.2.got = bf16[16,32,128]{2,1,0:T(8,128)(2,1)S(1)} async-done(((bf16[16,32,128]{2,1,0:T(8,128)(2,1)}), bf16[16,32,128]{2,1,0:T(8,128)(2,1)S(1)}, u32[]{:S(2)}, u32[]{:S(2)}) %all-to-all-start.2) | async-done | bytes 131104 | tf_op jit(solution)/shard_map/all_to_all | solution.py:164
  (42 shorter events, 15.6 us)
Async XLA Ops:
  3.0 10.1 %collective-permute-start = (bf16[64,4096]{1,0:T(8,128)(2,1)}, bf16[64,4096]{1,0:T(8,128)(2,1)S(1)}, u32[]{:S(2)}, u32[]{:S(2)}) collective-permute-start(bf16[64,4096]{1,0:T(8,128)(2,1)} %get-tuple-element.22), channel_id=1, source_target_pairs={{0,1},{1,0},{2,3},{3,2},{4,5},{5,4},{6,7},{7,6},{8,9},{9,8},{10,11... | collective-permute-start | bytes 1572872 | tf_op jit(solution)/shard_map/ppermute | solution.py:193
  3.1 20.4 %all-to-all-start = ((bf16[32,16,128]{2,1,0:T(8,128)(2,1)}), bf16[32,16,128]{2,1,0:T(8,128)(2,1)S(1)}, u32[]{:S(2)}, u32[]{:S(2)}) async-start(bf16[32,16,128]{2,1,0:T(8,128)(2,1)} %get-tuple-element.31), calls=%async_computation | async-start | bytes 262144 | tf_op jit(solution)/shard_map/all_to_all | solution.py:164
  16.8 16.5 %collective-permute-start.10 = (bf16[192,1024]{1,0:T(8,128)(2,1)}, bf16[192,1024]{1,0:T(8,128)(2,1)S(1)}, u32[]{:S(2)}, u32[]{:S(2)}) collective-permute-start(bf16[192,1024]{1,0:T(8,128)(2,1)} %get-tuple-element.23.refs_0_), channel_id=1, source_target_pairs={{0,32},{32,0},{1,33},{33,1},{2,34},{34,2},{3,35},{35,3},{4,36},{36... | collective-permute-start | bytes 1179656 | tf_op jit(solution)/shard_map/ppermute | solution.py:206
  19.8 16.1 %collective-permute-start.1 = (bf16[192,1024]{1,0:T(8,128)(2,1)}, bf16[192,1024]{1,0:T(8,128)(2,1)S(1)}, u32[]{:S(2)}, u32[]{:S(2)}) collective-permute-start(bf16[192,1024]{1,0:T(8,128)(2,1)} %get-tuple-element.24), channel_id=1, source_target_pairs={{0,64},{64,128},{128,192},{192,0},{1,65},{65,129},{129,193},{193,1... | collective-permute-start | bytes 1179656 | tf_op jit(solution)/shard_map/ppermute | solution.py:207
  21.0 20.8 %collective-permute-start.2 = (bf16[192,1024]{1,0:T(8,128)(2,1)}, bf16[192,1024]{1,0:T(8,128)(2,1)S(1)}, u32[]{:S(2)}, u32[]{:S(2)}) collective-permute-start(bf16[192,1024]{1,0:T(8,128)(2,1)} %get-tuple-element.25), channel_id=1, source_target_pairs={{0,128},{64,192},{128,0},{192,64},{1,129},{65,193},{129,1},{193,65... | collective-permute-start | bytes 1179656 | tf_op jit(solution)/shard_map/ppermute | solution.py:207
  21.8 20.7 %collective-permute-start.3 = (bf16[192,1024]{1,0:T(8,128)(2,1)}, bf16[192,1024]{1,0:T(8,128)(2,1)S(1)}, u32[]{:S(2)}, u32[]{:S(2)}) collective-permute-start(bf16[192,1024]{1,0:T(8,128)(2,1)} %get-tuple-element.26), channel_id=1, source_target_pairs={{0,192},{64,0},{128,64},{192,128},{1,193},{65,1},{129,65},{193,129... | collective-permute-start | bytes 1179656 | tf_op jit(solution)/shard_map/ppermute | solution.py:207
  24.3 17.5 %all-to-all-start.1 = ((bf16[32,16,128]{2,1,0:T(8,128)(2,1)}), bf16[32,16,128]{2,1,0:T(8,128)(2,1)S(1)}, u32[]{:S(2)}, u32[]{:S(2)}) async-start(bf16[32,16,128]{2,1,0:T(8,128)(2,1)} %broadcast_in_dim.3), calls=%async_computation.1 | async-start | bytes 262144 | tf_op jit(solution)/shard_map/all_to_all | solution.py:164
  32.2 14.6 %collective-permute-start.4 = (bf16[128,1024]{1,0:T(8,128)(2,1)}, bf16[128,1024]{1,0:T(8,128)(2,1)S(1)}, u32[]{:S(2)}, u32[]{:S(2)}) collective-permute-start(bf16[128,1024]{1,0:T(8,128)(2,1)} %get-tuple-element.28), channel_id=1, source_target_pairs={{0,64},{64,128},{128,192},{192,0},{1,65},{65,129},{129,193},{193,1... | collective-permute-start | bytes 786440 | tf_op jit(solution)/shard_map/ppermute | solution.py:212
  33.2 18.4 %collective-permute-start.5 = (bf16[128,1024]{1,0:T(8,128)(2,1)}, bf16[128,1024]{1,0:T(8,128)(2,1)S(1)}, u32[]{:S(2)}, u32[]{:S(2)}) collective-permute-start(bf16[128,1024]{1,0:T(8,128)(2,1)} %get-tuple-element.29), channel_id=1, source_target_pairs={{0,128},{64,192},{128,0},{192,64},{1,129},{65,193},{129,1},{193,65... | collective-permute-start | bytes 786440 | tf_op jit(solution)/shard_map/ppermute | solution.py:212
  35.9 18.4 %collective-permute-start.6 = (bf16[128,1024]{1,0:T(8,128)(2,1)S(1)}, bf16[128,1024]{1,0:T(8,128)(2,1)S(1)}, u32[]{:S(2)}, u32[]{:S(2)}) collective-permute-start(bf16[128,1024]{1,0:T(8,128)(2,1)S(1)} %get-tuple-element.30), channel_id=1, source_target_pairs={{0,192},{64,0},{128,64},{192,128},{1,193},{65,1},{129,65},{193,129... | collective-permute-start | bytes 786440 | tf_op jit(solution)/shard_map/ppermute | solution.py:212
  43.0 16.3 %collective-permute-start.11 = (bf16[3,64,1024]{2,1,0:T(8,128)(2,1)S(1)}, bf16[3,64,1024]{2,1,0:T(8,128)(2,1)S(1)}, u32[]{:S(2)}, u32[]{:S(2)}) collective-permute-start(bf16[3,64,1024]{2,1,0:T(8,128)(2,1)S(1)} %shard_map.53.refs_3_), channel_id=1, source_target_pairs={{0,32},{32,0},{1,33},{33,1},{2,34},{34,2},{3,35},{35,3},{4,36},{36... | collective-permute-start | bytes 1179656 | tf_op jit(solution)/shard_map/ppermute | solution.py:215
  44.3 30.0 %collective-permute-start.15 = (bf16[3,128,1024]{2,1,0:T(8,128)(2,1)S(1)}, bf16[3,128,1024]{2,1,0:T(8,128)(2,1)S(1)}, u32[]{:S(2)}, u32[]{:S(2)}) collective-permute-start(bf16[3,128,1024]{2,1,0:T(8,128)(2,1)S(1)} %shard_map.56), channel_id=1, source_target_pairs={{0,32},{32,0},{1,33},{33,1},{2,34},{34,2},{3,35},{35,3},{4,36},{36... | collective-permute-start | bytes 2359304 | tf_op jit(solution)/shard_map/ppermute | solution.py:216
  46.8 9.0 %collective-permute-start.7 = (bf16[32,16,128]{2,1,0:T(8,128)(2,1)S(1)}, bf16[32,16,128]{2,1,0:T(8,128)(2,1)S(1)}, u32[]{:S(2)}, u32[]{:S(2)}) collective-permute-start(bf16[32,16,128]{2,1,0:T(8,128)(2,1)S(1)} %all-to-all-done.1.refs_4_.refs_8_), channel_id=1, source_target_pairs={{0,64},{64,128},{128,192},{192,0},{1,65},{65,129},{129,193},{193,1... | collective-permute-start | bytes 393224 | tf_op jit(solution)/shard_map/ppermute | solution.py:208
  51.6 6.5 %collective-permute-start.8 = (bf16[32,16,128]{2,1,0:T(8,128)(2,1)S(1)}, bf16[32,16,128]{2,1,0:T(8,128)(2,1)S(1)}, u32[]{:S(2)}, u32[]{:S(2)}) collective-permute-start(bf16[32,16,128]{2,1,0:T(8,128)(2,1)S(1)} %all-to-all-done.1.refs_4_.refs_8_), channel_id=1, source_target_pairs={{0,128},{64,192},{128,0},{192,64},{1,129},{65,193},{129,1},{193,65... | collective-permute-start | bytes 393224 | tf_op jit(solution)/shard_map/ppermute | solution.py:208
  54.3 5.0 %collective-permute-start.9 = (bf16[32,16,128]{2,1,0:T(8,128)(2,1)S(1)}, bf16[32,16,128]{2,1,0:T(8,128)(2,1)S(1)}, u32[]{:S(2)}, u32[]{:S(2)}) collective-permute-start(bf16[32,16,128]{2,1,0:T(8,128)(2,1)S(1)} %all-to-all-done.1.refs_4_.refs_8_), channel_id=1, source_target_pairs={{0,192},{64,0},{128,64},{192,128},{1,193},{65,1},{129,65},{193,129... | collective-permute-start | bytes 393224 | tf_op jit(solution)/shard_map/ppermute | solution.py:208
  60.1 14.2 %collective-permute-start.16 = (bf16[256,1024]{1,0:T(8,128)(2,1)S(1)}, bf16[256,1024]{1,0:T(8,128)(2,1)S(1)}, u32[]{:S(2)}, u32[]{:S(2)}) collective-permute-start(bf16[256,1024]{1,0:T(8,128)(2,1)S(1)} %get-tuple-element.36.refs_4_), channel_id=1, source_target_pairs={{0,1},{1,0},{2,3},{3,2},{4,5},{5,4},{6,7},{7,6},{8,9},{9,8},{10,11... | collective-permute-start | bytes 1572872 | tf_op jit(solution)/shard_map/ppermute | solution.py:228
  60.2 14.1 %collective-permute-start.17 = (bf16[256,1024]{1,0:T(8,128)(2,1)S(1)}, bf16[256,1024]{1,0:T(8,128)(2,1)S(1)}, u32[]{:S(2)}, u32[]{:S(2)}) collective-permute-start(bf16[256,1024]{1,0:T(8,128)(2,1)S(1)} %get-tuple-element.37.refs_5_), channel_id=1, source_target_pairs={{0,1},{1,0},{2,3},{3,2},{4,5},{5,4},{6,7},{7,6},{8,9},{9,8},{10,11... | collective-permute-start | bytes 1572872 | tf_op jit(solution)/shard_map/ppermute | solution.py:228
  60.7 13.6 %collective-permute-start.12 = (bf16[128,1024]{1,0:T(8,128)(2,1)S(1)}, bf16[128,1024]{1,0:T(8,128)(2,1)S(1)}, u32[]{:S(2)}, u32[]{:S(2)}) collective-permute-start(bf16[128,1024]{1,0:T(8,128)(2,1)S(1)} %get-tuple-element.33), channel_id=1, source_target_pairs={{0,192},{64,0},{128,64},{192,128},{1,193},{65,1},{129,65},{193,129... | collective-permute-start | bytes 786440 | tf_op jit(solution)/shard_map/ppermute | solution.py:227
  62.9 11.5 %collective-permute-start.13 = (bf16[128,1024]{1,0:T(8,128)(2,1)S(1)}, bf16[128,1024]{1,0:T(8,128)(2,1)S(1)}, u32[]{:S(2)}, u32[]{:S(2)}) collective-permute-start(bf16[128,1024]{1,0:T(8,128)(2,1)S(1)} %get-tuple-element.34), channel_id=1, source_target_pairs={{0,128},{64,192},{128,0},{192,64},{1,129},{65,193},{129,1},{193,65... | collective-permute-start | bytes 786440 | tf_op jit(solution)/shard_map/ppermute | solution.py:227
  75.8 7.2 %collective-permute-start.18 = (bf16[512,128]{1,0:T(8,128)(2,1)S(1)}, bf16[512,128]{1,0:T(8,128)(2,1)S(1)}, u32[]{:S(2)}, u32[]{:S(2)}) collective-permute-start(bf16[512,128]{1,0:T(8,128)(2,1)S(1)} %get-tuple-element.39), channel_id=1, source_target_pairs={{0,192},{64,0},{128,64},{192,128},{1,193},{65,1},{129,65},{193,129... | collective-permute-start | bytes 393224 | tf_op jit(solution)/shard_map/ppermute | solution.py:240
  78.3 7.9 %collective-permute-start.19 = (bf16[512,128]{1,0:T(8,128)(2,1)S(1)}, bf16[512,128]{1,0:T(8,128)(2,1)S(1)}, u32[]{:S(2)}, u32[]{:S(2)}) collective-permute-start(bf16[512,128]{1,0:T(8,128)(2,1)S(1)} %get-tuple-element.40), channel_id=1, source_target_pairs={{0,128},{64,192},{128,0},{192,64},{1,129},{65,193},{129,1},{193,65... | collective-permute-start | bytes 393224 | tf_op jit(solution)/shard_map/ppermute | solution.py:240
  80.7 7.4 %collective-permute-start.20 = (bf16[512,128]{1,0:T(8,128)(2,1)S(1)}, bf16[512,128]{1,0:T(8,128)(2,1)S(1)}, u32[]{:S(2)}, u32[]{:S(2)}) collective-permute-start(bf16[512,128]{1,0:T(8,128)(2,1)S(1)} %get-tuple-element.41), channel_id=1, source_target_pairs={{0,64},{64,128},{128,192},{192,0},{1,65},{65,129},{129,193},{193,1... | collective-permute-start | bytes 393224 | tf_op jit(solution)/shard_map/ppermute | solution.py:240
  80.7 15.3 %collective-permute-start.14 = (bf16[128,1024]{1,0:T(8,128)(2,1)S(1)}, bf16[128,1024]{1,0:T(8,128)(2,1)S(1)}, u32[]{:S(2)}, u32[]{:S(2)}) collective-permute-start(bf16[128,1024]{1,0:T(8,128)(2,1)S(1)} %get-tuple-element.35), channel_id=1, source_target_pairs={{0,64},{64,128},{128,192},{192,0},{1,65},{65,129},{129,193},{193,1... | collective-permute-start | bytes 786440 | tf_op jit(solution)/shard_map/ppermute | solution.py:227
  88.8 15.7 %all-to-all-start.2 = ((bf16[16,32,128]{2,1,0:T(8,128)(2,1)}), bf16[16,32,128]{2,1,0:T(8,128)(2,1)S(1)}, u32[]{:S(2)}, u32[]{:S(2)}) async-start(bf16[16,32,128]{2,1,0:T(8,128)(2,1)} %bitcast.1), calls=%async_computation.2 | async-start | bytes 262144 | tf_op jit(solution)/shard_map/all_to_all | solution.py:164
  (3 other events, 35.3 us)

commit v12 on v8

--- a/solution.py
+++ b/solution.py
@@ -23,13 +23,14 @@
     return lax.rem(lax.axis_index("x") + X - d, X)
 
 
-def call(kernel, outs, ins, spec, scratch=(), flops=0, nbytes=0, vmem=1, behind=()):
+def call(kernel, outs, ins, spec, scratch=(), flops=0, nbytes=0, vmem=1, behind=(), aliases=None):
     return pl.pallas_call(
         kernel,
         out_shape=outs,
         in_specs=[spec] * len(ins) + [ANY] * len(behind),
         out_specs=jax.tree.map(lambda _: spec, outs),
         scratch_shapes=list(scratch),
+        input_output_aliases=aliases or {},
         cost_estimate=pl.CostEstimate(flops=flops, bytes_accessed=nbytes, transcendentals=0),
         compiler_params=pltpu.CompilerParams(vmem_limit_bytes=vmem * MIB),
     )(*ins, *behind)
@@ -51,29 +52,27 @@
     return pl.ds(pl.multiple_of(half * 64 + core * 32, 32), 32)
 
 
-def give_kernel(jac, give, panel, sems):
-    other = 1 - lax.axis_index("c")
-    copies = [(jac.at[slab(k, other), :], give.at[pl.ds(k * 32, 32), :]) for k in range(2)]
+def part(d):
+    at = lax.rem(lax.axis_index("x") + d, X)
+    return pl.ds(pl.multiple_of(at * 1024, 1024), 1024)
+
+
+def give_kernel(jac, cov, give, panel, *refs):
+    outs, sems = refs[:X], refs[X]
+    core = lax.axis_index("c")
+    copies = [(jac.at[slab(k, 1 - core), :], give.at[pl.ds(k * 32, 32), :]) for k in range(2)]
     for k in range(8):
         for n in range(4):
             copies.append((jac.at[pl.ds(k * 16, 16), pl.ds(n * 128, 128)], panel.at[k * 4 + n]))
-    run_copies(copies, sems)
-
-
-def part(d):
-    at = lax.rem(lax.axis_index("x") + d, X)
-    return pl.ds(pl.multiple_of(at * 1024, 1024), 1024)
-
-
-def pack_kernel(jac, got, cov, *refs):
-    outs, sems = refs[:X], refs[X]
-    core = lax.axis_index("c")
-    copies = []
     for d in range(X):
         copies += [(jac.at[slab(n, core), part(d)], outs[d].at[pl.ds(n * 32, 32), :]) for n in range(2)]
-        copies.append((got.at[:, part(d)], outs[d].at[pl.ds(64, 64), :]))
         copies.append((cov.at[:, part(d)], outs[d].at[pl.ds(128, 64), :]))
     run_copies(copies, sems)
+
+
+def fill_kernel(got, *refs):
+    outs, sems = refs[X : 2 * X], refs[2 * X]
+    run_copies([(got.at[:, part(d)], outs[d].at[pl.ds(64, 64), :]) for d in range(X)], sems)
 
 
 def carry_kernel(carry, *refs):
@@ -172,24 +171,25 @@
     )
 
 def body(jacobian, cov_rows, sens_carry):
-    give, panel = call(
+    give, panel, *packed = call(
         give_kernel,
-        [shape(64, 4096), shape(32, 16, 128)],
-        (jacobian,),
+        [shape(64, 4096), shape(32, 16, 128)] + [shape(192, 1024)] * X,
+        (jacobian, cov_rows),
         ANY,
-        dma(34),
-        nbytes=MIB,
+        dma(34 + 3 * X),
+        nbytes=4 * MIB,
     )
     got = lax.ppermute(give, "c", SWAP)
     mine = over(panel, ("l", "z", "c"))[0]
     panel = over(jnp.broadcast_to(mine, (32, 16, 128)), ("l", "z", "c"))
     packed = call(
-        pack_kernel,
+        fill_kernel,
         [shape(192, 1024)] * X,
-        (jacobian, got, cov_rows),
+        (got, *packed),
         ANY,
-        dma(4 * X),
-        nbytes=4 * MIB,
+        dma(X),
+        nbytes=MIB,
+        aliases={1 + d: d for d in range(X)},
     )
     own_got = lax.ppermute(packed[0], "h", SWAP)
     first = [packed[0]] + [lax.ppermute(packed[d], "x", ring(d)) for d in range(1, X)]
@@ -198,8 +198,8 @@
         carry_kernel, [shape(128, 1024)] * X, (sens_carry,), ANY, dma(X), nbytes=2 * MIB
     )
     carry = [packed[0]] + [lax.ppermute(packed[d], "x", ring(d)) for d in range(1, X)]
-    cov_rest = join(first, 128, 64, (own_got, panel))
-    jac_rest = join(first, 0, 128, (cov_rest,))
+    cov_rest = join(first, 128, 64, (panel,))
+    jac_rest = join(first, 0, 128, (cov_rest, own_got))
     cov_got = lax.ppermute(cov_rest, "h", SWAP)
     jac_got = lax.ppermute(jac_rest, "h", SWAP)
     *sens, low, high = call(

time: 107 us -> 107 us (level)
  starting transfers between devices: 49.1 us -> 54.6 us
  waiting for transfers between devices: 41.4 us -> 37.3 us
  local copies, waits for them, and re-layouts: 6.18 us -> 5.06 us
    ppermute x6, starting transfers between devices: 5.88 us -> 9.02 us  [body(): lax.ppermute(packed[d], 'x', ring(d))]
    ppermute x6, waiting for transfers between devices: 4.89 us -> 2.47 us  [body(): lax.ppermute(packed[d], 'x', ring(d))]
    ppermute x1, waiting for transfers between devices: 9.51 us -> 8.02 us  [body(): jac_got = lax.ppermute(jac_rest, 'h', SWAP)]
    ppermute x1, waiting for transfers between devices: 0.01 us -> 1.16 us  [body(): own_got = lax.ppermute(packed[0], 'h', SWAP)]
    unnamed x24 -> x18, local copies, waits for them, and re-layouts: 5.51 us -> 4.37 us
    all_to_all x3, starting transfers between devices: 24.3 us -> 25.4 us  [over(): return lax.all_to_all(value, axes, split_axis=0, concat_axis=0, tiled=True)]
  transfers between devices with their start and end apart: 21 -> 21, of which waited for: 9 -> 10; matrix products, arithmetic and copies ran while one was open for 1% -> 1% of each run, Pallas kernels for 4% -> 4%
where the time goes in v12:
time: 107 us; the launch traced here: 106 us
  starting transfers between devices  54.6 us (51%)
  waiting for transfers between devices  37.3 us (35%)
  Pallas kernels  8.46 us (8%)
  local copies, waits for them, and re-layouts  5.06 us (5%)
    all_to_all x3, starting transfers between devices, over(): return lax.all_to_all(value, axes, split_axis=0, concat_axis=0, tiled=True)  25.4 us
    ppermute x3, waiting for transfers between devices, body(): lax.ppermute(sens[d], 'x', ring(-d))  18.7 us
    ppermute x6, starting transfers between devices, body(): lax.ppermute(packed[d], 'x', ring(d))  9.02 us
    pallas_call x9, Pallas kernels, call(): pl.pallas_call(kernel, out_shape=outs, in_specs=[spec] * len(ins) + [ANY]...  8.46 us
    ppermute x1, waiting for transfers between devices, body(): jac_got = lax.ppermute(jac_rest, 'h', SWAP)  8.02 us
    unnamed x18, local copies, waits for them, and re-layouts  4.37 us
    ppermute x3, starting transfers between devices, body(): panels = [panel] + [lax.ppermute(panel, 'x', ring(d)) for d in range(1, X)]  4.06 us
    all_to_all x3, waiting for transfers between devices, over(): return lax.all_to_all(value, axes, split_axis=0, concat_axis=0, tiled=True)  3.88 us
  transfers between devices with their start and end apart: 21, of which 10 were waited for; matrix products, arithmetic and copies ran while one was open for 1% of the time, Pallas kernels for 4%

profile of v12, /device:TPU:1, one launch (start us, length us, event | category | flops | bytes accessed | tf_op | source)
XLA Modules:
  0.0 106.3 jit_solution(12487877711207752749)
XLA Ops:
  0.6 1.2 %copy-done = bf16[128,4096]{1,0:T(8,128)(2,1)S(1)} copy-done((bf16[128,4096]{1,0:T(8,128)(2,1)S(1)}, bf16[128,4096]{1,0:T(8,128)(2,1)}, u32[]{:S(2)}) %copy-start) | copy-done | bytes 1048600
  2.9 1.4 %shard_map.50 = (bf16[64,4096]{1,0:T(8,128)(2,1)S(1)}, bf16[32,16,128]{2,1,0:T(8,128)(2,1)}, bf16[192,1024]{1,0:T(8,128)(2,1)S(1)}, bf16[192,1024]{1,0:T(8,128)(...) custom-call(bf16[128,4096]{1,0:T(8,128)(2,1)S(1)} %copy-done, bf16[64,4096]{1,0:T(8,128)(2,1)S(1)} %copy-done.2), custom_call_target="tpu_custom_call" | custom-call | bytes 4194304 | tf_op jit(solution)/shard_map/pallas_call | solution.py:27
  4.3 3.3 %collective-permute-start = (bf16[64,4096]{1,0:T(8,128)(2,1)S(1)}, bf16[64,4096]{1,0:T(8,128)(2,1)S(1)}, u32[]{:S(2)}, u32[]{:S(2)}) collective-permute-start(bf16[64,4096]{1,0:T(8,128)(2,1)S(1)} %get-tuple-element.22), channel_id=1, source_target_pairs={{0,1},{1,0},{2,3},{3,2},{4,5},{5,4},{6,7},{7,6},{8,9},{9,8},{10,11... | collective-permute-start | bytes 1572872 | tf_op jit(solution)/shard_map/ppermute | solution.py:182
  7.6 8.0 %all-to-all-start = ((bf16[32,16,128]{2,1,0:T(8,128)(2,1)}), bf16[32,16,128]{2,1,0:T(8,128)(2,1)S(1)}, u32[]{:S(2)}, u32[]{:S(2)}) async-start(bf16[32,16,128]{2,1,0:T(8,128)(2,1)} %get-tuple-element.35), calls=%async_computation | async-start | bytes 262144 | tf_op jit(solution)/shard_map/all_to_all | solution.py:155
  16.5 1.3 %collective-permute-start.1 = (bf16[192,1024]{1,0:T(8,128)(2,1)S(1)}, bf16[192,1024]{1,0:T(8,128)(2,1)S(1)}, u32[]{:S(2)}, u32[]{:S(2)}) collective-permute-start(bf16[192,1024]{1,0:T(8,128)(2,1)S(1)} %get-tuple-element.28), channel_id=1, source_target_pairs={{0,64},{64,128},{128,192},{192,0},{1,65},{65,129},{129,193},{193,1... | collective-permute-start | bytes 1179656 | tf_op jit(solution)/shard_map/ppermute | solution.py:195
  17.8 2.5 %collective-permute-start.2 = (bf16[192,1024]{1,0:T(8,128)(2,1)}, bf16[192,1024]{1,0:T(8,128)(2,1)S(1)}, u32[]{:S(2)}, u32[]{:S(2)}) collective-permute-start(bf16[192,1024]{1,0:T(8,128)(2,1)} %get-tuple-element.29), channel_id=1, source_target_pairs={{0,128},{64,192},{128,0},{192,64},{1,129},{65,193},{129,1},{193,65... | collective-permute-start | bytes 1179656 | tf_op jit(solution)/shard_map/ppermute | solution.py:195
  21.4 3.3 %all-to-all-done = bf16[32,16,128]{2,1,0:T(8,128)(2,1)S(1)} async-done(((bf16[32,16,128]{2,1,0:T(8,128)(2,1)}), bf16[32,16,128]{2,1,0:T(8,128)(2,1)S(1)}, u32[]{:S(2)}, u32[]{:S(2)}) %all-to-all-start) | async-done | bytes 131104 | tf_op jit(solution)/shard_map/all_to_all | solution.py:155
  25.4 5.8 %all-to-all-start.1 = ((bf16[32,16,128]{2,1,0:T(8,128)(2,1)}), bf16[32,16,128]{2,1,0:T(8,128)(2,1)S(1)}, u32[]{:S(2)}, u32[]{:S(2)}) async-start(bf16[32,16,128]{2,1,0:T(8,128)(2,1)} %broadcast_in_dim.3), calls=%async_computation.1 | async-start | bytes 262144 | tf_op jit(solution)/shard_map/all_to_all | solution.py:155
  31.2 2.7 %collective-permute-start.10 = (bf16[192,1024]{1,0:T(8,128)(2,1)S(1)}, bf16[192,1024]{1,0:T(8,128)(2,1)S(1)}, u32[]{:S(2)}, u32[]{:S(2)}) collective-permute-start(bf16[192,1024]{1,0:T(8,128)(2,1)S(1)} %get-tuple-element.27.refs_0_), channel_id=1, source_target_pairs={{0,32},{32,0},{1,33},{33,1},{2,34},{34,2},{3,35},{35,3},{4,36},{36... | collective-permute-start | bytes 1179656 | tf_op jit(solution)/shard_map/ppermute | solution.py:194
  36.1 2.5 %collective-permute-start.5 = (bf16[128,1024]{1,0:T(8,128)(2,1)}, bf16[128,1024]{1,0:T(8,128)(2,1)S(1)}, u32[]{:S(2)}, u32[]{:S(2)}) collective-permute-start(bf16[128,1024]{1,0:T(8,128)(2,1)} %get-tuple-element.33), channel_id=1, source_target_pairs={{0,128},{64,192},{128,0},{192,64},{1,129},{65,193},{129,1},{193,65... | collective-permute-start | bytes 786440 | tf_op jit(solution)/shard_map/ppermute | solution.py:200
  40.8 2.7 %collective-permute-start.11 = (bf16[3,64,1024]{2,1,0:T(8,128)(2,1)S(1)}, bf16[3,64,1024]{2,1,0:T(8,128)(2,1)S(1)}, u32[]{:S(2)}, u32[]{:S(2)}) collective-permute-start(bf16[3,64,1024]{2,1,0:T(8,128)(2,1)S(1)} %shard_map.53.refs_3_), channel_id=1, source_target_pairs={{0,32},{32,0},{1,33},{33,1},{2,34},{34,2},{3,35},{35,3},{4,36},{36... | collective-permute-start | bytes 1179656 | tf_op jit(solution)/shard_map/ppermute | solution.py:203
  43.5 1.2 %collective-permute-done.10.refs_12_.refs_4_.own_got = bf16[192,1024]{1,0:T(8,128)(2,1)S(1)} collective-permute-done((bf16[192,1024]{1,0:T(8,128)(2,1)S(1)}, bf16[192,1024]{1,0:T(8,128)(2,1)S(1)}, u32[]{:S(2)}, u32[]{:S(2)}) %collective-permute-start.10) | collective-permute-done | bytes 393248 | tf_op jit(solution)/shard_map/ppermute | solution.py:194
  44.8 2.5 %collective-permute-start.15 = (bf16[3,128,1024]{2,1,0:T(8,128)(2,1)S(1)}, bf16[3,128,1024]{2,1,0:T(8,128)(2,1)S(1)}, u32[]{:S(2)}, u32[]{:S(2)}) collective-permute-start(bf16[3,128,1024]{2,1,0:T(8,128)(2,1)S(1)} %shard_map.56), channel_id=1, source_target_pairs={{0,32},{32,0},{1,33},{33,1},{2,34},{34,2},{3,35},{35,3},{4,36},{36... | collective-permute-start | bytes 2359304 | tf_op jit(solution)/shard_map/ppermute | solution.py:204
  47.7 2.5 %collective-permute-done.5.refs_6_ = bf16[128,1024]{1,0:T(8,128)(2,1)S(1)} collective-permute-done((bf16[128,1024]{1,0:T(8,128)(2,1)}, bf16[128,1024]{1,0:T(8,128)(2,1)S(1)}, u32[]{:S(2)}, u32[]{:S(2)}) %collective-permute-start.5) | collective-permute-done | bytes 262176 | tf_op jit(solution)/shard_map/ppermute | solution.py:200
  50.7 3.2 %collective-permute-start.9 = (bf16[32,16,128]{2,1,0:T(8,128)(2,1)S(1)}, bf16[32,16,128]{2,1,0:T(8,128)(2,1)S(1)}, u32[]{:S(2)}, u32[]{:S(2)}) collective-permute-start(bf16[32,16,128]{2,1,0:T(8,128)(2,1)S(1)} %all-to-all-done.1.refs_3_.refs_8_), channel_id=1, source_target_pairs={{0,192},{64,0},{128,64},{192,128},{1,193},{65,1},{129,65},{193,129... | collective-permute-start | bytes 393224 | tf_op jit(solution)/shard_map/ppermute | solution.py:196
  53.8 2.0 %collective-permute-done.8.refs_10_ = bf16[32,16,128]{2,1,0:T(8,128)(2,1)S(1)} collective-permute-done((bf16[32,16,128]{2,1,0:T(8,128)(2,1)S(1)}, bf16[32,16,128]{2,1,0:T(8,128)(2,1)S(1)}, u32[]{:S(2)}, u32[]{:S(2)}) %collective-permute-start.8) | collective-permute-done | bytes 131104 | tf_op jit(solution)/shard_map/ppermute | solution.py:196
  59.1 1.3 %collective-permute-start.16 = (bf16[256,1024]{1,0:T(8,128)(2,1)S(1)}, bf16[256,1024]{1,0:T(8,128)(2,1)S(1)}, u32[]{:S(2)}, u32[]{:S(2)}) collective-permute-start(bf16[256,1024]{1,0:T(8,128)(2,1)S(1)} %get-tuple-element.40.refs_4_), channel_id=1, source_target_pairs={{0,1},{1,0},{2,3},{3,2},{4,5},{5,4},{6,7},{7,6},{8,9},{9,8},{10,11... | collective-permute-start | bytes 1572872 | tf_op jit(solution)/shard_map/ppermute | solution.py:216
  60.5 8.0 %collective-permute-done.15.jac_got = bf16[3,128,1024]{2,1,0:T(8,128)(2,1)S(1)} collective-permute-done((bf16[3,128,1024]{2,1,0:T(8,128)(2,1)S(1)}, bf16[3,128,1024]{2,1,0:T(8,128)(2,1)S(1)}, u32[]{:S(2)}, u32[]{:S(2)}) %collective-permute-start.15) | collective-permute-done | bytes 786464 | tf_op jit(solution)/shard_map/ppermute | solution.py:204
  68.5 2.2 %shard_map.57 = bf16[4,512,128]{2,1,0:T(8,128)(2,1)} custom-call(bf16[192,1024]{1,0:T(8,128)(2,1)S(1)} %collective-permute-done.10.refs_12_.refs_4_.own_got, bf16[3,128,1024]{2,1,0:T(8,128)(2,1)S(1)} %collective-permute-done.15.jac_got, bf16[192,1024]{1,0:T(8,128)(2,1)S(1)} %get-tuple-element.27.refs_0_, ...), custom_call_target="tpu_custom_call" | custom-call | flops 1073741824 | bytes 2097152 | tf_op jit(solution)/shard_map/pallas_call | solution.py:27
  70.7 11.5 %all-to-all-start.2 = ((bf16[64,32,128]{2,1,0:T(8,128)(2,1)}), bf16[64,32,128]{2,1,0:T(8,128)(2,1)S(1)}, u32[]{:S(2)}, u32[]{:S(2)}) async-start(bf16[64,32,128]{2,1,0:T(8,128)(2,1)} %bitcast.1), calls=%async_computation.2 | async-start | bytes 1048576 | tf_op jit(solution)/shard_map/all_to_all | solution.py:155
  82.2 2.5 %collective-permute-start.12 = (bf16[128,1024]{1,0:T(8,128)(2,1)S(1)}, bf16[128,1024]{1,0:T(8,128)(2,1)S(1)}, u32[]{:S(2)}, u32[]{:S(2)}) collective-permute-start(bf16[128,1024]{1,0:T(8,128)(2,1)S(1)} %copy-done.8), channel_id=1, source_target_pairs={{0,192},{64,0},{128,64},{192,128},{1,193},{65,1},{129,65},{193,129... | collective-permute-start | bytes 786440 | tf_op jit(solution)/shard_map/ppermute | solution.py:215
  85.8 8.0 %collective-permute-done.12.refs_1_ = bf16[128,1024]{1,0:T(8,128)(2,1)S(1)} collective-permute-done((bf16[128,1024]{1,0:T(8,128)(2,1)S(1)}, bf16[128,1024]{1,0:T(8,128)(2,1)S(1)}, u32[]{:S(2)}, u32[]{:S(2)}) %collective-permute-start.12) | collective-permute-done | bytes 262176 | tf_op jit(solution)/shard_map/ppermute | solution.py:215
  93.8 3.7 %collective-permute-done.13.refs_2_ = bf16[128,1024]{1,0:T(8,128)(2,1)S(1)} collective-permute-done((bf16[128,1024]{1,0:T(8,128)(2,1)S(1)}, bf16[128,1024]{1,0:T(8,128)(2,1)S(1)}, u32[]{:S(2)}, u32[]{:S(2)}) %collective-permute-start.13) | collective-permute-done | bytes 262176 | tf_op jit(solution)/shard_map/ppermute | solution.py:215
  97.5 7.0 %collective-permute-done.14.refs_3_ = bf16[128,1024]{1,0:T(8,128)(2,1)S(1)} collective-permute-done((bf16[128,1024]{1,0:T(8,128)(2,1)S(1)}, bf16[128,1024]{1,0:T(8,128)(2,1)S(1)}, u32[]{:S(2)}, u32[]{:S(2)}) %collective-permute-start.14) | collective-permute-done | bytes 262176 | tf_op jit(solution)/shard_map/ppermute | solution.py:215
  (47 shorter events, 15.1 us)
Async XLA Ops:
  4.3 11.3 %collective-permute-start = (bf16[64,4096]{1,0:T(8,128)(2,1)S(1)}, bf16[64,4096]{1,0:T(8,128)(2,1)S(1)}, u32[]{:S(2)}, u32[]{:S(2)}) collective-permute-start(bf16[64,4096]{1,0:T(8,128)(2,1)S(1)} %get-tuple-element.22), channel_id=1, source_target_pairs={{0,1},{1,0},{2,3},{3,2},{4,5},{5,4},{6,7},{7,6},{8,9},{9,8},{10,11... | collective-permute-start | bytes 1572872 | tf_op jit(solution)/shard_map/ppermute | solution.py:182
  7.6 17.1 %all-to-all-start = ((bf16[32,16,128]{2,1,0:T(8,128)(2,1)}), bf16[32,16,128]{2,1,0:T(8,128)(2,1)S(1)}, u32[]{:S(2)}, u32[]{:S(2)}) async-start(bf16[32,16,128]{2,1,0:T(8,128)(2,1)} %get-tuple-element.35), calls=%async_computation | async-start | bytes 262144 | tf_op jit(solution)/shard_map/all_to_all | solution.py:155
  15.7 18.3 %copy-start.1 = (bf16[128,4096]{1,0:T(8,128)(2,1)S(1)}, bf16[128,4096]{1,0:T(8,128)(2,1)}, u32[]{:S(2)}) copy-start(bf16[128,4096]{1,0:T(8,128)(2,1)} %carry.1) | copy-start | bytes 3145732
  16.5 19.7 %collective-permute-start.1 = (bf16[192,1024]{1,0:T(8,128)(2,1)S(1)}, bf16[192,1024]{1,0:T(8,128)(2,1)S(1)}, u32[]{:S(2)}, u32[]{:S(2)}) collective-permute-start(bf16[192,1024]{1,0:T(8,128)(2,1)S(1)} %get-tuple-element.28), channel_id=1, source_target_pairs={{0,64},{64,128},{128,192},{192,0},{1,65},{65,129},{129,193},{193,1... | collective-permute-start | bytes 1179656 | tf_op jit(solution)/shard_map/ppermute | solution.py:195
  17.8 20.8 %collective-permute-start.2 = (bf16[192,1024]{1,0:T(8,128)(2,1)}, bf16[192,1024]{1,0:T(8,128)(2,1)S(1)}, u32[]{:S(2)}, u32[]{:S(2)}) collective-permute-start(bf16[192,1024]{1,0:T(8,128)(2,1)} %get-tuple-element.29), channel_id=1, source_target_pairs={{0,128},{64,192},{128,0},{192,64},{1,129},{65,193},{129,1},{193,65... | collective-permute-start | bytes 1179656 | tf_op jit(solution)/shard_map/ppermute | solution.py:195
  20.2 20.1 %collective-permute-start.3 = (bf16[192,1024]{1,0:T(8,128)(2,1)}, bf16[192,1024]{1,0:T(8,128)(2,1)S(1)}, u32[]{:S(2)}, u32[]{:S(2)}) collective-permute-start(bf16[192,1024]{1,0:T(8,128)(2,1)} %get-tuple-element.30), channel_id=1, source_target_pairs={{0,192},{64,0},{128,64},{192,128},{1,193},{65,1},{129,65},{193,129... | collective-permute-start | bytes 1179656 | tf_op jit(solution)/shard_map/ppermute | solution.py:195
  25.4 14.9 %all-to-all-start.1 = ((bf16[32,16,128]{2,1,0:T(8,128)(2,1)}), bf16[32,16,128]{2,1,0:T(8,128)(2,1)S(1)}, u32[]{:S(2)}, u32[]{:S(2)}) async-start(bf16[32,16,128]{2,1,0:T(8,128)(2,1)} %broadcast_in_dim.3), calls=%async_computation.1 | async-start | bytes 262144 | tf_op jit(solution)/shard_map/all_to_all | solution.py:155
  31.2 13.5 %collective-permute-start.10 = (bf16[192,1024]{1,0:T(8,128)(2,1)S(1)}, bf16[192,1024]{1,0:T(8,128)(2,1)S(1)}, u32[]{:S(2)}, u32[]{:S(2)}) collective-permute-start(bf16[192,1024]{1,0:T(8,128)(2,1)S(1)} %get-tuple-element.27.refs_0_), channel_id=1, source_target_pairs={{0,32},{32,0},{1,33},{33,1},{2,34},{34,2},{3,35},{35,3},{4,36},{36... | collective-permute-start | bytes 1179656 | tf_op jit(solution)/shard_map/ppermute | solution.py:194
  35.6 11.7 %collective-permute-start.4 = (bf16[128,1024]{1,0:T(8,128)(2,1)}, bf16[128,1024]{1,0:T(8,128)(2,1)S(1)}, u32[]{:S(2)}, u32[]{:S(2)}) collective-permute-start(bf16[128,1024]{1,0:T(8,128)(2,1)} %get-tuple-element.32), channel_id=1, source_target_pairs={{0,64},{64,128},{128,192},{192,0},{1,65},{65,129},{129,193},{193,1... | collective-permute-start | bytes 786440 | tf_op jit(solution)/shard_map/ppermute | solution.py:200
  36.1 14.0 %collective-permute-start.5 = (bf16[128,1024]{1,0:T(8,128)(2,1)}, bf16[128,1024]{1,0:T(8,128)(2,1)S(1)}, u32[]{:S(2)}, u32[]{:S(2)}) collective-permute-start(bf16[128,1024]{1,0:T(8,128)(2,1)} %get-tuple-element.33), channel_id=1, source_target_pairs={{0,128},{64,192},{128,0},{192,64},{1,129},{65,193},{129,1},{193,65... | collective-permute-start | bytes 786440 | tf_op jit(solution)/shard_map/ppermute | solution.py:200
  38.6 12.1 %collective-permute-start.6 = (bf16[128,1024]{1,0:T(8,128)(2,1)}, bf16[128,1024]{1,0:T(8,128)(2,1)S(1)}, u32[]{:S(2)}, u32[]{:S(2)}) collective-permute-start(bf16[128,1024]{1,0:T(8,128)(2,1)} %get-tuple-element.34), channel_id=1, source_target_pairs={{0,192},{64,0},{128,64},{192,128},{1,193},{65,1},{129,65},{193,129... | collective-permute-start | bytes 786440 | tf_op jit(solution)/shard_map/ppermute | solution.py:200
  40.8 16.1 %copy-start.4 = (bf16[128,1024]{1,0:T(8,128)(2,1)S(1)}, bf16[128,1024]{1,0:T(8,128)(2,1)}, u32[]{:S(2)}) copy-start(bf16[128,1024]{1,0:T(8,128)(2,1)} %copy-done.3) | copy-start | bytes 786436
  40.8 16.1 %collective-permute-start.11 = (bf16[3,64,1024]{2,1,0:T(8,128)(2,1)S(1)}, bf16[3,64,1024]{2,1,0:T(8,128)(2,1)S(1)}, u32[]{:S(2)}, u32[]{:S(2)}) collective-permute-start(bf16[3,64,1024]{2,1,0:T(8,128)(2,1)S(1)} %shard_map.53.refs_3_), channel_id=1, source_target_pairs={{0,32},{32,0},{1,33},{33,1},{2,34},{34,2},{3,35},{35,3},{4,36},{36... | collective-permute-start | bytes 1179656 | tf_op jit(solution)/shard_map/ppermute | solution.py:203
  44.8 23.7 %collective-permute-start.15 = (bf16[3,128,1024]{2,1,0:T(8,128)(2,1)S(1)}, bf16[3,128,1024]{2,1,0:T(8,128)(2,1)S(1)}, u32[]{:S(2)}, u32[]{:S(2)}) collective-permute-start(bf16[3,128,1024]{2,1,0:T(8,128)(2,1)S(1)} %shard_map.56), channel_id=1, source_target_pairs={{0,32},{32,0},{1,33},{33,1},{2,34},{34,2},{3,35},{35,3},{4,36},{36... | collective-permute-start | bytes 2359304 | tf_op jit(solution)/shard_map/ppermute | solution.py:204
  47.3 6.5 %collective-permute-start.7 = (bf16[32,16,128]{2,1,0:T(8,128)(2,1)S(1)}, bf16[32,16,128]{2,1,0:T(8,128)(2,1)S(1)}, u32[]{:S(2)}, u32[]{:S(2)}) collective-permute-start(bf16[32,16,128]{2,1,0:T(8,128)(2,1)S(1)} %all-to-all-done.1.refs_3_.refs_8_), channel_id=1, source_target_pairs={{0,64},{64,128},{128,192},{192,0},{1,65},{65,129},{129,193},{193,1... | collective-permute-start | bytes 393224 | tf_op jit(solution)/shard_map/ppermute | solution.py:196
  50.2 5.7 %collective-permute-start.8 = (bf16[32,16,128]{2,1,0:T(8,128)(2,1)S(1)}, bf16[32,16,128]{2,1,0:T(8,128)(2,1)S(1)}, u32[]{:S(2)}, u32[]{:S(2)}) collective-permute-start(bf16[32,16,128]{2,1,0:T(8,128)(2,1)S(1)} %all-to-all-done.1.refs_3_.refs_8_), channel_id=1, source_target_pairs={{0,128},{64,192},{128,0},{192,64},{1,129},{65,193},{129,1},{193,65... | collective-permute-start | bytes 393224 | tf_op jit(solution)/shard_map/ppermute | solution.py:196
  50.7 6.2 %collective-permute-start.9 = (bf16[32,16,128]{2,1,0:T(8,128)(2,1)S(1)}, bf16[32,16,128]{2,1,0:T(8,128)(2,1)S(1)}, u32[]{:S(2)}, u32[]{:S(2)}) collective-permute-start(bf16[32,16,128]{2,1,0:T(8,128)(2,1)S(1)} %all-to-all-done.1.refs_3_.refs_8_), channel_id=1, source_target_pairs={{0,192},{64,0},{128,64},{192,128},{1,193},{65,1},{129,65},{193,129... | collective-permute-start | bytes 393224 | tf_op jit(solution)/shard_map/ppermute | solution.py:196
  59.1 9.4 %collective-permute-start.16 = (bf16[256,1024]{1,0:T(8,128)(2,1)S(1)}, bf16[256,1024]{1,0:T(8,128)(2,1)S(1)}, u32[]{:S(2)}, u32[]{:S(2)}) collective-permute-start(bf16[256,1024]{1,0:T(8,128)(2,1)S(1)} %get-tuple-element.40.refs_4_), channel_id=1, source_target_pairs={{0,1},{1,0},{2,3},{3,2},{4,5},{5,4},{6,7},{7,6},{8,9},{9,8},{10,11... | collective-permute-start | bytes 1572872 | tf_op jit(solution)/shard_map/ppermute | solution.py:216
  60.5 8.0 %collective-permute-start.17 = (bf16[256,1024]{1,0:T(8,128)(2,1)S(1)}, bf16[256,1024]{1,0:T(8,128)(2,1)S(1)}, u32[]{:S(2)}, u32[]{:S(2)}) collective-permute-start(bf16[256,1024]{1,0:T(8,128)(2,1)S(1)} %get-tuple-element.41.refs_5_), channel_id=1, source_target_pairs={{0,1},{1,0},{2,3},{3,2},{4,5},{5,4},{6,7},{7,6},{8,9},{9,8},{10,11... | collective-permute-start | bytes 1572872 | tf_op jit(solution)/shard_map/ppermute | solution.py:216
  70.7 14.1 %copy-start.6 = (bf16[128,1024]{1,0:T(8,128)(2,1)S(1)}, bf16[128,1024]{1,0:T(8,128)(2,1)}, u32[]{:S(2)}) copy-start(bf16[128,1024]{1,0:T(8,128)(2,1)} %copy-done.5) | copy-start | bytes 786436
  70.7 34.9 %all-to-all-start.2 = ((bf16[64,32,128]{2,1,0:T(8,128)(2,1)}), bf16[64,32,128]{2,1,0:T(8,128)(2,1)S(1)}, u32[]{:S(2)}, u32[]{:S(2)}) async-start(bf16[64,32,128]{2,1,0:T(8,128)(2,1)} %bitcast.1), calls=%async_computation.2 | async-start | bytes 1048576 | tf_op jit(solution)/shard_map/all_to_all | solution.py:155
  82.2 11.6 %collective-permute-start.12 = (bf16[128,1024]{1,0:T(8,128)(2,1)S(1)}, bf16[128,1024]{1,0:T(8,128)(2,1)S(1)}, u32[]{:S(2)}, u32[]{:S(2)}) collective-permute-start(bf16[128,1024]{1,0:T(8,128)(2,1)S(1)} %copy-done.8), channel_id=1, source_target_pairs={{0,192},{64,0},{128,64},{192,128},{1,193},{65,1},{129,65},{193,129... | collective-permute-start | bytes 786440 | tf_op jit(solution)/shard_map/ppermute | solution.py:215
  84.8 12.8 %collective-permute-start.13 = (bf16[128,1024]{1,0:T(8,128)(2,1)S(1)}, bf16[128,1024]{1,0:T(8,128)(2,1)S(1)}, u32[]{:S(2)}, u32[]{:S(2)}) collective-permute-start(bf16[128,1024]{1,0:T(8,128)(2,1)S(1)} %copy-done.6), channel_id=1, source_target_pairs={{0,128},{64,192},{128,0},{192,64},{1,129},{65,193},{129,1},{193,65... | collective-permute-start | bytes 786440 | tf_op jit(solution)/shard_map/ppermute | solution.py:215
  85.1 19.4 %collective-permute-start.14 = (bf16[128,1024]{1,0:T(8,128)(2,1)S(1)}, bf16[128,1024]{1,0:T(8,128)(2,1)S(1)}, u32[]{:S(2)}, u32[]{:S(2)}) collective-permute-start(bf16[128,1024]{1,0:T(8,128)(2,1)S(1)} %get-tuple-element.39), channel_id=1, source_target_pairs={{0,64},{64,128},{128,192},{192,0},{1,65},{65,129},{129,193},{193,1... | collective-permute-start | bytes 786440 | tf_op jit(solution)/shard_map/ppermute | solution.py:215
  (6 other events, 15.9 us)

commit v13 on v12

--- a/solution.py
+++ b/solution.py
@@ -223,6 +223,7 @@
         flops=2 * 512 * 512 * 2048,
         nbytes=2 * MIB,
         vmem=16,
+        behind=(sens_back[1], sens_back[3]),
     )
     shared = over(parts.reshape(X * L * Z, 32, 128), ("x", "l", "z"))
     innovation = call(final_kernel, shape(32, 128, kind=F32), (shared,), VMEM, nbytes=2**19, vmem=4)

time: 107 us -> 103 us (0.963)
  the two profiles are of different devices: /device:TPU:1 before, /device:TPU:4 now
where the time goes in v13:
time: 103 us; the launch traced here: 101 us
  starting transfers between devices  55.4 us (54%)
  waiting for transfers between devices  30.5 us (30%)
  Pallas kernels  8.32 us (8%)
  local copies, waits for them, and re-layouts  6.1 us (6%)
    all_to_all x3, starting transfers between devices, over(): return lax.all_to_all(value, axes, split_axis=0, concat_axis=0, tiled=True)  25.7 us
    ppermute x3, waiting for transfers between devices, body(): lax.ppermute(sens[d], 'x', ring(-d))  18.6 us
    ppermute x6, starting transfers between devices, body(): lax.ppermute(packed[d], 'x', ring(d))  8.44 us
    ppermute x3, starting transfers between devices, body(): panels = [panel] + [lax.ppermute(panel, 'x', ring(d)) for d in range(1, X)]  8.4 us
    pallas_call x9, Pallas kernels, call(): pl.pallas_call(kernel, out_shape=outs, in_specs=[spec] * len(ins) + [ANY]...  8.32 us
    all_to_all x3, waiting for transfers between devices, over(): return lax.all_to_all(value, axes, split_axis=0, concat_axis=0, tiled=True)  8.03 us
    unnamed x16, local copies, waits for them, and re-layouts  5.43 us
    ppermute x3, waiting for transfers between devices, body(): panels = [panel] + [lax.ppermute(panel, 'x', ring(d)) for d in range(1, X)]  3.86 us
  transfers between devices with their start and end apart: 21, of which 7 were waited for; matrix products, arithmetic and copies ran while one was open for 1% of the time, Pallas kernels for 4%

profile of v13, /device:TPU:4, one launch (start us, length us, event | category | flops | bytes accessed | tf_op | source)
XLA Modules:
  0.0 101.2 jit_solution(5282152621462093497)
XLA Ops:
  0.6 1.2 %copy-done = bf16[128,4096]{1,0:T(8,128)(2,1)S(1)} copy-done((bf16[128,4096]{1,0:T(8,128)(2,1)S(1)}, bf16[128,4096]{1,0:T(8,128)(2,1)}, u32[]{:S(2)}) %copy-start) | copy-done | bytes 1048600
  2.9 1.3 %shard_map.50 = (bf16[64,4096]{1,0:T(8,128)(2,1)S(1)}, bf16[32,16,128]{2,1,0:T(8,128)(2,1)}, bf16[192,1024]{1,0:T(8,128)(2,1)S(1)}, bf16[192,1024]{1,0:T(8,128)(...) custom-call(bf16[128,4096]{1,0:T(8,128)(2,1)S(1)} %copy-done, bf16[64,4096]{1,0:T(8,128)(2,1)S(1)} %copy-done.2), custom_call_target="tpu_custom_call" | custom-call | bytes 4194304 | tf_op jit(solution)/shard_map/pallas_call | solution.py:27
  5.0 10.0 %all-to-all-start = ((bf16[32,16,128]{2,1,0:T(8,128)(2,1)}), bf16[32,16,128]{2,1,0:T(8,128)(2,1)S(1)}, u32[]{:S(2)}, u32[]{:S(2)}) async-start(bf16[32,16,128]{2,1,0:T(8,128)(2,1)} %get-tuple-element.35), calls=%async_computation | async-start | bytes 262144 | tf_op jit(solution)/shard_map/all_to_all | solution.py:155
  17.5 1.2 %collective-permute-start.1 = (bf16[192,1024]{1,0:T(8,128)(2,1)S(1)}, bf16[192,1024]{1,0:T(8,128)(2,1)S(1)}, u32[]{:S(2)}, u32[]{:S(2)}) collective-permute-start(bf16[192,1024]{1,0:T(8,128)(2,1)S(1)} %get-tuple-element.28), channel_id=1, source_target_pairs={{0,64},{64,128},{128,192},{192,0},{1,65},{65,129},{129,193},{193,1... | collective-permute-start | bytes 1179656 | tf_op jit(solution)/shard_map/ppermute | solution.py:195
  19.5 1.1 %collective-permute-start.3 = (bf16[192,1024]{1,0:T(8,128)(2,1)}, bf16[192,1024]{1,0:T(8,128)(2,1)S(1)}, u32[]{:S(2)}, u32[]{:S(2)}) collective-permute-start(bf16[192,1024]{1,0:T(8,128)(2,1)} %copy-done.5), channel_id=1, source_target_pairs={{0,192},{64,0},{128,64},{192,128},{1,193},{65,1},{129,65},{193,129... | collective-permute-start | bytes 1179656 | tf_op jit(solution)/shard_map/ppermute | solution.py:195
  20.6 4.8 %all-to-all-done = bf16[32,16,128]{2,1,0:T(8,128)(2,1)S(1)} async-done(((bf16[32,16,128]{2,1,0:T(8,128)(2,1)}), bf16[32,16,128]{2,1,0:T(8,128)(2,1)S(1)}, u32[]{:S(2)}, u32[]{:S(2)}) %all-to-all-start) | async-done | bytes 131104 | tf_op jit(solution)/shard_map/all_to_all | solution.py:155
  26.1 3.8 %all-to-all-start.1 = ((bf16[32,16,128]{2,1,0:T(8,128)(2,1)}), bf16[32,16,128]{2,1,0:T(8,128)(2,1)S(1)}, u32[]{:S(2)}, u32[]{:S(2)}) async-start(bf16[32,16,128]{2,1,0:T(8,128)(2,1)} %broadcast_in_dim.3), calls=%async_computation.1 | async-start | bytes 262144 | tf_op jit(solution)/shard_map/all_to_all | solution.py:155
  30.0 3.0 %collective-permute-start.10 = (bf16[192,1024]{1,0:T(8,128)(2,1)S(1)}, bf16[192,1024]{1,0:T(8,128)(2,1)S(1)}, u32[]{:S(2)}, u32[]{:S(2)}) collective-permute-start(bf16[192,1024]{1,0:T(8,128)(2,1)S(1)} %get-tuple-element.27.refs_0_), channel_id=1, source_target_pairs={{0,32},{32,0},{1,33},{33,1},{2,34},{34,2},{3,35},{35,3},{4,36},{36... | collective-permute-start | bytes 1179656 | tf_op jit(solution)/shard_map/ppermute | solution.py:194
  34.6 1.2 %collective-permute-start.4 = (bf16[128,1024]{1,0:T(8,128)(2,1)}, bf16[128,1024]{1,0:T(8,128)(2,1)S(1)}, u32[]{:S(2)}, u32[]{:S(2)}) collective-permute-start(bf16[128,1024]{1,0:T(8,128)(2,1)} %get-tuple-element.32), channel_id=1, source_target_pairs={{0,64},{64,128},{128,192},{192,0},{1,65},{65,129},{129,193},{193,1... | collective-permute-start | bytes 786440 | tf_op jit(solution)/shard_map/ppermute | solution.py:200
  35.8 2.1 %collective-permute-start.5 = (bf16[128,1024]{1,0:T(8,128)(2,1)}, bf16[128,1024]{1,0:T(8,128)(2,1)S(1)}, u32[]{:S(2)}, u32[]{:S(2)}) collective-permute-start(bf16[128,1024]{1,0:T(8,128)(2,1)} %get-tuple-element.33), channel_id=1, source_target_pairs={{0,128},{64,192},{128,0},{192,64},{1,129},{65,193},{129,1},{193,65... | collective-permute-start | bytes 786440 | tf_op jit(solution)/shard_map/ppermute | solution.py:200
  37.9 2.0 %collective-permute-start.6 = (bf16[128,1024]{1,0:T(8,128)(2,1)}, bf16[128,1024]{1,0:T(8,128)(2,1)S(1)}, u32[]{:S(2)}, u32[]{:S(2)}) collective-permute-start(bf16[128,1024]{1,0:T(8,128)(2,1)} %get-tuple-element.34), channel_id=1, source_target_pairs={{0,192},{64,0},{128,64},{192,128},{1,193},{65,1},{129,65},{193,129... | collective-permute-start | bytes 786440 | tf_op jit(solution)/shard_map/ppermute | solution.py:200
  41.0 3.0 %collective-permute-start.11 = (bf16[3,64,1024]{2,1,0:T(8,128)(2,1)S(1)}, bf16[3,64,1024]{2,1,0:T(8,128)(2,1)S(1)}, u32[]{:S(2)}, u32[]{:S(2)}) collective-permute-start(bf16[3,64,1024]{2,1,0:T(8,128)(2,1)S(1)} %shard_map.53.refs_3_), channel_id=1, source_target_pairs={{0,32},{32,0},{1,33},{33,1},{2,34},{34,2},{3,35},{35,3},{4,36},{36... | collective-permute-start | bytes 1179656 | tf_op jit(solution)/shard_map/ppermute | solution.py:203
  44.1 2.6 %collective-permute-start.15 = (bf16[3,128,1024]{2,1,0:T(8,128)(2,1)S(1)}, bf16[3,128,1024]{2,1,0:T(8,128)(2,1)S(1)}, u32[]{:S(2)}, u32[]{:S(2)}) collective-permute-start(bf16[3,128,1024]{2,1,0:T(8,128)(2,1)S(1)} %shard_map.56), channel_id=1, source_target_pairs={{0,32},{32,0},{1,33},{33,1},{2,34},{34,2},{3,35},{35,3},{4,36},{36... | collective-permute-start | bytes 2359304 | tf_op jit(solution)/shard_map/ppermute | solution.py:204
  46.8 3.4 %collective-permute-start.7 = (bf16[32,16,128]{2,1,0:T(8,128)(2,1)S(1)}, bf16[32,16,128]{2,1,0:T(8,128)(2,1)S(1)}, u32[]{:S(2)}, u32[]{:S(2)}) collective-permute-start(bf16[32,16,128]{2,1,0:T(8,128)(2,1)S(1)} %all-to-all-done.1.refs_3_.refs_8_), channel_id=1, source_target_pairs={{0,64},{64,128},{128,192},{192,0},{1,65},{65,129},{129,193},{193,1... | collective-permute-start | bytes 393224 | tf_op jit(solution)/shard_map/ppermute | solution.py:196
  50.2 2.4 %collective-permute-start.8 = (bf16[32,16,128]{2,1,0:T(8,128)(2,1)S(1)}, bf16[32,16,128]{2,1,0:T(8,128)(2,1)S(1)}, u32[]{:S(2)}, u32[]{:S(2)}) collective-permute-start(bf16[32,16,128]{2,1,0:T(8,128)(2,1)S(1)} %all-to-all-done.1.refs_3_.refs_8_), channel_id=1, source_target_pairs={{0,128},{64,192},{128,0},{192,64},{1,129},{65,193},{129,1},{193,65... | collective-permute-start | bytes 393224 | tf_op jit(solution)/shard_map/ppermute | solution.py:196
  52.5 2.6 %collective-permute-start.9 = (bf16[32,16,128]{2,1,0:T(8,128)(2,1)S(1)}, bf16[32,16,128]{2,1,0:T(8,128)(2,1)S(1)}, u32[]{:S(2)}, u32[]{:S(2)}) collective-permute-start(bf16[32,16,128]{2,1,0:T(8,128)(2,1)S(1)} %all-to-all-done.1.refs_3_.refs_8_), channel_id=1, source_target_pairs={{0,192},{64,0},{128,64},{192,128},{1,193},{65,1},{129,65},{193,129... | collective-permute-start | bytes 393224 | tf_op jit(solution)/shard_map/ppermute | solution.py:196
  55.2 3.0 %collective-permute-done.8.refs_10_ = bf16[32,16,128]{2,1,0:T(8,128)(2,1)S(1)} collective-permute-done((bf16[32,16,128]{2,1,0:T(8,128)(2,1)S(1)}, bf16[32,16,128]{2,1,0:T(8,128)(2,1)S(1)}, u32[]{:S(2)}, u32[]{:S(2)}) %collective-permute-start.8) | collective-permute-done | bytes 131104 | tf_op jit(solution)/shard_map/ppermute | solution.py:196
  60.5 1.5 %collective-permute-start.12 = (bf16[128,1024]{1,0:T(8,128)(2,1)S(1)}, bf16[128,1024]{1,0:T(8,128)(2,1)S(1)}, u32[]{:S(2)}, u32[]{:S(2)}) collective-permute-start(bf16[128,1024]{1,0:T(8,128)(2,1)S(1)} %get-tuple-element.37), channel_id=1, source_target_pairs={{0,192},{64,0},{128,64},{192,128},{1,193},{65,1},{129,65},{193,129... | collective-permute-start | bytes 786440 | tf_op jit(solution)/shard_map/ppermute | solution.py:215
  62.0 1.7 %collective-permute-start.14 = (bf16[128,1024]{1,0:T(8,128)(2,1)S(1)}, bf16[128,1024]{1,0:T(8,128)(2,1)S(1)}, u32[]{:S(2)}, u32[]{:S(2)}) collective-permute-start(bf16[128,1024]{1,0:T(8,128)(2,1)S(1)} %get-tuple-element.39), channel_id=1, source_target_pairs={{0,64},{64,128},{128,192},{192,0},{1,65},{65,129},{129,193},{193,1... | collective-permute-start | bytes 786440 | tf_op jit(solution)/shard_map/ppermute | solution.py:215
  63.7 6.6 %collective-permute-done.12.refs_1_.refs_8_ = bf16[128,1024]{1,0:T(8,128)(2,1)S(1)} collective-permute-done((bf16[128,1024]{1,0:T(8,128)(2,1)S(1)}, bf16[128,1024]{1,0:T(8,128)(2,1)S(1)}, u32[]{:S(2)}, u32[]{:S(2)}) %collective-permute-start.12) | collective-permute-done | bytes 262176 | tf_op jit(solution)/shard_map/ppermute | solution.py:215
  70.3 2.2 %shard_map.57 = bf16[4,512,128]{2,1,0:T(8,128)(2,1)} custom-call(bf16[192,1024]{1,0:T(8,128)(2,1)S(1)} %collective-permute-done.10.refs_12_.refs_4_.own_got, bf16[3,128,1024]{2,1,0:T(8,128)(2,1)S(1)} %collective-permute-done.15.jac_got, bf16[192,1024]{1,0:T(8,128)(2,1)S(1)} %get-tuple-element.27.refs_0_, ...), custom_call_target="tpu_custom_call" | custom-call | flops 1073741824 | bytes 2097152 | tf_op jit(solution)/shard_map/pallas_call | solution.py:27
  72.5 11.9 %all-to-all-start.2 = ((bf16[64,32,128]{2,1,0:T(8,128)(2,1)}), bf16[64,32,128]{2,1,0:T(8,128)(2,1)S(1)}, u32[]{:S(2)}, u32[]{:S(2)}) async-start(bf16[64,32,128]{2,1,0:T(8,128)(2,1)} %bitcast.1), calls=%async_computation.2 | async-start | bytes 1048576 | tf_op jit(solution)/shard_map/all_to_all | solution.py:155
  84.8 12.0 %collective-permute-done.13.refs_2_ = bf16[128,1024]{1,0:T(8,128)(2,1)S(1)} collective-permute-done((bf16[128,1024]{1,0:T(8,128)(2,1)S(1)}, bf16[128,1024]{1,0:T(8,128)(2,1)S(1)}, u32[]{:S(2)}, u32[]{:S(2)}) %collective-permute-start.13) | collective-permute-done | bytes 262176 | tf_op jit(solution)/shard_map/ppermute | solution.py:215
  97.8 2.6 %all-to-all-done.2.got = bf16[64,32,128]{2,1,0:T(8,128)(2,1)S(1)} async-done(((bf16[64,32,128]{2,1,0:T(8,128)(2,1)}), bf16[64,32,128]{2,1,0:T(8,128)(2,1)S(1)}, u32[]{:S(2)}, u32[]{:S(2)}) %all-to-all-start.2) | async-done | bytes 524320 | tf_op jit(solution)/shard_map/all_to_all | solution.py:155
  (45 shorter events, 13.1 us)
Async XLA Ops:
  0.6 1.2 %copy-start = (bf16[128,4096]{1,0:T(8,128)(2,1)S(1)}, bf16[128,4096]{1,0:T(8,128)(2,1)}, u32[]{:S(2)}) copy-start(bf16[128,4096]{1,0:T(8,128)(2,1)} %jac.1) | copy-start | bytes 3145732
  5.0 10.0 %collective-permute-start = (bf16[64,4096]{1,0:T(8,128)(2,1)S(1)}, bf16[64,4096]{1,0:T(8,128)(2,1)S(1)}, u32[]{:S(2)}, u32[]{:S(2)}) collective-permute-start(bf16[64,4096]{1,0:T(8,128)(2,1)S(1)} %get-tuple-element.22), channel_id=1, source_target_pairs={{0,1},{1,0},{2,3},{3,2},{4,5},{5,4},{6,7},{7,6},{8,9},{9,8},{10,11... | collective-permute-start | bytes 1572872 | tf_op jit(solution)/shard_map/ppermute | solution.py:182
  5.0 20.4 %all-to-all-start = ((bf16[32,16,128]{2,1,0:T(8,128)(2,1)}), bf16[32,16,128]{2,1,0:T(8,128)(2,1)S(1)}, u32[]{:S(2)}, u32[]{:S(2)}) async-start(bf16[32,16,128]{2,1,0:T(8,128)(2,1)} %get-tuple-element.35), calls=%async_computation | async-start | bytes 262144 | tf_op jit(solution)/shard_map/all_to_all | solution.py:155
  16.0 17.0 %copy-start.1 = (bf16[128,4096]{1,0:T(8,128)(2,1)S(1)}, bf16[128,4096]{1,0:T(8,128)(2,1)}, u32[]{:S(2)}) copy-start(bf16[128,4096]{1,0:T(8,128)(2,1)} %carry.1) | copy-start | bytes 3145732
  17.5 18.3 %collective-permute-start.1 = (bf16[192,1024]{1,0:T(8,128)(2,1)S(1)}, bf16[192,1024]{1,0:T(8,128)(2,1)S(1)}, u32[]{:S(2)}, u32[]{:S(2)}) collective-permute-start(bf16[192,1024]{1,0:T(8,128)(2,1)S(1)} %get-tuple-element.28), channel_id=1, source_target_pairs={{0,64},{64,128},{128,192},{192,0},{1,65},{65,129},{129,193},{193,1... | collective-permute-start | bytes 1179656 | tf_op jit(solution)/shard_map/ppermute | solution.py:195
  18.7 19.2 %collective-permute-start.2 = (bf16[192,1024]{1,0:T(8,128)(2,1)}, bf16[192,1024]{1,0:T(8,128)(2,1)S(1)}, u32[]{:S(2)}, u32[]{:S(2)}) collective-permute-start(bf16[192,1024]{1,0:T(8,128)(2,1)} %get-tuple-element.29), channel_id=1, source_target_pairs={{0,128},{64,192},{128,0},{192,64},{1,129},{65,193},{129,1},{193,65... | collective-permute-start | bytes 1179656 | tf_op jit(solution)/shard_map/ppermute | solution.py:195
  19.5 21.0 %collective-permute-start.3 = (bf16[192,1024]{1,0:T(8,128)(2,1)}, bf16[192,1024]{1,0:T(8,128)(2,1)S(1)}, u32[]{:S(2)}, u32[]{:S(2)}) collective-permute-start(bf16[192,1024]{1,0:T(8,128)(2,1)} %copy-done.5), channel_id=1, source_target_pairs={{0,192},{64,0},{128,64},{192,128},{1,193},{65,1},{129,65},{193,129... | collective-permute-start | bytes 1179656 | tf_op jit(solution)/shard_map/ppermute | solution.py:195
  26.1 14.4 %all-to-all-start.1 = ((bf16[32,16,128]{2,1,0:T(8,128)(2,1)}), bf16[32,16,128]{2,1,0:T(8,128)(2,1)S(1)}, u32[]{:S(2)}, u32[]{:S(2)}) async-start(bf16[32,16,128]{2,1,0:T(8,128)(2,1)} %broadcast_in_dim.3), calls=%async_computation.1 | async-start | bytes 262144 | tf_op jit(solution)/shard_map/all_to_all | solution.py:155
  30.0 14.1 %collective-permute-start.10 = (bf16[192,1024]{1,0:T(8,128)(2,1)S(1)}, bf16[192,1024]{1,0:T(8,128)(2,1)S(1)}, u32[]{:S(2)}, u32[]{:S(2)}) collective-permute-start(bf16[192,1024]{1,0:T(8,128)(2,1)S(1)} %get-tuple-element.27.refs_0_), channel_id=1, source_target_pairs={{0,32},{32,0},{1,33},{33,1},{2,34},{34,2},{3,35},{35,3},{4,36},{36... | collective-permute-start | bytes 1179656 | tf_op jit(solution)/shard_map/ppermute | solution.py:194
  34.6 12.2 %collective-permute-start.4 = (bf16[128,1024]{1,0:T(8,128)(2,1)}, bf16[128,1024]{1,0:T(8,128)(2,1)S(1)}, u32[]{:S(2)}, u32[]{:S(2)}) collective-permute-start(bf16[128,1024]{1,0:T(8,128)(2,1)} %get-tuple-element.32), channel_id=1, source_target_pairs={{0,64},{64,128},{128,192},{192,0},{1,65},{65,129},{129,193},{193,1... | collective-permute-start | bytes 786440 | tf_op jit(solution)/shard_map/ppermute | solution.py:200
  35.8 14.3 %collective-permute-start.5 = (bf16[128,1024]{1,0:T(8,128)(2,1)}, bf16[128,1024]{1,0:T(8,128)(2,1)S(1)}, u32[]{:S(2)}, u32[]{:S(2)}) collective-permute-start(bf16[128,1024]{1,0:T(8,128)(2,1)} %get-tuple-element.33), channel_id=1, source_target_pairs={{0,128},{64,192},{128,0},{192,64},{1,129},{65,193},{129,1},{193,65... | collective-permute-start | bytes 786440 | tf_op jit(solution)/shard_map/ppermute | solution.py:200
  37.9 14.7 %collective-permute-start.6 = (bf16[128,1024]{1,0:T(8,128)(2,1)}, bf16[128,1024]{1,0:T(8,128)(2,1)S(1)}, u32[]{:S(2)}, u32[]{:S(2)}) collective-permute-start(bf16[128,1024]{1,0:T(8,128)(2,1)} %get-tuple-element.34), channel_id=1, source_target_pairs={{0,192},{64,0},{128,64},{192,128},{1,193},{65,1},{129,65},{193,129... | collective-permute-start | bytes 786440 | tf_op jit(solution)/shard_map/ppermute | solution.py:200
  41.0 18.0 %copy-start.7 = (bf16[128,1024]{1,0:T(8,128)(2,1)S(1)}, bf16[128,1024]{1,0:T(8,128)(2,1)}, u32[]{:S(2)}) copy-start(bf16[128,1024]{1,0:T(8,128)(2,1)} %copy-done.6) | copy-start | bytes 786436
  41.0 18.0 %collective-permute-start.11 = (bf16[3,64,1024]{2,1,0:T(8,128)(2,1)S(1)}, bf16[3,64,1024]{2,1,0:T(8,128)(2,1)S(1)}, u32[]{:S(2)}, u32[]{:S(2)}) collective-permute-start(bf16[3,64,1024]{2,1,0:T(8,128)(2,1)S(1)} %shard_map.53.refs_3_), channel_id=1, source_target_pairs={{0,32},{32,0},{1,33},{33,1},{2,34},{34,2},{3,35},{35,3},{4,36},{36... | collective-permute-start | bytes 1179656 | tf_op jit(solution)/shard_map/ppermute | solution.py:203
  44.1 26.2 %collective-permute-start.15 = (bf16[3,128,1024]{2,1,0:T(8,128)(2,1)S(1)}, bf16[3,128,1024]{2,1,0:T(8,128)(2,1)S(1)}, u32[]{:S(2)}, u32[]{:S(2)}) collective-permute-start(bf16[3,128,1024]{2,1,0:T(8,128)(2,1)S(1)} %shard_map.56), channel_id=1, source_target_pairs={{0,32},{32,0},{1,33},{33,1},{2,34},{34,2},{3,35},{35,3},{4,36},{36... | collective-permute-start | bytes 2359304 | tf_op jit(solution)/shard_map/ppermute | solution.py:204
  46.8 8.4 %collective-permute-start.7 = (bf16[32,16,128]{2,1,0:T(8,128)(2,1)S(1)}, bf16[32,16,128]{2,1,0:T(8,128)(2,1)S(1)}, u32[]{:S(2)}, u32[]{:S(2)}) collective-permute-start(bf16[32,16,128]{2,1,0:T(8,128)(2,1)S(1)} %all-to-all-done.1.refs_3_.refs_8_), channel_id=1, source_target_pairs={{0,64},{64,128},{128,192},{192,0},{1,65},{65,129},{129,193},{193,1... | collective-permute-start | bytes 393224 | tf_op jit(solution)/shard_map/ppermute | solution.py:196
  50.2 8.0 %collective-permute-start.8 = (bf16[32,16,128]{2,1,0:T(8,128)(2,1)S(1)}, bf16[32,16,128]{2,1,0:T(8,128)(2,1)S(1)}, u32[]{:S(2)}, u32[]{:S(2)}) collective-permute-start(bf16[32,16,128]{2,1,0:T(8,128)(2,1)S(1)} %all-to-all-done.1.refs_3_.refs_8_), channel_id=1, source_target_pairs={{0,128},{64,192},{128,0},{192,64},{1,129},{65,193},{129,1},{193,65... | collective-permute-start | bytes 393224 | tf_op jit(solution)/shard_map/ppermute | solution.py:196
  52.5 6.5 %collective-permute-start.9 = (bf16[32,16,128]{2,1,0:T(8,128)(2,1)S(1)}, bf16[32,16,128]{2,1,0:T(8,128)(2,1)S(1)}, u32[]{:S(2)}, u32[]{:S(2)}) collective-permute-start(bf16[32,16,128]{2,1,0:T(8,128)(2,1)S(1)} %all-to-all-done.1.refs_3_.refs_8_), channel_id=1, source_target_pairs={{0,192},{64,0},{128,64},{192,128},{1,193},{65,1},{129,65},{193,129... | collective-permute-start | bytes 393224 | tf_op jit(solution)/shard_map/ppermute | solution.py:196
  59.9 10.4 %collective-permute-start.16 = (bf16[256,1024]{1,0:T(8,128)(2,1)S(1)}, bf16[256,1024]{1,0:T(8,128)(2,1)S(1)}, u32[]{:S(2)}, u32[]{:S(2)}) collective-permute-start(bf16[256,1024]{1,0:T(8,128)(2,1)S(1)} %get-tuple-element.40.refs_4_), channel_id=1, source_target_pairs={{0,1},{1,0},{2,3},{3,2},{4,5},{5,4},{6,7},{7,6},{8,9},{9,8},{10,11... | collective-permute-start | bytes 1572872 | tf_op jit(solution)/shard_map/ppermute | solution.py:216
  60.0 10.3 %collective-permute-start.17 = (bf16[256,1024]{1,0:T(8,128)(2,1)S(1)}, bf16[256,1024]{1,0:T(8,128)(2,1)S(1)}, u32[]{:S(2)}, u32[]{:S(2)}) collective-permute-start(bf16[256,1024]{1,0:T(8,128)(2,1)S(1)} %get-tuple-element.41.refs_5_), channel_id=1, source_target_pairs={{0,1},{1,0},{2,3},{3,2},{4,5},{5,4},{6,7},{7,6},{8,9},{9,8},{10,11... | collective-permute-start | bytes 1572872 | tf_op jit(solution)/shard_map/ppermute | solution.py:216
  60.5 9.8 %collective-permute-start.12 = (bf16[128,1024]{1,0:T(8,128)(2,1)S(1)}, bf16[128,1024]{1,0:T(8,128)(2,1)S(1)}, u32[]{:S(2)}, u32[]{:S(2)}) collective-permute-start(bf16[128,1024]{1,0:T(8,128)(2,1)S(1)} %get-tuple-element.37), channel_id=1, source_target_pairs={{0,192},{64,0},{128,64},{192,128},{1,193},{65,1},{129,65},{193,129... | collective-permute-start | bytes 786440 | tf_op jit(solution)/shard_map/ppermute | solution.py:215
  62.0 8.3 %collective-permute-start.14 = (bf16[128,1024]{1,0:T(8,128)(2,1)S(1)}, bf16[128,1024]{1,0:T(8,128)(2,1)S(1)}, u32[]{:S(2)}, u32[]{:S(2)}) collective-permute-start(bf16[128,1024]{1,0:T(8,128)(2,1)S(1)} %get-tuple-element.39), channel_id=1, source_target_pairs={{0,64},{64,128},{128,192},{192,0},{1,65},{65,129},{129,193},{193,1... | collective-permute-start | bytes 786440 | tf_op jit(solution)/shard_map/ppermute | solution.py:215
  72.5 28.0 %all-to-all-start.2 = ((bf16[64,32,128]{2,1,0:T(8,128)(2,1)}), bf16[64,32,128]{2,1,0:T(8,128)(2,1)S(1)}, u32[]{:S(2)}, u32[]{:S(2)}) async-start(bf16[64,32,128]{2,1,0:T(8,128)(2,1)} %bitcast.1), calls=%async_computation.2 | async-start | bytes 1048576 | tf_op jit(solution)/shard_map/all_to_all | solution.py:155
  84.4 12.5 %collective-permute-start.13 = (bf16[128,1024]{1,0:T(8,128)(2,1)S(1)}, bf16[128,1024]{1,0:T(8,128)(2,1)S(1)}, u32[]{:S(2)}, u32[]{:S(2)}) collective-permute-start(bf16[128,1024]{1,0:T(8,128)(2,1)S(1)} %get-tuple-element.38), channel_id=1, source_target_pairs={{0,128},{64,192},{128,0},{192,64},{1,129},{65,193},{129,1},{193,65... | collective-permute-start | bytes 786440 | tf_op jit(solution)/shard_map/ppermute | solution.py:215
  (5 other events, 4.2 us)
